TPU v7x, 32 devices: a whole 2x2x4 slice. The times are simulated.
32 devices in a mesh: row: 4 (over y, x), col: 8 (over z, core).
Axes of the slice: x: 2, y: 2, z: 4, core: 2. Of those that a mesh axis runs over, the one named last changes fastest.
Arguments:
- frontal: bfloat16 [4096, 49152], P('row', 'col')
- sample_cols: bfloat16 [49152, 64], P(('col', 'row')), may hold values from -6 to 6
- leaf_first: int32 [64], replicated, may hold values from 0 to 4064, as said below
- leaf_owner: int32 [64], replicated, may hold values from 0 to 7, as said below
- skeleton: int32 [64, 16], replicated, may hold values from 0 to 4095, as said below
Outputs:
- owner_samples: float32 [256, 2048], P('row', 'col')
- interp: float32 [64, 2048], P('row', 'col')
- worst: float32 [1], replicated
Inputs may be any that keep to these rules, and one draw needn't show every extreme that they name: `leaf_first`: leaves are consecutive and ascending; the first leaf of row group g starts at g * 1024; each row group has 16 leaves whose sizes are 1 to 5 times 32, in 4 runs of four consecutive leaves of together 256 rows. `leaf_owner`: each run of four leaves is owned by at most two devices of the group; the leaves one device owns in its group hold at most 256 rows and number at most 4; in every row group some device reaches both. Each leaf's skeleton rows are 16 distinct rows of that leaf, ascending.
All inputs are finite; a program needn't handle non-finite values.
Results may differ from a plain program's by a relative error of at most 0.0003.
Values may be sent and summed in bfloat16 or wider, within the bound.
No kernel may reach another device: no remote copies, remote signals or barrier semaphores. Data moves between devices by JAX's collectives and lax.ppermute only.
A program may use at most 64 MiB of HBM per device.

v0:
```python
import jax
import jax.numpy as jnp
from jax import lax
from jax.sharding import PartitionSpec as P

LEAF_MOST = 4


def leaf_index(values, leaf_first):
    return jnp.sum((leaf_first[None, :] <= values[:, None]).astype(jnp.int32), axis=1) - 1


def local(frontal, sample_cols, leaf_first, leaf_owner, skeleton):
    highest = lax.Precision.HIGHEST
    group_rows, width = frontal.shape
    samples_count = sample_cols.shape[1]
    skel_count = skeleton.shape[1]
    leaves = leaf_first.shape[0]
    n_col = lax.axis_size("col")
    n_row = lax.axis_size("row")
    per_group = leaves // n_row
    total_rows = group_rows * n_row
    share_rows = group_rows // n_col
    capacity = 2 * share_rows
    row_pos = lax.axis_index("row")
    col_pos = lax.axis_index("col")
    rows = row_pos * group_rows + jnp.arange(group_rows, dtype=jnp.int32)
    row_leaf = leaf_index(rows, leaf_first)
    zero_entry = jnp.zeros((), frontal.dtype)
    piece = lax.all_gather(sample_cols, "row", axis=0, tiled=True)
    span = piece.shape[0]
    cols = col_pos * width + jnp.arange(span, dtype=jnp.int32)
    col_leaf = leaf_index(cols, leaf_first)
    same = (row_leaf[:, None] == col_leaf[None, :]) & (cols[None, :] < total_rows)
    kept = jnp.where(same, zero_entry, frontal)
    partial_value = jnp.dot(kept, piece, preferred_element_type=jnp.float32)
    ends = jnp.concatenate([leaf_first[1:], jnp.full((1,), total_rows, jnp.int32)])
    sizes = ends - leaf_first
    leaf_ids = jnp.arange(leaves, dtype=jnp.int32)
    group_of = leaf_ids // per_group
    own_hot = (leaf_owner[:, None] == jnp.arange(n_col, dtype=jnp.int32)[None, :]).astype(jnp.int32)
    weighted = (own_hot * sizes[:, None]).reshape(n_row, per_group, n_col)
    before = (jnp.cumsum(weighted, axis=1) - weighted).reshape(leaves, n_col)
    offset = jnp.sum(before * own_hot, axis=1)
    counted = own_hot.reshape(n_row, per_group, n_col)
    earlier = (jnp.cumsum(counted, axis=1) - counted).reshape(leaves, n_col)
    rank = jnp.sum(earlier * own_hot, axis=1)
    owned = (leaf_owner == col_pos) & (group_of == row_pos)
    slots = jnp.arange(capacity, dtype=jnp.int32)
    slot_hit = (
        owned[None, :]
        & (offset[None, :] <= slots[:, None])
        & (slots[:, None] < (offset + sizes)[None, :])
    )
    slot_hit_int = slot_hit.astype(jnp.int32)
    valid = jnp.any(slot_hit, axis=1)
    local_row = (
        jnp.sum(slot_hit_int * (leaf_first[None, :] + slots[:, None] - offset[None, :]), axis=1)
        - row_pos * group_rows
    )
    local_row = jnp.clip(local_row, 0, group_rows - 1)
    valid_float = valid[:, None].astype(jnp.float32)
    summed = lax.psum(partial_value, "col")
    mine = jnp.take(summed, local_row, axis=0) * valid_float
    select = owned[None, :] & (rank[None, :] == jnp.arange(LEAF_MOST, dtype=jnp.int32)[:, None])
    select_int = select.astype(jnp.int32)
    present = jnp.any(select, axis=1).astype(jnp.float32)
    skel_slot = jnp.sum(
        select_int[:, :, None] * (offset[:, None] + skeleton - leaf_first[:, None])[None, :, :],
        axis=1,
    )
    skel_slot = jnp.clip(skel_slot, 0, capacity - 1)
    picked = jnp.take(mine, skel_slot.reshape(-1), axis=0).reshape(
        LEAF_MOST, skel_count, samples_count
    )
    picked = picked * present[:, None, None]
    identity = jnp.eye(skel_count, dtype=jnp.float32)
    gram = jnp.einsum("kjp,kip->kji", picked, picked, precision=highest)
    gram = gram + (1.0 - present)[:, None, None] * identity[None, :, :]
    factor = jnp.linalg.cholesky(gram)
    inverse = jax.vmap(lambda lower: jax.scipy.linalg.cho_solve((lower, True), identity))(factor)
    slot_rank = jnp.sum(slot_hit_int * rank[None, :], axis=1)
    slot_pick = (
        (slot_rank[:, None] == jnp.arange(LEAF_MOST, dtype=jnp.int32)[None, :]) & valid[:, None]
    ).astype(jnp.float32)
    project = jnp.einsum("sp,kjp->skj", mine, picked, precision=highest)
    coeff_all = jnp.einsum("skj,kji->ski", project, inverse, precision=highest)
    coeff = jnp.sum(coeff_all * slot_pick[:, :, None], axis=1)
    rebuilt_all = jnp.einsum("ski,kip->skp", coeff_all, picked, precision=highest)
    rebuilt = jnp.sum(rebuilt_all * slot_pick[:, :, None], axis=1)
    resid = mine - rebuilt
    err = jnp.sum(slot_pick * jnp.sum(resid * resid, axis=1)[:, None], axis=0)
    norm = jnp.sum(slot_pick * jnp.sum(mine * mine, axis=1)[:, None], axis=0)
    ratio = jnp.sqrt(err) / jnp.sqrt(norm + 1e-06)
    local_worst = jnp.max(jnp.where(present > 0.5, ratio, 0.0)).reshape(1)
    worst = lax.pmax(local_worst, ("row", "col"))
    return (mine.T, coeff.T, worst)


def solution(mesh):
    return jax.shard_map(
        local,
        mesh=mesh,
        in_specs=(P("row", "col"), P(("col", "row"), None), P(), P(), P()),
        out_specs=(P("row", "col"), P("row", "col"), P()),
        check_vma=False,
    )
```

profile of v0, /device:TPU:0, one launch (start us, length us, event | category | flops | bytes accessed | tf_op | source)
XLA Modules:
  0.0 150.9 jit_solution(9859000086458799244)
XLA Ops:
  7.2 0.0 all-reduce.2.cloned.1.call-start
  7.3 13.8 %all_gather.3 = bf16[6144,64]{0,1:T(8,128)(2,1)S(1)} all-gather(bf16[1536,64]{0,1:T(8,128)(2,1)} %param.6), channel_id=1, replica_groups=mesh['row'=4,'col'=8] {'row'}, dimensions={0}, use_global_device_ids=true | all-gather | bytes 983040 | tf_op jit(solution)/shard_map/all_gather | solution.py:30
  21.1 0.9 convert_reduce_fusion
  22.0 0.8 convert_reduce_fusion.1
  22.8 0.0 copy-start
  22.8 0.0 copy-start.2
  22.8 0.0 copy-start.1
  22.8 8.1 %fusion = f32[1024,64]{0,1:T(8,128)} fusion(bf16[6144,64]{0,1:T(8,128)(2,1)S(1)} %all_gather.3, bf16[1024,6144]{1,0:T(8,128)(2,1)} %param.5, s32[6144]{0:T(1024)S(1)} %broadcast_add_fusion, s32[1024]{0:T(1024)S(1)} %broadcast_add_fusion.1, pred[6144]{0:T(1024)(128)(4,1)S(1)} %broadcast_compare_fusion), kind=kOutput, calls=%fused_computation.3 | convolution fusion | flops 824180736 | bytes 13666304 | tf_op jit(solution)/shard_map/dot_general | solution.py:36
  31.0 0.0 all-reduce.2.cloned.1.call-update
  31.0 0.0 copy-done
  31.0 0.1 slice.21
  31.1 0.0 copy-done.2
  31.1 0.1 eq.93
  31.2 0.1 fusion.16
  31.2 0.1 add_subtract_fusion.1
  31.3 0.1 mul.125
  31.4 0.1 fusion.17
  31.6 0.3 select_reduce_fusion.3
  31.9 0.1 le.64
  32.0 0.1 eq.100
  32.1 0.1 fusion.33
  32.2 0.1 select_reduce_fusion
  32.3 0.1 fusion.34
  32.4 0.0 copy-done.1
  32.4 0.1 multiply_reduce_fusion.3
  32.7 0.1 min.25
  32.8 53.6 %all-reduce.2.cloned.1.call-done = f32[1024,64]{0,1:T(8,128)} async-done(((f32[1024,64]{0,1:T(8,128)}), f32[1024,64]{0,1:T(8,128)}) %all-reduce.2.cloned.1.call-update) | async-done | bytes 262160 | tf_op jit(solution)/shard_map/psum | solution.py:63
  86.4 1.1 copy.23
  87.6 0.7 gather_fusion
  88.3 0.1 fusion.48
  88.4 0.1 select_multiply_fusion
  88.6 0.6 gather_fusion.1
  89.2 0.3 fusion.18
  89.4 0.3 fusion.6
  89.7 0.7 copy.28
  90.5 0.1 copy.24
  90.5 0.1 fusion.15
  90.6 5.9 %custom-call.11 = f32[4,16,16]{2,1,0:T(8,128)S(1)} custom-call(f32[4,16,16]{2,1,0:T(8,128)S(1)} %fusion.15), custom_call_target="Cholesky" | custom-call | tf_op jit(solution)/shard_map/jit(cholesky)/cholesky | solution.py:80
  96.5 0.1 compare_reduce_fusion
  96.6 0.1 select_bitcast_fusion
  96.7 4.9 %custom-call.12 = f32[4,1,16,16]{2,3,1,0:T(8,128)S(1)} custom-call(f32[4,1,16,16]{3,2,1,0:T(8,128)S(1)} %select_bitcast_fusion), custom_call_target="InvertDiagBlocksLowerTriangular" | custom-call | tf_op jit(solution)/shard_map/vmap(jit(_cho_solve))/triangular_solve | solution.py:81
  101.6 0.3 fusion.12
  101.9 0.2 fusion.10
  102.2 0.8 multiply_reduce_fusion.2
  103.0 0.5 fusion.5
  103.5 0.1 copy.27
  103.6 0.3 multiply_reduce_fusion.1
  103.8 0.2 select_reduce_fusion.6
  104.0 0.6 fusion.36
  104.6 39.4 %pmax.7 = f32[1]{0:T(128)} all-reduce(f32[1]{0:T(128)} %bitcast.12), channel_id=1, replica_groups=mesh['row'=4,'col'=8] {'row','col'}, use_global_device_ids=true, to_apply=%region_21.22 | all-reduce | flops 1 | bytes 8 | tf_op jit(solution)/shard_map/pmax | solution.py:96
  (25 shorter events, 0.3 us)
Async XLA Ops:
  7.2 79.3 %all-reduce.2.cloned.1.call-start = ((), (), s32[]{:S(2)}) async-start(), calls=%async_computation | async-start | bytes 524288 | tf_op jit(solution)/shard_map/psum | solution.py:63
  22.8 8.2 %copy-start = (s32[64]{0:T(128)S(1)}, s32[64]{0:T(128)}, u32[]{:S(2)}) copy-start(s32[64]{0:T(128)} %param.7) | copy-start | bytes 772
  22.8 8.3 %copy-start.2 = (s32[64]{0:T(128)S(1)}, s32[64]{0:T(128)}, u32[]{:S(2)}) copy-start(s32[64]{0:T(128)} %param.8) | copy-start | bytes 772
  22.8 9.6 %copy-start.1 = (s32[64,16]{0,1:T(8,128)S(1)}, s32[64,16]{0,1:T(8,128)}, u32[]{:S(2)}) copy-start(s32[64,16]{0,1:T(8,128)} %param.9) | copy-start | bytes 12292
Sparse Core Ops, SparseCore 0:
  31.1 55.2 all-reduce.1
where the time goes:
time: 151 us
  waiting for transfers between devices  53.6 us (35%)
  blocking collectives  53.2 us (35%)
  other arithmetic  15.3 us (10%)
  between operations  14.3 us (9%)
  matrix products  10.5 us (7%)
  local copies, waits for them, and re-layouts  3.86 us (3%)
    psum x1, waiting for transfers between devices, local(): summed = lax.psum(partial_value, 'col')  53.6 us
    pmax x1, blocking collectives, local(): worst = lax.pmax(local_worst, ('row', 'col'))  39.4 us
    all_gather x1, blocking collectives, local(): piece = lax.all_gather(sample_cols, 'row', axis=0, tiled=True)  13.8 us
    dot_general x1, matrix products, local(): partial_value = jnp.dot(kept, piece, preferred_element_type=jnp.float32)  8.15 us
    another operation x4, other arithmetic, local(): factor = jnp.linalg.cholesky(gram)  6.03 us
    another operation x3, other arithmetic, local(): jax.scipy.linalg.cho_solve((lower, True), identity)  5 us
  transfers between devices with their start and end apart: 1, of which 1 were waited for; matrix products, arithmetic and copies ran while one was open for 1% of the time, Pallas kernels for 0%

commit v1 on v0

v1 whole, which is shorter than its diff:
```python
import functools

import jax
import jax.numpy as jnp
from jax import lax
from jax.experimental import pallas as pl
from jax.experimental.pallas import tpu as pltpu
from jax.sharding import PartitionSpec as P

UNIT = 32
LEAF_MOST = 4
RUN_LEAVES = 4
HIGHEST = lax.Precision.HIGHEST


def nt_dot(a, b, precision=None):
    return lax.dot_general(
        a, b, (((1,), (1,)), ((), ())), precision=precision, preferred_element_type=jnp.float32
    )


def product_kernel(
    tile, n_row, n_col, leaf_first, leaf_owner, frontal, cols, out, total, target, used
):
    group_rows = frontal.shape[0]
    leaves = leaf_first.shape[0]
    per_group = leaves // n_row
    runs = per_group // RUN_LEAVES
    run_rows = group_rows // runs
    capacity = 2 * group_rows // n_col
    half = capacity // 2
    per_owner = capacity // UNIT
    samples = cols.shape[1]
    units = group_rows // UNIT
    step = pl.program_id(0)
    steps = pl.num_programs(0)
    row_pos = lax.axis_index("row")
    col_pos = lax.axis_index("col")
    first_col = col_pos * (steps * tile) + step * tile

    block = cols[0]
    twice = jnp.concatenate([block, block], axis=0)

    @pl.when(step == 0)
    def _():
        total[...] = nt_dot(frontal[...], twice)

        def clear(owner, carry):
            used[owner] = 0
            return carry

        lax.fori_loop(0, n_col, clear, 0)

        def place(unit, leaf):
            row = row_pos * group_rows + unit * UNIT
            later = jnp.minimum(leaf + 1, leaves - 1)
            moved = (leaf + 1 < leaves) & (leaf_first[later] <= row)
            leaf = jnp.where(moved, later, leaf)
            owner = leaf_owner[leaf]
            slot = used[owner]
            used[owner] = slot + 1
            target[unit] = owner * per_owner + slot
            return leaf

        lax.fori_loop(0, units, place, row_pos * per_group)

    @pl.when(step > 0)
    def _():
        total[...] += nt_dot(frontal[...], twice)

    def remove(run, carry):
        begin = row_pos * group_rows + run * run_rows
        inside = begin - first_col

        @pl.when((inside >= 0) & (inside < tile))
        def _():
            at = pl.multiple_of(jnp.clip(inside, 0, tile - run_rows), run_rows)
            rows = pl.ds(pl.multiple_of(run * run_rows, run_rows), run_rows)
            part = frontal[rows, pl.ds(at, run_rows)]
            down = lax.broadcasted_iota(jnp.int32, (run_rows, run_rows), 0) + begin
            across = lax.broadcasted_iota(jnp.int32, (run_rows, run_rows), 1) + begin
            leaf_down = jnp.zeros((run_rows, run_rows), jnp.int32)
            leaf_across = jnp.zeros((run_rows, run_rows), jnp.int32)
            for k in range(1, RUN_LEAVES):
                edge = leaf_first[row_pos * per_group + run * RUN_LEAVES + k]
                leaf_down += (down >= edge).astype(jnp.int32)
                leaf_across += (across >= edge).astype(jnp.int32)
            kept = jnp.where(leaf_down == leaf_across, part.astype(jnp.float32), 0.0)
            near = cols[0, :, pl.ds(at, run_rows)]
            near = jnp.concatenate([near, near], axis=0)
            total[rows, :] -= nt_dot(kept.astype(jnp.bfloat16), near)

        return carry

    lax.fori_loop(0, runs, remove, 0)

    @pl.when(step == steps - 1)
    def _():
        out[...] = jnp.zeros_like(out)
        lane = lax.broadcasted_iota(jnp.int32, (UNIT, 2 * samples), 1) // samples

        def send(unit, carry):
            spot = target[unit]
            owner = spot // per_owner
            slot = lax.rem(spot, per_owner) * UNIT
            side = slot // half
            rows = pl.ds(pl.multiple_of(lax.rem(slot, half), UNIT), UNIT)
            value = total[pl.ds(pl.multiple_of(unit * UNIT, UNIT), UNIT), :]
            out[owner, rows, :] = jnp.where(lane == side, value, out[owner, rows, :])
            return carry

        lax.fori_loop(0, units, send, 0)


def product(frontal, pieces, leaf_first, leaf_owner, n_row, n_col):
    group_rows, width = frontal.shape
    n_piece, samples, depth = pieces.shape
    capacity = 2 * group_rows // n_col
    tile = 512 if depth % 512 == 0 else depth
    per_piece = depth // tile
    return pl.pallas_call(
        functools.partial(product_kernel, tile, n_row, n_col),
        grid=(width // tile,),
        in_specs=[
            pl.BlockSpec(memory_space=pltpu.SMEM),
            pl.BlockSpec(memory_space=pltpu.SMEM),
            pl.BlockSpec((group_rows, tile), lambda i: (0, i)),
            pl.BlockSpec((1, samples, tile), lambda i: (i // per_piece, 0, i % per_piece)),
        ],
        out_specs=pl.BlockSpec((n_col, capacity // 2, 2 * samples), lambda i: (0, 0, 0)),
        out_shape=jax.ShapeDtypeStruct((n_col, capacity // 2, 2 * samples), jnp.float32),
        scratch_shapes=[
            pltpu.VMEM((group_rows, 2 * samples), jnp.float32),
            pltpu.SMEM((group_rows // UNIT,), jnp.int32),
            pltpu.SMEM((n_col,), jnp.int32),
        ],
        compiler_params=pltpu.CompilerParams(vmem_limit_bytes=48 * 2**20),
    )(leaf_first, leaf_owner, frontal, pieces)


def leaf_kernel(
    n_row, leaf_first, leaf_owner, skeleton, parts, mine_out, coeff_out, worst_out, mine, picked
):
    leaves = leaf_first.shape[0]
    per_group = leaves // n_row
    half, wide = parts.shape[1:]
    samples = wide // 2
    capacity = 2 * half
    skel = skeleton.shape[0]
    every = LEAF_MOST * skel
    row_pos = lax.axis_index("row")
    col_pos = lax.axis_index("col")
    group_rows = mine_out.shape[1] * lax.axis_size("col") // 2
    group_end = (row_pos + 1) * group_rows

    total = parts[0]
    for k in range(1, parts.shape[0]):
        total = total + parts[k]
    mine[pl.ds(0, half), :] = total
    mine[pl.ds(half, half), :] = pltpu.roll(total, samples, 1)
    turned = total.T
    mine_t = jnp.concatenate([turned[:samples], turned[samples:]], axis=1)
    mine_out[...] = mine_t

    def find(at, carry):
        count, filled, begins, firsts, names = carry
        leaf = row_pos * per_group + at
        first = leaf_first[leaf]
        following = leaf_first[jnp.minimum(leaf + 1, leaves - 1)]
        end = jnp.where(at + 1 < per_group, following, group_end)
        hit = leaf_owner[leaf] == col_pos
        here = [hit & (count == k) for k in range(LEAF_MOST)]
        begins = tuple(jnp.where(h, filled, v) for h, v in zip(here, begins))
        firsts = tuple(jnp.where(h, first, v) for h, v in zip(here, firsts))
        names = tuple(jnp.where(h, leaf, v) for h, v in zip(here, names))
        filled = jnp.where(hit, filled + end - first, filled)
        return jnp.where(hit, count + 1, count), filled, begins, firsts, names

    zero = jnp.int32(0)
    far = jnp.int32(capacity)
    count, _, begins, firsts, names = lax.fori_loop(
        0,
        per_group,
        find,
        (zero, zero, (far,) * LEAF_MOST, (zero,) * LEAF_MOST, (zero,) * LEAF_MOST),
    )
    for b in range(LEAF_MOST):
        there = count > b
        for k in range(skel):
            at = begins[b] + skeleton[k, names[b]] - firsts[b]
            at = jnp.clip(jnp.where(there, at, 0), 0, capacity - 1)
            row = mine[pl.ds(at, 1), :]
            picked[pl.ds(b * skel + k, 1), :] = jnp.where(there, row, 0.0)
    chosen = picked[:, :samples]

    gram = nt_dot(chosen, chosen, HIGHEST)
    proj = jnp.dot(chosen, mine_t, precision=HIGHEST, preferred_element_type=jnp.float32)

    slot = lax.broadcasted_iota(jnp.int32, (skel, capacity), 1)
    rank = jnp.zeros((skel, capacity), jnp.int32)
    for b in range(1, LEAF_MOST):
        rank += (slot >= begins[b]).astype(jnp.int32)
    hot = [rank == b for b in range(LEAF_MOST)]
    hot_rows = jnp.concatenate([h.astype(jnp.float32) for h in hot], axis=0)

    lane_leaf = lax.broadcasted_iota(jnp.int32, (skel, every), 1) // skel
    lane_row = lax.broadcasted_iota(jnp.int32, (skel, every), 1) % skel
    down = lax.broadcasted_iota(jnp.int32, (skel, every), 0)
    joined = jnp.where((down == lane_row) & (count == 0), 1.0, 0.0)
    for b in range(LEAF_MOST):
        joined += jnp.where(lane_leaf == b, gram[b * skel : (b + 1) * skel], 0.0)
    spread = jnp.concatenate([jnp.where(lane_row == i, joined, 0.0) for i in range(skel)], axis=0)
    system = jnp.dot(spread, hot_rows, precision=HIGHEST, preferred_element_type=jnp.float32)

    lines = [system[i * skel : (i + 1) * skel] for i in range(skel)]
    right = jnp.zeros((skel, capacity), jnp.float32)
    for b in range(LEAF_MOST):
        right += jnp.where(hot[b], proj[b * skel : (b + 1) * skel], 0.0)
    index = lax.broadcasted_iota(jnp.int32, (skel, capacity), 0)
    uppers = []
    pivots = []
    for j in range(skel):
        line = lines[j]
        inverse = 1.0 / line[j : j + 1]
        upper = line * inverse
        uppers.append(upper)
        pivots.append(inverse)
        for i in range(j + 1, skel):
            lines[i] = lines[i] - line[i : i + 1] * upper
        right = right - jnp.where(index > j, upper * right[j : j + 1], 0.0)
    solved = right * jnp.concatenate(pivots, axis=0)
    for j in range(skel - 2, -1, -1):
        known = jnp.where(index > j, uppers[j] * solved, 0.0)
        less = jnp.sum(known, axis=0, keepdims=True)
        solved = jnp.where(index == j, solved - less, solved)
    coeff_out[...] = solved

    weights = jnp.concatenate([jnp.where(h, solved, 0.0) for h in hot], axis=0)
    rebuilt = lax.dot_general(
        chosen,
        weights,
        (((0,), (0,)), ((), ())),
        precision=HIGHEST,
        preferred_element_type=jnp.float32,
    )
    resid = mine_t - rebuilt
    err = jnp.sum(resid * resid, axis=0, keepdims=True)
    norm = jnp.sum(mine_t * mine_t, axis=0, keepdims=True)
    worst = jnp.zeros((1, 1), jnp.float32)
    for b in range(LEAF_MOST):
        near = hot[b][:1]
        err_leaf = jnp.sum(jnp.where(near, err, 0.0), axis=1, keepdims=True)
        norm_leaf = jnp.sum(jnp.where(near, norm, 0.0), axis=1, keepdims=True)
        worst = jnp.maximum(worst, jnp.sqrt(err_leaf) / jnp.sqrt(norm_leaf + 1e-06))
    worst_out[...] = jnp.broadcast_to(worst, worst_out.shape)


def leaf_work(parts, leaf_first, leaf_owner, skeleton, n_row):
    n_col, half, wide = parts.shape
    samples = wide // 2
    skel = skeleton.shape[0]
    return pl.pallas_call(
        functools.partial(leaf_kernel, n_row),
        in_specs=[
            pl.BlockSpec(memory_space=pltpu.SMEM),
            pl.BlockSpec(memory_space=pltpu.SMEM),
            pl.BlockSpec(memory_space=pltpu.SMEM),
            pl.BlockSpec(memory_space=pltpu.VMEM),
        ],
        out_specs=[pl.BlockSpec(memory_space=pltpu.VMEM)] * 3,
        out_shape=[
            jax.ShapeDtypeStruct((samples, 2 * half), jnp.float32),
            jax.ShapeDtypeStruct((skel, 2 * half), jnp.float32),
            jax.ShapeDtypeStruct((1, 128), jnp.float32),
        ],
        scratch_shapes=[
            pltpu.VMEM((2 * half, wide), jnp.float32),
            pltpu.VMEM((LEAF_MOST * skel, wide), jnp.float32),
        ],
        compiler_params=pltpu.CompilerParams(vmem_limit_bytes=32 * 2**20),
    )(leaf_first, leaf_owner, skeleton, parts)


def local(frontal, sample_cols, leaf_first, leaf_owner, skeleton):
    n_col = lax.axis_size("col")
    n_row = lax.axis_size("row")
    pieces = lax.all_gather(sample_cols.T, "row", axis=0)
    sent = product(frontal, pieces, leaf_first, leaf_owner, n_row, n_col)
    parts = lax.all_to_all(sent, "col", 0, 0)
    mine, coeff, worst = leaf_work(parts, leaf_first, leaf_owner, skeleton.T, n_row)
    worst = jnp.max(lax.all_gather(worst, ("row", "col"), axis=0, tiled=True), axis=0)
    return (mine, coeff, worst[:1])


def solution(mesh):
    return jax.shard_map(
        local,
        mesh=mesh,
        in_specs=(P("row", "col"), P(("col", "row"), None), P(), P(), P()),
        out_specs=(P("row", "col"), P("row", "col"), P()),
        check_vma=False,
    )
```

time: 151 us -> 90.6 us (0.60)
  waiting for transfers between devices: 53.6 us -> 0 us
  blocking collectives: 53.2 us -> 71.4 us
  Pallas kernels: 0 us -> 16.2 us
  other arithmetic: 15.3 us -> 0.56 us
  between operations: 14.3 us -> 0.65 us
  matrix products: 10.5 us -> 0 us
  local copies, waits for them, and re-layouts: 3.86 us -> 1.32 us
    psum x1 -> x0, waiting for transfers between devices: 53.6 us -> none  [local(): summed = lax.psum(partial_value, 'col')]
    pmax x1 -> x0, blocking collectives: 39.4 us -> none  [local(): worst = lax.pmax(local_worst, ('row', 'col'))]
    all_gather x1 -> x2, blocking collectives: 13.8 us -> 52.1 us  [the longest x1 38.3 us: local(): lax.all_gather(worst, ('row', 'col'), axis=0, tiled=True)]
    all_to_all x0 -> x1, blocking collectives: none -> 19.3 us  [local(): parts = lax.all_to_all(sent, 'col', 0, 0)]
    pallas_call x0 -> x2, Pallas kernels: none -> 16.2 us  [the longest x1 13.3 us: product(): pl.pallas_call(functools.partial(product_kernel, tile, n_row, n_col), gri...]
    another operation x9 -> x0, other arithmetic: 11.1 us -> none  [the longest x4 6.03 us: local(): factor = jnp.linalg.cholesky(gram)]
    dot_general x5 -> x0, matrix products: 10 us -> none  [the longest x1 8.15 us: local(): partial_value = jnp.dot(kept, piece, preferred_element_type=jnp.float32)]
    reduce_sum x7 -> x0, other arithmetic: 2.65 us -> none  [the longest x2 1.67 us: leaf_index(): jnp.sum((leaf_first[None, :] <= values[:, None]).astype(jnp.int32), axis=1)]
  transfers between devices with their start and end apart: 1 -> 0, of which waited for: 1 -> 0; matrix products, arithmetic and copies ran while one was open for 1% -> 0% of each run, Pallas kernels for 0% -> 0%
where the time goes in v1:
time: 90.6 us; the launch traced here: 90.2 us
  blocking collectives  71.4 us (79%)
  Pallas kernels  16.2 us (18%)
  local copies, waits for them, and re-layouts  1.32 us (1%)
    all_gather x1, blocking collectives, local(): lax.all_gather(worst, ('row', 'col'), axis=0, tiled=True)  38.3 us
    all_to_all x1, blocking collectives, local(): parts = lax.all_to_all(sent, 'col', 0, 0)  19.3 us
    all_gather x1, blocking collectives, local(): pieces = lax.all_gather(sample_cols.T, 'row', axis=0)  13.8 us
    pallas_call x1, Pallas kernels, product(): pl.pallas_call(functools.partial(product_kernel, tile, n_row, n_col), gri...  13.3 us
    pallas_call x1, Pallas kernels, leaf_work(): pl.pallas_call(functools.partial(leaf_kernel, n_row), in_specs=[pl.BlockS...  2.9 us

profile of v1, /device:TPU:0, one launch (start us, length us, event | category | flops | bytes accessed | tf_op | source)
XLA Modules:
  0.0 90.2 jit_solution(15444049980015100194)
XLA Ops:
  0.6 0.0 copy-start
  0.6 13.8 %all-gather = bf16[256,1536]{1,0:T(8,128)(2,1)S(1)} all-gather(bf16[64,1536]{1,0:T(8,128)(2,1)} %bitcast.8), channel_id=2, replica_groups=mesh['row'=4,'col'=8] {'row'}, dimensions={0}, use_global_device_ids=true | all-gather | bytes 983040 | tf_op jit(solution)/shard_map/all_gather | solution.py:287
  14.5 0.0 copy-start.1
  14.5 0.7 copy-done.1
  15.1 0.0 copy-start.2
  15.1 0.7 copy-done.2
  15.8 13.3 %shard_map.76 = f32[8,128,128]{2,1,0:T(8,128)S(1)} custom-call(s32[64]{0:T(128)S(1)} %copy-done.1, s32[64]{0:T(128)S(1)} %copy-done.2, bf16[1024,6144]{1,0:T(8,128)(2,1)} %frontal.1, bf16[4,64,1536]{2,1,0:T(8,128)(2,1)S(1)} %bitcast.5), custom_call_target="tpu_custom_call" | custom-call | tf_op jit(solution)/shard_map/pallas_call | solution.py:121
  29.1 19.3 %all_to_all.5.parts = f32[8,128,128]{2,1,0:T(8,128)S(1)} all-to-all(f32[8,128,128]{2,1,0:T(8,128)S(1)} %shard_map.76), channel_id=1, replica_groups=mesh['row'=4,'col'=8] {'col'}, dimensions={0} | all-to-all | bytes 1048576 | tf_op jit(solution)/shard_map/all_to_all | solution.py:289
  48.4 0.0 copy-done
  48.4 2.9 %shard_map.77 = (f32[64,256]{1,0:T(8,128)}, f32[16,256]{1,0:T(8,128)}, f32[1,128]{1,0:T(1,128)S(1)}) custom-call(s32[64]{0:T(128)S(1)} %copy-done.1, s32[64]{0:T(128)S(1)} %copy-done.2, s32[16,64]{1,0:T(8,128)S(1)} %bitcast.6, f32[8,128,128]{2,1,0:T(8,128)S(1)} %all_to_all.5.parts), custom_call_target="tpu_custom_call" | custom-call | tf_op jit(solution)/shard_map/pallas_call | solution.py:262
  51.3 38.3 %all-gather.1 = f32[32,1,128]{2,1,0:T(1,128)S(1)} all-gather(f32[1,1,128]{2,1,0:T(1,128)S(1)} %bitcast.7), channel_id=1, replica_groups=mesh['row'=4,'col'=8] {'row','col'}, dimensions={0}, use_global_device_ids=true | all-gather | bytes 16896 | tf_op jit(solution)/shard_map/all_gather | solution.py:291
  89.6 0.6 reduce_max.9
Async XLA Ops:
  0.6 47.8 %copy-start = (s32[64,16]{0,1:T(8,128)S(1)}, s32[64,16]{0,1:T(8,128)}, u32[]{:S(2)}) copy-start(s32[64,16]{0,1:T(8,128)} %param.9) | copy-start | bytes 12292
  14.5 0.7 copy-start.1
  15.1 0.7 copy-start.2

commit v2 on v1

v2 whole, which is shorter than its diff:
```python
import functools

import jax
import jax.numpy as jnp
from jax import lax
from jax.experimental import pallas as pl
from jax.experimental.pallas import tpu as pltpu
from jax.sharding import PartitionSpec as P

UNIT = 32
LANES = 128
LEAF_MOST = 4
RUN_LEAVES = 4
HIGHEST = lax.Precision.HIGHEST


def nt_dot(a, b, precision=None):
    return lax.dot_general(
        a, b, (((1,), (1,)), ((), ())), precision=precision, preferred_element_type=jnp.float32
    )


def remove_runs(pick, n_row, frontal, leaf_first, slabs, total):
    group_rows, width = frontal.shape
    depth = slabs[0].shape[1]
    per_group = leaf_first.shape[0] // n_row
    runs = per_group // RUN_LEAVES
    run_rows = group_rows // runs
    row_pos = lax.axis_index("row")
    first_col = lax.axis_index("col") * width

    def remove(at, carry):
        run = at // (run_rows // LANES)
        begin = row_pos * group_rows + run * run_rows
        begin_col = row_pos * group_rows + at * LANES
        inside = begin_col - first_col
        held = (inside >= 0) & (inside < width)
        inside = jnp.clip(inside, 0, width - LANES)
        turn = (inside // depth) ^ row_pos
        for k, slab in zip(pick, slabs):

            @pl.when(held & (turn == k))
            def _():
                rows = pl.ds(pl.multiple_of(run * run_rows, run_rows), run_rows)
                part = frontal[rows, pl.ds(pl.multiple_of(inside, LANES), LANES)]
                down = lax.broadcasted_iota(jnp.int32, part.shape, 0) + begin
                across = lax.broadcasted_iota(jnp.int32, part.shape, 1) + begin_col
                leaf_down = jnp.zeros(part.shape, jnp.int32)
                leaf_across = jnp.zeros(part.shape, jnp.int32)
                for k in range(1, RUN_LEAVES):
                    edge = leaf_first[row_pos * per_group + run * RUN_LEAVES + k]
                    leaf_down += (down >= edge).astype(jnp.int32)
                    leaf_across += (across >= edge).astype(jnp.int32)
                kept = jnp.where(leaf_down == leaf_across, part.astype(jnp.float32), 0.0)
                near = slab[:, pl.ds(pl.multiple_of(lax.rem(inside, depth), LANES), LANES)]
                near = jnp.concatenate([near, near], axis=0)
                total[rows, :] -= nt_dot(kept.astype(jnp.bfloat16), near)

        return carry

    lax.fori_loop(0, group_rows // LANES, remove, 0)


def multiply(pick, frontal, slabs, total, first):
    group_rows = frontal.shape[0]
    depth = slabs[0].shape[1]
    row_pos = lax.axis_index("row")
    part = min(group_rows, 512)

    def rows_of(at, carry):
        rows = pl.ds(pl.multiple_of(at * part, part), part)
        value = None if first else total[rows, :]
        for k, slab in zip(pick, slabs):
            begin = pl.multiple_of((row_pos ^ k) * depth, LANES)
            twice = jnp.concatenate([slab[...], slab[...]], axis=0)
            add = nt_dot(frontal[rows, pl.ds(begin, depth)], twice)
            value = add if value is None else value + add
        total[rows, :] = value
        return carry

    lax.fori_loop(0, group_rows // part, rows_of, 0)


def own_kernel(n_row, n_col, leaf_first, leaf_owner, frontal, slab, total, source, used):
    group_rows = frontal.shape[0]
    leaves = leaf_first.shape[0]
    per_group = leaves // n_row
    per_owner = 2 * group_rows // n_col // UNIT
    units = group_rows // UNIT
    row_pos = lax.axis_index("row")
    multiply((0,), frontal, (slab,), total, True)
    remove_runs((0,), n_row, frontal, leaf_first, (slab,), total)

    def clear(at, carry):
        source[at] = units
        used[at // per_owner] = 0
        return carry

    lax.fori_loop(0, n_col * per_owner, clear, 0)

    def place(unit, leaf):
        row = row_pos * group_rows + unit * UNIT
        later = jnp.minimum(leaf + 1, leaves - 1)
        moved = (leaf + 1 < leaves) & (leaf_first[later] <= row)
        leaf = jnp.where(moved, later, leaf)
        owner = leaf_owner[leaf]
        slot = used[owner]
        used[owner] = slot + 1
        source[owner * per_owner + slot] = unit
        return leaf

    lax.fori_loop(0, units, place, row_pos * per_group)


def rest_kernel(n_row, pick, leaf_first, source, frontal, begun, *refs):
    slabs, (keep, swap, total) = refs[: len(pick)], refs[len(pick) :]
    group_rows = frontal.shape[0]
    chips, half, wide = keep.shape
    per_half = half // UNIT
    samples = wide // 2
    core = lax.rem(lax.axis_index("col"), 2)
    chip = lax.axis_index("col") // 2
    total[pl.ds(0, group_rows), :] = begun[...]
    total[pl.ds(group_rows, UNIT), :] = jnp.zeros((UNIT, wide), jnp.float32)
    multiply(pick, frontal, slabs, total, False)
    remove_runs(pick, n_row, frontal, leaf_first, slabs, total)
    lane = lax.broadcasted_iota(jnp.int32, (UNIT, wide), 1)

    def lay(turn, carry):
        for other, out in ((0, keep), (1, swap)):
            owner = (chip ^ turn) * 2 + (core ^ other)
            for at in range(per_half):
                values = []
                for side in range(2):
                    unit = source[owner * (2 * per_half) + side * per_half + at]
                    values.append(total[pl.ds(pl.multiple_of(unit * UNIT, UNIT), UNIT), :])
                out[turn, pl.ds(at * UNIT, UNIT), :] = jnp.where(lane < samples, *values)
        return carry

    lax.fori_loop(0, chips, lay, 0, unroll=min(chips, 4))


def vmem(count=None):
    spec = pl.BlockSpec(memory_space=pltpu.VMEM)
    return spec if count is None else [spec] * count


def smem():
    return pl.BlockSpec(memory_space=pltpu.SMEM)


def own_product(frontal, slab, leaf_first, leaf_owner, n_row, n_col):
    group_rows, width = frontal.shape
    samples, depth = slab.shape
    per_owner = 2 * group_rows // n_col // UNIT
    return pl.pallas_call(
        functools.partial(own_kernel, n_row, n_col),
        in_specs=[smem(), smem(), vmem(), vmem()],
        out_specs=[vmem(), smem()],
        out_shape=[
            jax.ShapeDtypeStruct((group_rows, 2 * samples), jnp.float32),
            jax.ShapeDtypeStruct((n_col * per_owner,), jnp.int32),
        ],
        scratch_shapes=[pltpu.SMEM((n_col,), jnp.int32)],
        cost_estimate=pl.CostEstimate(
            flops=8 * group_rows * depth * samples,
            bytes_accessed=2 * group_rows * depth,
            transcendentals=0,
        ),
        compiler_params=pltpu.CompilerParams(vmem_limit_bytes=12 * 2**20),
    )(leaf_first, leaf_owner, frontal, slab)


def rest_product(frontal, begun, source, slabs, leaf_first, n_row, n_col):
    group_rows, width = frontal.shape
    samples, depth = slabs[0].shape
    pick = tuple(range(1, n_row))
    half = group_rows // n_col
    block = jax.ShapeDtypeStruct((n_col // 2, half, 2 * samples), jnp.float32)
    return pl.pallas_call(
        functools.partial(rest_kernel, n_row, pick),
        in_specs=[smem(), smem(), vmem(), vmem()] + vmem(len(slabs)),
        out_specs=vmem(2),
        out_shape=[block, block],
        scratch_shapes=[pltpu.VMEM((group_rows + UNIT, 2 * samples), jnp.float32)],
        cost_estimate=pl.CostEstimate(
            flops=8 * group_rows * depth * samples * len(slabs),
            bytes_accessed=2 * group_rows * depth * len(slabs),
            transcendentals=0,
        ),
        compiler_params=pltpu.CompilerParams(vmem_limit_bytes=12 * 2**20),
    )(leaf_first, source, frontal, begun, *slabs)


def leaf_kernel(
    n_row, count_parts, leaf_first, leaf_owner, skeleton, *refs
):
    leaves = leaf_first.shape[0]
    per_group = leaves // n_row
    parts = refs[:count_parts]
    mine_out, coeff_out, worst_out, mine, picked = refs[count_parts:]
    half, wide = parts[0].shape
    samples = wide // 2
    capacity = 2 * half
    skel = skeleton.shape[0]
    every = LEAF_MOST * skel
    row_pos = lax.axis_index("row")
    col_pos = lax.axis_index("col")
    group_rows = mine_out.shape[1] * lax.axis_size("col") // 2
    group_end = (row_pos + 1) * group_rows

    total = parts[0][...]
    for part in parts[1:]:
        total = total + part[...]
    mine[pl.ds(0, half), :] = total
    mine[pl.ds(half, half), :] = pltpu.roll(total, samples, 1)
    turned = total.T
    mine_t = jnp.concatenate([turned[:samples], turned[samples:]], axis=1)
    mine_out[...] = mine_t

    def find(at, carry):
        count, filled, begins, firsts, names = carry
        leaf = row_pos * per_group + at
        first = leaf_first[leaf]
        following = leaf_first[jnp.minimum(leaf + 1, leaves - 1)]
        end = jnp.where(at + 1 < per_group, following, group_end)
        hit = leaf_owner[leaf] == col_pos
        here = [hit & (count == k) for k in range(LEAF_MOST)]
        begins = tuple(jnp.where(h, filled, v) for h, v in zip(here, begins))
        firsts = tuple(jnp.where(h, first, v) for h, v in zip(here, firsts))
        names = tuple(jnp.where(h, leaf, v) for h, v in zip(here, names))
        filled = jnp.where(hit, filled + end - first, filled)
        return jnp.where(hit, count + 1, count), filled, begins, firsts, names

    zero = jnp.int32(0)
    far = jnp.int32(capacity)
    count, _, begins, firsts, names = lax.fori_loop(
        0,
        per_group,
        find,
        (zero, zero, (far,) * LEAF_MOST, (zero,) * LEAF_MOST, (zero,) * LEAF_MOST),
    )
    for b in range(LEAF_MOST):
        there = count > b
        for k in range(skel):
            at = begins[b] + skeleton[k, names[b]] - firsts[b]
            at = jnp.clip(jnp.where(there, at, 0), 0, capacity - 1)
            row = mine[pl.ds(at, 1), :]
            picked[pl.ds(b * skel + k, 1), :] = jnp.where(there, row, 0.0)
    chosen = picked[:, :samples]

    gram = nt_dot(chosen, chosen, HIGHEST)
    proj = jnp.dot(chosen, mine_t, precision=HIGHEST, preferred_element_type=jnp.float32)

    slot = lax.broadcasted_iota(jnp.int32, (skel, capacity), 1)
    rank = jnp.zeros((skel, capacity), jnp.int32)
    for b in range(1, LEAF_MOST):
        rank += (slot >= begins[b]).astype(jnp.int32)
    hot = [rank == b for b in range(LEAF_MOST)]
    hot_rows = jnp.concatenate([h.astype(jnp.float32) for h in hot], axis=0)

    lane_leaf = lax.broadcasted_iota(jnp.int32, (skel, every), 1) // skel
    lane_row = lax.broadcasted_iota(jnp.int32, (skel, every), 1) % skel
    down = lax.broadcasted_iota(jnp.int32, (skel, every), 0)
    joined = jnp.where((down == lane_row) & (count == 0), 1.0, 0.0)
    for b in range(LEAF_MOST):
        joined += jnp.where(lane_leaf == b, gram[b * skel : (b + 1) * skel], 0.0)
    spread = jnp.concatenate([jnp.where(lane_row == i, joined, 0.0) for i in range(skel)], axis=0)
    system = jnp.dot(spread, hot_rows, precision=HIGHEST, preferred_element_type=jnp.float32)

    lines = [system[i * skel : (i + 1) * skel] for i in range(skel)]
    right = jnp.zeros((skel, capacity), jnp.float32)
    for b in range(LEAF_MOST):
        right += jnp.where(hot[b], proj[b * skel : (b + 1) * skel], 0.0)
    index = lax.broadcasted_iota(jnp.int32, (skel, capacity), 0)
    uppers = []
    pivots = []
    for j in range(skel):
        line = lines[j]
        inverse = 1.0 / line[j : j + 1]
        upper = line * inverse
        uppers.append(upper)
        pivots.append(inverse)
        for i in range(j + 1, skel):
            lines[i] = lines[i] - line[i : i + 1] * upper
        right = right - jnp.where(index > j, upper * right[j : j + 1], 0.0)
    solved = right * jnp.concatenate(pivots, axis=0)
    for j in range(skel - 2, -1, -1):
        known = jnp.where(index > j, uppers[j] * solved, 0.0)
        less = jnp.sum(known, axis=0, keepdims=True)
        solved = jnp.where(index == j, solved - less, solved)
    coeff_out[...] = solved

    weights = jnp.concatenate([jnp.where(h, solved, 0.0) for h in hot], axis=0)
    rebuilt = lax.dot_general(
        chosen,
        weights,
        (((0,), (0,)), ((), ())),
        precision=HIGHEST,
        preferred_element_type=jnp.float32,
    )
    resid = mine_t - rebuilt
    err = jnp.sum(resid * resid, axis=0, keepdims=True)
    norm = jnp.sum(mine_t * mine_t, axis=0, keepdims=True)
    worst = jnp.zeros((1, 1), jnp.float32)
    for b in range(LEAF_MOST):
        near = hot[b][:1]
        err_leaf = jnp.sum(jnp.where(near, err, 0.0), axis=1, keepdims=True)
        norm_leaf = jnp.sum(jnp.where(near, norm, 0.0), axis=1, keepdims=True)
        worst = jnp.maximum(worst, jnp.sqrt(err_leaf) / jnp.sqrt(norm_leaf + 1e-06))
    worst_out[...] = jnp.broadcast_to(worst, worst_out.shape)


def leaf_work(parts, leaf_first, leaf_owner, skeleton, n_row):
    half, wide = parts[0].shape
    samples = wide // 2
    skel = skeleton.shape[0]
    return pl.pallas_call(
        functools.partial(leaf_kernel, n_row, len(parts)),
        in_specs=[smem(), smem(), smem()] + vmem(len(parts)),
        out_specs=vmem(3),
        out_shape=[
            jax.ShapeDtypeStruct((samples, 2 * half), jnp.float32),
            jax.ShapeDtypeStruct((skel, 2 * half), jnp.float32),
            jax.ShapeDtypeStruct((1, LANES), jnp.float32),
        ],
        scratch_shapes=[
            pltpu.VMEM((2 * half, wide), jnp.float32),
            pltpu.VMEM((LEAF_MOST * skel, wide), jnp.float32),
        ],
        compiler_params=pltpu.CompilerParams(vmem_limit_bytes=12 * 2**20),
    )(leaf_first, leaf_owner, skeleton, *parts)


def exchange(value, axis, flip):
    pairs = [(k, k ^ flip) for k in range(lax.axis_size(axis))]
    return lax.ppermute(value, axis, pairs)


def local(frontal, sample_cols, leaf_first, leaf_owner, skeleton):
    n_col = lax.axis_size("col")
    n_row = lax.axis_size("row")
    own = sample_cols.T
    slabs = [exchange(own, "row", k) for k in range(1, n_row)]
    frontal = pltpu.with_memory_space_constraint(frontal, pltpu.VMEM)
    begun, source = own_product(frontal, own, leaf_first, leaf_owner, n_row, n_col)
    keep, swap = rest_product(frontal, begun, source, slabs, leaf_first, n_row, n_col)
    summed = keep + exchange(swap, "col", 1)
    parts = [summed[0]] + [exchange(summed[k], "col", 2 * k) for k in range(1, n_col // 2)]
    mine, coeff, worst = leaf_work(parts, leaf_first, leaf_owner, skeleton.T, n_row)
    for axis, size in (("col", n_col), ("row", n_row)):
        others = [exchange(worst, axis, k) for k in range(1, size)]
        for other in others:
            worst = jnp.maximum(worst, other)
    return (mine, coeff, worst[0, :1])


def solution(mesh):
    return jax.shard_map(
        local,
        mesh=mesh,
        in_specs=(P("row", "col"), P(("col", "row"), None), P(), P(), P()),
        out_specs=(P("row", "col"), P("row", "col"), P()),
        check_vma=False,
    )
```

time: 90.6 us -> 52 us (0.57)
  blocking collectives: 71.4 us -> 0 us
  starting transfers between devices: 0 us -> 20.8 us
  waiting for transfers between devices: 0 us -> 11.1 us
  local copies, waits for them, and re-layouts: 1.32 us -> 6.84 us
  Pallas kernels: 16.2 us -> 11.7 us
    all_gather x2 -> x0, blocking collectives: 52.1 us -> none  [the longest x1 38.3 us: local(): lax.all_gather(worst, ('row', 'col'), axis=0, tiled=True)]
    ppermute x0 -> x17, starting transfers between devices: none -> 20.8 us  [exchange(): return lax.ppermute(value, axis, pairs)]
    all_to_all x1 -> x0, blocking collectives: 19.3 us -> none  [local(): parts = lax.all_to_all(sent, 'col', 0, 0)]
    ppermute x0 -> x17, waiting for transfers between devices: none -> 11.1 us  [exchange(): return lax.ppermute(value, axis, pairs)]
    unnamed x6 -> x12, local copies, waits for them, and re-layouts: 1.32 us -> 6.82 us
    pallas_call x2 -> x3, Pallas kernels: 16.2 us -> 11.7 us  [the longest x1 5.1 us: own_product(): pl.pallas_call(functools.partial(own_kernel, n_row, n_col), in_specs=[sme...]
  transfers between devices with their start and end apart: 0 -> 17, of which waited for: 0 -> 7; matrix products, arithmetic and copies ran while one was open for 0% -> 0% of each run, Pallas kernels for 0% -> 10%
where the time goes in v2:
time: 52 us; the launch traced here: 51.8 us
  starting transfers between devices  20.8 us (40%)
  Pallas kernels  11.7 us (22%)
  waiting for transfers between devices  11.1 us (21%)
  local copies, waits for them, and re-layouts  6.84 us (13%)
  between operations  0.72 us (1%)
  other arithmetic  0.56 us (1%)
    ppermute x17, starting transfers between devices, exchange(): return lax.ppermute(value, axis, pairs)  20.8 us
    ppermute x17, waiting for transfers between devices, exchange(): return lax.ppermute(value, axis, pairs)  11.1 us
    unnamed x12, local copies, waits for them, and re-layouts  6.82 us
    pallas_call x1, Pallas kernels, own_product(): pl.pallas_call(functools.partial(own_kernel, n_row, n_col), in_specs=[sme...  5.1 us
    pallas_call x1, Pallas kernels, rest_product(): pl.pallas_call(functools.partial(rest_kernel, n_row, pick), in_specs=[sme...  3.74 us
    pallas_call x1, Pallas kernels, leaf_work(): pl.pallas_call(functools.partial(leaf_kernel, n_row, len(parts)), in_spec...  2.9 us
  transfers between devices with their start and end apart: 17, of which 7 were waited for; matrix products, arithmetic and copies ran while one was open for 0% of the time, Pallas kernels for 10%

profile of v2, /device:TPU:0, one launch (start us, length us, event | category | flops | bytes accessed | tf_op | source)
XLA Modules:
  0.0 51.8 jit_solution(17500154935622305132)
XLA Ops:
  0.6 4.0 %collective-permute-start.2 = (bf16[64,1536]{1,0:T(8,128)(2,1)}, bf16[64,1536]{1,0:T(8,128)(2,1)S(1)}, u32[]{:S(2)}, u32[]{:S(2)}) collective-permute-start(bf16[64,1536]{1,0:T(8,128)(2,1)} %bitcast.12), channel_id=1, source_target_pairs={{0,24},{8,16},{16,8},{24,0},{1,25},{9,17},{17,9},{25,1},{2,26},{10... | collective-permute-start | bytes 589832 | tf_op jit(solution)/shard_map/ppermute | solution.py:337
  4.6 0.5 collective-permute-start.1
  5.1 0.1 collective-permute-start
  5.2 0.0 copy-start
  5.2 4.6 %copy-done = bf16[1024,6144]{1,0:T(8,128)(2,1)S(1)} copy-done((bf16[1024,6144]{1,0:T(8,128)(2,1)S(1)}, bf16[1024,6144]{1,0:T(8,128)(2,1)}, u32[]{:S(2)}) %copy-start) | copy-done | bytes 12582936
  9.8 0.0 copy-start.2
  9.8 0.9 %copy-done.2 = bf16[1536,64]{0,1:T(8,128)(2,1)S(1)} copy-done((bf16[1536,64]{0,1:T(8,128)(2,1)S(1)}, bf16[1536,64]{0,1:T(8,128)(2,1)}, u32[]{:S(2)}) %copy-start.2) | copy-done | bytes 196632
  10.7 0.0 copy-start.4
  10.7 0.7 %copy-done.4 = s32[64]{0:T(128)S(1)} copy-done((s32[64]{0:T(128)S(1)}, s32[64]{0:T(128)}, u32[]{:S(2)}) %copy-start.4) | copy-done | bytes 280
  11.4 0.0 copy-start.5
  11.4 0.7 %copy-done.5 = s32[64]{0:T(128)S(1)} copy-done((s32[64]{0:T(128)S(1)}, s32[64]{0:T(128)}, u32[]{:S(2)}) %copy-start.5) | copy-done | bytes 280
  12.0 0.0 copy-start.1
  12.1 0.0 copy-start.3
  12.1 5.1 %shard_map.76 = (f32[1024,128]{1,0:T(8,128)S(1)}, s32[64]{0:T(128)S(1)}) custom-call(s32[64]{0:T(128)S(1)} %copy-done.4, s32[64]{0:T(128)S(1)} %copy-done.5, bf16[1024,6144]{1,0:T(8,128)(2,1)S(1)} %copy-done, bf16[64,1536]{1,0:T(8,128)(2,1)S(1)} %bitcast.15), custom_call_target="tpu_custom_call" | custom-call | flops 805306368 | bytes 3145728 | tf_op jit(solution)/shard_map/pallas_call | solution.py:156
  17.2 0.0 collective-permute-done.2.refs_2_
  17.2 0.0 collective-permute-done.1.refs_1_
  17.2 0.0 collective-permute-done.refs_0_
  17.2 0.0 copy-done.1
  17.2 3.7 %shard_map.77 = (f32[4,128,128]{2,1,0:T(8,128)S(1)}, f32[4,128,128]{2,1,0:T(8,128)S(1)}) custom-call(s32[64]{0:T(128)S(1)} %copy-done.4, s32[64]{0:T(128)S(1)} %get-tuple-element.10.source, bf16[1024,6144]{1,0:T(8,128)(2,1)S(1)} %copy-done.1, f32[1024,128]{1,0:T(8,128)S(1)} %get-tuple-element.11.begun, bf16[64,1536]{1,0:T(8,128)(2,1)S(1)} %collective-permute-done.refs_0_, ...), custom_call_target="tpu_custom_call" | custom-call | flops 2415919104 | bytes 9437184 | tf_op jit(solution)/shard_map/pallas_call | solution.py:180
  20.9 0.1 collective-permute-start.3
  21.0 1.5 %collective-permute-done.3 = f32[4,128,128]{2,1,0:T(8,128)S(1)} collective-permute-done((f32[4,128,128]{2,1,0:T(8,128)S(1)}, f32[4,128,128]{2,1,0:T(8,128)S(1)}, u32[]{:S(2)}, u32[]{:S(2)}) %collective-permute-start.3) | collective-permute-done | bytes 262176 | tf_op jit(solution)/shard_map/ppermute | solution.py:337
  22.6 3.5 %collective-permute-start.6 = (f32[128,128]{1,0:T(8,128)S(1)}, f32[128,128]{1,0:T(8,128)S(1)}, u32[]{:S(2)}, u32[]{:S(2)}) collective-permute-start(f32[128,128]{1,0:T(8,128)S(1)} %get-tuple-element.17), channel_id=1, source_target_pairs={{0,6},{1,7},{2,4},{3,5},{4,2},{5,3},{6,0},{7,1},{8,14},{9,15},{10,... | collective-permute-start | bytes 196616 | tf_op jit(solution)/shard_map/ppermute | solution.py:337
  26.1 0.0 collective-permute-start.5
  26.1 1.0 %collective-permute-start.4 = (f32[128,128]{1,0:T(8,128)S(1)}, f32[128,128]{1,0:T(8,128)S(1)}, u32[]{:S(2)}, u32[]{:S(2)}) collective-permute-start(f32[128,128]{1,0:T(8,128)S(1)} %get-tuple-element.19), channel_id=1, source_target_pairs={{0,2},{1,3},{2,0},{3,1},{4,6},{5,7},{6,4},{7,5},{8,10},{9,11},{10,... | collective-permute-start | bytes 196616 | tf_op jit(solution)/shard_map/ppermute | solution.py:337
  27.1 2.1 %collective-permute-done.6.refs_3_ = f32[128,128]{1,0:T(8,128)S(1)} collective-permute-done((f32[128,128]{1,0:T(8,128)S(1)}, f32[128,128]{1,0:T(8,128)S(1)}, u32[]{:S(2)}, u32[]{:S(2)}) %collective-permute-start.6) | collective-permute-done | bytes 65568 | tf_op jit(solution)/shard_map/ppermute | solution.py:337
  29.2 2.8 %collective-permute-done.5.refs_2_ = f32[128,128]{1,0:T(8,128)S(1)} collective-permute-done((f32[128,128]{1,0:T(8,128)S(1)}, f32[128,128]{1,0:T(8,128)S(1)}, u32[]{:S(2)}, u32[]{:S(2)}) %collective-permute-start.5) | collective-permute-done | bytes 65568 | tf_op jit(solution)/shard_map/ppermute | solution.py:337
  32.0 0.0 collective-permute-done.4.refs_1_
  32.0 0.0 copy-done.3
  32.0 2.9 %shard_map.78 = (f32[64,256]{1,0:T(8,128)}, f32[16,256]{1,0:T(8,128)}, f32[1,128]{1,0:T(1,128)S(1)}) custom-call(s32[64]{0:T(128)S(1)} %copy-done.4, s32[64]{0:T(128)S(1)} %copy-done.5, s32[16,64]{1,0:T(8,128)S(1)} %bitcast.16, f32[128,128]{1,0:T(8,128)S(1)} %get-tuple-element.20.refs_0_, f32[128,128]{1,0:T(8,128)S(1)} %collective-permute-done.4.refs_1_, ...), custom_call_target="tpu_custom_call" | custom-call | tf_op jit(solution)/shard_map/pallas_call | solution.py:318
  34.9 1.4 %collective-permute-start.13 = (f32[1,128]{1,0:T(1,128)S(1)}, f32[1,128]{1,0:T(1,128)S(1)}, u32[]{:S(2)}, u32[]{:S(2)}) collective-permute-start(f32[1,128]{1,0:T(1,128)S(1)} %get-tuple-element.16), channel_id=1, source_target_pairs={{0,7},{1,6},{2,5},{3,4},{4,3},{5,2},{6,1},{7,0},{8,15},{9,14},{10,... | collective-permute-start | bytes 1544 | tf_op jit(solution)/shard_map/ppermute | solution.py:337
  36.3 1.8 %collective-permute-start.12 = (f32[1,128]{1,0:T(1,128)S(1)}, f32[1,128]{1,0:T(1,128)S(1)}, u32[]{:S(2)}, u32[]{:S(2)}) collective-permute-start(f32[1,128]{1,0:T(1,128)S(1)} %get-tuple-element.16), channel_id=1, source_target_pairs={{0,6},{1,7},{2,4},{3,5},{4,2},{5,3},{6,0},{7,1},{8,14},{9,15},{10,... | collective-permute-start | bytes 1544 | tf_op jit(solution)/shard_map/ppermute | solution.py:337
  38.1 0.0 collective-permute-start.11
  38.1 3.0 %collective-permute-start.10 = (f32[1,128]{1,0:T(1,128)S(1)}, f32[1,128]{1,0:T(1,128)S(1)}, u32[]{:S(2)}, u32[]{:S(2)}) collective-permute-start(f32[1,128]{1,0:T(1,128)S(1)} %get-tuple-element.16), channel_id=1, source_target_pairs={{0,4},{1,5},{2,6},{3,7},{4,0},{5,1},{6,2},{7,3},{8,12},{9,13},{10,... | collective-permute-start | bytes 1544 | tf_op jit(solution)/shard_map/ppermute | solution.py:337
  41.1 0.0 collective-permute-start.9
  41.1 0.0 collective-permute-done.13
  41.1 1.3 %collective-permute-start.8 = (f32[1,128]{1,0:T(1,128)S(1)}, f32[1,128]{1,0:T(1,128)S(1)}, u32[]{:S(2)}, u32[]{:S(2)}) collective-permute-start(f32[1,128]{1,0:T(1,128)S(1)} %get-tuple-element.16), channel_id=1, source_target_pairs={{0,2},{1,3},{2,0},{3,1},{4,6},{5,7},{6,4},{7,5},{8,10},{9,11},{10,... | collective-permute-start | bytes 1544 | tf_op jit(solution)/shard_map/ppermute | solution.py:337
  42.5 0.0 collective-permute-done.12
  42.5 0.5 collective-permute-start.7
  43.0 0.0 collective-permute-done.11
  43.0 0.0 collective-permute-done.10
  43.0 1.1 %collective-permute-done.9 = f32[1,128]{1,0:T(1,128)S(1)} collective-permute-done((f32[1,128]{1,0:T(1,128)S(1)}, f32[1,128]{1,0:T(1,128)S(1)}, u32[]{:S(2)}, u32[]{:S(2)}) %collective-permute-start.9) | collective-permute-done | bytes 544 | tf_op jit(solution)/shard_map/ppermute | solution.py:337
  44.1 0.6 %collective-permute-done.8 = f32[1,128]{1,0:T(1,128)S(1)} collective-permute-done((f32[1,128]{1,0:T(1,128)S(1)}, f32[1,128]{1,0:T(1,128)S(1)}, u32[]{:S(2)}, u32[]{:S(2)}) %collective-permute-start.8) | collective-permute-done | bytes 544 | tf_op jit(solution)/shard_map/ppermute | solution.py:337
  44.7 0.0 collective-permute-done.7
  44.7 3.0 %collective-permute-start.16 = (f32[1,128]{1,0:T(1,128)S(1)}, f32[1,128]{1,0:T(1,128)S(1)}, u32[]{:S(2)}, u32[]{:S(2)}) collective-permute-start(f32[1,128]{1,0:T(1,128)S(1)} %maximum_maximum_fusion.1), channel_id=1, source_target_pairs={{0,24},{8,16},{16,8},{24,0},{1,25},{9,17},{17,9},{25,1},{2,26},{10... | collective-permute-start | bytes 1544 | tf_op jit(solution)/shard_map/ppermute | solution.py:337
  47.7 0.0 collective-permute-start.15
  47.8 0.6 %collective-permute-start.14 = (f32[1,128]{1,0:T(1,128)S(1)}, f32[1,128]{1,0:T(1,128)S(1)}, u32[]{:S(2)}, u32[]{:S(2)}) collective-permute-start(f32[1,128]{1,0:T(1,128)S(1)} %maximum_maximum_fusion.1), channel_id=1, source_target_pairs={{0,8},{8,0},{16,24},{24,16},{1,9},{9,1},{17,25},{25,17},{2,10},{10... | collective-permute-start | bytes 1544 | tf_op jit(solution)/shard_map/ppermute | solution.py:337
  48.4 0.9 %collective-permute-done.16 = f32[1,128]{1,0:T(1,128)S(1)} collective-permute-done((f32[1,128]{1,0:T(1,128)S(1)}, f32[1,128]{1,0:T(1,128)S(1)}, u32[]{:S(2)}, u32[]{:S(2)}) %collective-permute-start.16) | collective-permute-done | bytes 544 | tf_op jit(solution)/shard_map/ppermute | solution.py:337
  49.2 2.0 %collective-permute-done.15 = f32[1,128]{1,0:T(1,128)S(1)} collective-permute-done((f32[1,128]{1,0:T(1,128)S(1)}, f32[1,128]{1,0:T(1,128)S(1)}, u32[]{:S(2)}, u32[]{:S(2)}) %collective-permute-start.15) | collective-permute-done | bytes 544 | tf_op jit(solution)/shard_map/ppermute | solution.py:337
  51.3 0.0 collective-permute-done.14
  51.3 0.5 maximum_maximum_fusion
  (3 shorter events, 0.1 us)
Async XLA Ops:
  0.6 16.5 %collective-permute-start.2 = (bf16[64,1536]{1,0:T(8,128)(2,1)}, bf16[64,1536]{1,0:T(8,128)(2,1)S(1)}, u32[]{:S(2)}, u32[]{:S(2)}) collective-permute-start(bf16[64,1536]{1,0:T(8,128)(2,1)} %bitcast.12), channel_id=1, source_target_pairs={{0,24},{8,16},{16,8},{24,0},{1,25},{9,17},{17,9},{25,1},{2,26},{10... | collective-permute-start | bytes 589832 | tf_op jit(solution)/shard_map/ppermute | solution.py:337
  4.6 12.6 %collective-permute-start.1 = (bf16[64,1536]{1,0:T(8,128)(2,1)}, bf16[64,1536]{1,0:T(8,128)(2,1)S(1)}, u32[]{:S(2)}, u32[]{:S(2)}) collective-permute-start(bf16[64,1536]{1,0:T(8,128)(2,1)} %bitcast.13), channel_id=1, source_target_pairs={{0,16},{8,24},{16,0},{24,8},{1,17},{9,25},{17,1},{25,9},{2,18},{10... | collective-permute-start | bytes 589832 | tf_op jit(solution)/shard_map/ppermute | solution.py:337
  5.1 12.1 %collective-permute-start = (bf16[64,1536]{1,0:T(8,128)(2,1)}, bf16[64,1536]{1,0:T(8,128)(2,1)S(1)}, u32[]{:S(2)}, u32[]{:S(2)}) collective-permute-start(bf16[64,1536]{1,0:T(8,128)(2,1)} %bitcast.14), channel_id=1, source_target_pairs={{0,8},{8,0},{16,24},{24,16},{1,9},{9,1},{17,25},{25,17},{2,10},{10... | collective-permute-start | bytes 589832 | tf_op jit(solution)/shard_map/ppermute | solution.py:337
  5.2 4.6 %copy-start = (bf16[1024,6144]{1,0:T(8,128)(2,1)S(1)}, bf16[1024,6144]{1,0:T(8,128)(2,1)}, u32[]{:S(2)}) copy-start(bf16[1024,6144]{1,0:T(8,128)(2,1)} %frontal.3) | copy-start | bytes 37748740
  9.8 0.9 %copy-start.2 = (bf16[1536,64]{0,1:T(8,128)(2,1)S(1)}, bf16[1536,64]{0,1:T(8,128)(2,1)}, u32[]{:S(2)}) copy-start(bf16[1536,64]{0,1:T(8,128)(2,1)} %param.6) | copy-start | bytes 589828
  10.7 0.7 %copy-start.4 = (s32[64]{0:T(128)S(1)}, s32[64]{0:T(128)}, u32[]{:S(2)}) copy-start(s32[64]{0:T(128)} %leaf_first.5) | copy-start | bytes 772
  11.4 0.7 %copy-start.5 = (s32[64]{0:T(128)S(1)}, s32[64]{0:T(128)}, u32[]{:S(2)}) copy-start(s32[64]{0:T(128)} %leaf_owner.3) | copy-start | bytes 772
  12.0 5.1 %copy-start.1 = (bf16[1024,6144]{1,0:T(8,128)(2,1)S(1)}, bf16[1024,6144]{1,0:T(8,128)(2,1)}, u32[]{:S(2)}) copy-start(bf16[1024,6144]{1,0:T(8,128)(2,1)} %frontal.3) | copy-start | bytes 37748740
  12.1 20.0 %copy-start.3 = (s32[64,16]{0,1:T(8,128)S(1)}, s32[64,16]{0,1:T(8,128)}, u32[]{:S(2)}) copy-start(s32[64,16]{0,1:T(8,128)} %param.9) | copy-start | bytes 12292
  20.9 1.6 %collective-permute-start.3 = (f32[4,128,128]{2,1,0:T(8,128)S(1)}, f32[4,128,128]{2,1,0:T(8,128)S(1)}, u32[]{:S(2)}, u32[]{:S(2)}) collective-permute-start(f32[4,128,128]{2,1,0:T(8,128)S(1)} %get-tuple-element.13), channel_id=1, source_target_pairs={{0,1},{1,0},{2,3},{3,2},{4,5},{5,4},{6,7},{7,6},{8,9},{9,8},{10,11... | collective-permute-start | bytes 786440 | tf_op jit(solution)/shard_map/ppermute | solution.py:337
  22.6 6.6 %collective-permute-start.6 = (f32[128,128]{1,0:T(8,128)S(1)}, f32[128,128]{1,0:T(8,128)S(1)}, u32[]{:S(2)}, u32[]{:S(2)}) collective-permute-start(f32[128,128]{1,0:T(8,128)S(1)} %get-tuple-element.17), channel_id=1, source_target_pairs={{0,6},{1,7},{2,4},{3,5},{4,2},{5,3},{6,0},{7,1},{8,14},{9,15},{10,... | collective-permute-start | bytes 196616 | tf_op jit(solution)/shard_map/ppermute | solution.py:337
  26.1 5.9 %collective-permute-start.5 = (f32[128,128]{1,0:T(8,128)S(1)}, f32[128,128]{1,0:T(8,128)S(1)}, u32[]{:S(2)}, u32[]{:S(2)}) collective-permute-start(f32[128,128]{1,0:T(8,128)S(1)} %get-tuple-element.18), channel_id=1, source_target_pairs={{0,4},{1,5},{2,6},{3,7},{4,0},{5,1},{6,2},{7,3},{8,12},{9,13},{10,... | collective-permute-start | bytes 196616 | tf_op jit(solution)/shard_map/ppermute | solution.py:337
  26.1 5.9 %collective-permute-start.4 = (f32[128,128]{1,0:T(8,128)S(1)}, f32[128,128]{1,0:T(8,128)S(1)}, u32[]{:S(2)}, u32[]{:S(2)}) collective-permute-start(f32[128,128]{1,0:T(8,128)S(1)} %get-tuple-element.19), channel_id=1, source_target_pairs={{0,2},{1,3},{2,0},{3,1},{4,6},{5,7},{6,4},{7,5},{8,10},{9,11},{10,... | collective-permute-start | bytes 196616 | tf_op jit(solution)/shard_map/ppermute | solution.py:337
  34.9 6.2 %collective-permute-start.13 = (f32[1,128]{1,0:T(1,128)S(1)}, f32[1,128]{1,0:T(1,128)S(1)}, u32[]{:S(2)}, u32[]{:S(2)}) collective-permute-start(f32[1,128]{1,0:T(1,128)S(1)} %get-tuple-element.16), channel_id=1, source_target_pairs={{0,7},{1,6},{2,5},{3,4},{4,3},{5,2},{6,1},{7,0},{8,15},{9,14},{10,... | collective-permute-start | bytes 1544 | tf_op jit(solution)/shard_map/ppermute | solution.py:337
  36.3 6.2 %collective-permute-start.12 = (f32[1,128]{1,0:T(1,128)S(1)}, f32[1,128]{1,0:T(1,128)S(1)}, u32[]{:S(2)}, u32[]{:S(2)}) collective-permute-start(f32[1,128]{1,0:T(1,128)S(1)} %get-tuple-element.16), channel_id=1, source_target_pairs={{0,6},{1,7},{2,4},{3,5},{4,2},{5,3},{6,0},{7,1},{8,14},{9,15},{10,... | collective-permute-start | bytes 1544 | tf_op jit(solution)/shard_map/ppermute | solution.py:337
  38.1 4.9 %collective-permute-start.11 = (f32[1,128]{1,0:T(1,128)S(1)}, f32[1,128]{1,0:T(1,128)S(1)}, u32[]{:S(2)}, u32[]{:S(2)}) collective-permute-start(f32[1,128]{1,0:T(1,128)S(1)} %get-tuple-element.16), channel_id=1, source_target_pairs={{0,5},{1,4},{2,7},{3,6},{4,1},{5,0},{6,3},{7,2},{8,13},{9,12},{10,... | collective-permute-start | bytes 1544 | tf_op jit(solution)/shard_map/ppermute | solution.py:337
  38.1 4.9 %collective-permute-start.10 = (f32[1,128]{1,0:T(1,128)S(1)}, f32[1,128]{1,0:T(1,128)S(1)}, u32[]{:S(2)}, u32[]{:S(2)}) collective-permute-start(f32[1,128]{1,0:T(1,128)S(1)} %get-tuple-element.16), channel_id=1, source_target_pairs={{0,4},{1,5},{2,6},{3,7},{4,0},{5,1},{6,2},{7,3},{8,12},{9,13},{10,... | collective-permute-start | bytes 1544 | tf_op jit(solution)/shard_map/ppermute | solution.py:337
  41.1 3.0 %collective-permute-start.9 = (f32[1,128]{1,0:T(1,128)S(1)}, f32[1,128]{1,0:T(1,128)S(1)}, u32[]{:S(2)}, u32[]{:S(2)}) collective-permute-start(f32[1,128]{1,0:T(1,128)S(1)} %get-tuple-element.16), channel_id=1, source_target_pairs={{0,3},{1,2},{2,1},{3,0},{4,7},{5,6},{6,5},{7,4},{8,11},{9,10},{10,... | collective-permute-start | bytes 1544 | tf_op jit(solution)/shard_map/ppermute | solution.py:337
  41.1 3.6 %collective-permute-start.8 = (f32[1,128]{1,0:T(1,128)S(1)}, f32[1,128]{1,0:T(1,128)S(1)}, u32[]{:S(2)}, u32[]{:S(2)}) collective-permute-start(f32[1,128]{1,0:T(1,128)S(1)} %get-tuple-element.16), channel_id=1, source_target_pairs={{0,2},{1,3},{2,0},{3,1},{4,6},{5,7},{6,4},{7,5},{8,10},{9,11},{10,... | collective-permute-start | bytes 1544 | tf_op jit(solution)/shard_map/ppermute | solution.py:337
  42.5 2.2 %collective-permute-start.7 = (f32[1,128]{1,0:T(1,128)S(1)}, f32[1,128]{1,0:T(1,128)S(1)}, u32[]{:S(2)}, u32[]{:S(2)}) collective-permute-start(f32[1,128]{1,0:T(1,128)S(1)} %get-tuple-element.16), channel_id=1, source_target_pairs={{0,1},{1,0},{2,3},{3,2},{4,5},{5,4},{6,7},{7,6},{8,9},{9,8},{10,11... | collective-permute-start | bytes 1544 | tf_op jit(solution)/shard_map/ppermute | solution.py:337
  44.7 4.5 %collective-permute-start.16 = (f32[1,128]{1,0:T(1,128)S(1)}, f32[1,128]{1,0:T(1,128)S(1)}, u32[]{:S(2)}, u32[]{:S(2)}) collective-permute-start(f32[1,128]{1,0:T(1,128)S(1)} %maximum_maximum_fusion.1), channel_id=1, source_target_pairs={{0,24},{8,16},{16,8},{24,0},{1,25},{9,17},{17,9},{25,1},{2,26},{10... | collective-permute-start | bytes 1544 | tf_op jit(solution)/shard_map/ppermute | solution.py:337
  47.7 3.5 %collective-permute-start.15 = (f32[1,128]{1,0:T(1,128)S(1)}, f32[1,128]{1,0:T(1,128)S(1)}, u32[]{:S(2)}, u32[]{:S(2)}) collective-permute-start(f32[1,128]{1,0:T(1,128)S(1)} %maximum_maximum_fusion.1), channel_id=1, source_target_pairs={{0,16},{8,24},{16,0},{24,8},{1,17},{9,25},{17,1},{25,9},{2,18},{10... | collective-permute-start | bytes 1544 | tf_op jit(solution)/shard_map/ppermute | solution.py:337
  47.8 3.5 %collective-permute-start.14 = (f32[1,128]{1,0:T(1,128)S(1)}, f32[1,128]{1,0:T(1,128)S(1)}, u32[]{:S(2)}, u32[]{:S(2)}) collective-permute-start(f32[1,128]{1,0:T(1,128)S(1)} %maximum_maximum_fusion.1), channel_id=1, source_target_pairs={{0,8},{8,0},{16,24},{24,16},{1,9},{9,1},{17,25},{25,17},{2,10},{10... | collective-permute-start | bytes 1544 | tf_op jit(solution)/shard_map/ppermute | solution.py:337

commit v3 on v2

v3 whole, which is shorter than its diff:
```python
import functools

import jax
import jax.numpy as jnp
from jax import lax
from jax.experimental import pallas as pl
from jax.experimental.pallas import tpu as pltpu
from jax.sharding import PartitionSpec as P

UNIT = 32
LANES = 128
LEAF_MOST = 4
PICKS = 8
FAN = 6
RUN_LEAVES = 4
HIGHEST = lax.Precision.HIGHEST


def nt_dot(a, b, precision=None):
    return lax.dot_general(
        a, b, (((1,), (1,)), ((), ())), precision=precision, preferred_element_type=jnp.float32
    )


def clear_runs(pick, n_row, depth, frontal, leaf_first):
    group_rows, width = frontal.shape
    per_group = leaf_first.shape[0] // n_row
    runs = per_group // RUN_LEAVES
    run_rows = group_rows // runs
    row_pos = lax.axis_index("row")
    first_col = lax.axis_index("col") * width

    def clear(at, carry):
        run = at // (run_rows // LANES)
        begin = row_pos * group_rows + run * run_rows
        begin_col = row_pos * group_rows + at * LANES
        inside = begin_col - first_col
        held = (inside >= 0) & (inside < width)
        inside = jnp.clip(inside, 0, width - LANES)

        @pl.when(held & (((inside // depth) ^ row_pos) == pick))
        def _():
            rows = pl.ds(pl.multiple_of(run * run_rows, run_rows), run_rows)
            lanes = pl.ds(pl.multiple_of(inside, LANES), LANES)
            part = frontal[rows, lanes]
            down = lax.broadcasted_iota(jnp.int32, part.shape, 0) + begin
            across = lax.broadcasted_iota(jnp.int32, part.shape, 1) + begin_col
            leaf_down = jnp.zeros(part.shape, jnp.int32)
            leaf_across = jnp.zeros(part.shape, jnp.int32)
            for k in range(1, RUN_LEAVES):
                edge = leaf_first[row_pos * per_group + run * RUN_LEAVES + k]
                leaf_down += (down >= edge).astype(jnp.int32)
                leaf_across += (across >= edge).astype(jnp.int32)
            kept = jnp.where(leaf_down == leaf_across, 0.0, part.astype(jnp.float32))
            frontal[rows, lanes] = kept.astype(jnp.bfloat16)

        return carry

    lax.fori_loop(0, group_rows // LANES, clear, 0)


def multiply(pick, frontal, slabs, begun, total):
    group_rows = frontal.shape[0]
    depth = slabs[0].shape[1]
    row_pos = lax.axis_index("row")
    part = min(group_rows, 512)

    def rows_of(at, carry):
        rows = pl.ds(pl.multiple_of(at * part, part), part)
        value = None if begun is None else begun[rows, :]
        for k, slab in zip(pick, slabs):
            begin = pl.multiple_of((row_pos ^ k) * depth, LANES)
            twice = jnp.concatenate([slab[...], slab[...]], axis=0)
            add = nt_dot(frontal[rows, pl.ds(begin, depth)], twice)
            value = add if value is None else value + add
        total[rows, :] = value
        return carry

    lax.fori_loop(0, group_rows // part, rows_of, 0)


def plan_leaves(n_row, group_rows, capacity, first, owners, skel, plan):
    leaves = first.shape[0]
    per_group = leaves // n_row
    count_skel = skel.shape[0]
    row_pos = lax.axis_index("row")
    col_pos = lax.axis_index("col")

    def clear(at, carry):
        plan[at] = capacity
        return carry

    lax.fori_loop(0, plan.shape[0], clear, 0)

    def find(at, carry):
        count, filled = carry
        leaf = row_pos * per_group + at
        begin = first[leaf]
        following = first[jnp.minimum(leaf + 1, leaves - 1)]
        end = jnp.where(at + 1 < per_group, following, (row_pos + 1) * group_rows)
        hit = (owners[leaf] == col_pos) & (count < LEAF_MOST)

        @pl.when(hit)
        def _():
            plan[count] = filled
            for k in range(count_skel):
                plan[PICKS + count * count_skel + k] = filled + skel[k, leaf] - begin

        return jnp.where(hit, count + 1, count), jnp.where(hit, filled + end - begin, filled)

    count, _ = lax.fori_loop(0, per_group, find, (jnp.int32(0), jnp.int32(0)))
    plan[LEAF_MOST] = count


def own_kernel(
    n_row,
    n_col,
    leaf_first,
    leaf_owner,
    skeleton,
    frontal,
    slab,
    held,
    total,
    source,
    plan,
    first,
    owners,
    skel,
    near,
    used,
    table_sems,
    slab_sem,
    sems,
):
    group_rows = frontal.shape[0]
    depth = slab.shape[1]
    leaves = leaf_first.shape[0]
    per_group = leaves // n_row
    per_owner = 2 * group_rows // n_col // UNIT
    units = group_rows // UNIT
    row_pos = lax.axis_index("row")
    tables = [
        pltpu.make_async_copy(leaf_first, first, table_sems.at[0]),
        pltpu.make_async_copy(leaf_owner, owners, table_sems.at[1]),
        pltpu.make_async_copy(skeleton, skel, table_sems.at[2]),
    ]
    bring = pltpu.make_async_copy(slab, near, slab_sem)
    moves = []
    for k in range(n_row):
        lanes = pl.ds(pl.multiple_of((row_pos ^ k) * depth, LANES), depth)
        moves.append(
            pltpu.make_async_copy(frontal.at[:, lanes], held.at[:, lanes], sems.at[k])
        )
    for copy in tables + [bring] + moves:
        copy.start()

    def clear(at, carry):
        source[at] = units
        used[at // per_owner] = 0
        return carry

    lax.fori_loop(0, n_col * per_owner, clear, 0)
    for copy in tables:
        copy.wait()

    def place(unit, leaf):
        row = row_pos * group_rows + unit * UNIT
        later = jnp.minimum(leaf + 1, leaves - 1)
        moved = (leaf + 1 < leaves) & (first[later] <= row)
        leaf = jnp.where(moved, later, leaf)
        owner = owners[leaf]
        slot = used[owner]
        used[owner] = slot + 1
        source[owner * per_owner + slot] = unit
        return leaf

    lax.fori_loop(0, units, place, row_pos * per_group)
    plan_leaves(n_row, group_rows, per_owner * UNIT, first, owners, skel, plan)
    bring.wait()
    moves[0].wait()
    clear_runs(0, n_row, depth, held, first)
    multiply((0,), held, (near,), None, total)
    for k in range(1, n_row):
        moves[k].wait()
        clear_runs(k, n_row, depth, held, first)


def middle_kernel(pick, frontal, begun, *refs):
    multiply(pick, frontal, refs[: len(pick)], begun, refs[len(pick)])


def lay(other, source, total, out):
    chips, half, wide = out.shape
    per_half = half // UNIT
    core = lax.rem(lax.axis_index("col"), 2)
    chip = lax.axis_index("col") // 2
    lane = lax.broadcasted_iota(jnp.int32, (UNIT, wide), 1)

    def one(turn, carry):
        owner = (chip ^ turn) * 2 + (core ^ other)
        for at in range(per_half):
            values = []
            for side in range(2):
                unit = source[owner * (2 * per_half) + side * per_half + at]
                values.append(total[pl.ds(pl.multiple_of(unit * UNIT, UNIT), UNIT), :])
            out[turn, pl.ds(at * UNIT, UNIT), :] = jnp.where(lane < wide // 2, *values)
        return carry

    lax.fori_loop(0, chips, one, 0, unroll=min(chips, 4))


def last_kernel(pick, source, frontal, begun, *refs):
    slabs, (swap, total) = refs[: len(pick)], refs[len(pick) :]
    group_rows = frontal.shape[0]
    total[pl.ds(group_rows, UNIT), :] = jnp.zeros((UNIT, total.shape[1]), jnp.float32)
    multiply(pick, frontal, slabs, begun, total)
    lay(1, source, total, swap)


def keep_kernel(source, total, keep):
    lay(0, source, total, keep)


def vmem(count=None):
    spec = pl.BlockSpec(memory_space=pltpu.VMEM)
    return spec if count is None else [spec] * count


def smem():
    return pl.BlockSpec(memory_space=pltpu.SMEM)


def hbm():
    return pl.BlockSpec(memory_space=pltpu.HBM)


def in_hbm(value):
    return pltpu.with_memory_space_constraint(value, pltpu.HBM)


def product_cost(frontal, slabs):
    group_rows = frontal.shape[0]
    samples, depth = slabs[0].shape
    return pl.CostEstimate(
        flops=8 * group_rows * depth * samples * len(slabs),
        bytes_accessed=2 * group_rows * depth * len(slabs),
        transcendentals=0,
    )


def own_product(frontal, slab, leaf_first, leaf_owner, skeleton, n_row, n_col):
    group_rows, width = frontal.shape
    samples, depth = slab.shape
    per_owner = 2 * group_rows // n_col // UNIT
    leaves = leaf_first.shape[0]
    return pl.pallas_call(
        functools.partial(own_kernel, n_row, n_col),
        in_specs=[hbm()] * 5,
        out_specs=[vmem(), vmem(), smem(), smem()],
        out_shape=[
            jax.ShapeDtypeStruct(frontal.shape, frontal.dtype),
            jax.ShapeDtypeStruct((group_rows, 2 * samples), jnp.float32),
            jax.ShapeDtypeStruct((n_col * per_owner,), jnp.int32),
            jax.ShapeDtypeStruct((PICKS + LEAF_MOST * skeleton.shape[0],), jnp.int32),
        ],
        scratch_shapes=[
            pltpu.SMEM((leaves,), jnp.int32),
            pltpu.SMEM((leaves,), jnp.int32),
            pltpu.SMEM(skeleton.shape, jnp.int32),
            pltpu.VMEM((samples, depth), slab.dtype),
            pltpu.SMEM((n_col,), jnp.int32),
            pltpu.SemaphoreType.DMA((3,)),
            pltpu.SemaphoreType.DMA,
            pltpu.SemaphoreType.DMA((n_row,)),
        ],
        cost_estimate=product_cost(frontal, [slab] * n_row),
        compiler_params=pltpu.CompilerParams(vmem_limit_bytes=24 * 2**20),
    )(*(in_hbm(x) for x in (leaf_first, leaf_owner, skeleton, frontal, slab)))


def middle_product(frontal, begun, slabs, pick):
    return pl.pallas_call(
        functools.partial(middle_kernel, pick),
        in_specs=vmem(2 + len(slabs)),
        out_specs=vmem(),
        out_shape=jax.ShapeDtypeStruct(begun.shape, jnp.float32),
        cost_estimate=product_cost(frontal, slabs),
        compiler_params=pltpu.CompilerParams(vmem_limit_bytes=24 * 2**20),
    )(frontal, begun, *slabs)


def last_product(frontal, begun, source, slabs, pick, n_col):
    group_rows, wide = begun.shape
    block = jax.ShapeDtypeStruct((n_col // 2, group_rows // n_col, wide), jnp.float32)
    return pl.pallas_call(
        functools.partial(last_kernel, pick),
        in_specs=[smem()] + vmem(2 + len(slabs)),
        out_specs=vmem(2),
        out_shape=[block, jax.ShapeDtypeStruct((group_rows + UNIT, wide), jnp.float32)],
        cost_estimate=product_cost(frontal, slabs),
        compiler_params=pltpu.CompilerParams(vmem_limit_bytes=24 * 2**20),
    )(source, frontal, begun, *slabs)


def keep_rows(total, source, n_col):
    group_rows, wide = total.shape[0] - UNIT, total.shape[1]
    return pl.pallas_call(
        keep_kernel,
        in_specs=[smem(), vmem()],
        out_specs=vmem(),
        out_shape=jax.ShapeDtypeStruct((n_col // 2, group_rows // n_col, wide), jnp.float32),
        cost_estimate=pl.CostEstimate(
            flops=group_rows * wide, bytes_accessed=8 * group_rows * wide, transcendentals=0
        ),
        compiler_params=pltpu.CompilerParams(vmem_limit_bytes=24 * 2**20),
    )(source, total)


def leaf_kernel(
    skel, plan, *refs
):
    parts = refs[:-5]
    mine_out, coeff_out, worst_out, mine, picked = refs[-5:]
    half, wide = parts[0].shape
    samples = wide // 2
    capacity = 2 * half
    every = LEAF_MOST * skel

    total = parts[0][...]
    for part in parts[1:]:
        total = total + part[...]
    mine[pl.ds(0, half), :] = total
    mine[pl.ds(half, half), :] = pltpu.roll(total, samples, 1)
    turned = total.T
    mine_t = jnp.concatenate([turned[:samples], turned[samples:]], axis=1)
    mine_out[...] = mine_t

    mine[pl.ds(capacity, 8), :] = jnp.zeros((8, wide), jnp.float32)
    for k in range(every):
        picked[pl.ds(k, 1), :] = mine[pl.ds(plan[PICKS + k], 1), :]
    begins = [plan[b] for b in range(LEAF_MOST)]
    count = plan[LEAF_MOST]
    chosen = picked[:, :samples]

    gram = nt_dot(chosen, chosen, HIGHEST)
    proj = jnp.dot(chosen, mine_t, precision=HIGHEST, preferred_element_type=jnp.float32)

    slot = lax.broadcasted_iota(jnp.int32, (skel, capacity), 1)
    rank = jnp.zeros((skel, capacity), jnp.int32)
    for b in range(1, LEAF_MOST):
        rank += (slot >= begins[b]).astype(jnp.int32)
    hot = [rank == b for b in range(LEAF_MOST)]
    hot_rows = jnp.concatenate([h.astype(jnp.float32) for h in hot], axis=0)

    lane_leaf = lax.broadcasted_iota(jnp.int32, (skel, every), 1) // skel
    lane_row = lax.broadcasted_iota(jnp.int32, (skel, every), 1) % skel
    down = lax.broadcasted_iota(jnp.int32, (skel, every), 0)
    joined = jnp.where((down == lane_row) & (count == 0), 1.0, 0.0)
    for b in range(LEAF_MOST):
        joined += jnp.where(lane_leaf == b, gram[b * skel : (b + 1) * skel], 0.0)
    spread = jnp.concatenate([jnp.where(lane_row == i, joined, 0.0) for i in range(skel)], axis=0)
    system = jnp.dot(spread, hot_rows, precision=HIGHEST, preferred_element_type=jnp.float32)

    lines = [system[i * skel : (i + 1) * skel] for i in range(skel)]
    right = jnp.zeros((skel, capacity), jnp.float32)
    for b in range(LEAF_MOST):
        right += jnp.where(hot[b], proj[b * skel : (b + 1) * skel], 0.0)
    index = lax.broadcasted_iota(jnp.int32, (skel, capacity), 0)
    uppers = []
    pivots = []
    for j in range(skel):
        line = lines[j]
        inverse = 1.0 / line[j : j + 1]
        upper = line * inverse
        uppers.append(upper)
        pivots.append(inverse)
        for i in range(j + 1, skel):
            lines[i] = lines[i] - line[i : i + 1] * upper
        right = right - jnp.where(index > j, upper * right[j : j + 1], 0.0)
    solved = right * jnp.concatenate(pivots, axis=0)
    for j in range(skel - 2, -1, -1):
        known = jnp.where(index > j, uppers[j] * solved, 0.0)
        less = jnp.sum(known, axis=0, keepdims=True)
        solved = jnp.where(index == j, solved - less, solved)
    coeff_out[...] = solved

    weights = jnp.concatenate([jnp.where(h, solved, 0.0) for h in hot], axis=0)
    rebuilt = lax.dot_general(
        chosen,
        weights,
        (((0,), (0,)), ((), ())),
        precision=HIGHEST,
        preferred_element_type=jnp.float32,
    )
    resid = mine_t - rebuilt
    err = jnp.sum(resid * resid, axis=0, keepdims=True)
    norm = jnp.sum(mine_t * mine_t, axis=0, keepdims=True)
    worst = jnp.zeros((1, 1), jnp.float32)
    for b in range(LEAF_MOST):
        near = hot[b][:1]
        err_leaf = jnp.sum(jnp.where(near, err, 0.0), axis=1, keepdims=True)
        norm_leaf = jnp.sum(jnp.where(near, norm, 0.0), axis=1, keepdims=True)
        worst = jnp.maximum(worst, jnp.sqrt(err_leaf) / jnp.sqrt(norm_leaf + 1e-06))
    worst_out[...] = jnp.broadcast_to(worst, worst_out.shape)


def leaf_work(parts, plan):
    half, wide = parts[0].shape
    samples = wide // 2
    skel = (plan.shape[0] - PICKS) // LEAF_MOST
    return pl.pallas_call(
        functools.partial(leaf_kernel, skel),
        in_specs=[smem()] + vmem(len(parts)),
        out_specs=vmem(3),
        out_shape=[
            jax.ShapeDtypeStruct((samples, 2 * half), jnp.float32),
            jax.ShapeDtypeStruct((skel, 2 * half), jnp.float32),
            jax.ShapeDtypeStruct((1, LANES), jnp.float32),
        ],
        scratch_shapes=[
            pltpu.VMEM((2 * half + 8, wide), jnp.float32),
            pltpu.VMEM((LEAF_MOST * skel, wide), jnp.float32),
        ],
        compiler_params=pltpu.CompilerParams(vmem_limit_bytes=12 * 2**20),
    )(plan, *parts)


def exchange(value, axis, flip):
    pairs = [(k, k ^ flip) for k in range(lax.axis_size(axis))]
    return lax.ppermute(value, axis, pairs)


def largest(value, axes):
    size = lax.axis_size(axes)
    strides = [1]
    while strides[-1] * FAN < size:
        strides.append(strides[-1] * FAN)

    def pass_on(value, stride, up):
        others = []
        for k in range(1, FAN):
            pairs = [(at + k * stride, at) for at in range(0, size, FAN * stride)]
            pairs = [pair for pair in pairs if pair[0] < size]
            if pairs:
                pairs = pairs if up else [pair[::-1] for pair in pairs]
                others.append(lax.ppermute(value, axes, pairs))
        return functools.reduce(jnp.maximum, others, value)

    for stride in strides:
        value = pass_on(value, stride, True)
    for stride in strides[::-1]:
        value = pass_on(value, stride, False)
    return value


def local(frontal, sample_cols, leaf_first, leaf_owner, skeleton):
    n_col = lax.axis_size("col")
    n_row = lax.axis_size("row")
    own = sample_cols.T
    slabs = [exchange(own, "row", k) for k in range(1, n_row)]
    held, begun, source, plan = own_product(
        frontal, own, leaf_first, leaf_owner, skeleton.T, n_row, n_col
    )
    pick = tuple(range(1, n_row))
    begun = middle_product(held, begun, slabs[:-1], pick[:-1])
    swap, total = last_product(held, begun, source, slabs[-1:], pick[-1:], n_col)
    swapped = exchange(swap, "col", 1)
    summed = keep_rows(total, source, n_col) + swapped
    parts = [summed[0]] + [exchange(summed[k], "col", 2 * k) for k in range(1, n_col // 2)]
    mine, coeff, worst = leaf_work(parts, plan)
    worst = largest(worst, ("row", "col"))
    return (mine, coeff, worst[0, :1])


def solution(mesh):
    return jax.shard_map(
        local,
        mesh=mesh,
        in_specs=(P("row", "col"), P(("col", "row"), None), P(), P(), P()),
        out_specs=(P("row", "col"), P("row", "col"), P()),
        check_vma=False,
    )
```

time: 52 us -> 72.2 us (1.39)
  the two profiles are of different devices: /device:TPU:0 before, /device:TPU:2 now
where the time goes in v3:
time: 72.2 us; the launch traced here: 71.7 us
  starting transfers between devices  28.8 us (40%)
  waiting for transfers between devices  28.8 us (40%)
  Pallas kernels  12.5 us (17%)
  between operations  1.01 us (1%)
    ppermute x20, waiting for transfers between devices, pass_on(): others.append(lax.ppermute(value, axes, pairs))  21 us
    ppermute x20, starting transfers between devices, pass_on(): others.append(lax.ppermute(value, axes, pairs))  20.7 us
    ppermute x7, starting transfers between devices, exchange(): return lax.ppermute(value, axis, pairs)  8.07 us
    ppermute x7, waiting for transfers between devices, exchange(): return lax.ppermute(value, axis, pairs)  7.87 us
    pallas_call x1, Pallas kernels, own_product(): pl.pallas_call(functools.partial(own_kernel, n_row, n_col), in_specs=[hbm...  6 us
    pallas_call x1, Pallas kernels, leaf_work(): pl.pallas_call(functools.partial(leaf_kernel, skel), in_specs=[smem()] +...  2.19 us
    pallas_call x1, Pallas kernels, middle_product(): pl.pallas_call(functools.partial(middle_kernel, pick), in_specs=vmem(2 +...  1.95 us
    pallas_call x1, Pallas kernels, last_product(): pl.pallas_call(functools.partial(last_kernel, pick), in_specs=[smem()] +...  1.74 us
  transfers between devices with their start and end apart: 27, of which 6 were waited for; matrix products, arithmetic and copies ran while one was open for 0% of the time, Pallas kernels for 12%

profile of v3, /device:TPU:2, one launch (start us, length us, event | category | flops | bytes accessed | tf_op | source)
XLA Modules:
  0.0 71.7 jit_solution(16429252553875314892)
XLA Ops:
  0.6 0.1 collective-permute-start
  0.7 2.0 %collective-permute-start.1 = (bf16[64,1536]{1,0:T(8,128)(2,1)}, bf16[64,1536]{1,0:T(8,128)(2,1)S(1)}, u32[]{:S(2)}, u32[]{:S(2)}) collective-permute-start(bf16[64,1536]{1,0:T(8,128)(2,1)} %bitcast.13), channel_id=1, source_target_pairs={{0,16},{8,24},{16,0},{24,8},{1,17},{9,25},{17,1},{25,9},{2,18},{10... | collective-permute-start | bytes 589832 | tf_op jit(solution)/shard_map/ppermute | solution.py:431
  2.8 1.4 %collective-permute-start.2 = (bf16[64,1536]{1,0:T(8,128)(2,1)}, bf16[64,1536]{1,0:T(8,128)(2,1)S(1)}, u32[]{:S(2)}, u32[]{:S(2)}) collective-permute-start(bf16[64,1536]{1,0:T(8,128)(2,1)} %bitcast.14), channel_id=1, source_target_pairs={{0,24},{8,16},{16,8},{24,0},{1,25},{9,17},{17,9},{25,1},{2,26},{10... | collective-permute-start | bytes 589832 | tf_op jit(solution)/shard_map/ppermute | solution.py:431
  4.2 6.0 %shard_map.76 = (bf16[1024,6144]{1,0:T(8,128)(2,1)S(1)}, f32[1024,128]{1,0:T(8,128)S(1)}, s32[64]{0:T(128)S(1)}, s32[72]{0:T(128)S(1)}) custom-call(s32[64]{0:T(128)} %leaf_first.1, s32[64]{0:T(128)} %leaf_owner.1, s32[16,64]{1,0:T(8,128)} %bitcast.16, bf16[1024,6144]{1,0:T(8,128)(2,1)} %frontal.1, bf16[64,1536]{1,0:T(8,128)(2,1)} %bitcast.15), custom_call_target="tpu_custom_call" | custom-call | flops 3221225472 | bytes 12582912 | tf_op jit(solution)/shard_map/pallas_call | solution.py:257
  10.2 0.0 collective-permute-done.refs_0_
  10.2 1.0 %collective-permute-done.1.refs_1_ = bf16[64,1536]{1,0:T(8,128)(2,1)S(1)} collective-permute-done((bf16[64,1536]{1,0:T(8,128)(2,1)}, bf16[64,1536]{1,0:T(8,128)(2,1)S(1)}, u32[]{:S(2)}, u32[]{:S(2)}) %collective-permute-start.1) | collective-permute-done | bytes 196640 | tf_op jit(solution)/shard_map/ppermute | solution.py:431
  11.2 2.0 %shard_map.77.begun = f32[1024,128]{1,0:T(8,128)S(1)} custom-call(bf16[1024,6144]{1,0:T(8,128)(2,1)S(1)} %get-tuple-element.14.frontal, f32[1024,128]{1,0:T(8,128)S(1)} %get-tuple-element.15.begun, bf16[64,1536]{1,0:T(8,128)(2,1)S(1)} %collective-permute-done.refs_0_, bf16[64,1536]{1,0:T(8,128)(2,1)S(1)} %collective-permute-done.1.refs_1_), custom_call_target="tpu_custom_call" | custom-call | flops 1610612736 | bytes 6291456 | tf_op jit(solution)/shard_map/pallas_call | solution.py:283
  13.2 0.0 collective-permute-done.2.refs_0_
  13.2 1.7 %shard_map.78 = (f32[4,128,128]{2,1,0:T(8,128)S(1)}, f32[1056,128]{1,0:T(8,128)S(1)}) custom-call(s32[64]{0:T(128)S(1)} %get-tuple-element.13.source, bf16[1024,6144]{1,0:T(8,128)(2,1)S(1)} %get-tuple-element.14.frontal, f32[1024,128]{1,0:T(8,128)S(1)} %shard_map.77.begun, bf16[64,1536]{1,0:T(8,128)(2,1)S(1)} %collective-permute-done.2.refs_0_), custom_call_target="tpu_custom_call" | custom-call | flops 805306368 | bytes 3145728 | tf_op jit(solution)/shard_map/pallas_call | solution.py:296
  14.9 0.1 collective-permute-start.3
  15.0 0.6 shard_map.79
  15.6 0.9 %collective-permute-done.3 = f32[4,128,128]{2,1,0:T(8,128)S(1)} collective-permute-done((f32[4,128,128]{2,1,0:T(8,128)S(1)}, f32[4,128,128]{2,1,0:T(8,128)S(1)}, u32[]{:S(2)}, u32[]{:S(2)}) %collective-permute-start.3) | collective-permute-done | bytes 262176 | tf_op jit(solution)/shard_map/ppermute | solution.py:431
  16.6 1.6 %collective-permute-start.4 = (f32[128,128]{1,0:T(8,128)S(1)}, f32[128,128]{1,0:T(8,128)S(1)}, u32[]{:S(2)}, u32[]{:S(2)}) collective-permute-start(f32[128,128]{1,0:T(8,128)S(1)} %get-tuple-element.23), channel_id=1, source_target_pairs={{0,2},{1,3},{2,0},{3,1},{4,6},{5,7},{6,4},{7,5},{8,10},{9,11},{10,... | collective-permute-start | bytes 196616 | tf_op jit(solution)/shard_map/ppermute | solution.py:431
  18.2 2.6 %collective-permute-start.5 = (f32[128,128]{1,0:T(8,128)S(1)}, f32[128,128]{1,0:T(8,128)S(1)}, u32[]{:S(2)}, u32[]{:S(2)}) collective-permute-start(f32[128,128]{1,0:T(8,128)S(1)} %get-tuple-element.22), channel_id=1, source_target_pairs={{0,4},{1,5},{2,6},{3,7},{4,0},{5,1},{6,2},{7,3},{8,12},{9,13},{10,... | collective-permute-start | bytes 196616 | tf_op jit(solution)/shard_map/ppermute | solution.py:431
  20.8 0.2 collective-permute-start.6
  21.0 0.0 collective-permute-done.4.refs_1_
  21.0 4.7 %collective-permute-done.5.refs_2_ = f32[128,128]{1,0:T(8,128)S(1)} collective-permute-done((f32[128,128]{1,0:T(8,128)S(1)}, f32[128,128]{1,0:T(8,128)S(1)}, u32[]{:S(2)}, u32[]{:S(2)}) %collective-permute-start.5) | collective-permute-done | bytes 65568 | tf_op jit(solution)/shard_map/ppermute | solution.py:431
  25.8 1.2 %collective-permute-done.6.refs_3_ = f32[128,128]{1,0:T(8,128)S(1)} collective-permute-done((f32[128,128]{1,0:T(8,128)S(1)}, f32[128,128]{1,0:T(8,128)S(1)}, u32[]{:S(2)}, u32[]{:S(2)}) %collective-permute-start.6) | collective-permute-done | bytes 65568 | tf_op jit(solution)/shard_map/ppermute | solution.py:431
  27.0 2.2 %shard_map.80 = (f32[64,256]{1,0:T(8,128)}, f32[16,256]{1,0:T(8,128)}, f32[1,128]{1,0:T(1,128)S(1)}) custom-call(s32[72]{0:T(128)S(1)} %get-tuple-element.12.plan, f32[128,128]{1,0:T(8,128)S(1)} %get-tuple-element.24.refs_0_, f32[128,128]{1,0:T(8,128)S(1)} %collective-permute-done.4.refs_1_, f32[128,128]{1,0:T(8,128)S(1)} %collective-permute-done.5.refs_2_, ...), custom_call_target="tpu_custom_call" | custom-call | tf_op jit(solution)/shard_map/pallas_call | solution.py:412
  29.2 0.6 collective-permute-start.11
  29.8 0.7 collective-permute-start.10
  30.5 0.7 collective-permute-start.9
  31.2 7.5 %collective-permute-start.8 = (f32[1,128]{1,0:T(1,128)S(1)}, f32[1,128]{1,0:T(1,128)S(1)}, u32[]{:S(2)}, u32[]{:S(2)}) collective-permute-start(f32[1,128]{1,0:T(1,128)S(1)} %get-tuple-element.20), channel_id=1, source_target_pairs={{2,0},{8,6},{14,12},{20,18},{26,24}} | collective-permute-start | bytes 1544 | tf_op jit(solution)/shard_map/ppermute | solution.py:447
  38.7 0.7 collective-permute-start.7
  39.4 0.0 collective-permute-done.11
  39.4 0.0 collective-permute-done.10
  39.4 0.0 collective-permute-done.9
  39.4 0.6 collective-permute-done.8
  40.0 0.0 collective-permute-done.7
  40.0 0.7 collective-permute-start.16
  40.7 0.7 collective-permute-start.15
  41.3 0.7 collective-permute-start.14
  42.0 0.7 collective-permute-start.13
  42.7 0.7 collective-permute-start.12
  43.3 0.0 collective-permute-done.16
  43.3 0.0 collective-permute-done.15
  43.4 0.0 collective-permute-done.14
  43.4 0.0 collective-permute-done.13
  43.4 0.0 collective-permute-done.12
  43.4 0.7 collective-permute-start.21
  44.1 0.7 collective-permute-start.20
  44.7 0.7 collective-permute-start.19
  45.4 0.7 collective-permute-start.18
  46.1 0.7 collective-permute-start.17
  46.8 0.0 collective-permute-done.21
  46.8 0.0 collective-permute-done.20
  46.8 0.0 collective-permute-done.19
  46.8 0.0 collective-permute-done.18
  46.8 0.0 collective-permute-done.17
  46.8 0.7 collective-permute-start.26
  47.5 0.7 collective-permute-start.25
  48.2 0.7 collective-permute-start.24
  48.8 1.3 %collective-permute-start.23 = (f32[1,128]{1,0:T(1,128)S(1)}, f32[1,128]{1,0:T(1,128)S(1)}, u32[]{:S(2)}, u32[]{:S(2)}) collective-permute-start(f32[1,128]{1,0:T(1,128)S(1)} %maximum_maximum_fusion.1), channel_id=1, source_target_pairs={{0,2},{6,8},{12,14},{18,20},{24,26}} | collective-permute-start | bytes 1544 | tf_op jit(solution)/shard_map/ppermute | solution.py:447
  50.1 0.7 collective-permute-start.22
  50.8 0.0 collective-permute-done.26
  50.8 0.0 collective-permute-done.25
  50.8 0.0 collective-permute-done.24
  50.8 20.3 %collective-permute-done.23 = f32[1,128]{1,0:T(1,128)S(1)} collective-permute-done((f32[1,128]{1,0:T(1,128)S(1)}, f32[1,128]{1,0:T(1,128)S(1)}, u32[]{:S(2)}, u32[]{:S(2)}) %collective-permute-start.23) | collective-permute-done | bytes 544 | tf_op jit(solution)/shard_map/ppermute | solution.py:447
  71.2 0.0 collective-permute-done.22
  71.2 0.5 maximum_maximum_fusion
  (5 shorter events, 0.1 us)
Async XLA Ops:
  0.6 9.6 %collective-permute-start = (bf16[64,1536]{1,0:T(8,128)(2,1)}, bf16[64,1536]{1,0:T(8,128)(2,1)S(1)}, u32[]{:S(2)}, u32[]{:S(2)}) collective-permute-start(bf16[64,1536]{1,0:T(8,128)(2,1)} %bitcast.12), channel_id=1, source_target_pairs={{0,8},{8,0},{16,24},{24,16},{1,9},{9,1},{17,25},{25,17},{2,10},{10... | collective-permute-start | bytes 589832 | tf_op jit(solution)/shard_map/ppermute | solution.py:431
  0.7 10.5 %collective-permute-start.1 = (bf16[64,1536]{1,0:T(8,128)(2,1)}, bf16[64,1536]{1,0:T(8,128)(2,1)S(1)}, u32[]{:S(2)}, u32[]{:S(2)}) collective-permute-start(bf16[64,1536]{1,0:T(8,128)(2,1)} %bitcast.13), channel_id=1, source_target_pairs={{0,16},{8,24},{16,0},{24,8},{1,17},{9,25},{17,1},{25,9},{2,18},{10... | collective-permute-start | bytes 589832 | tf_op jit(solution)/shard_map/ppermute | solution.py:431
  2.8 10.4 %collective-permute-start.2 = (bf16[64,1536]{1,0:T(8,128)(2,1)}, bf16[64,1536]{1,0:T(8,128)(2,1)S(1)}, u32[]{:S(2)}, u32[]{:S(2)}) collective-permute-start(bf16[64,1536]{1,0:T(8,128)(2,1)} %bitcast.14), channel_id=1, source_target_pairs={{0,24},{8,16},{16,8},{24,0},{1,25},{9,17},{17,9},{25,1},{2,26},{10... | collective-permute-start | bytes 589832 | tf_op jit(solution)/shard_map/ppermute | solution.py:431
  14.9 1.6 %collective-permute-start.3 = (f32[4,128,128]{2,1,0:T(8,128)S(1)}, f32[4,128,128]{2,1,0:T(8,128)S(1)}, u32[]{:S(2)}, u32[]{:S(2)}) collective-permute-start(f32[4,128,128]{2,1,0:T(8,128)S(1)} %get-tuple-element.17), channel_id=1, source_target_pairs={{0,1},{1,0},{2,3},{3,2},{4,5},{5,4},{6,7},{7,6},{8,9},{9,8},{10,11... | collective-permute-start | bytes 786440 | tf_op jit(solution)/shard_map/ppermute | solution.py:431
  16.6 4.5 %collective-permute-start.4 = (f32[128,128]{1,0:T(8,128)S(1)}, f32[128,128]{1,0:T(8,128)S(1)}, u32[]{:S(2)}, u32[]{:S(2)}) collective-permute-start(f32[128,128]{1,0:T(8,128)S(1)} %get-tuple-element.23), channel_id=1, source_target_pairs={{0,2},{1,3},{2,0},{3,1},{4,6},{5,7},{6,4},{7,5},{8,10},{9,11},{10,... | collective-permute-start | bytes 196616 | tf_op jit(solution)/shard_map/ppermute | solution.py:431
  18.2 7.5 %collective-permute-start.5 = (f32[128,128]{1,0:T(8,128)S(1)}, f32[128,128]{1,0:T(8,128)S(1)}, u32[]{:S(2)}, u32[]{:S(2)}) collective-permute-start(f32[128,128]{1,0:T(8,128)S(1)} %get-tuple-element.22), channel_id=1, source_target_pairs={{0,4},{1,5},{2,6},{3,7},{4,0},{5,1},{6,2},{7,3},{8,12},{9,13},{10,... | collective-permute-start | bytes 196616 | tf_op jit(solution)/shard_map/ppermute | solution.py:431
  20.8 6.2 %collective-permute-start.6 = (f32[128,128]{1,0:T(8,128)S(1)}, f32[128,128]{1,0:T(8,128)S(1)}, u32[]{:S(2)}, u32[]{:S(2)}) collective-permute-start(f32[128,128]{1,0:T(8,128)S(1)} %get-tuple-element.21), channel_id=1, source_target_pairs={{0,6},{1,7},{2,4},{3,5},{4,2},{5,3},{6,0},{7,1},{8,14},{9,15},{10,... | collective-permute-start | bytes 196616 | tf_op jit(solution)/shard_map/ppermute | solution.py:431
  29.2 10.2 %collective-permute-start.11 = (f32[1,128]{1,0:T(1,128)S(1)}, f32[1,128]{1,0:T(1,128)S(1)}, u32[]{:S(2)}, u32[]{:S(2)}) collective-permute-start(f32[1,128]{1,0:T(1,128)S(1)} %get-tuple-element.20), channel_id=1, source_target_pairs={{5,0},{11,6},{17,12},{23,18},{29,24}} | collective-permute-start | bytes 1544 | tf_op jit(solution)/shard_map/ppermute | solution.py:447
  29.8 9.6 %collective-permute-start.10 = (f32[1,128]{1,0:T(1,128)S(1)}, f32[1,128]{1,0:T(1,128)S(1)}, u32[]{:S(2)}, u32[]{:S(2)}) collective-permute-start(f32[1,128]{1,0:T(1,128)S(1)} %get-tuple-element.20), channel_id=1, source_target_pairs={{4,0},{10,6},{16,12},{22,18},{28,24}} | collective-permute-start | bytes 1544 | tf_op jit(solution)/shard_map/ppermute | solution.py:447
  30.5 8.9 %collective-permute-start.9 = (f32[1,128]{1,0:T(1,128)S(1)}, f32[1,128]{1,0:T(1,128)S(1)}, u32[]{:S(2)}, u32[]{:S(2)}) collective-permute-start(f32[1,128]{1,0:T(1,128)S(1)} %get-tuple-element.20), channel_id=1, source_target_pairs={{3,0},{9,6},{15,12},{21,18},{27,24}} | collective-permute-start | bytes 1544 | tf_op jit(solution)/shard_map/ppermute | solution.py:447
  31.2 8.8 %collective-permute-start.8 = (f32[1,128]{1,0:T(1,128)S(1)}, f32[1,128]{1,0:T(1,128)S(1)}, u32[]{:S(2)}, u32[]{:S(2)}) collective-permute-start(f32[1,128]{1,0:T(1,128)S(1)} %get-tuple-element.20), channel_id=1, source_target_pairs={{2,0},{8,6},{14,12},{20,18},{26,24}} | collective-permute-start | bytes 1544 | tf_op jit(solution)/shard_map/ppermute | solution.py:447
  38.7 1.3 %collective-permute-start.7 = (f32[1,128]{1,0:T(1,128)S(1)}, f32[1,128]{1,0:T(1,128)S(1)}, u32[]{:S(2)}, u32[]{:S(2)}) collective-permute-start(f32[1,128]{1,0:T(1,128)S(1)} %get-tuple-element.20), channel_id=1, source_target_pairs={{1,0},{7,6},{13,12},{19,18},{25,24},{31,30}} | collective-permute-start | bytes 1544 | tf_op jit(solution)/shard_map/ppermute | solution.py:447
  40.0 3.4 %collective-permute-start.16 = (f32[1,128]{1,0:T(1,128)S(1)}, f32[1,128]{1,0:T(1,128)S(1)}, u32[]{:S(2)}, u32[]{:S(2)}) collective-permute-start(f32[1,128]{1,0:T(1,128)S(1)} %maximum_maximum_fusion.3), channel_id=1, source_target_pairs={{30,0}} | collective-permute-start | bytes 1544 | tf_op jit(solution)/shard_map/ppermute | solution.py:447
  40.7 2.7 %collective-permute-start.15 = (f32[1,128]{1,0:T(1,128)S(1)}, f32[1,128]{1,0:T(1,128)S(1)}, u32[]{:S(2)}, u32[]{:S(2)}) collective-permute-start(f32[1,128]{1,0:T(1,128)S(1)} %maximum_maximum_fusion.3), channel_id=1, source_target_pairs={{24,0}} | collective-permute-start | bytes 1544 | tf_op jit(solution)/shard_map/ppermute | solution.py:447
  41.3 2.0 %collective-permute-start.14 = (f32[1,128]{1,0:T(1,128)S(1)}, f32[1,128]{1,0:T(1,128)S(1)}, u32[]{:S(2)}, u32[]{:S(2)}) collective-permute-start(f32[1,128]{1,0:T(1,128)S(1)} %maximum_maximum_fusion.3), channel_id=1, source_target_pairs={{18,0}} | collective-permute-start | bytes 1544 | tf_op jit(solution)/shard_map/ppermute | solution.py:447
  42.0 1.4 %collective-permute-start.13 = (f32[1,128]{1,0:T(1,128)S(1)}, f32[1,128]{1,0:T(1,128)S(1)}, u32[]{:S(2)}, u32[]{:S(2)}) collective-permute-start(f32[1,128]{1,0:T(1,128)S(1)} %maximum_maximum_fusion.3), channel_id=1, source_target_pairs={{12,0}} | collective-permute-start | bytes 1544 | tf_op jit(solution)/shard_map/ppermute | solution.py:447
  42.7 0.7 collective-permute-start.12
  43.4 3.4 %collective-permute-start.21 = (f32[1,128]{1,0:T(1,128)S(1)}, f32[1,128]{1,0:T(1,128)S(1)}, u32[]{:S(2)}, u32[]{:S(2)}) collective-permute-start(f32[1,128]{1,0:T(1,128)S(1)} %maximum_maximum_fusion.2), channel_id=1, source_target_pairs={{0,30}} | collective-permute-start | bytes 1544 | tf_op jit(solution)/shard_map/ppermute | solution.py:447
  44.1 2.7 %collective-permute-start.20 = (f32[1,128]{1,0:T(1,128)S(1)}, f32[1,128]{1,0:T(1,128)S(1)}, u32[]{:S(2)}, u32[]{:S(2)}) collective-permute-start(f32[1,128]{1,0:T(1,128)S(1)} %maximum_maximum_fusion.2), channel_id=1, source_target_pairs={{0,24}} | collective-permute-start | bytes 1544 | tf_op jit(solution)/shard_map/ppermute | solution.py:447
  44.7 2.0 %collective-permute-start.19 = (f32[1,128]{1,0:T(1,128)S(1)}, f32[1,128]{1,0:T(1,128)S(1)}, u32[]{:S(2)}, u32[]{:S(2)}) collective-permute-start(f32[1,128]{1,0:T(1,128)S(1)} %maximum_maximum_fusion.2), channel_id=1, source_target_pairs={{0,18}} | collective-permute-start | bytes 1544 | tf_op jit(solution)/shard_map/ppermute | solution.py:447
  45.4 1.4 %collective-permute-start.18 = (f32[1,128]{1,0:T(1,128)S(1)}, f32[1,128]{1,0:T(1,128)S(1)}, u32[]{:S(2)}, u32[]{:S(2)}) collective-permute-start(f32[1,128]{1,0:T(1,128)S(1)} %maximum_maximum_fusion.2), channel_id=1, source_target_pairs={{0,12}} | collective-permute-start | bytes 1544 | tf_op jit(solution)/shard_map/ppermute | solution.py:447
  46.1 0.7 collective-permute-start.17
  46.8 4.0 %collective-permute-start.26 = (f32[1,128]{1,0:T(1,128)S(1)}, f32[1,128]{1,0:T(1,128)S(1)}, u32[]{:S(2)}, u32[]{:S(2)}) collective-permute-start(f32[1,128]{1,0:T(1,128)S(1)} %maximum_maximum_fusion.1), channel_id=1, source_target_pairs={{0,5},{6,11},{12,17},{18,23},{24,29}} | collective-permute-start | bytes 1544 | tf_op jit(solution)/shard_map/ppermute | solution.py:447
  47.5 3.3 %collective-permute-start.25 = (f32[1,128]{1,0:T(1,128)S(1)}, f32[1,128]{1,0:T(1,128)S(1)}, u32[]{:S(2)}, u32[]{:S(2)}) collective-permute-start(f32[1,128]{1,0:T(1,128)S(1)} %maximum_maximum_fusion.1), channel_id=1, source_target_pairs={{0,4},{6,10},{12,16},{18,22},{24,28}} | collective-permute-start | bytes 1544 | tf_op jit(solution)/shard_map/ppermute | solution.py:447
  48.2 2.7 %collective-permute-start.24 = (f32[1,128]{1,0:T(1,128)S(1)}, f32[1,128]{1,0:T(1,128)S(1)}, u32[]{:S(2)}, u32[]{:S(2)}) collective-permute-start(f32[1,128]{1,0:T(1,128)S(1)} %maximum_maximum_fusion.1), channel_id=1, source_target_pairs={{0,3},{6,9},{12,15},{18,21},{24,27}} | collective-permute-start | bytes 1544 | tf_op jit(solution)/shard_map/ppermute | solution.py:447
  48.8 22.3 %collective-permute-start.23 = (f32[1,128]{1,0:T(1,128)S(1)}, f32[1,128]{1,0:T(1,128)S(1)}, u32[]{:S(2)}, u32[]{:S(2)}) collective-permute-start(f32[1,128]{1,0:T(1,128)S(1)} %maximum_maximum_fusion.1), channel_id=1, source_target_pairs={{0,2},{6,8},{12,14},{18,20},{24,26}} | collective-permute-start | bytes 1544 | tf_op jit(solution)/shard_map/ppermute | solution.py:447
  50.1 21.0 %collective-permute-start.22 = (f32[1,128]{1,0:T(1,128)S(1)}, f32[1,128]{1,0:T(1,128)S(1)}, u32[]{:S(2)}, u32[]{:S(2)}) collective-permute-start(f32[1,128]{1,0:T(1,128)S(1)} %maximum_maximum_fusion.1), channel_id=1, source_target_pairs={{0,1},{6,7},{12,13},{18,19},{24,25},{30,31}} | collective-permute-start | bytes 1544 | tf_op jit(solution)/shard_map/ppermute | solution.py:447

commit v4 on v3

--- a/solution.py
+++ b/solution.py
@@ -11,7 +11,9 @@
 LANES = 128
 LEAF_MOST = 4
 PICKS = 8
-FAN = 6
+LEVELS = 32760.0
+EXTRA = 16
+STEPS = 64.0
 RUN_LEAVES = 4
 HIGHEST = lax.Precision.HIGHEST
 
@@ -317,25 +319,59 @@
     )(source, total)
 
 
+def squeeze_kernel(keep, swapped, here, *away):
+    samples = keep.shape[2] // 2
+    here[...] = (keep[0] + swapped[0]).T
+    row = lax.broadcasted_iota(jnp.int32, (EXTRA, keep.shape[1]), 0)
+    for k, out in enumerate(away):
+        block = (keep[k + 1] + swapped[k + 1]).T
+        tail = jnp.zeros(row.shape, jnp.float32)
+        for side in range(2):
+            rows = slice(side * samples, (side + 1) * samples)
+            part = block[rows]
+            most = jnp.maximum(jnp.max(jnp.abs(part), axis=0, keepdims=True), 1e-30)
+            power = jnp.ceil(jnp.log2(most) * STEPS)
+            scaled = part * (LEVELS * jnp.exp2(power * (-1.0 / STEPS)))
+            whole = jnp.floor(scaled + 0.5).astype(jnp.int32)
+            out[rows, :] = whole.astype(jnp.int16)
+            tail = jnp.where(row == side, power, tail)
+        out[pl.ds(2 * samples, EXTRA), :] = tail.astype(jnp.int32).astype(jnp.int16)
+
+
+def squeeze(keep, swapped):
+    chips, half, wide = keep.shape
+    small = jax.ShapeDtypeStruct((wide + EXTRA, half), jnp.int16)
+    return pl.pallas_call(
+        squeeze_kernel,
+        in_specs=vmem(2),
+        out_specs=vmem(chips),
+        out_shape=[jax.ShapeDtypeStruct((wide, half), jnp.float32)] + [small] * (chips - 1),
+        compiler_params=pltpu.CompilerParams(vmem_limit_bytes=24 * 2**20),
+    )(keep, swapped)
+
+
 def leaf_kernel(
     skel, plan, *refs
 ):
-    parts = refs[:-5]
+    here, *parts = refs[:-5]
     mine_out, coeff_out, worst_out, mine, picked = refs[-5:]
-    half, wide = parts[0].shape
+    wide, half = here.shape
     samples = wide // 2
     capacity = 2 * half
     every = LEAF_MOST * skel
 
-    total = parts[0][...]
-    for part in parts[1:]:
-        total = total + part[...]
+    sides = [here[pl.ds(0, samples), :], here[pl.ds(samples, samples), :]]
+    for part in parts:
+        tail = part[pl.ds(wide, EXTRA), :].astype(jnp.int32).astype(jnp.float32)
+        step = jnp.exp2(tail * (1.0 / STEPS)) * (1.0 / LEVELS)
+        for side in range(2):
+            value = part[pl.ds(side * samples, samples), :].astype(jnp.int32).astype(jnp.float32)
+            sides[side] = sides[side] + value * step[side : side + 1]
+    mine_t = jnp.concatenate(sides, axis=1)
+    mine_out[...] = mine_t
+    total = jnp.concatenate(sides, axis=0).T
     mine[pl.ds(0, half), :] = total
     mine[pl.ds(half, half), :] = pltpu.roll(total, samples, 1)
-    turned = total.T
-    mine_t = jnp.concatenate([turned[:samples], turned[samples:]], axis=1)
-    mine_out[...] = mine_t
-
     mine[pl.ds(capacity, 8), :] = jnp.zeros((8, wide), jnp.float32)
     for k in range(every):
         picked[pl.ds(k, 1), :] = mine[pl.ds(plan[PICKS + k], 1), :]
@@ -405,13 +441,13 @@
     worst_out[...] = jnp.broadcast_to(worst, worst_out.shape)
 
 
-def leaf_work(parts, plan):
-    half, wide = parts[0].shape
+def leaf_work(here, parts, plan):
+    wide, half = here.shape
     samples = wide // 2
     skel = (plan.shape[0] - PICKS) // LEAF_MOST
     return pl.pallas_call(
         functools.partial(leaf_kernel, skel),
-        in_specs=[smem()] + vmem(len(parts)),
+        in_specs=[smem()] + vmem(1 + len(parts)),
         out_specs=vmem(3),
         out_shape=[
             jax.ShapeDtypeStruct((samples, 2 * half), jnp.float32),
@@ -423,7 +459,7 @@
             pltpu.VMEM((LEAF_MOST * skel, wide), jnp.float32),
         ],
         compiler_params=pltpu.CompilerParams(vmem_limit_bytes=12 * 2**20),
-    )(plan, *parts)
+    )(plan, here, *parts)
 
 
 def exchange(value, axis, flip):
@@ -433,25 +469,8 @@
 
 def largest(value, axes):
     size = lax.axis_size(axes)
-    strides = [1]
-    while strides[-1] * FAN < size:
-        strides.append(strides[-1] * FAN)
-
-    def pass_on(value, stride, up):
-        others = []
-        for k in range(1, FAN):
-            pairs = [(at + k * stride, at) for at in range(0, size, FAN * stride)]
-            pairs = [pair for pair in pairs if pair[0] < size]
-            if pairs:
-                pairs = pairs if up else [pair[::-1] for pair in pairs]
-                others.append(lax.ppermute(value, axes, pairs))
-        return functools.reduce(jnp.maximum, others, value)
-
-    for stride in strides:
-        value = pass_on(value, stride, True)
-    for stride in strides[::-1]:
-        value = pass_on(value, stride, False)
-    return value
+    every = jnp.broadcast_to(value[None], (size, *value.shape))
+    return jnp.max(lax.all_to_all(every, axes, 0, 0), axis=0)
 
 
 def local(frontal, sample_cols, leaf_first, leaf_owner, skeleton):
@@ -466,9 +485,9 @@
     begun = middle_product(held, begun, slabs[:-1], pick[:-1])
     swap, total = last_product(held, begun, source, slabs[-1:], pick[-1:], n_col)
     swapped = exchange(swap, "col", 1)
-    summed = keep_rows(total, source, n_col) + swapped
-    parts = [summed[0]] + [exchange(summed[k], "col", 2 * k) for k in range(1, n_col // 2)]
-    mine, coeff, worst = leaf_work(parts, plan)
+    here, *away = squeeze(keep_rows(total, source, n_col), swapped)
+    parts = [exchange(value, "col", 2 * (k + 1)) for k, value in enumerate(away)]
+    mine, coeff, worst = leaf_work(here, parts, plan)
     worst = largest(worst, ("row", "col"))
     return (mine, coeff, worst[0, :1])
 

time: 72.2 us -> 41.8 us (0.58)
  the two profiles are of different devices: /device:TPU:2 before, /device:TPU:0 now
where the time goes in v4:
time: 41.8 us; the launch traced here: 41.6 us
  Pallas kernels  12.7 us (30%)
  waiting for transfers between devices  9.69 us (23%)
  starting transfers between devices  9.07 us (22%)
  blocking collectives  8.85 us (21%)
  between operations  0.7 us (2%)
  other arithmetic  0.53 us (1%)
    ppermute x7, waiting for transfers between devices, exchange(): return lax.ppermute(value, axis, pairs)  9.69 us
    ppermute x7, starting transfers between devices, exchange(): return lax.ppermute(value, axis, pairs)  9.07 us
    all_to_all x1, blocking collectives, largest(): return jnp.max(lax.all_to_all(every, axes, 0, 0), axis=0)  8.85 us
    pallas_call x1, Pallas kernels, own_product(): pl.pallas_call(functools.partial(own_kernel, n_row, n_col), in_specs=[hbm...  5.99 us
    pallas_call x1, Pallas kernels, leaf_work(): pl.pallas_call(functools.partial(leaf_kernel, skel), in_specs=[smem()] +...  2.29 us
    pallas_call x1, Pallas kernels, middle_product(): pl.pallas_call(functools.partial(middle_kernel, pick), in_specs=vmem(2 +...  1.95 us
    pallas_call x1, Pallas kernels, last_product(): pl.pallas_call(functools.partial(last_kernel, pick), in_specs=[smem()] +...  1.74 us
  transfers between devices with their start and end apart: 7, of which 4 were waited for; matrix products, arithmetic and copies ran while one was open for 0% of the time, Pallas kernels for 21%

profile of v4, /device:TPU:0, one launch (start us, length us, event | category | flops | bytes accessed | tf_op | source)
XLA Modules:
  0.0 41.6 jit_solution(8338940807021748621)
XLA Ops:
  0.6 3.0 %collective-permute-start = (bf16[64,1536]{1,0:T(8,128)(2,1)}, bf16[64,1536]{1,0:T(8,128)(2,1)S(1)}, u32[]{:S(2)}, u32[]{:S(2)}) collective-permute-start(bf16[64,1536]{1,0:T(8,128)(2,1)} %bitcast.8), channel_id=1, source_target_pairs={{0,8},{8,0},{16,24},{24,16},{1,9},{9,1},{17,25},{25,17},{2,10},{10... | collective-permute-start | bytes 589832 | tf_op jit(solution)/shard_map/ppermute | solution.py:467
  3.6 1.5 %collective-permute-start.1 = (bf16[64,1536]{1,0:T(8,128)(2,1)}, bf16[64,1536]{1,0:T(8,128)(2,1)S(1)}, u32[]{:S(2)}, u32[]{:S(2)}) collective-permute-start(bf16[64,1536]{1,0:T(8,128)(2,1)} %bitcast.9), channel_id=1, source_target_pairs={{0,16},{8,24},{16,0},{24,8},{1,17},{9,25},{17,1},{25,9},{2,18},{10... | collective-permute-start | bytes 589832 | tf_op jit(solution)/shard_map/ppermute | solution.py:467
  5.2 0.0 collective-permute-start.2
  5.2 6.0 %shard_map.76 = (bf16[1024,6144]{1,0:T(8,128)(2,1)S(1)}, f32[1024,128]{1,0:T(8,128)S(1)}, s32[64]{0:T(128)S(1)}, s32[72]{0:T(128)S(1)}) custom-call(s32[64]{0:T(128)} %leaf_first.1, s32[64]{0:T(128)} %leaf_owner.1, s32[16,64]{1,0:T(8,128)} %bitcast.13, bf16[1024,6144]{1,0:T(8,128)(2,1)} %frontal.1, bf16[64,1536]{1,0:T(8,128)(2,1)} %bitcast.11), custom_call_target="tpu_custom_call" | custom-call | flops 3221225472 | bytes 12582912 | tf_op jit(solution)/shard_map/pallas_call | solution.py:259
  11.2 0.0 collective-permute-done.refs_0_
  11.2 3.2 %collective-permute-done.1.refs_1_ = bf16[64,1536]{1,0:T(8,128)(2,1)S(1)} collective-permute-done((bf16[64,1536]{1,0:T(8,128)(2,1)}, bf16[64,1536]{1,0:T(8,128)(2,1)S(1)}, u32[]{:S(2)}, u32[]{:S(2)}) %collective-permute-start.1) | collective-permute-done | bytes 196640 | tf_op jit(solution)/shard_map/ppermute | solution.py:467
  14.4 2.0 %shard_map.77.begun = f32[1024,128]{1,0:T(8,128)S(1)} custom-call(bf16[1024,6144]{1,0:T(8,128)(2,1)S(1)} %get-tuple-element.18.frontal, f32[1024,128]{1,0:T(8,128)S(1)} %get-tuple-element.19.begun, bf16[64,1536]{1,0:T(8,128)(2,1)S(1)} %collective-permute-done.refs_0_, bf16[64,1536]{1,0:T(8,128)(2,1)S(1)} %collective-permute-done.1.refs_1_), custom_call_target="tpu_custom_call" | custom-call | flops 1610612736 | bytes 6291456 | tf_op jit(solution)/shard_map/pallas_call | solution.py:285
  16.4 0.0 collective-permute-done.2.refs_0_
  16.4 1.7 %shard_map.78 = (f32[4,128,128]{2,1,0:T(8,128)S(1)}, f32[1056,128]{1,0:T(8,128)S(1)}) custom-call(s32[64]{0:T(128)S(1)} %get-tuple-element.17.source, bf16[1024,6144]{1,0:T(8,128)(2,1)S(1)} %get-tuple-element.18.frontal, f32[1024,128]{1,0:T(8,128)S(1)} %shard_map.77.begun, bf16[64,1536]{1,0:T(8,128)(2,1)S(1)} %collective-permute-done.2.refs_0_), custom_call_target="tpu_custom_call" | custom-call | flops 805306368 | bytes 3145728 | tf_op jit(solution)/shard_map/pallas_call | solution.py:298
  18.1 0.1 collective-permute-start.3
  18.2 0.6 %shard_map.79.keep = f32[4,128,128]{2,1,0:T(8,128)S(1)} custom-call(s32[64]{0:T(128)S(1)} %get-tuple-element.17.source, f32[1056,128]{1,0:T(8,128)S(1)} %get-tuple-element.20.total), custom_call_target="tpu_custom_call" | custom-call | flops 131072 | bytes 1048576 | tf_op jit(solution)/shard_map/pallas_call | solution.py:310
  18.8 0.9 %collective-permute-done.3.swapped = f32[4,128,128]{2,1,0:T(8,128)S(1)} collective-permute-done((f32[4,128,128]{2,1,0:T(8,128)S(1)}, f32[4,128,128]{2,1,0:T(8,128)S(1)}, u32[]{:S(2)}, u32[]{:S(2)}) %collective-permute-start.3) | collective-permute-done | bytes 262176 | tf_op jit(solution)/shard_map/ppermute | solution.py:467
  19.7 0.2 shard_map.80
  19.9 1.6 %collective-permute-start.4 = (s16[144,128]{1,0:T(8,128)(2,1)S(1)}, s16[144,128]{1,0:T(8,128)(2,1)S(1)}, u32[]{:S(2)}, u32[]{:S(2)}) collective-permute-start(s16[144,128]{1,0:T(8,128)(2,1)S(1)} %get-tuple-element.23), channel_id=1, source_target_pairs={{0,2},{1,3},{2,0},{3,1},{4,6},{5,7},{6,4},{7,5},{8,10},{9,11},{10,... | collective-permute-start | bytes 110600 | tf_op jit(solution)/shard_map/ppermute | solution.py:467
  21.6 2.6 %collective-permute-start.5 = (s16[144,128]{1,0:T(8,128)(2,1)S(1)}, s16[144,128]{1,0:T(8,128)(2,1)S(1)}, u32[]{:S(2)}, u32[]{:S(2)}) collective-permute-start(s16[144,128]{1,0:T(8,128)(2,1)S(1)} %get-tuple-element.24), channel_id=1, source_target_pairs={{0,4},{1,5},{2,6},{3,7},{4,0},{5,1},{6,2},{7,3},{8,12},{9,13},{10,... | collective-permute-start | bytes 110600 | tf_op jit(solution)/shard_map/ppermute | solution.py:467
  24.2 0.2 collective-permute-start.6
  24.4 0.0 collective-permute-done.4.refs_1_
  24.4 2.8 %collective-permute-done.5.refs_2_ = s16[144,128]{1,0:T(8,128)(2,1)S(1)} collective-permute-done((s16[144,128]{1,0:T(8,128)(2,1)S(1)}, s16[144,128]{1,0:T(8,128)(2,1)S(1)}, u32[]{:S(2)}, u32[]{:S(2)}) %collective-permute-start.5) | collective-permute-done | bytes 36896 | tf_op jit(solution)/shard_map/ppermute | solution.py:467
  27.2 2.8 %collective-permute-done.6.refs_3_ = s16[144,128]{1,0:T(8,128)(2,1)S(1)} collective-permute-done((s16[144,128]{1,0:T(8,128)(2,1)S(1)}, s16[144,128]{1,0:T(8,128)(2,1)S(1)}, u32[]{:S(2)}, u32[]{:S(2)}) %collective-permute-start.6) | collective-permute-done | bytes 36896 | tf_op jit(solution)/shard_map/ppermute | solution.py:467
  29.9 2.3 %shard_map.81 = (f32[64,256]{1,0:T(8,128)}, f32[16,256]{1,0:T(8,128)}, f32[1,128]{1,0:T(1,128)S(1)}) custom-call(s32[72]{0:T(128)S(1)} %get-tuple-element.16.plan, f32[128,128]{1,0:T(8,128)S(1)} %get-tuple-element.22.refs_0_, s16[144,128]{1,0:T(8,128)(2,1)S(1)} %collective-permute-done.4.refs_1_, s16[144,128]{1,0:T(8,128)(2,1)S(1)} %collective-permute-done.5.refs_2_, ...), custom_call_target="tpu_custom_call" | custom-call | tf_op jit(solution)/shard_map/pallas_call | solution.py:448
  32.2 8.8 %all_to_all.5 = f32[32,1,128]{2,1,0:T(1,128)S(1)} all-to-all(f32[32,1,128]{2,1,0:T(1,128)S(1)} %broadcast_in_dim.9), channel_id=1, replica_groups=mesh['row'=4,'col'=8] {'row','col'}, dimensions={0} | all-to-all | bytes 32768 | tf_op jit(solution)/shard_map/all_to_all | solution.py:473
  41.1 0.5 %reduce_max.11 = f32[128]{0:T(128)} reduce(f32[32,1,128]{2,0,1:T(8,128)S(1)} %bitcast.12, f32[]{:T(128)} %constant.0.clone.1), dimensions={0,1}, to_apply=%region_0.0 | reduce | flops 3968 | bytes 16900 | tf_op jit(solution)/shard_map/reduce_max | solution.py:473
  (1 shorter events, 0.0 us)
Async XLA Ops:
  0.6 10.5 %collective-permute-start = (bf16[64,1536]{1,0:T(8,128)(2,1)}, bf16[64,1536]{1,0:T(8,128)(2,1)S(1)}, u32[]{:S(2)}, u32[]{:S(2)}) collective-permute-start(bf16[64,1536]{1,0:T(8,128)(2,1)} %bitcast.8), channel_id=1, source_target_pairs={{0,8},{8,0},{16,24},{24,16},{1,9},{9,1},{17,25},{25,17},{2,10},{10... | collective-permute-start | bytes 589832 | tf_op jit(solution)/shard_map/ppermute | solution.py:467
  3.6 10.8 %collective-permute-start.1 = (bf16[64,1536]{1,0:T(8,128)(2,1)}, bf16[64,1536]{1,0:T(8,128)(2,1)S(1)}, u32[]{:S(2)}, u32[]{:S(2)}) collective-permute-start(bf16[64,1536]{1,0:T(8,128)(2,1)} %bitcast.9), channel_id=1, source_target_pairs={{0,16},{8,24},{16,0},{24,8},{1,17},{9,25},{17,1},{25,9},{2,18},{10... | collective-permute-start | bytes 589832 | tf_op jit(solution)/shard_map/ppermute | solution.py:467
  5.2 11.2 %collective-permute-start.2 = (bf16[64,1536]{1,0:T(8,128)(2,1)}, bf16[64,1536]{1,0:T(8,128)(2,1)S(1)}, u32[]{:S(2)}, u32[]{:S(2)}) collective-permute-start(bf16[64,1536]{1,0:T(8,128)(2,1)} %bitcast.10), channel_id=1, source_target_pairs={{0,24},{8,16},{16,8},{24,0},{1,25},{9,17},{17,9},{25,1},{2,26},{10... | collective-permute-start | bytes 589832 | tf_op jit(solution)/shard_map/ppermute | solution.py:467
  18.1 1.6 %collective-permute-start.3 = (f32[4,128,128]{2,1,0:T(8,128)S(1)}, f32[4,128,128]{2,1,0:T(8,128)S(1)}, u32[]{:S(2)}, u32[]{:S(2)}) collective-permute-start(f32[4,128,128]{2,1,0:T(8,128)S(1)} %get-tuple-element.21), channel_id=1, source_target_pairs={{0,1},{1,0},{2,3},{3,2},{4,5},{5,4},{6,7},{7,6},{8,9},{9,8},{10,11... | collective-permute-start | bytes 786440 | tf_op jit(solution)/shard_map/ppermute | solution.py:467
  19.9 4.5 %collective-permute-start.4 = (s16[144,128]{1,0:T(8,128)(2,1)S(1)}, s16[144,128]{1,0:T(8,128)(2,1)S(1)}, u32[]{:S(2)}, u32[]{:S(2)}) collective-permute-start(s16[144,128]{1,0:T(8,128)(2,1)S(1)} %get-tuple-element.23), channel_id=1, source_target_pairs={{0,2},{1,3},{2,0},{3,1},{4,6},{5,7},{6,4},{7,5},{8,10},{9,11},{10,... | collective-permute-start | bytes 110600 | tf_op jit(solution)/shard_map/ppermute | solution.py:467
  21.6 5.6 %collective-permute-start.5 = (s16[144,128]{1,0:T(8,128)(2,1)S(1)}, s16[144,128]{1,0:T(8,128)(2,1)S(1)}, u32[]{:S(2)}, u32[]{:S(2)}) collective-permute-start(s16[144,128]{1,0:T(8,128)(2,1)S(1)} %get-tuple-element.24), channel_id=1, source_target_pairs={{0,4},{1,5},{2,6},{3,7},{4,0},{5,1},{6,2},{7,3},{8,12},{9,13},{10,... | collective-permute-start | bytes 110600 | tf_op jit(solution)/shard_map/ppermute | solution.py:467
  24.2 5.8 %collective-permute-start.6 = (s16[144,128]{1,0:T(8,128)(2,1)S(1)}, s16[144,128]{1,0:T(8,128)(2,1)S(1)}, u32[]{:S(2)}, u32[]{:S(2)}) collective-permute-start(s16[144,128]{1,0:T(8,128)(2,1)S(1)} %get-tuple-element.25), channel_id=1, source_target_pairs={{0,6},{1,7},{2,4},{3,5},{4,2},{5,3},{6,0},{7,1},{8,14},{9,15},{10,... | collective-permute-start | bytes 110600 | tf_op jit(solution)/shard_map/ppermute | solution.py:467

commit v5 on v4

--- a/solution.py
+++ b/solution.py
@@ -62,18 +62,18 @@
 
 
 def multiply(pick, frontal, slabs, begun, total):
-    group_rows = frontal.shape[0]
-    depth = slabs[0].shape[1]
+    group_rows, width = frontal.shape
+    depth = width // lax.axis_size("row")
     row_pos = lax.axis_index("row")
     part = min(group_rows, 512)
 
     def rows_of(at, carry):
         rows = pl.ds(pl.multiple_of(at * part, part), part)
         value = None if begun is None else begun[rows, :]
-        for k, slab in zip(pick, slabs):
-            begin = pl.multiple_of((row_pos ^ k) * depth, LANES)
+        for (k, offset), slab in zip(pick, slabs):
+            begin = pl.multiple_of((row_pos ^ k) * depth + offset, LANES)
             twice = jnp.concatenate([slab[...], slab[...]], axis=0)
-            add = nt_dot(frontal[rows, pl.ds(begin, depth)], twice)
+            add = nt_dot(frontal[rows, pl.ds(begin, slab.shape[1])], twice)
             value = add if value is None else value + add
         total[rows, :] = value
         return carry
@@ -182,7 +182,7 @@
     bring.wait()
     moves[0].wait()
     clear_runs(0, n_row, depth, held, first)
-    multiply((0,), held, (near,), None, total)
+    multiply(((0, 0),), held, (near,), None, total)
     for k in range(1, n_row):
         moves[k].wait()
         clear_runs(k, n_row, depth, held, first)
@@ -243,10 +243,11 @@
 
 def product_cost(frontal, slabs):
     group_rows = frontal.shape[0]
-    samples, depth = slabs[0].shape
+    samples = slabs[0].shape[0]
+    depth = sum(slab.shape[1] for slab in slabs)
     return pl.CostEstimate(
-        flops=8 * group_rows * depth * samples * len(slabs),
-        bytes_accessed=2 * group_rows * depth * len(slabs),
+        flops=8 * group_rows * depth * samples,
+        bytes_accessed=2 * group_rows * depth,
         transcendentals=0,
     )
 
@@ -467,28 +468,40 @@
     return lax.ppermute(value, axis, pairs)
 
 
-def largest(value, axes):
-    size = lax.axis_size(axes)
+def largest(value, axis):
+    size = lax.axis_size(axis)
     every = jnp.broadcast_to(value[None], (size, *value.shape))
-    return jnp.max(lax.all_to_all(every, axes, 0, 0), axis=0)
+    return jnp.max(lax.all_to_all(every, axis, 0, 0), axis=0)
+
+
+def gather_near(own, n_row):
+    depth = own.shape[1]
+    near = {(k, 0): exchange(own, "row", k) for k in range(1, n_row - 1)}
+    if n_row != 4:
+        return near, {(n_row - 1, 0): exchange(own, "row", n_row - 1)}
+    cut = depth // 2 // LANES * LANES
+    left = exchange(near[2, 0][:, :cut], "row", 1)
+    right = exchange(near[1, 0][:, cut:], "row", 2)
+    return near, {(3, 0): left, (3, cut): right}
 
 
 def local(frontal, sample_cols, leaf_first, leaf_owner, skeleton):
     n_col = lax.axis_size("col")
     n_row = lax.axis_size("row")
     own = sample_cols.T
-    slabs = [exchange(own, "row", k) for k in range(1, n_row)]
+    first, second = gather_near(own, n_row)
     held, begun, source, plan = own_product(
         frontal, own, leaf_first, leaf_owner, skeleton.T, n_row, n_col
     )
-    pick = tuple(range(1, n_row))
-    begun = middle_product(held, begun, slabs[:-1], pick[:-1])
-    swap, total = last_product(held, begun, source, slabs[-1:], pick[-1:], n_col)
+    begun = middle_product(held, begun, list(first.values()), tuple(first))
+    swap, total = last_product(
+        held, begun, source, list(second.values()), tuple(second), n_col
+    )
     swapped = exchange(swap, "col", 1)
     here, *away = squeeze(keep_rows(total, source, n_col), swapped)
     parts = [exchange(value, "col", 2 * (k + 1)) for k, value in enumerate(away)]
     mine, coeff, worst = leaf_work(here, parts, plan)
-    worst = largest(worst, ("row", "col"))
+    worst = largest(largest(worst, "col"), "row")
     return (mine, coeff, worst[0, :1])
 
 

time: 41.8 us -> 48.2 us (1.15)
  blocking collectives: 8.85 us -> 15.6 us
  waiting for transfers between devices: 9.69 us -> 8.06 us
  starting transfers between devices: 9.07 us -> 10.3 us
    all_to_all x1 -> x2, blocking collectives: 8.85 us -> 15.6 us  [largest(): return jnp.max(lax.all_to_all(every, axis, 0, 0), axis=0)]
    ppermute x7 -> x8, waiting for transfers between devices: 9.69 us -> 8.06 us  [exchange(): return lax.ppermute(value, axis, pairs)]
    ppermute x7 -> x8, starting transfers between devices: 9.07 us -> 10.3 us  [exchange(): return lax.ppermute(value, axis, pairs)]
  transfers between devices with their start and end apart: 7 -> 8, of which waited for: 4 -> 5; matrix products, arithmetic and copies ran while one was open for 0% -> 0% of each run, Pallas kernels for 21% -> 18%
where the time goes in v5:
time: 48.2 us; the launch traced here: 47.9 us
  blocking collectives  15.6 us (32%)
  Pallas kernels  12.7 us (26%)
  starting transfers between devices  10.3 us (21%)
  waiting for transfers between devices  8.06 us (17%)
  between operations  0.71 us (1%)
  other arithmetic  0.54 us (1%)
    all_to_all x2, blocking collectives, largest(): return jnp.max(lax.all_to_all(every, axis, 0, 0), axis=0)  15.6 us
    ppermute x8, starting transfers between devices, exchange(): return lax.ppermute(value, axis, pairs)  10.3 us
    ppermute x8, waiting for transfers between devices, exchange(): return lax.ppermute(value, axis, pairs)  8.06 us
    pallas_call x1, Pallas kernels, own_product(): pl.pallas_call(functools.partial(own_kernel, n_row, n_col), in_specs=[hbm...  5.99 us
    pallas_call x1, Pallas kernels, leaf_work(): pl.pallas_call(functools.partial(leaf_kernel, skel), in_specs=[smem()] +...  2.29 us
    pallas_call x1, Pallas kernels, middle_product(): pl.pallas_call(functools.partial(middle_kernel, pick), in_specs=vmem(2 +...  1.95 us
    pallas_call x1, Pallas kernels, last_product(): pl.pallas_call(functools.partial(last_kernel, pick), in_specs=[smem()] +...  1.73 us
  transfers between devices with their start and end apart: 8, of which 5 were waited for; matrix products, arithmetic and copies ran while one was open for 0% of the time, Pallas kernels for 18%

profile of v5, /device:TPU:0, one launch (start us, length us, event | category | flops | bytes accessed | tf_op | source)
XLA Modules:
  0.0 47.9 jit_solution(1857039303084185443)
XLA Ops:
  0.6 3.0 %collective-permute-start = (bf16[64,1536]{1,0:T(8,128)(2,1)}, bf16[64,1536]{1,0:T(8,128)(2,1)S(1)}, u32[]{:S(2)}, u32[]{:S(2)}) collective-permute-start(bf16[64,1536]{1,0:T(8,128)(2,1)} %bitcast.9), channel_id=1, source_target_pairs={{0,8},{8,0},{16,24},{24,16},{1,9},{9,1},{17,25},{25,17},{2,10},{10... | collective-permute-start | bytes 589832 | tf_op jit(solution)/shard_map/ppermute | solution.py:468
  3.6 1.5 %collective-permute-start.1 = (bf16[64,1536]{1,0:T(8,128)(2,1)}, bf16[64,1536]{1,0:T(8,128)(2,1)S(1)}, u32[]{:S(2)}, u32[]{:S(2)}) collective-permute-start(bf16[64,1536]{1,0:T(8,128)(2,1)} %bitcast.10), channel_id=1, source_target_pairs={{0,16},{8,24},{16,0},{24,8},{1,17},{9,25},{17,1},{25,9},{2,18},{10... | collective-permute-start | bytes 589832 | tf_op jit(solution)/shard_map/ppermute | solution.py:468
  5.2 6.0 %shard_map.76 = (bf16[1024,6144]{1,0:T(8,128)(2,1)S(1)}, f32[1024,128]{1,0:T(8,128)S(1)}, s32[64]{0:T(128)S(1)}, s32[72]{0:T(128)S(1)}) custom-call(s32[64]{0:T(128)} %leaf_first.1, s32[64]{0:T(128)} %leaf_owner.1, s32[16,64]{1,0:T(8,128)} %bitcast.14, bf16[1024,6144]{1,0:T(8,128)(2,1)} %frontal.1, bf16[64,1536]{1,0:T(8,128)(2,1)} %bitcast.11), custom_call_target="tpu_custom_call" | custom-call | flops 3221225472 | bytes 12582912 | tf_op jit(solution)/shard_map/pallas_call | solution.py:260
  11.2 0.0 collective-permute-done.1.refs_1_
  11.2 0.6 %collective-permute-start.2 = (bf16[64,768]{1,0:T(8,128)(2,1)S(1)}, bf16[64,768]{1,0:T(8,128)(2,1)S(1)}, u32[]{:S(2)}, u32[]{:S(2)}) collective-permute-start(bf16[64,768]{1,0:T(8,128)(2,1)S(1)} %slice.12), channel_id=1, source_target_pairs={{0,8},{8,0},{16,24},{24,16},{1,9},{9,1},{17,25},{25,17},{2,10},{10... | collective-permute-start | bytes 294920 | tf_op jit(solution)/shard_map/ppermute | solution.py:468
  11.8 0.0 collective-permute-done.refs_0_
  11.8 0.6 %collective-permute-start.3 = (bf16[64,768]{1,0:T(8,128)(2,1)S(1)}, bf16[64,768]{1,0:T(8,128)(2,1)S(1)}, u32[]{:S(2)}, u32[]{:S(2)}) collective-permute-start(bf16[64,768]{1,0:T(8,128)(2,1)S(1)} %slice.13), channel_id=1, source_target_pairs={{0,16},{8,24},{16,0},{24,8},{1,17},{9,25},{17,1},{25,9},{2,18},{10... | collective-permute-start | bytes 294920 | tf_op jit(solution)/shard_map/ppermute | solution.py:468
  12.4 1.9 %shard_map.77.begun = f32[1024,128]{1,0:T(8,128)S(1)} custom-call(bf16[1024,6144]{1,0:T(8,128)(2,1)S(1)} %get-tuple-element.18.frontal, f32[1024,128]{1,0:T(8,128)S(1)} %get-tuple-element.19.begun, bf16[64,1536]{1,0:T(8,128)(2,1)S(1)} %collective-permute-done.refs_0_, bf16[64,1536]{1,0:T(8,128)(2,1)S(1)} %collective-permute-done.1.refs_1_), custom_call_target="tpu_custom_call" | custom-call | flops 1610612736 | bytes 6291456 | tf_op jit(solution)/shard_map/pallas_call | solution.py:286
  14.4 1.5 %collective-permute-done.2.refs_0_ = bf16[64,768]{1,0:T(8,128)(2,1)S(1)} collective-permute-done((bf16[64,768]{1,0:T(8,128)(2,1)S(1)}, bf16[64,768]{1,0:T(8,128)(2,1)S(1)}, u32[]{:S(2)}, u32[]{:S(2)}) %collective-permute-start.2) | collective-permute-done | bytes 98336 | tf_op jit(solution)/shard_map/ppermute | solution.py:468
  15.9 0.6 %collective-permute-done.3.refs_1_ = bf16[64,768]{1,0:T(8,128)(2,1)S(1)} collective-permute-done((bf16[64,768]{1,0:T(8,128)(2,1)S(1)}, bf16[64,768]{1,0:T(8,128)(2,1)S(1)}, u32[]{:S(2)}, u32[]{:S(2)}) %collective-permute-start.3) | collective-permute-done | bytes 98336 | tf_op jit(solution)/shard_map/ppermute | solution.py:468
  16.5 1.7 %shard_map.78 = (f32[4,128,128]{2,1,0:T(8,128)S(1)}, f32[1056,128]{1,0:T(8,128)S(1)}) custom-call(s32[64]{0:T(128)S(1)} %get-tuple-element.17.source, bf16[1024,6144]{1,0:T(8,128)(2,1)S(1)} %get-tuple-element.18.frontal, f32[1024,128]{1,0:T(8,128)S(1)} %shard_map.77.begun, bf16[64,768]{1,0:T(8,128)(2,1)S(1)} %collective-permute-done.2.refs_0_, ...), custom_call_target="tpu_custom_call" | custom-call | flops 805306368 | bytes 3145728 | tf_op jit(solution)/shard_map/pallas_call | solution.py:299
  18.2 0.1 collective-permute-start.4
  18.3 0.6 %shard_map.79.keep = f32[4,128,128]{2,1,0:T(8,128)S(1)} custom-call(s32[64]{0:T(128)S(1)} %get-tuple-element.17.source, f32[1056,128]{1,0:T(8,128)S(1)} %get-tuple-element.20.total), custom_call_target="tpu_custom_call" | custom-call | flops 131072 | bytes 1048576 | tf_op jit(solution)/shard_map/pallas_call | solution.py:311
  18.9 0.9 %collective-permute-done.4.swapped = f32[4,128,128]{2,1,0:T(8,128)S(1)} collective-permute-done((f32[4,128,128]{2,1,0:T(8,128)S(1)}, f32[4,128,128]{2,1,0:T(8,128)S(1)}, u32[]{:S(2)}, u32[]{:S(2)}) %collective-permute-start.4) | collective-permute-done | bytes 262176 | tf_op jit(solution)/shard_map/ppermute | solution.py:468
  19.8 0.2 shard_map.80
  20.0 1.2 %collective-permute-start.5 = (s16[144,128]{1,0:T(8,128)(2,1)S(1)}, s16[144,128]{1,0:T(8,128)(2,1)S(1)}, u32[]{:S(2)}, u32[]{:S(2)}) collective-permute-start(s16[144,128]{1,0:T(8,128)(2,1)S(1)} %get-tuple-element.23), channel_id=1, source_target_pairs={{0,2},{1,3},{2,0},{3,1},{4,6},{5,7},{6,4},{7,5},{8,10},{9,11},{10,... | collective-permute-start | bytes 110600 | tf_op jit(solution)/shard_map/ppermute | solution.py:468
  21.2 2.6 %collective-permute-start.6 = (s16[144,128]{1,0:T(8,128)(2,1)S(1)}, s16[144,128]{1,0:T(8,128)(2,1)S(1)}, u32[]{:S(2)}, u32[]{:S(2)}) collective-permute-start(s16[144,128]{1,0:T(8,128)(2,1)S(1)} %get-tuple-element.24), channel_id=1, source_target_pairs={{0,4},{1,5},{2,6},{3,7},{4,0},{5,1},{6,2},{7,3},{8,12},{9,13},{10,... | collective-permute-start | bytes 110600 | tf_op jit(solution)/shard_map/ppermute | solution.py:468
  23.7 0.7 %collective-permute-start.7 = (s16[144,128]{1,0:T(8,128)(2,1)S(1)}, s16[144,128]{1,0:T(8,128)(2,1)S(1)}, u32[]{:S(2)}, u32[]{:S(2)}) collective-permute-start(s16[144,128]{1,0:T(8,128)(2,1)S(1)} %get-tuple-element.25), channel_id=1, source_target_pairs={{0,6},{1,7},{2,4},{3,5},{4,2},{5,3},{6,0},{7,1},{8,14},{9,15},{10,... | collective-permute-start | bytes 110600 | tf_op jit(solution)/shard_map/ppermute | solution.py:468
  24.5 0.0 collective-permute-done.5.refs_1_
  24.5 2.2 %collective-permute-done.6.refs_2_ = s16[144,128]{1,0:T(8,128)(2,1)S(1)} collective-permute-done((s16[144,128]{1,0:T(8,128)(2,1)S(1)}, s16[144,128]{1,0:T(8,128)(2,1)S(1)}, u32[]{:S(2)}, u32[]{:S(2)}) %collective-permute-start.6) | collective-permute-done | bytes 36896 | tf_op jit(solution)/shard_map/ppermute | solution.py:468
  26.6 2.9 %collective-permute-done.7.refs_3_ = s16[144,128]{1,0:T(8,128)(2,1)S(1)} collective-permute-done((s16[144,128]{1,0:T(8,128)(2,1)S(1)}, s16[144,128]{1,0:T(8,128)(2,1)S(1)}, u32[]{:S(2)}, u32[]{:S(2)}) %collective-permute-start.7) | collective-permute-done | bytes 36896 | tf_op jit(solution)/shard_map/ppermute | solution.py:468
  29.5 2.3 %shard_map.81 = (f32[64,256]{1,0:T(8,128)}, f32[16,256]{1,0:T(8,128)}, f32[1,128]{1,0:T(1,128)S(1)}) custom-call(s32[72]{0:T(128)S(1)} %get-tuple-element.16.plan, f32[128,128]{1,0:T(8,128)S(1)} %get-tuple-element.22.refs_0_, s16[144,128]{1,0:T(8,128)(2,1)S(1)} %collective-permute-done.5.refs_1_, s16[144,128]{1,0:T(8,128)(2,1)S(1)} %collective-permute-done.6.refs_2_, ...), custom_call_target="tpu_custom_call" | custom-call | tf_op jit(solution)/shard_map/pallas_call | solution.py:449
  31.8 7.9 %all_to_all.10 = f32[8,1,128]{2,1,0:T(1,128)S(1)} all-to-all(f32[8,1,128]{2,1,0:T(1,128)S(1)} %broadcast_in_dim.7), channel_id=1, replica_groups=mesh['row'=4,'col'=8] {'col'}, dimensions={0} | all-to-all | bytes 8192 | tf_op jit(solution)/shard_map/all_to_all | solution.py:474
  39.7 7.7 %all_to_all.11 = f32[4,1,128]{2,1,0:T(1,128)S(1)} all-to-all(f32[4,1,128]{2,1,0:T(1,128)S(1)} %broadcast_in_dim.16), channel_id=1, replica_groups=mesh['row'=4,'col'=8] {'row'}, dimensions={0} | all-to-all | bytes 4096 | tf_op jit(solution)/shard_map/all_to_all | solution.py:474
  47.4 0.5 %reduce_max.21 = f32[128]{0:T(128)} reduce(f32[4,1,128]{2,0,1:T(4,128)S(1)} %bitcast.13, f32[]{:T(128)} %constant.0.clone.1), dimensions={0,1}, to_apply=%region_1.0 | reduce | flops 384 | bytes 2564 | tf_op jit(solution)/shard_map/reduce_max | solution.py:474
  (5 shorter events, 0.0 us)
Async XLA Ops:
  0.6 11.2 %collective-permute-start = (bf16[64,1536]{1,0:T(8,128)(2,1)}, bf16[64,1536]{1,0:T(8,128)(2,1)S(1)}, u32[]{:S(2)}, u32[]{:S(2)}) collective-permute-start(bf16[64,1536]{1,0:T(8,128)(2,1)} %bitcast.9), channel_id=1, source_target_pairs={{0,8},{8,0},{16,24},{24,16},{1,9},{9,1},{17,25},{25,17},{2,10},{10... | collective-permute-start | bytes 589832 | tf_op jit(solution)/shard_map/ppermute | solution.py:468
  3.6 7.5 %collective-permute-start.1 = (bf16[64,1536]{1,0:T(8,128)(2,1)}, bf16[64,1536]{1,0:T(8,128)(2,1)S(1)}, u32[]{:S(2)}, u32[]{:S(2)}) collective-permute-start(bf16[64,1536]{1,0:T(8,128)(2,1)} %bitcast.10), channel_id=1, source_target_pairs={{0,16},{8,24},{16,0},{24,8},{1,17},{9,25},{17,1},{25,9},{2,18},{10... | collective-permute-start | bytes 589832 | tf_op jit(solution)/shard_map/ppermute | solution.py:468
  11.2 4.7 %collective-permute-start.2 = (bf16[64,768]{1,0:T(8,128)(2,1)S(1)}, bf16[64,768]{1,0:T(8,128)(2,1)S(1)}, u32[]{:S(2)}, u32[]{:S(2)}) collective-permute-start(bf16[64,768]{1,0:T(8,128)(2,1)S(1)} %slice.12), channel_id=1, source_target_pairs={{0,8},{8,0},{16,24},{24,16},{1,9},{9,1},{17,25},{25,17},{2,10},{10... | collective-permute-start | bytes 294920 | tf_op jit(solution)/shard_map/ppermute | solution.py:468
  11.8 4.7 %collective-permute-start.3 = (bf16[64,768]{1,0:T(8,128)(2,1)S(1)}, bf16[64,768]{1,0:T(8,128)(2,1)S(1)}, u32[]{:S(2)}, u32[]{:S(2)}) collective-permute-start(bf16[64,768]{1,0:T(8,128)(2,1)S(1)} %slice.13), channel_id=1, source_target_pairs={{0,16},{8,24},{16,0},{24,8},{1,17},{9,25},{17,1},{25,9},{2,18},{10... | collective-permute-start | bytes 294920 | tf_op jit(solution)/shard_map/ppermute | solution.py:468
  18.2 1.6 %collective-permute-start.4 = (f32[4,128,128]{2,1,0:T(8,128)S(1)}, f32[4,128,128]{2,1,0:T(8,128)S(1)}, u32[]{:S(2)}, u32[]{:S(2)}) collective-permute-start(f32[4,128,128]{2,1,0:T(8,128)S(1)} %get-tuple-element.21), channel_id=1, source_target_pairs={{0,1},{1,0},{2,3},{3,2},{4,5},{5,4},{6,7},{7,6},{8,9},{9,8},{10,11... | collective-permute-start | bytes 786440 | tf_op jit(solution)/shard_map/ppermute | solution.py:468
  20.0 4.5 %collective-permute-start.5 = (s16[144,128]{1,0:T(8,128)(2,1)S(1)}, s16[144,128]{1,0:T(8,128)(2,1)S(1)}, u32[]{:S(2)}, u32[]{:S(2)}) collective-permute-start(s16[144,128]{1,0:T(8,128)(2,1)S(1)} %get-tuple-element.23), channel_id=1, source_target_pairs={{0,2},{1,3},{2,0},{3,1},{4,6},{5,7},{6,4},{7,5},{8,10},{9,11},{10,... | collective-permute-start | bytes 110600 | tf_op jit(solution)/shard_map/ppermute | solution.py:468
  21.2 5.5 %collective-permute-start.6 = (s16[144,128]{1,0:T(8,128)(2,1)S(1)}, s16[144,128]{1,0:T(8,128)(2,1)S(1)}, u32[]{:S(2)}, u32[]{:S(2)}) collective-permute-start(s16[144,128]{1,0:T(8,128)(2,1)S(1)} %get-tuple-element.24), channel_id=1, source_target_pairs={{0,4},{1,5},{2,6},{3,7},{4,0},{5,1},{6,2},{7,3},{8,12},{9,13},{10,... | collective-permute-start | bytes 110600 | tf_op jit(solution)/shard_map/ppermute | solution.py:468
  23.7 5.8 %collective-permute-start.7 = (s16[144,128]{1,0:T(8,128)(2,1)S(1)}, s16[144,128]{1,0:T(8,128)(2,1)S(1)}, u32[]{:S(2)}, u32[]{:S(2)}) collective-permute-start(s16[144,128]{1,0:T(8,128)(2,1)S(1)} %get-tuple-element.25), channel_id=1, source_target_pairs={{0,6},{1,7},{2,4},{3,5},{4,2},{5,3},{6,0},{7,1},{8,14},{9,15},{10,... | collective-permute-start | bytes 110600 | tf_op jit(solution)/shard_map/ppermute | solution.py:468

commit v6 on v5

--- a/solution.py
+++ b/solution.py
@@ -13,15 +13,13 @@
 PICKS = 8
 LEVELS = 32760.0
 EXTRA = 16
+PART = 256
 STEPS = 64.0
 RUN_LEAVES = 4
-HIGHEST = lax.Precision.HIGHEST
-
-
-def nt_dot(a, b, precision=None):
-    return lax.dot_general(
-        a, b, (((1,), (1,)), ((), ())), precision=precision, preferred_element_type=jnp.float32
-    )
+
+
+def nt_dot(a, b):
+    return lax.dot_general(a, b, (((1,), (1,)), ((), ())), preferred_element_type=jnp.float32)
 
 
 def clear_runs(pick, n_row, depth, frontal, leaf_first):
@@ -124,7 +122,7 @@
     slab,
     held,
     total,
-    source,
+    target,
     plan,
     first,
     owners,
@@ -142,6 +140,7 @@
     per_owner = 2 * group_rows // n_col // UNIT
     units = group_rows // UNIT
     row_pos = lax.axis_index("row")
+    col_pos = lax.axis_index("col")
     tables = [
         pltpu.make_async_copy(leaf_first, first, table_sems.at[0]),
         pltpu.make_async_copy(leaf_owner, owners, table_sems.at[1]),
@@ -158,11 +157,10 @@
         copy.start()
 
     def clear(at, carry):
-        source[at] = units
-        used[at // per_owner] = 0
+        used[at] = 0
         return carry
 
-    lax.fori_loop(0, n_col * per_owner, clear, 0)
+    lax.fori_loop(0, n_col, clear, 0)
     for copy in tables:
         copy.wait()
 
@@ -174,7 +172,7 @@
         owner = owners[leaf]
         slot = used[owner]
         used[owner] = slot + 1
-        source[owner * per_owner + slot] = unit
+        target[unit] = (owner ^ col_pos) * per_owner + slot
         return leaf
 
     lax.fori_loop(0, units, place, row_pos * per_group)
@@ -192,36 +190,37 @@
     multiply(pick, frontal, refs[: len(pick)], begun, refs[len(pick)])
 
 
-def lay(other, source, total, out):
-    chips, half, wide = out.shape
+def last_kernel(pick, target, frontal, begun, *refs):
+    slabs, (keep, swap) = refs[: len(pick)], refs[len(pick) :]
+    group_rows, width = frontal.shape
+    depth = width // lax.axis_size("row")
+    row_pos = lax.axis_index("row")
+    chips, half, wide = keep.shape
     per_half = half // UNIT
-    core = lax.rem(lax.axis_index("col"), 2)
-    chip = lax.axis_index("col") // 2
-    lane = lax.broadcasted_iota(jnp.int32, (UNIT, wide), 1)
-
-    def one(turn, carry):
-        owner = (chip ^ turn) * 2 + (core ^ other)
-        for at in range(per_half):
-            values = []
-            for side in range(2):
-                unit = source[owner * (2 * per_half) + side * per_half + at]
-                values.append(total[pl.ds(pl.multiple_of(unit * UNIT, UNIT), UNIT), :])
-            out[turn, pl.ds(at * UNIT, UNIT), :] = jnp.where(lane < wide // 2, *values)
+    lane = lax.broadcasted_iota(jnp.int32, (UNIT, wide), 1) // (wide // 2)
+    twice = [jnp.concatenate([slab[...], slab[...]], axis=0) for slab in slabs]
+    keep[...] = jnp.zeros(keep.shape, jnp.float32)
+    swap[...] = jnp.zeros(swap.shape, jnp.float32)
+
+    def rows_of(at, carry):
+        rows = pl.ds(pl.multiple_of(at * PART, PART), PART)
+        value = begun[rows, :]
+        for (k, offset), slab in zip(pick, twice):
+            begin = pl.multiple_of((row_pos ^ k) * depth + offset, LANES)
+            value = value + nt_dot(frontal[rows, pl.ds(begin, slab.shape[1])], slab)
+        for unit in range(PART // UNIT):
+            spot = target[at * (PART // UNIT) + unit]
+            turn, slot = spot // (2 * per_half), spot % (2 * per_half)
+            to_rows = pl.ds(pl.multiple_of(slot % per_half * UNIT, UNIT), UNIT)
+            piece = value[unit * UNIT : (unit + 1) * UNIT]
+            near = lane == slot // per_half
+            for other, out in ((0, keep), (1, swap)):
+                mask = near & (turn % 2 == other)
+                pltpu.store(out.at[turn // 2, to_rows, :], piece, mask=mask)
         return carry
 
-    lax.fori_loop(0, chips, one, 0, unroll=min(chips, 4))
-
-
-def last_kernel(pick, source, frontal, begun, *refs):
-    slabs, (swap, total) = refs[: len(pick)], refs[len(pick) :]
-    group_rows = frontal.shape[0]
-    total[pl.ds(group_rows, UNIT), :] = jnp.zeros((UNIT, total.shape[1]), jnp.float32)
-    multiply(pick, frontal, slabs, begun, total)
-    lay(1, source, total, swap)
-
-
-def keep_kernel(source, total, keep):
-    lay(0, source, total, keep)
+    steps = group_rows // PART
+    lax.fori_loop(0, steps, rows_of, 0, unroll=min(steps, 4))
 
 
 def vmem(count=None):
@@ -255,7 +254,6 @@
 def own_product(frontal, slab, leaf_first, leaf_owner, skeleton, n_row, n_col):
     group_rows, width = frontal.shape
     samples, depth = slab.shape
-    per_owner = 2 * group_rows // n_col // UNIT
     leaves = leaf_first.shape[0]
     return pl.pallas_call(
         functools.partial(own_kernel, n_row, n_col),
@@ -264,7 +262,7 @@
         out_shape=[
             jax.ShapeDtypeStruct(frontal.shape, frontal.dtype),
             jax.ShapeDtypeStruct((group_rows, 2 * samples), jnp.float32),
-            jax.ShapeDtypeStruct((n_col * per_owner,), jnp.int32),
+            jax.ShapeDtypeStruct((group_rows // UNIT,), jnp.int32),
             jax.ShapeDtypeStruct((PICKS + LEAF_MOST * skeleton.shape[0],), jnp.int32),
         ],
         scratch_shapes=[
@@ -293,31 +291,17 @@
     )(frontal, begun, *slabs)
 
 
-def last_product(frontal, begun, source, slabs, pick, n_col):
+def last_product(frontal, begun, target, slabs, pick, n_col):
     group_rows, wide = begun.shape
     block = jax.ShapeDtypeStruct((n_col // 2, group_rows // n_col, wide), jnp.float32)
     return pl.pallas_call(
         functools.partial(last_kernel, pick),
         in_specs=[smem()] + vmem(2 + len(slabs)),
         out_specs=vmem(2),
-        out_shape=[block, jax.ShapeDtypeStruct((group_rows + UNIT, wide), jnp.float32)],
+        out_shape=[block, block],
         cost_estimate=product_cost(frontal, slabs),
         compiler_params=pltpu.CompilerParams(vmem_limit_bytes=24 * 2**20),
-    )(source, frontal, begun, *slabs)
-
-
-def keep_rows(total, source, n_col):
-    group_rows, wide = total.shape[0] - UNIT, total.shape[1]
-    return pl.pallas_call(
-        keep_kernel,
-        in_specs=[smem(), vmem()],
-        out_specs=vmem(),
-        out_shape=jax.ShapeDtypeStruct((n_col // 2, group_rows // n_col, wide), jnp.float32),
-        cost_estimate=pl.CostEstimate(
-            flops=group_rows * wide, bytes_accessed=8 * group_rows * wide, transcendentals=0
-        ),
-        compiler_params=pltpu.CompilerParams(vmem_limit_bytes=24 * 2**20),
-    )(source, total)
+    )(target, frontal, begun, *slabs)
 
 
 def squeeze_kernel(keep, swapped, here, *away):
@@ -351,11 +335,36 @@
     )(keep, swapped)
 
 
-def leaf_kernel(
-    skel, plan, *refs
-):
-    here, *parts = refs[:-5]
-    mine_out, coeff_out, worst_out, mine, picked = refs[-5:]
+def thirds(value):
+    high = value.astype(jnp.bfloat16)
+    rest = value - high.astype(jnp.float32)
+    middle = rest.astype(jnp.bfloat16)
+    low = (rest - middle.astype(jnp.float32)).astype(jnp.bfloat16)
+    return high, middle, low
+
+
+def beside(left, right):
+    wide = left.shape[1]
+    lane = lax.broadcasted_iota(jnp.int32, left.shape, 1)
+    joined = jnp.where(lane < wide // 2, left.astype(jnp.float32), right.astype(jnp.float32))
+    return joined.astype(jnp.bfloat16)
+
+
+def left_terms(high, middle, low):
+    return jnp.concatenate([high, beside(middle, high), beside(low, middle)], axis=1)
+
+
+def right_terms(high, middle, low):
+    return jnp.concatenate([high, middle, high, low, high, middle], axis=0)
+
+
+def plain_dot(a, b):
+    return jnp.dot(a, b, preferred_element_type=jnp.float32)
+
+
+def leaf_kernel(skel, plan, *refs):
+    here, *parts = refs[:-8]
+    mine_out, coeff_out, worst_out, mine, picked, turned, coeff, sems = refs[-8:]
     wide, half = here.shape
     samples = wide // 2
     capacity = 2 * half
@@ -369,35 +378,45 @@
             value = part[pl.ds(side * samples, samples), :].astype(jnp.int32).astype(jnp.float32)
             sides[side] = sides[side] + value * step[side : side + 1]
     mine_t = jnp.concatenate(sides, axis=1)
-    mine_out[...] = mine_t
+    turned[...] = mine_t
+    send_mine = pltpu.make_async_copy(turned, mine_out, sems.at[0])
+    send_mine.start()
     total = jnp.concatenate(sides, axis=0).T
-    mine[pl.ds(0, half), :] = total
-    mine[pl.ds(half, half), :] = pltpu.roll(total, samples, 1)
+    other = pltpu.roll(total, samples, 1)
+    low_half = lax.broadcasted_iota(jnp.int32, total.shape, 1) < samples
+    mine[pl.ds(0, half), :] = jnp.where(low_half, total, other)
+    mine[pl.ds(half, half), :] = jnp.where(low_half, other, total)
     mine[pl.ds(capacity, 8), :] = jnp.zeros((8, wide), jnp.float32)
     for k in range(every):
         picked[pl.ds(k, 1), :] = mine[pl.ds(plan[PICKS + k], 1), :]
     begins = [plan[b] for b in range(LEAF_MOST)]
     count = plan[LEAF_MOST]
-    chosen = picked[:, :samples]
-
-    gram = nt_dot(chosen, chosen, HIGHEST)
-    proj = jnp.dot(chosen, mine_t, precision=HIGHEST, preferred_element_type=jnp.float32)
+    chosen = picked[...]
+
+    high, middle, low = thirds(chosen)
+    across = left_terms(high, middle, low)
+    down = jnp.concatenate([beside(high, middle), beside(high, low), beside(high, middle)], axis=1)
+    gram = nt_dot(across, down)
+    proj = plain_dot(across, right_terms(*thirds(mine_t)))
 
     slot = lax.broadcasted_iota(jnp.int32, (skel, capacity), 1)
     rank = jnp.zeros((skel, capacity), jnp.int32)
     for b in range(1, LEAF_MOST):
         rank += (slot >= begins[b]).astype(jnp.int32)
     hot = [rank == b for b in range(LEAF_MOST)]
-    hot_rows = jnp.concatenate([h.astype(jnp.float32) for h in hot], axis=0)
+    hot_rows = jnp.concatenate([h.astype(jnp.float32) for h in hot], axis=0).astype(jnp.bfloat16)
 
     lane_leaf = lax.broadcasted_iota(jnp.int32, (skel, every), 1) // skel
     lane_row = lax.broadcasted_iota(jnp.int32, (skel, every), 1) % skel
-    down = lax.broadcasted_iota(jnp.int32, (skel, every), 0)
-    joined = jnp.where((down == lane_row) & (count == 0), 1.0, 0.0)
+    below = lax.broadcasted_iota(jnp.int32, (skel, every), 0)
+    joined = jnp.where((below == lane_row) & (count == 0), 1.0, 0.0)
     for b in range(LEAF_MOST):
         joined += jnp.where(lane_leaf == b, gram[b * skel : (b + 1) * skel], 0.0)
-    spread = jnp.concatenate([jnp.where(lane_row == i, joined, 0.0) for i in range(skel)], axis=0)
-    system = jnp.dot(spread, hot_rows, precision=HIGHEST, preferred_element_type=jnp.float32)
+    terms = [term.astype(jnp.float32) for term in thirds(joined)]
+    terms = jnp.concatenate(terms + [jnp.zeros_like(joined)], axis=1)
+    turn = lax.broadcasted_iota(jnp.int32, terms.shape, 1) % skel
+    spread = jnp.concatenate([jnp.where(turn == i, terms, 0.0) for i in range(skel)], axis=0)
+    system = plain_dot(spread.astype(jnp.bfloat16), jnp.concatenate([hot_rows] * 4, axis=0))
 
     lines = [system[i * skel : (i + 1) * skel] for i in range(skel)]
     right = jnp.zeros((skel, capacity), jnp.float32)
@@ -420,16 +439,14 @@
         known = jnp.where(index > j, uppers[j] * solved, 0.0)
         less = jnp.sum(known, axis=0, keepdims=True)
         solved = jnp.where(index == j, solved - less, solved)
-    coeff_out[...] = solved
+    coeff[...] = solved
+    send_coeff = pltpu.make_async_copy(coeff, coeff_out, sems.at[1])
+    send_coeff.start()
 
     weights = jnp.concatenate([jnp.where(h, solved, 0.0) for h in hot], axis=0)
-    rebuilt = lax.dot_general(
-        chosen,
-        weights,
-        (((0,), (0,)), ((), ())),
-        precision=HIGHEST,
-        preferred_element_type=jnp.float32,
-    )
+    upright = chosen.T[:samples]
+    upright = thirds(jnp.concatenate([upright, upright], axis=1))
+    rebuilt = plain_dot(left_terms(*upright), right_terms(*thirds(weights)))
     resid = mine_t - rebuilt
     err = jnp.sum(resid * resid, axis=0, keepdims=True)
     norm = jnp.sum(mine_t * mine_t, axis=0, keepdims=True)
@@ -440,6 +457,8 @@
         norm_leaf = jnp.sum(jnp.where(near, norm, 0.0), axis=1, keepdims=True)
         worst = jnp.maximum(worst, jnp.sqrt(err_leaf) / jnp.sqrt(norm_leaf + 1e-06))
     worst_out[...] = jnp.broadcast_to(worst, worst_out.shape)
+    send_mine.wait()
+    send_coeff.wait()
 
 
 def leaf_work(here, parts, plan):
@@ -449,7 +468,7 @@
     return pl.pallas_call(
         functools.partial(leaf_kernel, skel),
         in_specs=[smem()] + vmem(1 + len(parts)),
-        out_specs=vmem(3),
+        out_specs=[hbm(), hbm(), vmem()],
         out_shape=[
             jax.ShapeDtypeStruct((samples, 2 * half), jnp.float32),
             jax.ShapeDtypeStruct((skel, 2 * half), jnp.float32),
@@ -458,6 +477,9 @@
         scratch_shapes=[
             pltpu.VMEM((2 * half + 8, wide), jnp.float32),
             pltpu.VMEM((LEAF_MOST * skel, wide), jnp.float32),
+            pltpu.VMEM((samples, 2 * half), jnp.float32),
+            pltpu.VMEM((skel, 2 * half), jnp.float32),
+            pltpu.SemaphoreType.DMA((2,)),
         ],
         compiler_params=pltpu.CompilerParams(vmem_limit_bytes=12 * 2**20),
     )(plan, here, *parts)
@@ -490,18 +512,16 @@
     n_row = lax.axis_size("row")
     own = sample_cols.T
     first, second = gather_near(own, n_row)
-    held, begun, source, plan = own_product(
+    held, begun, target, plan = own_product(
         frontal, own, leaf_first, leaf_owner, skeleton.T, n_row, n_col
     )
     begun = middle_product(held, begun, list(first.values()), tuple(first))
-    swap, total = last_product(
-        held, begun, source, list(second.values()), tuple(second), n_col
-    )
+    keep, swap = last_product(held, begun, target, list(second.values()), tuple(second), n_col)
     swapped = exchange(swap, "col", 1)
-    here, *away = squeeze(keep_rows(total, source, n_col), swapped)
-    parts = [exchange(value, "col", 2 * (k + 1)) for k, value in enumerate(away)]
+    here, *away = squeeze(keep, swapped)
+    parts = [exchange(away[k - 1], "col", 2 * k) for k in range(n_col // 2 - 1, 0, -1)]
     mine, coeff, worst = leaf_work(here, parts, plan)
-    worst = largest(largest(worst, "col"), "row")
+    worst = largest(worst, ("row", "col"))
     return (mine, coeff, worst[0, :1])
 
 

time: 48.2 us -> 41.9 us (0.87)
  blocking collectives: 15.6 us -> 10.3 us
  starting transfers between devices: 10.3 us -> 9.59 us
    all_to_all x2 -> x1, blocking collectives: 15.6 us -> 10.3 us  [largest(): return jnp.max(lax.all_to_all(every, axis, 0, 0), axis=0)]
    pallas_call x1, Pallas kernels: 5.99 us -> 6.93 us  [own_product(): pl.pallas_call(functools.partial(own_kernel, n_row, n_col), in_specs=[hbm...]
    ppermute x8, starting transfers between devices: 10.3 us -> 9.59 us  [exchange(): return lax.ppermute(value, axis, pairs)]
    pallas_call x1 -> x0, Pallas kernels: 0.6 us -> none  [keep_rows(): pl.pallas_call(keep_kernel, in_specs=[smem(), vmem()], out_specs=vmem(),...]
  transfers between devices with their start and end apart: 8 -> 8, of which waited for: 5 -> 5; matrix products, arithmetic and copies ran while one was open for 0% -> 0% of each run, Pallas kernels for 18% -> 21%
where the time goes in v6:
time: 41.9 us; the launch traced here: 41.8 us
  Pallas kernels  13 us (31%)
  blocking collectives  10.3 us (25%)
  starting transfers between devices  9.59 us (23%)
  waiting for transfers between devices  7.66 us (18%)
  between operations  0.72 us (2%)
  other arithmetic  0.53 us (1%)
    all_to_all x1, blocking collectives, largest(): return jnp.max(lax.all_to_all(every, axis, 0, 0), axis=0)  10.3 us
    ppermute x8, starting transfers between devices, exchange(): return lax.ppermute(value, axis, pairs)  9.59 us
    ppermute x8, waiting for transfers between devices, exchange(): return lax.ppermute(value, axis, pairs)  7.66 us
    pallas_call x1, Pallas kernels, own_product(): pl.pallas_call(functools.partial(own_kernel, n_row, n_col), in_specs=[hbm...  6.93 us
    pallas_call x1, Pallas kernels, leaf_work(): pl.pallas_call(functools.partial(leaf_kernel, skel), in_specs=[smem()] +...  2.13 us
    pallas_call x1, Pallas kernels, middle_product(): pl.pallas_call(functools.partial(middle_kernel, pick), in_specs=vmem(2 +...  1.95 us
    pallas_call x1, Pallas kernels, last_product(): pl.pallas_call(functools.partial(last_kernel, pick), in_specs=[smem()] +...  1.78 us
  transfers between devices with their start and end apart: 8, of which 5 were waited for; matrix products, arithmetic and copies ran while one was open for 0% of the time, Pallas kernels for 21%

profile of v6, /device:TPU:0, one launch (start us, length us, event | category | flops | bytes accessed | tf_op | source)
XLA Modules:
  0.0 41.8 jit_solution(2237087069193412015)
XLA Ops:
  0.6 3.0 %collective-permute-start = (bf16[64,1536]{1,0:T(8,128)(2,1)}, bf16[64,1536]{1,0:T(8,128)(2,1)S(1)}, u32[]{:S(2)}, u32[]{:S(2)}) collective-permute-start(bf16[64,1536]{1,0:T(8,128)(2,1)} %bitcast.8), channel_id=1, source_target_pairs={{0,8},{8,0},{16,24},{24,16},{1,9},{9,1},{17,25},{25,17},{2,10},{10... | collective-permute-start | bytes 589832 | tf_op jit(solution)/shard_map/ppermute | solution.py:490
  3.6 1.5 %collective-permute-start.1 = (bf16[64,1536]{1,0:T(8,128)(2,1)}, bf16[64,1536]{1,0:T(8,128)(2,1)S(1)}, u32[]{:S(2)}, u32[]{:S(2)}) collective-permute-start(bf16[64,1536]{1,0:T(8,128)(2,1)} %bitcast.9), channel_id=1, source_target_pairs={{0,16},{8,24},{16,0},{24,8},{1,17},{9,25},{17,1},{25,9},{2,18},{10... | collective-permute-start | bytes 589832 | tf_op jit(solution)/shard_map/ppermute | solution.py:490
  5.2 6.9 %shard_map.76 = (bf16[1024,6144]{1,0:T(8,128)(2,1)S(1)}, f32[1024,128]{1,0:T(8,128)S(1)}, s32[32]{0:T(128)S(1)}, s32[72]{0:T(128)S(1)}) custom-call(s32[64]{0:T(128)} %leaf_first.1, s32[64]{0:T(128)} %leaf_owner.1, s32[16,64]{1,0:T(8,128)} %bitcast.12, bf16[1024,6144]{1,0:T(8,128)(2,1)} %frontal.1, bf16[64,1536]{1,0:T(8,128)(2,1)} %bitcast.10), custom_call_target="tpu_custom_call" | custom-call | flops 3221225472 | bytes 12582912 | tf_op jit(solution)/shard_map/pallas_call | solution.py:258
  12.1 0.0 collective-permute-done.1.refs_1_
  12.1 0.5 %collective-permute-start.2 = (bf16[64,768]{1,0:T(8,128)(2,1)S(1)}, bf16[64,768]{1,0:T(8,128)(2,1)S(1)}, u32[]{:S(2)}, u32[]{:S(2)}) collective-permute-start(bf16[64,768]{1,0:T(8,128)(2,1)S(1)} %slice.12), channel_id=1, source_target_pairs={{0,8},{8,0},{16,24},{24,16},{1,9},{9,1},{17,25},{25,17},{2,10},{10... | collective-permute-start | bytes 294920 | tf_op jit(solution)/shard_map/ppermute | solution.py:490
  12.6 0.0 collective-permute-done.refs_0_
  12.6 0.1 collective-permute-start.3
  12.7 2.0 %shard_map.77.begun = f32[1024,128]{1,0:T(8,128)S(1)} custom-call(bf16[1024,6144]{1,0:T(8,128)(2,1)S(1)} %get-tuple-element.18.frontal, f32[1024,128]{1,0:T(8,128)S(1)} %get-tuple-element.19.begun, bf16[64,1536]{1,0:T(8,128)(2,1)S(1)} %collective-permute-done.refs_0_, bf16[64,1536]{1,0:T(8,128)(2,1)S(1)} %collective-permute-done.1.refs_1_), custom_call_target="tpu_custom_call" | custom-call | flops 1610612736 | bytes 6291456 | tf_op jit(solution)/shard_map/pallas_call | solution.py:284
  14.6 2.2 %collective-permute-done.2.refs_0_ = bf16[64,768]{1,0:T(8,128)(2,1)S(1)} collective-permute-done((bf16[64,768]{1,0:T(8,128)(2,1)S(1)}, bf16[64,768]{1,0:T(8,128)(2,1)S(1)}, u32[]{:S(2)}, u32[]{:S(2)}) %collective-permute-start.2) | collective-permute-done | bytes 98336 | tf_op jit(solution)/shard_map/ppermute | solution.py:490
  16.8 0.5 %collective-permute-done.3.refs_1_ = bf16[64,768]{1,0:T(8,128)(2,1)S(1)} collective-permute-done((bf16[64,768]{1,0:T(8,128)(2,1)S(1)}, bf16[64,768]{1,0:T(8,128)(2,1)S(1)}, u32[]{:S(2)}, u32[]{:S(2)}) %collective-permute-start.3) | collective-permute-done | bytes 98336 | tf_op jit(solution)/shard_map/ppermute | solution.py:490
  17.3 1.8 %shard_map.78 = (f32[4,128,128]{2,1,0:T(8,128)S(1)}, f32[4,128,128]{2,1,0:T(8,128)S(1)}) custom-call(s32[32]{0:T(128)S(1)} %get-tuple-element.17.target, bf16[1024,6144]{1,0:T(8,128)(2,1)S(1)} %get-tuple-element.18.frontal, f32[1024,128]{1,0:T(8,128)S(1)} %shard_map.77.begun, bf16[64,768]{1,0:T(8,128)(2,1)S(1)} %collective-permute-done.2.refs_0_, ...), custom_call_target="tpu_custom_call" | custom-call | flops 805306368 | bytes 3145728 | tf_op jit(solution)/shard_map/pallas_call | solution.py:297
  19.1 0.1 collective-permute-start.4
  19.2 1.5 %collective-permute-done.4.swapped = f32[4,128,128]{2,1,0:T(8,128)S(1)} collective-permute-done((f32[4,128,128]{2,1,0:T(8,128)S(1)}, f32[4,128,128]{2,1,0:T(8,128)S(1)}, u32[]{:S(2)}, u32[]{:S(2)}) %collective-permute-start.4) | collective-permute-done | bytes 262176 | tf_op jit(solution)/shard_map/ppermute | solution.py:490
  20.7 0.2 shard_map.79
  20.9 3.1 %collective-permute-start.5 = (s16[144,128]{1,0:T(8,128)(2,1)S(1)}, s16[144,128]{1,0:T(8,128)(2,1)S(1)}, u32[]{:S(2)}, u32[]{:S(2)}) collective-permute-start(s16[144,128]{1,0:T(8,128)(2,1)S(1)} %get-tuple-element.23), channel_id=1, source_target_pairs={{0,6},{1,7},{2,4},{3,5},{4,2},{5,3},{6,0},{7,1},{8,14},{9,15},{10,... | collective-permute-start | bytes 110600 | tf_op jit(solution)/shard_map/ppermute | solution.py:490
  24.0 0.0 collective-permute-start.6
  24.0 1.4 %collective-permute-start.7 = (s16[144,128]{1,0:T(8,128)(2,1)S(1)}, s16[144,128]{1,0:T(8,128)(2,1)S(1)}, u32[]{:S(2)}, u32[]{:S(2)}) collective-permute-start(s16[144,128]{1,0:T(8,128)(2,1)S(1)} %get-tuple-element.25), channel_id=1, source_target_pairs={{0,2},{1,3},{2,0},{3,1},{4,6},{5,7},{6,4},{7,5},{8,10},{9,11},{10,... | collective-permute-start | bytes 110600 | tf_op jit(solution)/shard_map/ppermute | solution.py:490
  25.3 1.8 %collective-permute-done.5.refs_1_ = s16[144,128]{1,0:T(8,128)(2,1)S(1)} collective-permute-done((s16[144,128]{1,0:T(8,128)(2,1)S(1)}, s16[144,128]{1,0:T(8,128)(2,1)S(1)}, u32[]{:S(2)}, u32[]{:S(2)}) %collective-permute-start.5) | collective-permute-done | bytes 36896 | tf_op jit(solution)/shard_map/ppermute | solution.py:490
  27.1 1.7 %collective-permute-done.6.refs_2_ = s16[144,128]{1,0:T(8,128)(2,1)S(1)} collective-permute-done((s16[144,128]{1,0:T(8,128)(2,1)S(1)}, s16[144,128]{1,0:T(8,128)(2,1)S(1)}, u32[]{:S(2)}, u32[]{:S(2)}) %collective-permute-start.6) | collective-permute-done | bytes 36896 | tf_op jit(solution)/shard_map/ppermute | solution.py:490
  28.8 0.0 collective-permute-done.7.refs_3_
  28.8 2.1 %shard_map.80 = (f32[64,256]{1,0:T(8,128)}, f32[16,256]{1,0:T(8,128)}, f32[1,128]{1,0:T(1,128)S(1)}) custom-call(s32[72]{0:T(128)S(1)} %get-tuple-element.16.plan, f32[128,128]{1,0:T(8,128)S(1)} %get-tuple-element.22.refs_0_, s16[144,128]{1,0:T(8,128)(2,1)S(1)} %collective-permute-done.5.refs_1_, s16[144,128]{1,0:T(8,128)(2,1)S(1)} %collective-permute-done.6.refs_2_, ...), custom_call_target="tpu_custom_call" | custom-call | tf_op jit(solution)/shard_map/pallas_call | solution.py:468
  31.0 10.3 %all_to_all.5 = f32[32,1,128]{2,1,0:T(1,128)S(1)} all-to-all(f32[32,1,128]{2,1,0:T(1,128)S(1)} %broadcast_in_dim.9), channel_id=1, replica_groups=mesh['row'=4,'col'=8] {'row','col'}, dimensions={0} | all-to-all | bytes 32768 | tf_op jit(solution)/shard_map/all_to_all | solution.py:496
  41.2 0.5 %reduce_max.11 = f32[128]{0:T(128)} reduce(f32[32,1,128]{2,0,1:T(8,128)S(1)} %bitcast.11, f32[]{:T(128)} %constant.0.clone.1), dimensions={0,1}, to_apply=%region_0.0 | reduce | flops 3968 | bytes 16900 | tf_op jit(solution)/shard_map/reduce_max | solution.py:496
  (3 shorter events, 0.0 us)
Async XLA Ops:
  0.6 12.0 %collective-permute-start = (bf16[64,1536]{1,0:T(8,128)(2,1)}, bf16[64,1536]{1,0:T(8,128)(2,1)S(1)}, u32[]{:S(2)}, u32[]{:S(2)}) collective-permute-start(bf16[64,1536]{1,0:T(8,128)(2,1)} %bitcast.8), channel_id=1, source_target_pairs={{0,8},{8,0},{16,24},{24,16},{1,9},{9,1},{17,25},{25,17},{2,10},{10... | collective-permute-start | bytes 589832 | tf_op jit(solution)/shard_map/ppermute | solution.py:490
  3.6 8.5 %collective-permute-start.1 = (bf16[64,1536]{1,0:T(8,128)(2,1)}, bf16[64,1536]{1,0:T(8,128)(2,1)S(1)}, u32[]{:S(2)}, u32[]{:S(2)}) collective-permute-start(bf16[64,1536]{1,0:T(8,128)(2,1)} %bitcast.9), channel_id=1, source_target_pairs={{0,16},{8,24},{16,0},{24,8},{1,17},{9,25},{17,1},{25,9},{2,18},{10... | collective-permute-start | bytes 589832 | tf_op jit(solution)/shard_map/ppermute | solution.py:490
  12.1 4.7 %collective-permute-start.2 = (bf16[64,768]{1,0:T(8,128)(2,1)S(1)}, bf16[64,768]{1,0:T(8,128)(2,1)S(1)}, u32[]{:S(2)}, u32[]{:S(2)}) collective-permute-start(bf16[64,768]{1,0:T(8,128)(2,1)S(1)} %slice.12), channel_id=1, source_target_pairs={{0,8},{8,0},{16,24},{24,16},{1,9},{9,1},{17,25},{25,17},{2,10},{10... | collective-permute-start | bytes 294920 | tf_op jit(solution)/shard_map/ppermute | solution.py:490
  12.6 4.7 %collective-permute-start.3 = (bf16[64,768]{1,0:T(8,128)(2,1)S(1)}, bf16[64,768]{1,0:T(8,128)(2,1)S(1)}, u32[]{:S(2)}, u32[]{:S(2)}) collective-permute-start(bf16[64,768]{1,0:T(8,128)(2,1)S(1)} %slice.13), channel_id=1, source_target_pairs={{0,16},{8,24},{16,0},{24,8},{1,17},{9,25},{17,1},{25,9},{2,18},{10... | collective-permute-start | bytes 294920 | tf_op jit(solution)/shard_map/ppermute | solution.py:490
  19.1 1.6 %collective-permute-start.4 = (f32[4,128,128]{2,1,0:T(8,128)S(1)}, f32[4,128,128]{2,1,0:T(8,128)S(1)}, u32[]{:S(2)}, u32[]{:S(2)}) collective-permute-start(f32[4,128,128]{2,1,0:T(8,128)S(1)} %get-tuple-element.21), channel_id=1, source_target_pairs={{0,1},{1,0},{2,3},{3,2},{4,5},{5,4},{6,7},{7,6},{8,9},{9,8},{10,11... | collective-permute-start | bytes 786440 | tf_op jit(solution)/shard_map/ppermute | solution.py:490
  20.9 6.2 %collective-permute-start.5 = (s16[144,128]{1,0:T(8,128)(2,1)S(1)}, s16[144,128]{1,0:T(8,128)(2,1)S(1)}, u32[]{:S(2)}, u32[]{:S(2)}) collective-permute-start(s16[144,128]{1,0:T(8,128)(2,1)S(1)} %get-tuple-element.23), channel_id=1, source_target_pairs={{0,6},{1,7},{2,4},{3,5},{4,2},{5,3},{6,0},{7,1},{8,14},{9,15},{10,... | collective-permute-start | bytes 110600 | tf_op jit(solution)/shard_map/ppermute | solution.py:490
  24.0 4.9 %collective-permute-start.6 = (s16[144,128]{1,0:T(8,128)(2,1)S(1)}, s16[144,128]{1,0:T(8,128)(2,1)S(1)}, u32[]{:S(2)}, u32[]{:S(2)}) collective-permute-start(s16[144,128]{1,0:T(8,128)(2,1)S(1)} %get-tuple-element.24), channel_id=1, source_target_pairs={{0,4},{1,5},{2,6},{3,7},{4,0},{5,1},{6,2},{7,3},{8,12},{9,13},{10,... | collective-permute-start | bytes 110600 | tf_op jit(solution)/shard_map/ppermute | solution.py:490
  24.0 4.9 %collective-permute-start.7 = (s16[144,128]{1,0:T(8,128)(2,1)S(1)}, s16[144,128]{1,0:T(8,128)(2,1)S(1)}, u32[]{:S(2)}, u32[]{:S(2)}) collective-permute-start(s16[144,128]{1,0:T(8,128)(2,1)S(1)} %get-tuple-element.25), channel_id=1, source_target_pairs={{0,2},{1,3},{2,0},{3,1},{4,6},{5,7},{6,4},{7,5},{8,10},{9,11},{10,... | collective-permute-start | bytes 110600 | tf_op jit(solution)/shard_map/ppermute | solution.py:490

commit v7 on v6

--- a/solution.py
+++ b/solution.py
@@ -13,7 +13,7 @@
 PICKS = 8
 LEVELS = 32760.0
 EXTRA = 16
-PART = 256
+PART = 1024
 STEPS = 64.0
 RUN_LEAVES = 4
 
@@ -22,61 +22,67 @@
     return lax.dot_general(a, b, (((1,), (1,)), ((), ())), preferred_element_type=jnp.float32)
 
 
-def clear_runs(pick, n_row, depth, frontal, leaf_first):
-    group_rows, width = frontal.shape
-    per_group = leaf_first.shape[0] // n_row
-    runs = per_group // RUN_LEAVES
-    run_rows = group_rows // runs
+def leaf_blocks(run_rows, width, edges, act):
+    group_rows = edges.shape[0] // RUN_LEAVES * run_rows
     row_pos = lax.axis_index("row")
     first_col = lax.axis_index("col") * width
-
-    def clear(at, carry):
+    depth = width // lax.axis_size("row")
+
+    def one(at, carry):
         run = at // (run_rows // LANES)
-        begin = row_pos * group_rows + run * run_rows
+        begin_row = row_pos * group_rows + run * run_rows
         begin_col = row_pos * group_rows + at * LANES
         inside = begin_col - first_col
-        held = (inside >= 0) & (inside < width)
-        inside = jnp.clip(inside, 0, width - LANES)
-
-        @pl.when(held & (((inside // depth) ^ row_pos) == pick))
+
+        @pl.when((inside >= 0) & (inside < width))
         def _():
-            rows = pl.ds(pl.multiple_of(run * run_rows, run_rows), run_rows)
-            lanes = pl.ds(pl.multiple_of(inside, LANES), LANES)
-            part = frontal[rows, lanes]
-            down = lax.broadcasted_iota(jnp.int32, part.shape, 0) + begin
-            across = lax.broadcasted_iota(jnp.int32, part.shape, 1) + begin_col
-            leaf_down = jnp.zeros(part.shape, jnp.int32)
-            leaf_across = jnp.zeros(part.shape, jnp.int32)
+            shape = (run_rows, LANES)
+            down = lax.broadcasted_iota(jnp.int32, shape, 0) + begin_row
+            across = lax.broadcasted_iota(jnp.int32, shape, 1) + begin_col
+            leaf_down = jnp.zeros(shape, jnp.int32)
+            leaf_across = jnp.zeros(shape, jnp.int32)
             for k in range(1, RUN_LEAVES):
-                edge = leaf_first[row_pos * per_group + run * RUN_LEAVES + k]
+                edge = edges[run * RUN_LEAVES + k]
                 leaf_down += (down >= edge).astype(jnp.int32)
                 leaf_across += (across >= edge).astype(jnp.int32)
-            kept = jnp.where(leaf_down == leaf_across, 0.0, part.astype(jnp.float32))
-            frontal[rows, lanes] = kept.astype(jnp.bfloat16)
+            column = jnp.clip(inside, 0, width - LANES)
+            rows = pl.ds(pl.multiple_of(run * run_rows, run_rows), run_rows)
+            act((column // depth) ^ row_pos, rows, column, leaf_down == leaf_across)
 
         return carry
 
-    lax.fori_loop(0, group_rows // LANES, clear, 0)
-
-
-def multiply(pick, frontal, slabs, begun, total):
-    group_rows, width = frontal.shape
-    depth = width // lax.axis_size("row")
-    row_pos = lax.axis_index("row")
-    part = min(group_rows, 512)
-
-    def rows_of(at, carry):
-        rows = pl.ds(pl.multiple_of(at * part, part), part)
-        value = None if begun is None else begun[rows, :]
-        for (k, offset), slab in zip(pick, slabs):
-            begin = pl.multiple_of((row_pos ^ k) * depth + offset, LANES)
-            twice = jnp.concatenate([slab[...], slab[...]], axis=0)
-            add = nt_dot(frontal[rows, pl.ds(begin, slab.shape[1])], twice)
-            value = add if value is None else value + add
-        total[rows, :] = value
-        return carry
-
-    lax.fori_loop(0, group_rows // part, rows_of, 0)
+    lax.fori_loop(0, group_rows // LANES, one, 0)
+
+
+def multiply(items, value, rows):
+    for block, begin, slab in items:
+        twice = jnp.concatenate([slab[...], slab[...]], axis=0)
+        add = nt_dot(block[rows, pl.ds(begin, slab.shape[1])], twice)
+        value = add if value is None else value + add
+    return value
+
+
+def clear_runs(run_rows, width, edges, turn, block):
+    def act(here, rows, column, same):
+        @pl.when(here == turn)
+        def _():
+            inside = lax.rem(column, block.shape[1])
+            lanes = pl.ds(pl.multiple_of(inside, LANES), LANES)
+            part = block[rows, lanes].astype(jnp.float32)
+            block[rows, lanes] = jnp.where(same, 0.0, part).astype(jnp.bfloat16)
+
+    leaf_blocks(run_rows, width, edges, act)
+
+
+def bring_block(frontal, turn, block, sem):
+    depth = block.shape[1]
+    begin = pl.multiple_of((lax.axis_index("row") ^ turn) * depth, LANES)
+    return pltpu.make_async_copy(frontal.at[:, pl.ds(begin, depth)], block, sem)
+
+
+def parts_of(group_rows):
+    part = min(group_rows, PART)
+    return [pl.ds(at, part) for at in range(0, group_rows, part)]
 
 
 def plan_leaves(n_row, group_rows, capacity, first, owners, skel, plan):
@@ -119,41 +125,36 @@
     leaf_owner,
     skeleton,
     frontal,
-    slab,
-    held,
+    own,
+    block_one,
     total,
     target,
     plan,
+    edges,
     first,
     owners,
     skel,
+    used,
+    block_own,
     near,
-    used,
-    table_sems,
-    slab_sem,
     sems,
 ):
-    group_rows = frontal.shape[0]
-    depth = slab.shape[1]
+    group_rows, width = frontal.shape
     leaves = leaf_first.shape[0]
     per_group = leaves // n_row
+    run_rows = group_rows // (per_group // RUN_LEAVES)
     per_owner = 2 * group_rows // n_col // UNIT
-    units = group_rows // UNIT
     row_pos = lax.axis_index("row")
     col_pos = lax.axis_index("col")
-    tables = [
-        pltpu.make_async_copy(leaf_first, first, table_sems.at[0]),
-        pltpu.make_async_copy(leaf_owner, owners, table_sems.at[1]),
-        pltpu.make_async_copy(skeleton, skel, table_sems.at[2]),
+    copies = [
+        pltpu.make_async_copy(leaf_first, first, sems.at[0]),
+        pltpu.make_async_copy(leaf_owner, owners, sems.at[1]),
+        pltpu.make_async_copy(skeleton, skel, sems.at[2]),
+        pltpu.make_async_copy(own, near, sems.at[3]),
+        bring_block(frontal, 0, block_own, sems.at[4]),
+        bring_block(frontal, 1, block_one, sems.at[5]),
     ]
-    bring = pltpu.make_async_copy(slab, near, slab_sem)
-    moves = []
-    for k in range(n_row):
-        lanes = pl.ds(pl.multiple_of((row_pos ^ k) * depth, LANES), depth)
-        moves.append(
-            pltpu.make_async_copy(frontal.at[:, lanes], held.at[:, lanes], sems.at[k])
-        )
-    for copy in tables + [bring] + moves:
+    for copy in copies:
         copy.start()
 
     def clear(at, carry):
@@ -161,8 +162,14 @@
         return carry
 
     lax.fori_loop(0, n_col, clear, 0)
-    for copy in tables:
+    for copy in copies[:3]:
         copy.wait()
+
+    def edge(at, carry):
+        edges[at] = first[row_pos * per_group + at]
+        return carry
+
+    lax.fori_loop(0, per_group, edge, 0)
 
     def place(unit, leaf):
         row = row_pos * group_rows + unit * UNIT
@@ -175,52 +182,62 @@
         target[unit] = (owner ^ col_pos) * per_owner + slot
         return leaf
 
-    lax.fori_loop(0, units, place, row_pos * per_group)
+    lax.fori_loop(0, group_rows // UNIT, place, row_pos * per_group)
     plan_leaves(n_row, group_rows, per_owner * UNIT, first, owners, skel, plan)
-    bring.wait()
-    moves[0].wait()
-    clear_runs(0, n_row, depth, held, first)
-    multiply(((0, 0),), held, (near,), None, total)
-    for k in range(1, n_row):
-        moves[k].wait()
-        clear_runs(k, n_row, depth, held, first)
-
-
-def middle_kernel(pick, frontal, begun, *refs):
-    multiply(pick, frontal, refs[: len(pick)], begun, refs[len(pick)])
-
-
-def last_kernel(pick, target, frontal, begun, *refs):
-    slabs, (keep, swap) = refs[: len(pick)], refs[len(pick) :]
+    for copy in copies[3:5]:
+        copy.wait()
+    clear_runs(run_rows, width, edges, 0, block_own)
+    for rows in parts_of(group_rows):
+        total[rows, :] = multiply([(block_own, 0, near)], None, rows)
+    copies[5].wait()
+    clear_runs(run_rows, width, edges, 1, block_one)
+
+
+def near_kernel(edges, frontal, block_one, begun, one, two, block_two, block_last, total, sems):
     group_rows, width = frontal.shape
-    depth = width // lax.axis_size("row")
-    row_pos = lax.axis_index("row")
+    run_rows = group_rows // (edges.shape[0] // RUN_LEAVES)
+    copies = [
+        bring_block(frontal, 2, block_two, sems.at[0]),
+        bring_block(frontal, 3, block_last, sems.at[1]),
+    ]
+    for copy in copies:
+        copy.start()
+    from_one = block_one.shape[1] - one.shape[1]
+    for rows in parts_of(group_rows):
+        total[rows, :] = multiply([(block_one, from_one, one)], begun[rows, :], rows)
+    copies[0].wait()
+    clear_runs(run_rows, width, edges, 2, block_two)
+    for rows in parts_of(group_rows):
+        total[rows, :] = multiply([(block_two, 0, two)], total[rows, :], rows)
+    copies[1].wait()
+    clear_runs(run_rows, width, edges, 3, block_last)
+
+
+def middle_kernel(block_one, block_two, begun, one, two, total):
+    from_two = block_two.shape[1] - two.shape[1]
+    items = [(block_one, 0, one), (block_two, from_two, two)]
+    for rows in parts_of(begun.shape[0]):
+        total[rows, :] = multiply(items, begun[rows, :], rows)
+
+
+def last_kernel(target, block, begun, left, right, keep, swap):
+    items = [(block, 0, left), (block, left.shape[1], right)]
     chips, half, wide = keep.shape
     per_half = half // UNIT
     lane = lax.broadcasted_iota(jnp.int32, (UNIT, wide), 1) // (wide // 2)
-    twice = [jnp.concatenate([slab[...], slab[...]], axis=0) for slab in slabs]
     keep[...] = jnp.zeros(keep.shape, jnp.float32)
     swap[...] = jnp.zeros(swap.shape, jnp.float32)
-
-    def rows_of(at, carry):
-        rows = pl.ds(pl.multiple_of(at * PART, PART), PART)
-        value = begun[rows, :]
-        for (k, offset), slab in zip(pick, twice):
-            begin = pl.multiple_of((row_pos ^ k) * depth + offset, LANES)
-            value = value + nt_dot(frontal[rows, pl.ds(begin, slab.shape[1])], slab)
-        for unit in range(PART // UNIT):
-            spot = target[at * (PART // UNIT) + unit]
-            turn, slot = spot // (2 * per_half), spot % (2 * per_half)
+    for rows in parts_of(block.shape[0]):
+        value = multiply(items, begun[rows, :], rows)
+        for unit in range(rows.size // UNIT):
+            spot = target[rows.start // UNIT + unit]
+            step, slot = spot // (2 * per_half), spot % (2 * per_half)
             to_rows = pl.ds(pl.multiple_of(slot % per_half * UNIT, UNIT), UNIT)
             piece = value[unit * UNIT : (unit + 1) * UNIT]
             near = lane == slot // per_half
             for other, out in ((0, keep), (1, swap)):
-                mask = near & (turn % 2 == other)
-                pltpu.store(out.at[turn // 2, to_rows, :], piece, mask=mask)
-        return carry
-
-    steps = group_rows // PART
-    lax.fori_loop(0, steps, rows_of, 0, unroll=min(steps, 4))
+                mask = near & (step % 2 == other)
+                pltpu.store(out.at[step // 2, to_rows, :], piece, mask=mask)
 
 
 def vmem(count=None):
@@ -240,68 +257,77 @@
     return pltpu.with_memory_space_constraint(value, pltpu.HBM)
 
 
-def product_cost(frontal, slabs):
-    group_rows = frontal.shape[0]
-    samples = slabs[0].shape[0]
-    depth = sum(slab.shape[1] for slab in slabs)
-    return pl.CostEstimate(
-        flops=8 * group_rows * depth * samples,
-        bytes_accessed=2 * group_rows * depth,
-        transcendentals=0,
-    )
-
-
-def own_product(frontal, slab, leaf_first, leaf_owner, skeleton, n_row, n_col):
+def product_cost(frontal, samples, slabs):
     group_rows, width = frontal.shape
-    samples, depth = slab.shape
+    flops = 8 * group_rows * width * samples * slabs // 4
+    return pl.CostEstimate(flops=flops, bytes_accessed=flops // samples, transcendentals=0)
+
+
+def own_product(frontal, own, leaf_first, leaf_owner, skeleton, n_row, n_col):
+    group_rows, width = frontal.shape
     leaves = leaf_first.shape[0]
+    samples, depth = own.shape
     return pl.pallas_call(
         functools.partial(own_kernel, n_row, n_col),
         in_specs=[hbm()] * 5,
-        out_specs=[vmem(), vmem(), smem(), smem()],
+        out_specs=vmem(2) + [smem()] * 3,
         out_shape=[
-            jax.ShapeDtypeStruct(frontal.shape, frontal.dtype),
+            jax.ShapeDtypeStruct((group_rows, depth), frontal.dtype),
             jax.ShapeDtypeStruct((group_rows, 2 * samples), jnp.float32),
             jax.ShapeDtypeStruct((group_rows // UNIT,), jnp.int32),
             jax.ShapeDtypeStruct((PICKS + LEAF_MOST * skeleton.shape[0],), jnp.int32),
+            jax.ShapeDtypeStruct((leaves // n_row,), jnp.int32),
         ],
         scratch_shapes=[
             pltpu.SMEM((leaves,), jnp.int32),
             pltpu.SMEM((leaves,), jnp.int32),
             pltpu.SMEM(skeleton.shape, jnp.int32),
-            pltpu.VMEM((samples, depth), slab.dtype),
             pltpu.SMEM((n_col,), jnp.int32),
-            pltpu.SemaphoreType.DMA((3,)),
-            pltpu.SemaphoreType.DMA,
-            pltpu.SemaphoreType.DMA((n_row,)),
+            pltpu.VMEM((group_rows, depth), frontal.dtype),
+            pltpu.VMEM(own.shape, own.dtype),
+            pltpu.SemaphoreType.DMA((6,)),
         ],
-        cost_estimate=product_cost(frontal, [slab] * n_row),
+        cost_estimate=product_cost(frontal, samples, 2),
         compiler_params=pltpu.CompilerParams(vmem_limit_bytes=24 * 2**20),
-    )(*(in_hbm(x) for x in (leaf_first, leaf_owner, skeleton, frontal, slab)))
-
-
-def middle_product(frontal, begun, slabs, pick):
+    )(*(in_hbm(x) for x in (leaf_first, leaf_owner, skeleton, frontal, own)))
+
+
+def near_product(frontal, block_one, begun, edges, one, two):
+    group_rows, width = frontal.shape
+    block = jax.ShapeDtypeStruct(block_one.shape, frontal.dtype)
     return pl.pallas_call(
-        functools.partial(middle_kernel, pick),
-        in_specs=vmem(2 + len(slabs)),
+        near_kernel,
+        in_specs=[smem(), hbm()] + vmem(4),
+        out_specs=vmem(3),
+        out_shape=[block, block, jax.ShapeDtypeStruct(begun.shape, jnp.float32)],
+        scratch_shapes=[pltpu.SemaphoreType.DMA((2,))],
+        cost_estimate=product_cost(frontal, one.shape[0], 2),
+        compiler_params=pltpu.CompilerParams(vmem_limit_bytes=24 * 2**20),
+    )(edges, in_hbm(frontal), block_one, begun, one, two)
+
+
+def middle_product(block_one, block_two, begun, one, two):
+    return pl.pallas_call(
+        middle_kernel,
+        in_specs=vmem(5),
         out_specs=vmem(),
         out_shape=jax.ShapeDtypeStruct(begun.shape, jnp.float32),
-        cost_estimate=product_cost(frontal, slabs),
+        cost_estimate=product_cost(block_one, one.shape[0], 4),
         compiler_params=pltpu.CompilerParams(vmem_limit_bytes=24 * 2**20),
-    )(frontal, begun, *slabs)
-
-
-def last_product(frontal, begun, target, slabs, pick, n_col):
+    )(block_one, block_two, begun, one, two)
+
+
+def last_product(frontal, begun, target, slab, n_col):
     group_rows, wide = begun.shape
     block = jax.ShapeDtypeStruct((n_col // 2, group_rows // n_col, wide), jnp.float32)
     return pl.pallas_call(
-        functools.partial(last_kernel, pick),
-        in_specs=[smem()] + vmem(2 + len(slabs)),
+        last_kernel,
+        in_specs=[smem()] + vmem(2 + len(slab)),
         out_specs=vmem(2),
         out_shape=[block, block],
-        cost_estimate=product_cost(frontal, slabs),
+        cost_estimate=product_cost(frontal, wide // 2, 4),
         compiler_params=pltpu.CompilerParams(vmem_limit_bytes=24 * 2**20),
-    )(target, frontal, begun, *slabs)
+    )(target, frontal, begun, *slab)
 
 
 def squeeze_kernel(keep, swapped, here, *away):
@@ -496,27 +522,28 @@
     return jnp.max(lax.all_to_all(every, axis, 0, 0), axis=0)
 
 
-def gather_near(own, n_row):
-    depth = own.shape[1]
-    near = {(k, 0): exchange(own, "row", k) for k in range(1, n_row - 1)}
-    if n_row != 4:
-        return near, {(n_row - 1, 0): exchange(own, "row", n_row - 1)}
-    cut = depth // 2 // LANES * LANES
-    left = exchange(near[2, 0][:, :cut], "row", 1)
-    right = exchange(near[1, 0][:, cut:], "row", 2)
-    return near, {(3, 0): left, (3, cut): right}
-
-
 def local(frontal, sample_cols, leaf_first, leaf_owner, skeleton):
     n_col = lax.axis_size("col")
     n_row = lax.axis_size("row")
     own = sample_cols.T
-    first, second = gather_near(own, n_row)
-    held, begun, target, plan = own_product(
+    cut = own.shape[1] // 2 // LANES * LANES
+    left, right = own[:, :cut], own[:, cut:]
+    one_right = exchange(right, "row", 1)
+    two_left = exchange(left, "row", 2)
+    block_one, begun, target, plan, edges = own_product(
         frontal, own, leaf_first, leaf_owner, skeleton.T, n_row, n_col
     )
-    begun = middle_product(held, begun, list(first.values()), tuple(first))
-    keep, swap = last_product(held, begun, target, list(second.values()), tuple(second), n_col)
+    left, right, one_right, two_left, edges = lax.optimization_barrier(
+        (left, right, one_right, two_left, edges)
+    )
+    one_left = exchange(left, "row", 1)
+    two_right = exchange(right, "row", 2)
+    last = [exchange(two_left, "row", 1), exchange(one_right, "row", 2)]
+    block_two, block_last, begun = near_product(
+        frontal, block_one, begun, edges, one_right, two_left
+    )
+    begun = middle_product(block_one, block_two, begun, one_left, two_right)
+    keep, swap = last_product(block_last, begun, target, last, n_col)
     swapped = exchange(swap, "col", 1)
     here, *away = squeeze(keep, swapped)
     parts = [exchange(away[k - 1], "col", 2 * k) for k in range(n_col // 2 - 1, 0, -1)]

time: 41.9 us -> 44.8 us (1.069)
  starting transfers between devices: 9.59 us -> 13.2 us
  waiting for transfers between devices: 7.66 us -> 4.16 us
  Pallas kernels: 13 us -> 15.9 us
  blocking collectives: 10.3 us -> 9.14 us
  local copies, waits for them, and re-layouts: 0.03 us -> 0.97 us
    pallas_call x2 -> x3, Pallas kernels: 3.74 us -> 8.07 us  [the longest x1 5.21 us: near_product(): pl.pallas_call(near_kernel, in_specs=[smem(), hbm()] + vmem(4), out_specs...]
    ppermute x8 -> x10, starting transfers between devices: 9.59 us -> 13.2 us  [exchange(): return lax.ppermute(value, axis, pairs)]
    ppermute x8 -> x10, waiting for transfers between devices: 7.66 us -> 4.16 us  [exchange(): return lax.ppermute(value, axis, pairs)]
    pallas_call x1, Pallas kernels: 6.93 us -> 5.52 us  [own_product(): pl.pallas_call(functools.partial(own_kernel, n_row, n_col), in_specs=[hbm...]
    all_to_all x1, blocking collectives: 10.3 us -> 9.14 us  [largest(): return jnp.max(lax.all_to_all(every, axis, 0, 0), axis=0)]
    slice x2 -> x1, local copies, waits for them, and re-layouts: 0.02 us -> 0.96 us  [local(): left, right = (own[:, :cut], own[:, cut:])]
  transfers between devices with their start and end apart: 8 -> 10, of which waited for: 5 -> 4; matrix products, arithmetic and copies ran while one was open for 0% -> 0% of each run, Pallas kernels for 21% -> 26%
where the time goes in v7:
time: 44.8 us; the launch traced here: 44.6 us
  Pallas kernels  15.9 us (35%)
  starting transfers between devices  13.2 us (29%)
  blocking collectives  9.14 us (20%)
  waiting for transfers between devices  4.16 us (9%)
  local copies, waits for them, and re-layouts  0.97 us (2%)
  between operations  0.74 us (2%)
  other arithmetic  0.53 us (1%)
    ppermute x10, starting transfers between devices, exchange(): return lax.ppermute(value, axis, pairs)  13.2 us
    all_to_all x1, blocking collectives, largest(): return jnp.max(lax.all_to_all(every, axis, 0, 0), axis=0)  9.14 us
    pallas_call x1, Pallas kernels, own_product(): pl.pallas_call(functools.partial(own_kernel, n_row, n_col), in_specs=[hbm...  5.52 us
    pallas_call x1, Pallas kernels, near_product(): pl.pallas_call(near_kernel, in_specs=[smem(), hbm()] + vmem(4), out_specs...  5.21 us
    ppermute x10, waiting for transfers between devices, exchange(): return lax.ppermute(value, axis, pairs)  4.16 us
    pallas_call x1, Pallas kernels, leaf_work(): pl.pallas_call(functools.partial(leaf_kernel, skel), in_specs=[smem()] +...  2.12 us
    pallas_call x1, Pallas kernels, last_product(): pl.pallas_call(last_kernel, in_specs=[smem()] + vmem(2 + len(slab)), out_...  1.88 us
    pallas_call x1, Pallas kernels, middle_product(): pl.pallas_call(middle_kernel, in_specs=vmem(5), out_specs=vmem(), out_sha...  0.98 us
  transfers between devices with their start and end apart: 10, of which 4 were waited for; matrix products, arithmetic and copies ran while one was open for 0% of the time, Pallas kernels for 26%

profile of v7, /device:TPU:0, one launch (start us, length us, event | category | flops | bytes accessed | tf_op | source)
XLA Modules:
  0.0 44.6 jit_solution(10071060716694244507)
XLA Ops:
  0.6 1.0 %fusion = (bf16[64,768]{1,0:T(8,128)(2,1)S(1)}, bf16[64,768]{1,0:T(8,128)(2,1)S(1)}) fusion(bf16[64,1536]{1,0:T(8,128)(2,1)} %bitcast.8), kind=kLoop, calls=%fused_computation | loop fusion | bytes 393216 | tf_op jit(solution)/shard_map/slice | solution.py:530
  1.6 3.0 %collective-permute-start = (bf16[64,768]{1,0:T(8,128)(2,1)S(1)}, bf16[64,768]{1,0:T(8,128)(2,1)S(1)}, u32[]{:S(2)}, u32[]{:S(2)}) collective-permute-start(bf16[64,768]{1,0:T(8,128)(2,1)S(1)} %get-tuple-element.37), channel_id=1, source_target_pairs={{0,8},{8,0},{16,24},{24,16},{1,9},{9,1},{17,25},{25,17},{2,10},{10... | collective-permute-start | bytes 294920 | tf_op jit(solution)/shard_map/ppermute | solution.py:516
  4.6 1.5 %collective-permute-start.1 = (bf16[64,768]{1,0:T(8,128)(2,1)S(1)}, bf16[64,768]{1,0:T(8,128)(2,1)S(1)}, u32[]{:S(2)}, u32[]{:S(2)}) collective-permute-start(bf16[64,768]{1,0:T(8,128)(2,1)S(1)} %get-tuple-element.36), channel_id=1, source_target_pairs={{0,16},{8,24},{16,0},{24,8},{1,17},{9,25},{17,1},{25,9},{2,18},{10... | collective-permute-start | bytes 294920 | tf_op jit(solution)/shard_map/ppermute | solution.py:516
  6.1 5.5 %shard_map.76 = (bf16[1024,1536]{1,0:T(8,128)(2,1)S(1)}, f32[1024,128]{1,0:T(8,128)S(1)}, s32[32]{0:T(128)S(1)}, s32[72]{0:T(128)S(1)}, s32[16]{0:T(128)S(1)}) custom-call(s32[64]{0:T(128)} %leaf_first.1, s32[64]{0:T(128)} %leaf_owner.1, s32[16,64]{1,0:T(8,128)} %bitcast.11, bf16[1024,6144]{1,0:T(8,128)(2,1)} %frontal.3, bf16[64,1536]{1,0:T(8,128)(2,1)} %bitcast.9), custom_call_target="tpu_custom_call" | custom-call | flops 1610612736 | bytes 25165824 | tf_op jit(solution)/shard_map/pallas_call | solution.py:270
  11.6 0.0 collective-permute-done.one
  11.7 0.0 collective-permute-done.1.two
  11.7 0.6 %collective-permute-start.2 = (bf16[64,768]{1,0:T(8,128)(2,1)S(1)}, bf16[64,768]{1,0:T(8,128)(2,1)S(1)}, u32[]{:S(2)}, u32[]{:S(2)}) collective-permute-start(bf16[64,768]{1,0:T(8,128)(2,1)S(1)} %get-tuple-element.36), channel_id=1, source_target_pairs={{0,8},{8,0},{16,24},{24,16},{1,9},{9,1},{17,25},{25,17},{2,10},{10... | collective-permute-start | bytes 294920 | tf_op jit(solution)/shard_map/ppermute | solution.py:516
  12.3 0.0 collective-permute-start.3
  12.3 1.8 %collective-permute-start.4 = (bf16[64,768]{1,0:T(8,128)(2,1)S(1)}, bf16[64,768]{1,0:T(8,128)(2,1)S(1)}, u32[]{:S(2)}, u32[]{:S(2)}) collective-permute-start(bf16[64,768]{1,0:T(8,128)(2,1)S(1)} %collective-permute-done.1.two), channel_id=1, source_target_pairs={{0,8},{8,0},{16,24},{24,16},{1,9},{9,1},{17,25},{25,17},{2,10},{10... | collective-permute-start | bytes 294920 | tf_op jit(solution)/shard_map/ppermute | solution.py:516
  14.1 1.7 %collective-permute-start.5 = (bf16[64,768]{1,0:T(8,128)(2,1)S(1)}, bf16[64,768]{1,0:T(8,128)(2,1)S(1)}, u32[]{:S(2)}, u32[]{:S(2)}) collective-permute-start(bf16[64,768]{1,0:T(8,128)(2,1)S(1)} %collective-permute-done.one), channel_id=1, source_target_pairs={{0,16},{8,24},{16,0},{24,8},{1,17},{9,25},{17,1},{25,9},{2,18},{10... | collective-permute-start | bytes 294920 | tf_op jit(solution)/shard_map/ppermute | solution.py:516
  15.8 5.2 %shard_map.77 = (bf16[1024,1536]{1,0:T(8,128)(2,1)S(1)}, bf16[1024,1536]{1,0:T(8,128)(2,1)S(1)}, f32[1024,128]{1,0:T(8,128)S(1)}) custom-call(s32[16]{0:T(128)S(1)} %get-tuple-element.28.edges, bf16[1024,6144]{1,0:T(8,128)(2,1)} %frontal.3, bf16[1024,1536]{1,0:T(8,128)(2,1)S(1)} %get-tuple-element.29.block_one, f32[1024,128]{1,0:T(8,128)S(1)} %get-tuple-element.30.begun, ...), custom_call_target="tpu_custom_call" | custom-call | flops 1610612736 | bytes 25165824 | tf_op jit(solution)/shard_map/pallas_call | solution.py:298
  21.0 0.0 collective-permute-done.2.one
  21.0 0.0 collective-permute-done.3.two
  21.0 1.0 %shard_map.78.begun = f32[1024,128]{1,0:T(8,128)S(1)} custom-call(bf16[1024,1536]{1,0:T(8,128)(2,1)S(1)} %get-tuple-element.29.block_one, bf16[1024,1536]{1,0:T(8,128)(2,1)S(1)} %get-tuple-element.34.block_two, f32[1024,128]{1,0:T(8,128)S(1)} %get-tuple-element.35.begun, bf16[64,768]{1,0:T(8,128)(2,1)S(1)} %collective-permute-done.2.one, ...), custom_call_target="tpu_custom_call" | custom-call | flops 805306368 | bytes 12582912 | tf_op jit(solution)/shard_map/pallas_call | solution.py:310
  22.0 0.0 collective-permute-done.4.left
  22.0 0.0 collective-permute-done.5.right
  22.0 1.9 %shard_map.79 = (f32[4,128,128]{2,1,0:T(8,128)S(1)}, f32[4,128,128]{2,1,0:T(8,128)S(1)}) custom-call(s32[32]{0:T(128)S(1)} %get-tuple-element.26.target, bf16[1024,1536]{1,0:T(8,128)(2,1)S(1)} %get-tuple-element.33.block, f32[1024,128]{1,0:T(8,128)S(1)} %shard_map.78.begun, bf16[64,768]{1,0:T(8,128)(2,1)S(1)} %collective-permute-done.4.left, ...), custom_call_target="tpu_custom_call" | custom-call | flops 805306368 | bytes 12582912 | tf_op jit(solution)/shard_map/pallas_call | solution.py:323
  23.9 0.1 collective-permute-start.6
  24.0 1.5 %collective-permute-done.6.swapped = f32[4,128,128]{2,1,0:T(8,128)S(1)} collective-permute-done((f32[4,128,128]{2,1,0:T(8,128)S(1)}, f32[4,128,128]{2,1,0:T(8,128)S(1)}, u32[]{:S(2)}, u32[]{:S(2)}) %collective-permute-start.6) | collective-permute-done | bytes 262176 | tf_op jit(solution)/shard_map/ppermute | solution.py:516
  25.5 0.2 shard_map.80
  25.7 1.9 %collective-permute-start.7 = (s16[144,128]{1,0:T(8,128)(2,1)S(1)}, s16[144,128]{1,0:T(8,128)(2,1)S(1)}, u32[]{:S(2)}, u32[]{:S(2)}) collective-permute-start(s16[144,128]{1,0:T(8,128)(2,1)S(1)} %get-tuple-element.41), channel_id=1, source_target_pairs={{0,6},{1,7},{2,4},{3,5},{4,2},{5,3},{6,0},{7,1},{8,14},{9,15},{10,... | collective-permute-start | bytes 110600 | tf_op jit(solution)/shard_map/ppermute | solution.py:516
  27.6 0.0 collective-permute-start.8
  27.6 2.5 %collective-permute-start.9 = (s16[144,128]{1,0:T(8,128)(2,1)S(1)}, s16[144,128]{1,0:T(8,128)(2,1)S(1)}, u32[]{:S(2)}, u32[]{:S(2)}) collective-permute-start(s16[144,128]{1,0:T(8,128)(2,1)S(1)} %get-tuple-element.43), channel_id=1, source_target_pairs={{0,2},{1,3},{2,0},{3,1},{4,6},{5,7},{6,4},{7,5},{8,10},{9,11},{10,... | collective-permute-start | bytes 110600 | tf_op jit(solution)/shard_map/ppermute | solution.py:516
  30.2 1.4 %collective-permute-done.7.refs_1_ = s16[144,128]{1,0:T(8,128)(2,1)S(1)} collective-permute-done((s16[144,128]{1,0:T(8,128)(2,1)S(1)}, s16[144,128]{1,0:T(8,128)(2,1)S(1)}, u32[]{:S(2)}, u32[]{:S(2)}) %collective-permute-start.7) | collective-permute-done | bytes 36896 | tf_op jit(solution)/shard_map/ppermute | solution.py:516
  31.6 1.2 %collective-permute-done.8.refs_2_ = s16[144,128]{1,0:T(8,128)(2,1)S(1)} collective-permute-done((s16[144,128]{1,0:T(8,128)(2,1)S(1)}, s16[144,128]{1,0:T(8,128)(2,1)S(1)}, u32[]{:S(2)}, u32[]{:S(2)}) %collective-permute-start.8) | collective-permute-done | bytes 36896 | tf_op jit(solution)/shard_map/ppermute | solution.py:516
  32.7 0.1 collective-permute-done.9.refs_3_
  32.8 2.1 %shard_map.81 = (f32[64,256]{1,0:T(8,128)}, f32[16,256]{1,0:T(8,128)}, f32[1,128]{1,0:T(1,128)S(1)}) custom-call(s32[72]{0:T(128)S(1)} %get-tuple-element.25.plan, f32[128,128]{1,0:T(8,128)S(1)} %get-tuple-element.40.refs_0_, s16[144,128]{1,0:T(8,128)(2,1)S(1)} %collective-permute-done.7.refs_1_, s16[144,128]{1,0:T(8,128)(2,1)S(1)} %collective-permute-done.8.refs_2_, ...), custom_call_target="tpu_custom_call" | custom-call | tf_op jit(solution)/shard_map/pallas_call | solution.py:494
  34.9 9.1 %all_to_all.5 = f32[32,1,128]{2,1,0:T(1,128)S(1)} all-to-all(f32[32,1,128]{2,1,0:T(1,128)S(1)} %broadcast_in_dim.9), channel_id=1, replica_groups=mesh['row'=4,'col'=8] {'row','col'}, dimensions={0} | all-to-all | bytes 32768 | tf_op jit(solution)/shard_map/all_to_all | solution.py:522
  44.1 0.5 %reduce_max.11 = f32[128]{0:T(128)} reduce(f32[32,1,128]{2,0,1:T(8,128)S(1)} %bitcast.10, f32[]{:T(128)} %constant.0.clone.1), dimensions={0,1}, to_apply=%region_0.0 | reduce | flops 3968 | bytes 16900 | tf_op jit(solution)/shard_map/reduce_max | solution.py:522
  (1 shorter events, 0.0 us)
Async XLA Ops:
  1.6 10.1 %collective-permute-start = (bf16[64,768]{1,0:T(8,128)(2,1)S(1)}, bf16[64,768]{1,0:T(8,128)(2,1)S(1)}, u32[]{:S(2)}, u32[]{:S(2)}) collective-permute-start(bf16[64,768]{1,0:T(8,128)(2,1)S(1)} %get-tuple-element.37), channel_id=1, source_target_pairs={{0,8},{8,0},{16,24},{24,16},{1,9},{9,1},{17,25},{25,17},{2,10},{10... | collective-permute-start | bytes 294920 | tf_op jit(solution)/shard_map/ppermute | solution.py:516
  4.6 7.1 %collective-permute-start.1 = (bf16[64,768]{1,0:T(8,128)(2,1)S(1)}, bf16[64,768]{1,0:T(8,128)(2,1)S(1)}, u32[]{:S(2)}, u32[]{:S(2)}) collective-permute-start(bf16[64,768]{1,0:T(8,128)(2,1)S(1)} %get-tuple-element.36), channel_id=1, source_target_pairs={{0,16},{8,24},{16,0},{24,8},{1,17},{9,25},{17,1},{25,9},{2,18},{10... | collective-permute-start | bytes 294920 | tf_op jit(solution)/shard_map/ppermute | solution.py:516
  11.7 9.3 %collective-permute-start.2 = (bf16[64,768]{1,0:T(8,128)(2,1)S(1)}, bf16[64,768]{1,0:T(8,128)(2,1)S(1)}, u32[]{:S(2)}, u32[]{:S(2)}) collective-permute-start(bf16[64,768]{1,0:T(8,128)(2,1)S(1)} %get-tuple-element.36), channel_id=1, source_target_pairs={{0,8},{8,0},{16,24},{24,16},{1,9},{9,1},{17,25},{25,17},{2,10},{10... | collective-permute-start | bytes 294920 | tf_op jit(solution)/shard_map/ppermute | solution.py:516
  12.3 8.8 %collective-permute-start.3 = (bf16[64,768]{1,0:T(8,128)(2,1)S(1)}, bf16[64,768]{1,0:T(8,128)(2,1)S(1)}, u32[]{:S(2)}, u32[]{:S(2)}) collective-permute-start(bf16[64,768]{1,0:T(8,128)(2,1)S(1)} %get-tuple-element.37), channel_id=1, source_target_pairs={{0,16},{8,24},{16,0},{24,8},{1,17},{9,25},{17,1},{25,9},{2,18},{10... | collective-permute-start | bytes 294920 | tf_op jit(solution)/shard_map/ppermute | solution.py:516
  12.3 9.7 %collective-permute-start.4 = (bf16[64,768]{1,0:T(8,128)(2,1)S(1)}, bf16[64,768]{1,0:T(8,128)(2,1)S(1)}, u32[]{:S(2)}, u32[]{:S(2)}) collective-permute-start(bf16[64,768]{1,0:T(8,128)(2,1)S(1)} %collective-permute-done.1.two), channel_id=1, source_target_pairs={{0,8},{8,0},{16,24},{24,16},{1,9},{9,1},{17,25},{25,17},{2,10},{10... | collective-permute-start | bytes 294920 | tf_op jit(solution)/shard_map/ppermute | solution.py:516
  14.1 7.9 %collective-permute-start.5 = (bf16[64,768]{1,0:T(8,128)(2,1)S(1)}, bf16[64,768]{1,0:T(8,128)(2,1)S(1)}, u32[]{:S(2)}, u32[]{:S(2)}) collective-permute-start(bf16[64,768]{1,0:T(8,128)(2,1)S(1)} %collective-permute-done.one), channel_id=1, source_target_pairs={{0,16},{8,24},{16,0},{24,8},{1,17},{9,25},{17,1},{25,9},{2,18},{10... | collective-permute-start | bytes 294920 | tf_op jit(solution)/shard_map/ppermute | solution.py:516
  23.9 1.6 %collective-permute-start.6 = (f32[4,128,128]{2,1,0:T(8,128)S(1)}, f32[4,128,128]{2,1,0:T(8,128)S(1)}, u32[]{:S(2)}, u32[]{:S(2)}) collective-permute-start(f32[4,128,128]{2,1,0:T(8,128)S(1)} %get-tuple-element.39), channel_id=1, source_target_pairs={{0,1},{1,0},{2,3},{3,2},{4,5},{5,4},{6,7},{7,6},{8,9},{9,8},{10,11... | collective-permute-start | bytes 786440 | tf_op jit(solution)/shard_map/ppermute | solution.py:516
  25.7 5.9 %collective-permute-start.7 = (s16[144,128]{1,0:T(8,128)(2,1)S(1)}, s16[144,128]{1,0:T(8,128)(2,1)S(1)}, u32[]{:S(2)}, u32[]{:S(2)}) collective-permute-start(s16[144,128]{1,0:T(8,128)(2,1)S(1)} %get-tuple-element.41), channel_id=1, source_target_pairs={{0,6},{1,7},{2,4},{3,5},{4,2},{5,3},{6,0},{7,1},{8,14},{9,15},{10,... | collective-permute-start | bytes 110600 | tf_op jit(solution)/shard_map/ppermute | solution.py:516
  27.6 5.1 %collective-permute-start.8 = (s16[144,128]{1,0:T(8,128)(2,1)S(1)}, s16[144,128]{1,0:T(8,128)(2,1)S(1)}, u32[]{:S(2)}, u32[]{:S(2)}) collective-permute-start(s16[144,128]{1,0:T(8,128)(2,1)S(1)} %get-tuple-element.42), channel_id=1, source_target_pairs={{0,4},{1,5},{2,6},{3,7},{4,0},{5,1},{6,2},{7,3},{8,12},{9,13},{10,... | collective-permute-start | bytes 110600 | tf_op jit(solution)/shard_map/ppermute | solution.py:516
  27.6 5.1 %collective-permute-start.9 = (s16[144,128]{1,0:T(8,128)(2,1)S(1)}, s16[144,128]{1,0:T(8,128)(2,1)S(1)}, u32[]{:S(2)}, u32[]{:S(2)}) collective-permute-start(s16[144,128]{1,0:T(8,128)(2,1)S(1)} %get-tuple-element.43), channel_id=1, source_target_pairs={{0,2},{1,3},{2,0},{3,1},{4,6},{5,7},{6,4},{7,5},{8,10},{9,11},{10,... | collective-permute-start | bytes 110600 | tf_op jit(solution)/shard_map/ppermute | solution.py:516

commit v8 on v7

--- a/solution.py
+++ b/solution.py
@@ -62,14 +62,16 @@
     return value
 
 
-def clear_runs(run_rows, width, edges, turn, block):
+def clear_runs(run_rows, width, edges, turns, blocks):
     def act(here, rows, column, same):
-        @pl.when(here == turn)
-        def _():
-            inside = lax.rem(column, block.shape[1])
-            lanes = pl.ds(pl.multiple_of(inside, LANES), LANES)
-            part = block[rows, lanes].astype(jnp.float32)
-            block[rows, lanes] = jnp.where(same, 0.0, part).astype(jnp.bfloat16)
+        for turn, block in zip(turns, blocks):
+
+            @pl.when(here == turn)
+            def _():
+                inside = lax.rem(column, block.shape[1])
+                lanes = pl.ds(pl.multiple_of(inside, LANES), LANES)
+                part = block[rows, lanes].astype(jnp.float32)
+                block[rows, lanes] = jnp.where(same, 0.0, part).astype(jnp.bfloat16)
 
     leaf_blocks(run_rows, width, edges, act)
 
@@ -118,42 +120,22 @@
     plan[LEAF_MOST] = count
 
 
-def own_kernel(
-    n_row,
-    n_col,
-    leaf_first,
-    leaf_owner,
-    skeleton,
-    frontal,
-    own,
-    block_one,
-    total,
-    target,
-    plan,
-    edges,
-    first,
-    owners,
-    skel,
-    used,
-    block_own,
-    near,
-    sems,
-):
+def bring_kernel(n_row, n_col, leaf_first, leaf_owner, frontal, *refs):
+    *blocks, place_row, place_kind, edges, first, owners, used, sems = refs
     group_rows, width = frontal.shape
     leaves = leaf_first.shape[0]
     per_group = leaves // n_row
     run_rows = group_rows // (per_group // RUN_LEAVES)
-    per_owner = 2 * group_rows // n_col // UNIT
+    half = group_rows // n_col
+    per_half = half // UNIT
     row_pos = lax.axis_index("row")
     col_pos = lax.axis_index("col")
     copies = [
         pltpu.make_async_copy(leaf_first, first, sems.at[0]),
         pltpu.make_async_copy(leaf_owner, owners, sems.at[1]),
-        pltpu.make_async_copy(skeleton, skel, sems.at[2]),
-        pltpu.make_async_copy(own, near, sems.at[3]),
-        bring_block(frontal, 0, block_own, sems.at[4]),
-        bring_block(frontal, 1, block_one, sems.at[5]),
     ]
+    for turn, block in enumerate(blocks):
+        copies.append(bring_block(frontal, turn, block, sems.at[2 + turn]))
     for copy in copies:
         copy.start()
 
@@ -162,7 +144,7 @@
         return carry
 
     lax.fori_loop(0, n_col, clear, 0)
-    for copy in copies[:3]:
+    for copy in copies[:2]:
         copy.wait()
 
     def edge(at, carry):
@@ -179,65 +161,55 @@
         owner = owners[leaf]
         slot = used[owner]
         used[owner] = slot + 1
-        target[unit] = (owner ^ col_pos) * per_owner + slot
+        step = owner ^ col_pos
+        place_row[unit] = step // 2 * half + slot % per_half * UNIT
+        place_kind[unit] = step % 2 * 2 + slot // per_half
         return leaf
 
     lax.fori_loop(0, group_rows // UNIT, place, row_pos * per_group)
-    plan_leaves(n_row, group_rows, per_owner * UNIT, first, owners, skel, plan)
-    for copy in copies[3:5]:
+    for copy in copies[2:]:
         copy.wait()
-    clear_runs(run_rows, width, edges, 0, block_own)
-    for rows in parts_of(group_rows):
-        total[rows, :] = multiply([(block_own, 0, near)], None, rows)
-    copies[5].wait()
-    clear_runs(run_rows, width, edges, 1, block_one)
-
-
-def near_kernel(edges, frontal, block_one, begun, one, two, block_two, block_last, total, sems):
+    clear_runs(run_rows, width, edges, range(len(blocks)), blocks)
+
+
+def near_kernel(edges, frontal, own, *refs):
+    *blocks, one, two, block_last, total, near, sems = refs
     group_rows, width = frontal.shape
     run_rows = group_rows // (edges.shape[0] // RUN_LEAVES)
     copies = [
-        bring_block(frontal, 2, block_two, sems.at[0]),
-        bring_block(frontal, 3, block_last, sems.at[1]),
+        pltpu.make_async_copy(own, near, sems.at[0]),
+        bring_block(frontal, len(blocks), block_last, sems.at[1]),
     ]
     for copy in copies:
         copy.start()
-    from_one = block_one.shape[1] - one.shape[1]
     for rows in parts_of(group_rows):
-        total[rows, :] = multiply([(block_one, from_one, one)], begun[rows, :], rows)
+        total[rows, :] = multiply([(blocks[1], 0, one), (blocks[2], 0, two)], None, rows)
     copies[0].wait()
-    clear_runs(run_rows, width, edges, 2, block_two)
     for rows in parts_of(group_rows):
-        total[rows, :] = multiply([(block_two, 0, two)], total[rows, :], rows)
+        total[rows, :] = multiply([(blocks[0], 0, near)], total[rows, :], rows)
     copies[1].wait()
-    clear_runs(run_rows, width, edges, 3, block_last)
-
-
-def middle_kernel(block_one, block_two, begun, one, two, total):
-    from_two = block_two.shape[1] - two.shape[1]
-    items = [(block_one, 0, one), (block_two, from_two, two)]
-    for rows in parts_of(begun.shape[0]):
-        total[rows, :] = multiply(items, begun[rows, :], rows)
-
-
-def last_kernel(target, block, begun, left, right, keep, swap):
+    clear_runs(run_rows, width, edges, [len(blocks)], [block_last])
+
+
+def last_kernel(place_row, place_kind, block, begun, left, right, keep, swap):
     items = [(block, 0, left), (block, left.shape[1], right)]
-    chips, half, wide = keep.shape
-    per_half = half // UNIT
+    wide = keep.shape[1]
     lane = lax.broadcasted_iota(jnp.int32, (UNIT, wide), 1) // (wide // 2)
     keep[...] = jnp.zeros(keep.shape, jnp.float32)
     swap[...] = jnp.zeros(swap.shape, jnp.float32)
     for rows in parts_of(block.shape[0]):
         value = multiply(items, begun[rows, :], rows)
-        for unit in range(rows.size // UNIT):
-            spot = target[rows.start // UNIT + unit]
-            step, slot = spot // (2 * per_half), spot % (2 * per_half)
-            to_rows = pl.ds(pl.multiple_of(slot % per_half * UNIT, UNIT), UNIT)
-            piece = value[unit * UNIT : (unit + 1) * UNIT]
-            near = lane == slot // per_half
-            for other, out in ((0, keep), (1, swap)):
-                mask = near & (step % 2 == other)
-                pltpu.store(out.at[step // 2, to_rows, :], piece, mask=mask)
+        for at in range(rows.size // UNIT):
+            unit = rows.start // UNIT + at
+            to_rows = pl.ds(pl.multiple_of(place_row[unit], UNIT), UNIT)
+            piece = value[at * UNIT : (at + 1) * UNIT]
+            kind = place_kind[unit]
+            pltpu.store(keep.at[to_rows, :], piece, mask=lane == kind)
+            pltpu.store(swap.at[to_rows, :], piece, mask=lane + 2 == kind)
+
+
+def plan_kernel(n_row, group_rows, capacity, first, owners, skel, plan):
+    plan_leaves(n_row, group_rows, capacity, first, owners, skel, plan)
 
 
 def vmem(count=None):
@@ -263,79 +235,77 @@
     return pl.CostEstimate(flops=flops, bytes_accessed=flops // samples, transcendentals=0)
 
 
-def own_product(frontal, own, leaf_first, leaf_owner, skeleton, n_row, n_col):
+def bring(frontal, leaf_first, leaf_owner, depth, n_row, n_col):
     group_rows, width = frontal.shape
     leaves = leaf_first.shape[0]
-    samples, depth = own.shape
+    units = jax.ShapeDtypeStruct((group_rows // UNIT,), jnp.int32)
+    block = jax.ShapeDtypeStruct((group_rows, depth), frontal.dtype)
     return pl.pallas_call(
-        functools.partial(own_kernel, n_row, n_col),
-        in_specs=[hbm()] * 5,
-        out_specs=vmem(2) + [smem()] * 3,
-        out_shape=[
-            jax.ShapeDtypeStruct((group_rows, depth), frontal.dtype),
-            jax.ShapeDtypeStruct((group_rows, 2 * samples), jnp.float32),
-            jax.ShapeDtypeStruct((group_rows // UNIT,), jnp.int32),
-            jax.ShapeDtypeStruct((PICKS + LEAF_MOST * skeleton.shape[0],), jnp.int32),
-            jax.ShapeDtypeStruct((leaves // n_row,), jnp.int32),
-        ],
+        functools.partial(bring_kernel, n_row, n_col),
+        in_specs=[hbm()] * 3,
+        out_specs=vmem(n_row - 1) + [smem()] * 3,
+        out_shape=[block] * (n_row - 1)
+        + [units, units, jax.ShapeDtypeStruct((leaves // n_row,), jnp.int32)],
         scratch_shapes=[
             pltpu.SMEM((leaves,), jnp.int32),
             pltpu.SMEM((leaves,), jnp.int32),
-            pltpu.SMEM(skeleton.shape, jnp.int32),
             pltpu.SMEM((n_col,), jnp.int32),
-            pltpu.VMEM((group_rows, depth), frontal.dtype),
-            pltpu.VMEM(own.shape, own.dtype),
-            pltpu.SemaphoreType.DMA((6,)),
+            pltpu.SemaphoreType.DMA((1 + n_row,)),
         ],
-        cost_estimate=product_cost(frontal, samples, 2),
+        cost_estimate=product_cost(frontal, 64, 4),
         compiler_params=pltpu.CompilerParams(vmem_limit_bytes=24 * 2**20),
-    )(*(in_hbm(x) for x in (leaf_first, leaf_owner, skeleton, frontal, own)))
-
-
-def near_product(frontal, block_one, begun, edges, one, two):
+    )(*(in_hbm(x) for x in (leaf_first, leaf_owner, frontal)))
+
+
+def near_product(frontal, own, edges, blocks, one, two):
     group_rows, width = frontal.shape
-    block = jax.ShapeDtypeStruct(block_one.shape, frontal.dtype)
+    samples = own.shape[0]
     return pl.pallas_call(
         near_kernel,
-        in_specs=[smem(), hbm()] + vmem(4),
-        out_specs=vmem(3),
-        out_shape=[block, block, jax.ShapeDtypeStruct(begun.shape, jnp.float32)],
-        scratch_shapes=[pltpu.SemaphoreType.DMA((2,))],
-        cost_estimate=product_cost(frontal, one.shape[0], 2),
+        in_specs=[smem(), hbm(), hbm()] + vmem(len(blocks) + 2),
+        out_specs=vmem(2),
+        out_shape=[
+            jax.ShapeDtypeStruct(blocks[0].shape, frontal.dtype),
+            jax.ShapeDtypeStruct((group_rows, 2 * samples), jnp.float32),
+        ],
+        scratch_shapes=[pltpu.VMEM(own.shape, own.dtype), pltpu.SemaphoreType.DMA((2,))],
+        cost_estimate=product_cost(frontal, samples, 4),
         compiler_params=pltpu.CompilerParams(vmem_limit_bytes=24 * 2**20),
-    )(edges, in_hbm(frontal), block_one, begun, one, two)
-
-
-def middle_product(block_one, block_two, begun, one, two):
+    )(edges, in_hbm(frontal), in_hbm(own), *blocks, one, two)
+
+
+def plan_of(leaf_first, leaf_owner, skeleton, group_rows, n_row, n_col):
+    size = PICKS + LEAF_MOST * skeleton.shape[0]
     return pl.pallas_call(
-        middle_kernel,
-        in_specs=vmem(5),
-        out_specs=vmem(),
-        out_shape=jax.ShapeDtypeStruct(begun.shape, jnp.float32),
-        cost_estimate=product_cost(block_one, one.shape[0], 4),
-        compiler_params=pltpu.CompilerParams(vmem_limit_bytes=24 * 2**20),
-    )(block_one, block_two, begun, one, two)
-
-
-def last_product(frontal, begun, target, slab, n_col):
+        functools.partial(plan_kernel, n_row, group_rows, 2 * group_rows // n_col),
+        in_specs=[smem()] * 3,
+        out_specs=smem(),
+        out_shape=jax.ShapeDtypeStruct((size,), jnp.int32),
+        cost_estimate=pl.CostEstimate(flops=10**6, bytes_accessed=2**20, transcendentals=0),
+    )(leaf_first, leaf_owner, skeleton)
+
+
+def last_product(block, begun, places, last, n_col):
     group_rows, wide = begun.shape
-    block = jax.ShapeDtypeStruct((n_col // 2, group_rows // n_col, wide), jnp.float32)
+    laid = jax.ShapeDtypeStruct((group_rows // 2, wide), jnp.float32)
     return pl.pallas_call(
         last_kernel,
-        in_specs=[smem()] + vmem(2 + len(slab)),
+        in_specs=[smem()] * 2 + vmem(4),
         out_specs=vmem(2),
-        out_shape=[block, block],
-        cost_estimate=product_cost(frontal, wide // 2, 4),
+        out_shape=[laid, laid],
+        cost_estimate=product_cost(block, wide // 2, 4),
         compiler_params=pltpu.CompilerParams(vmem_limit_bytes=24 * 2**20),
-    )(target, frontal, begun, *slab)
+    )(*places, block, begun, *last)
 
 
 def squeeze_kernel(keep, swapped, here, *away):
-    samples = keep.shape[2] // 2
-    here[...] = (keep[0] + swapped[0]).T
-    row = lax.broadcasted_iota(jnp.int32, (EXTRA, keep.shape[1]), 0)
+    wide, half = here.shape
+    samples = wide // 2
+    here[...] = (keep[:half] + swapped[:half]).T
+    row = lax.broadcasted_iota(jnp.int32, (EXTRA, half), 0)
     for k, out in enumerate(away):
-        block = (keep[k + 1] + swapped[k + 1]).T
+        at = pl.ds((k + 1) * half, half)
+        block = (keep[at, :] + swapped[at, :]).T
         tail = jnp.zeros(row.shape, jnp.float32)
         for side in range(2):
             rows = slice(side * samples, (side + 1) * samples)
@@ -349,8 +319,9 @@
         out[pl.ds(2 * samples, EXTRA), :] = tail.astype(jnp.int32).astype(jnp.int16)
 
 
-def squeeze(keep, swapped):
-    chips, half, wide = keep.shape
+def squeeze(keep, swapped, chips):
+    rows, wide = keep.shape
+    half = rows // chips
     small = jax.ShapeDtypeStruct((wide + EXTRA, half), jnp.int16)
     return pl.pallas_call(
         squeeze_kernel,
@@ -526,26 +497,22 @@
     n_col = lax.axis_size("col")
     n_row = lax.axis_size("row")
     own = sample_cols.T
-    cut = own.shape[1] // 2 // LANES * LANES
-    left, right = own[:, :cut], own[:, cut:]
-    one_right = exchange(right, "row", 1)
-    two_left = exchange(left, "row", 2)
-    block_one, begun, target, plan, edges = own_product(
-        frontal, own, leaf_first, leaf_owner, skeleton.T, n_row, n_col
+    group_rows = frontal.shape[0]
+    depth = own.shape[1]
+    cut = depth // 2 // LANES * LANES
+    one = exchange(own, "row", 1)
+    two = exchange(own, "row", 2)
+    *blocks, place_row, place_kind, edges = bring(
+        frontal, leaf_first, leaf_owner, depth, n_row, n_col
     )
-    left, right, one_right, two_left, edges = lax.optimization_barrier(
-        (left, right, one_right, two_left, edges)
-    )
-    one_left = exchange(left, "row", 1)
-    two_right = exchange(right, "row", 2)
-    last = [exchange(two_left, "row", 1), exchange(one_right, "row", 2)]
-    block_two, block_last, begun = near_product(
-        frontal, block_one, begun, edges, one_right, two_left
-    )
-    begun = middle_product(block_one, block_two, begun, one_left, two_right)
-    keep, swap = last_product(block_last, begun, target, last, n_col)
+    one, two, edges = lax.optimization_barrier((one, two, edges))
+    last = [exchange(two[:, :cut], "row", 1), exchange(one[:, cut:], "row", 2)]
+    block_last, begun = near_product(frontal, own, edges, blocks, one, two)
+    keep, swap = last_product(block_last, begun, (place_row, place_kind), last, n_col)
+    swap, leaf_first = lax.optimization_barrier((swap, leaf_first))
     swapped = exchange(swap, "col", 1)
-    here, *away = squeeze(keep, swapped)
+    plan = plan_of(leaf_first, leaf_owner, skeleton.T, group_rows, n_row, n_col)
+    here, *away = squeeze(keep, swapped, n_col // 2)
     parts = [exchange(away[k - 1], "col", 2 * k) for k in range(n_col // 2 - 1, 0, -1)]
     mine, coeff, worst = leaf_work(here, parts, plan)
     worst = largest(worst, ("row", "col"))

time: 44.8 us -> 43.3 us (0.967)
  starting transfers between devices: 13.2 us -> 11 us
  waiting for transfers between devices: 4.16 us -> 2.59 us
  blocking collectives: 9.14 us -> 10.5 us
  Pallas kernels: 15.9 us -> 17 us
    ppermute x10 -> x8, starting transfers between devices: 13.2 us -> 11 us  [exchange(): return lax.ppermute(value, axis, pairs)]
    ppermute x10 -> x8, waiting for transfers between devices: 4.16 us -> 2.59 us  [exchange(): return lax.ppermute(value, axis, pairs)]
    all_to_all x1, blocking collectives: 9.14 us -> 10.5 us  [largest(): return jnp.max(lax.all_to_all(every, axis, 0, 0), axis=0)]
    pallas_call x4, Pallas kernels: 13.6 us -> 14.7 us  [the longest x1 5.4 us: near_product(): pl.pallas_call(near_kernel, in_specs=[smem(), hbm(), hbm()] + vmem(len(bl...]
    slice x1 -> x2, local copies, waits for them, and re-layouts: 0.96 us -> 0.02 us  [local(): last = [exchange(two[:, :cut], 'row', 1), exchange(one[:, cut:], 'row', 2)]]
    unnamed x0 -> x2, local copies, waits for them, and re-layouts: none -> 0.66 us
  transfers between devices with their start and end apart: 10 -> 8, of which waited for: 4 -> 2; matrix products, arithmetic and copies ran while one was open for 0% -> 0% of each run, Pallas kernels for 26% -> 31%
where the time goes in v8:
time: 43.3 us; the launch traced here: 43 us
  Pallas kernels  17 us (39%)
  starting transfers between devices  11 us (25%)
  blocking collectives  10.5 us (24%)
  waiting for transfers between devices  2.59 us (6%)
  between operations  0.75 us (2%)
  local copies, waits for them, and re-layouts  0.68 us (2%)
  other arithmetic  0.53 us (1%)
    ppermute x8, starting transfers between devices, exchange(): return lax.ppermute(value, axis, pairs)  11 us
    all_to_all x1, blocking collectives, largest(): return jnp.max(lax.all_to_all(every, axis, 0, 0), axis=0)  10.5 us
    pallas_call x1, Pallas kernels, near_product(): pl.pallas_call(near_kernel, in_specs=[smem(), hbm(), hbm()] + vmem(len(bl...  5.4 us
    pallas_call x1, Pallas kernels, bring(): pl.pallas_call(functools.partial(bring_kernel, n_row, n_col), in_specs=[h...  5.13 us
    pallas_call x1, Pallas kernels, plan_of(): pl.pallas_call(functools.partial(plan_kernel, n_row, group_rows, 2 * grou...  2.63 us
    ppermute x8, waiting for transfers between devices, exchange(): return lax.ppermute(value, axis, pairs)  2.59 us
    pallas_call x1, Pallas kernels, leaf_work(): pl.pallas_call(functools.partial(leaf_kernel, skel), in_specs=[smem()] +...  2.12 us
    pallas_call x1, Pallas kernels, last_product(): pl.pallas_call(last_kernel, in_specs=[smem()] * 2 + vmem(4), out_specs=vm...  1.52 us
  transfers between devices with their start and end apart: 8, of which 2 were waited for; matrix products, arithmetic and copies ran while one was open for 0% of the time, Pallas kernels for 31%

profile of v8, /device:TPU:0, one launch (start us, length us, event | category | flops | bytes accessed | tf_op | source)
XLA Modules:
  0.0 43.0 jit_solution(17435932819187423905)
XLA Ops:
  0.6 3.0 %collective-permute-start.1 = (bf16[64,1536]{1,0:T(8,128)(2,1)}, bf16[64,1536]{1,0:T(8,128)(2,1)S(1)}, u32[]{:S(2)}, u32[]{:S(2)}) collective-permute-start(bf16[64,1536]{1,0:T(8,128)(2,1)} %bitcast.8), channel_id=1, source_target_pairs={{0,16},{8,24},{16,0},{24,8},{1,17},{9,25},{17,1},{25,9},{2,18},{10... | collective-permute-start | bytes 589832 | tf_op jit(solution)/shard_map/ppermute | solution.py:487
  3.7 1.5 %collective-permute-start = (bf16[64,1536]{1,0:T(8,128)(2,1)}, bf16[64,1536]{1,0:T(8,128)(2,1)S(1)}, u32[]{:S(2)}, u32[]{:S(2)}) collective-permute-start(bf16[64,1536]{1,0:T(8,128)(2,1)} %bitcast.9), channel_id=1, source_target_pairs={{0,8},{8,0},{16,24},{24,16},{1,9},{9,1},{17,25},{25,17},{2,10},{10... | collective-permute-start | bytes 589832 | tf_op jit(solution)/shard_map/ppermute | solution.py:487
  5.2 5.1 %shard_map.76 = (bf16[1024,1536]{1,0:T(8,128)(2,1)S(1)}, bf16[1024,1536]{1,0:T(8,128)(2,1)S(1)}, bf16[1024,1536]{1,0:T(8,128)(2,1)S(1)}, s32[32]{0:T(128)S(1)}, s32[32]{0:T(128)S(1)}, /*index=5*/s32[16]{0:T(128)S(1)}) custom-call(s32[64]{0:T(128)} %first, s32[64]{0:T(128)} %owners.1, bf16[1024,6144]{1,0:T(8,128)(2,1)} %frontal.3), custom_call_target="tpu_custom_call" | custom-call | flops 3221225472 | bytes 50331648 | tf_op jit(solution)/shard_map/pallas_call | solution.py:243
  10.3 0.0 collective-permute-done.1.refs_4_
  10.3 0.0 collective-permute-done.refs_3_
  10.3 0.4 %collective-permute-start.3 = (bf16[64,768]{1,0:T(8,128)(2,1)S(1)}, bf16[64,768]{1,0:T(8,128)(2,1)S(1)}, u32[]{:S(2)}, u32[]{:S(2)}) collective-permute-start(bf16[64,768]{1,0:T(8,128)(2,1)S(1)} %slice.10), channel_id=1, source_target_pairs={{0,16},{8,24},{16,0},{24,8},{1,17},{9,25},{17,1},{25,9},{2,18},{10... | collective-permute-start | bytes 294920 | tf_op jit(solution)/shard_map/ppermute | solution.py:487
  10.8 1.5 %collective-permute-start.2 = (bf16[64,768]{1,0:T(8,128)(2,1)S(1)}, bf16[64,768]{1,0:T(8,128)(2,1)S(1)}, u32[]{:S(2)}, u32[]{:S(2)}) collective-permute-start(bf16[64,768]{1,0:T(8,128)(2,1)S(1)} %slice.9), channel_id=1, source_target_pairs={{0,8},{8,0},{16,24},{24,16},{1,9},{9,1},{17,25},{25,17},{2,10},{10... | collective-permute-start | bytes 294920 | tf_op jit(solution)/shard_map/ppermute | solution.py:487
  12.3 5.4 %shard_map.77 = (bf16[1024,1536]{1,0:T(8,128)(2,1)S(1)}, f32[1024,128]{1,0:T(8,128)S(1)}) custom-call(s32[16]{0:T(128)S(1)} %get-tuple-element.28.edges, bf16[1024,6144]{1,0:T(8,128)(2,1)} %frontal.3, bf16[64,1536]{1,0:T(8,128)(2,1)} %bitcast.10, bf16[1024,1536]{1,0:T(8,128)(2,1)S(1)} %get-tuple-element.29.refs_0_, ...), custom_call_target="tpu_custom_call" | custom-call | flops 3221225472 | bytes 50331648 | tf_op jit(solution)/shard_map/pallas_call | solution.py:263
  17.7 0.0 collective-permute-done.3.right
  17.7 0.0 collective-permute-done.2.left
  17.8 1.5 %shard_map.78 = (f32[512,128]{1,0:T(8,128)S(1)}, f32[512,128]{1,0:T(8,128)S(1)}) custom-call(s32[32]{0:T(128)S(1)} %get-tuple-element.25.place_row, s32[32]{0:T(128)S(1)} %get-tuple-element.26.place_kind, bf16[1024,1536]{1,0:T(8,128)(2,1)S(1)} %get-tuple-element.34.block, f32[1024,128]{1,0:T(8,128)S(1)} %get-tuple-element.35.begun, ...), custom_call_target="tpu_custom_call" | custom-call | flops 805306368 | bytes 12582912 | tf_op jit(solution)/shard_map/pallas_call | solution.py:291
  19.3 0.1 collective-permute-start.4
  19.4 1.5 %collective-permute-done.4.swapped = f32[512,128]{1,0:T(8,128)S(1)} collective-permute-done((f32[512,128]{1,0:T(8,128)S(1)}, f32[512,128]{1,0:T(8,128)S(1)}, u32[]{:S(2)}, u32[]{:S(2)}) %collective-permute-start.4) | collective-permute-done | bytes 262176 | tf_op jit(solution)/shard_map/ppermute | solution.py:487
  20.9 0.2 shard_map.80
  21.1 3.3 %collective-permute-start.5 = (s16[144,128]{1,0:T(8,128)(2,1)S(1)}, s16[144,128]{1,0:T(8,128)(2,1)S(1)}, u32[]{:S(2)}, u32[]{:S(2)}) collective-permute-start(s16[144,128]{1,0:T(8,128)(2,1)S(1)} %get-tuple-element.41), channel_id=1, source_target_pairs={{0,6},{1,7},{2,4},{3,5},{4,2},{5,3},{6,0},{7,1},{8,14},{9,15},{10,... | collective-permute-start | bytes 110600 | tf_op jit(solution)/shard_map/ppermute | solution.py:487
  24.4 0.0 collective-permute-start.6
  24.4 1.2 %collective-permute-start.7 = (s16[144,128]{1,0:T(8,128)(2,1)S(1)}, s16[144,128]{1,0:T(8,128)(2,1)S(1)}, u32[]{:S(2)}, u32[]{:S(2)}) collective-permute-start(s16[144,128]{1,0:T(8,128)(2,1)S(1)} %get-tuple-element.43), channel_id=1, source_target_pairs={{0,2},{1,3},{2,0},{3,1},{4,6},{5,7},{6,4},{7,5},{8,10},{9,11},{10,... | collective-permute-start | bytes 110600 | tf_op jit(solution)/shard_map/ppermute | solution.py:487
  25.5 2.6 %shard_map.79.plan = s32[72]{0:T(128)} custom-call(s32[64]{0:T(128)} %first, s32[64]{0:T(128)} %owners.1, s32[16,64]{1,0:T(8,128)} %bitcast.12), custom_call_target="tpu_custom_call" | custom-call | flops 1000000 | bytes 1048576 | tf_op jit(solution)/shard_map/pallas_call | solution.py:279
  28.2 0.0 collective-permute-done.5.refs_1_
  28.2 1.1 %collective-permute-done.6.refs_2_ = s16[144,128]{1,0:T(8,128)(2,1)S(1)} collective-permute-done((s16[144,128]{1,0:T(8,128)(2,1)S(1)}, s16[144,128]{1,0:T(8,128)(2,1)S(1)}, u32[]{:S(2)}, u32[]{:S(2)}) %collective-permute-start.6) | collective-permute-done | bytes 36896 | tf_op jit(solution)/shard_map/ppermute | solution.py:487
  29.2 0.0 collective-permute-done.7.refs_3_
  29.2 0.0 copy-start
  29.2 0.7 %copy-done = s32[72]{0:T(128)S(1)} copy-done((s32[72]{0:T(128)S(1)}, s32[72]{0:T(128)}, u32[]{:S(2)}) %copy-start) | copy-done | bytes 312
  29.9 2.1 %shard_map.81 = (f32[64,256]{1,0:T(8,128)}, f32[16,256]{1,0:T(8,128)}, f32[1,128]{1,0:T(1,128)S(1)}) custom-call(s32[72]{0:T(128)S(1)} %copy-done, f32[128,128]{1,0:T(8,128)S(1)} %get-tuple-element.40.refs_0_, s16[144,128]{1,0:T(8,128)(2,1)S(1)} %collective-permute-done.5.refs_1_, s16[144,128]{1,0:T(8,128)(2,1)S(1)} %collective-permute-done.6.refs_2_, ...), custom_call_target="tpu_custom_call" | custom-call | tf_op jit(solution)/shard_map/pallas_call | solution.py:465
  32.0 10.5 %all_to_all.5 = f32[32,1,128]{2,1,0:T(1,128)S(1)} all-to-all(f32[32,1,128]{2,1,0:T(1,128)S(1)} %broadcast_in_dim.9), channel_id=1, replica_groups=mesh['row'=4,'col'=8] {'row','col'}, dimensions={0} | all-to-all | bytes 32768 | tf_op jit(solution)/shard_map/all_to_all | solution.py:493
  42.5 0.5 %reduce_max.11 = f32[128]{0:T(128)} reduce(f32[32,1,128]{2,0,1:T(8,128)S(1)} %bitcast.11, f32[]{:T(128)} %constant.0.clone.1), dimensions={0,1}, to_apply=%region_0.0 | reduce | flops 3968 | bytes 16900 | tf_op jit(solution)/shard_map/reduce_max | solution.py:493
  (3 shorter events, 0.0 us)
Async XLA Ops:
  0.6 9.7 %collective-permute-start.1 = (bf16[64,1536]{1,0:T(8,128)(2,1)}, bf16[64,1536]{1,0:T(8,128)(2,1)S(1)}, u32[]{:S(2)}, u32[]{:S(2)}) collective-permute-start(bf16[64,1536]{1,0:T(8,128)(2,1)} %bitcast.8), channel_id=1, source_target_pairs={{0,16},{8,24},{16,0},{24,8},{1,17},{9,25},{17,1},{25,9},{2,18},{10... | collective-permute-start | bytes 589832 | tf_op jit(solution)/shard_map/ppermute | solution.py:487
  3.7 6.6 %collective-permute-start = (bf16[64,1536]{1,0:T(8,128)(2,1)}, bf16[64,1536]{1,0:T(8,128)(2,1)S(1)}, u32[]{:S(2)}, u32[]{:S(2)}) collective-permute-start(bf16[64,1536]{1,0:T(8,128)(2,1)} %bitcast.9), channel_id=1, source_target_pairs={{0,8},{8,0},{16,24},{24,16},{1,9},{9,1},{17,25},{25,17},{2,10},{10... | collective-permute-start | bytes 589832 | tf_op jit(solution)/shard_map/ppermute | solution.py:487
  10.3 7.4 %collective-permute-start.3 = (bf16[64,768]{1,0:T(8,128)(2,1)S(1)}, bf16[64,768]{1,0:T(8,128)(2,1)S(1)}, u32[]{:S(2)}, u32[]{:S(2)}) collective-permute-start(bf16[64,768]{1,0:T(8,128)(2,1)S(1)} %slice.10), channel_id=1, source_target_pairs={{0,16},{8,24},{16,0},{24,8},{1,17},{9,25},{17,1},{25,9},{2,18},{10... | collective-permute-start | bytes 294920 | tf_op jit(solution)/shard_map/ppermute | solution.py:487
  10.8 7.0 %collective-permute-start.2 = (bf16[64,768]{1,0:T(8,128)(2,1)S(1)}, bf16[64,768]{1,0:T(8,128)(2,1)S(1)}, u32[]{:S(2)}, u32[]{:S(2)}) collective-permute-start(bf16[64,768]{1,0:T(8,128)(2,1)S(1)} %slice.9), channel_id=1, source_target_pairs={{0,8},{8,0},{16,24},{24,16},{1,9},{9,1},{17,25},{25,17},{2,10},{10... | collective-permute-start | bytes 294920 | tf_op jit(solution)/shard_map/ppermute | solution.py:487
  19.3 1.6 %collective-permute-start.4 = (f32[512,128]{1,0:T(8,128)S(1)}, f32[512,128]{1,0:T(8,128)S(1)}, u32[]{:S(2)}, u32[]{:S(2)}) collective-permute-start(f32[512,128]{1,0:T(8,128)S(1)} %get-tuple-element.39), channel_id=1, source_target_pairs={{0,1},{1,0},{2,3},{3,2},{4,5},{5,4},{6,7},{7,6},{8,9},{9,8},{10,11... | collective-permute-start | bytes 786440 | tf_op jit(solution)/shard_map/ppermute | solution.py:487
  21.1 7.1 %collective-permute-start.5 = (s16[144,128]{1,0:T(8,128)(2,1)S(1)}, s16[144,128]{1,0:T(8,128)(2,1)S(1)}, u32[]{:S(2)}, u32[]{:S(2)}) collective-permute-start(s16[144,128]{1,0:T(8,128)(2,1)S(1)} %get-tuple-element.41), channel_id=1, source_target_pairs={{0,6},{1,7},{2,4},{3,5},{4,2},{5,3},{6,0},{7,1},{8,14},{9,15},{10,... | collective-permute-start | bytes 110600 | tf_op jit(solution)/shard_map/ppermute | solution.py:487
  24.4 4.9 %collective-permute-start.6 = (s16[144,128]{1,0:T(8,128)(2,1)S(1)}, s16[144,128]{1,0:T(8,128)(2,1)S(1)}, u32[]{:S(2)}, u32[]{:S(2)}) collective-permute-start(s16[144,128]{1,0:T(8,128)(2,1)S(1)} %get-tuple-element.42), channel_id=1, source_target_pairs={{0,4},{1,5},{2,6},{3,7},{4,0},{5,1},{6,2},{7,3},{8,12},{9,13},{10,... | collective-permute-start | bytes 110600 | tf_op jit(solution)/shard_map/ppermute | solution.py:487
  24.4 4.9 %collective-permute-start.7 = (s16[144,128]{1,0:T(8,128)(2,1)S(1)}, s16[144,128]{1,0:T(8,128)(2,1)S(1)}, u32[]{:S(2)}, u32[]{:S(2)}) collective-permute-start(s16[144,128]{1,0:T(8,128)(2,1)S(1)} %get-tuple-element.43), channel_id=1, source_target_pairs={{0,2},{1,3},{2,0},{3,1},{4,6},{5,7},{6,4},{7,5},{8,10},{9,11},{10,... | collective-permute-start | bytes 110600 | tf_op jit(solution)/shard_map/ppermute | solution.py:487
  29.2 0.7 %copy-start = (s32[72]{0:T(128)S(1)}, s32[72]{0:T(128)}, u32[]{:S(2)}) copy-start(s32[72]{0:T(128)} %shard_map.79.plan) | copy-start | bytes 868

commit v9 on v8

--- a/solution.py
+++ b/solution.py
@@ -11,6 +11,7 @@
 LANES = 128
 LEAF_MOST = 4
 PICKS = 8
+COPIES = 4
 LEVELS = 32760.0
 EXTRA = 16
 PART = 1024
@@ -76,10 +77,16 @@
     leaf_blocks(run_rows, width, edges, act)
 
 
-def bring_block(frontal, turn, block, sem):
-    depth = block.shape[1]
+def bring_block(frontal, turn, block, sems):
+    group_rows, depth = block.shape
     begin = pl.multiple_of((lax.axis_index("row") ^ turn) * depth, LANES)
-    return pltpu.make_async_copy(frontal.at[:, pl.ds(begin, depth)], block, sem)
+    part = group_rows // COPIES
+    copies = []
+    for at in range(COPIES):
+        rows = pl.ds(at * part, part)
+        piece = frontal.at[rows, pl.ds(begin, depth)]
+        copies.append(pltpu.make_async_copy(piece, block.at[rows, :], sems.at[at]))
+    return copies
 
 
 def parts_of(group_rows):
@@ -120,8 +127,8 @@
     plan[LEAF_MOST] = count
 
 
-def bring_kernel(n_row, n_col, leaf_first, leaf_owner, frontal, *refs):
-    *blocks, place_row, place_kind, edges, first, owners, used, sems = refs
+def bring_kernel(n_row, n_col, leaf_first, leaf_owner, skeleton, frontal, *refs):
+    *blocks, place_row, place_kind, plan, edges, first, owners, skel, used, sems, block_sems = refs
     group_rows, width = frontal.shape
     leaves = leaf_first.shape[0]
     per_group = leaves // n_row
@@ -133,9 +140,10 @@
     copies = [
         pltpu.make_async_copy(leaf_first, first, sems.at[0]),
         pltpu.make_async_copy(leaf_owner, owners, sems.at[1]),
+        pltpu.make_async_copy(skeleton, skel, sems.at[2]),
     ]
     for turn, block in enumerate(blocks):
-        copies.append(bring_block(frontal, turn, block, sems.at[2 + turn]))
+        copies.extend(bring_block(frontal, turn, block, block_sems.at[turn]))
     for copy in copies:
         copy.start()
 
@@ -144,7 +152,7 @@
         return carry
 
     lax.fori_loop(0, n_col, clear, 0)
-    for copy in copies[:2]:
+    for copy in copies[:3]:
         copy.wait()
 
     def edge(at, carry):
@@ -167,27 +175,27 @@
         return leaf
 
     lax.fori_loop(0, group_rows // UNIT, place, row_pos * per_group)
-    for copy in copies[2:]:
+    plan_leaves(n_row, group_rows, 2 * half, first, owners, skel, plan)
+    for copy in copies[3:]:
         copy.wait()
     clear_runs(run_rows, width, edges, range(len(blocks)), blocks)
 
 
 def near_kernel(edges, frontal, own, *refs):
-    *blocks, one, two, block_last, total, near, sems = refs
+    *blocks, one, two, block_last, total, near, sem, sems = refs
     group_rows, width = frontal.shape
     run_rows = group_rows // (edges.shape[0] // RUN_LEAVES)
-    copies = [
-        pltpu.make_async_copy(own, near, sems.at[0]),
-        bring_block(frontal, len(blocks), block_last, sems.at[1]),
-    ]
-    for copy in copies:
+    own_copy = pltpu.make_async_copy(own, near, sem)
+    copies = bring_block(frontal, len(blocks), block_last, sems)
+    for copy in [own_copy, *copies]:
         copy.start()
     for rows in parts_of(group_rows):
         total[rows, :] = multiply([(blocks[1], 0, one), (blocks[2], 0, two)], None, rows)
-    copies[0].wait()
+    own_copy.wait()
     for rows in parts_of(group_rows):
         total[rows, :] = multiply([(blocks[0], 0, near)], total[rows, :], rows)
-    copies[1].wait()
+    for copy in copies:
+        copy.wait()
     clear_runs(run_rows, width, edges, [len(blocks)], [block_last])
 
 
@@ -208,10 +216,6 @@
             pltpu.store(swap.at[to_rows, :], piece, mask=lane + 2 == kind)
 
 
-def plan_kernel(n_row, group_rows, capacity, first, owners, skel, plan):
-    plan_leaves(n_row, group_rows, capacity, first, owners, skel, plan)
-
-
 def vmem(count=None):
     spec = pl.BlockSpec(memory_space=pltpu.VMEM)
     return spec if count is None else [spec] * count
@@ -235,26 +239,33 @@
     return pl.CostEstimate(flops=flops, bytes_accessed=flops // samples, transcendentals=0)
 
 
-def bring(frontal, leaf_first, leaf_owner, depth, n_row, n_col):
+def bring(frontal, leaf_first, leaf_owner, skeleton, depth, n_row, n_col):
     group_rows, width = frontal.shape
     leaves = leaf_first.shape[0]
     units = jax.ShapeDtypeStruct((group_rows // UNIT,), jnp.int32)
     block = jax.ShapeDtypeStruct((group_rows, depth), frontal.dtype)
     return pl.pallas_call(
         functools.partial(bring_kernel, n_row, n_col),
-        in_specs=[hbm()] * 3,
-        out_specs=vmem(n_row - 1) + [smem()] * 3,
+        in_specs=[hbm()] * 4,
+        out_specs=vmem(n_row - 1) + [smem()] * 4,
         out_shape=[block] * (n_row - 1)
-        + [units, units, jax.ShapeDtypeStruct((leaves // n_row,), jnp.int32)],
+        + [
+            units,
+            units,
+            jax.ShapeDtypeStruct((PICKS + LEAF_MOST * skeleton.shape[0],), jnp.int32),
+            jax.ShapeDtypeStruct((leaves // n_row,), jnp.int32),
+        ],
         scratch_shapes=[
             pltpu.SMEM((leaves,), jnp.int32),
             pltpu.SMEM((leaves,), jnp.int32),
+            pltpu.SMEM(skeleton.shape, jnp.int32),
             pltpu.SMEM((n_col,), jnp.int32),
-            pltpu.SemaphoreType.DMA((1 + n_row,)),
+            pltpu.SemaphoreType.DMA((3,)),
+            pltpu.SemaphoreType.DMA((n_row - 1, COPIES)),
         ],
         cost_estimate=product_cost(frontal, 64, 4),
         compiler_params=pltpu.CompilerParams(vmem_limit_bytes=24 * 2**20),
-    )(*(in_hbm(x) for x in (leaf_first, leaf_owner, frontal)))
+    )(*(in_hbm(x) for x in (leaf_first, leaf_owner, skeleton, frontal)))
 
 
 def near_product(frontal, own, edges, blocks, one, two):
@@ -268,21 +279,14 @@
             jax.ShapeDtypeStruct(blocks[0].shape, frontal.dtype),
             jax.ShapeDtypeStruct((group_rows, 2 * samples), jnp.float32),
         ],
-        scratch_shapes=[pltpu.VMEM(own.shape, own.dtype), pltpu.SemaphoreType.DMA((2,))],
+        scratch_shapes=[
+            pltpu.VMEM(own.shape, own.dtype),
+            pltpu.SemaphoreType.DMA,
+            pltpu.SemaphoreType.DMA((COPIES,)),
+        ],
         cost_estimate=product_cost(frontal, samples, 4),
         compiler_params=pltpu.CompilerParams(vmem_limit_bytes=24 * 2**20),
     )(edges, in_hbm(frontal), in_hbm(own), *blocks, one, two)
-
-
-def plan_of(leaf_first, leaf_owner, skeleton, group_rows, n_row, n_col):
-    size = PICKS + LEAF_MOST * skeleton.shape[0]
-    return pl.pallas_call(
-        functools.partial(plan_kernel, n_row, group_rows, 2 * group_rows // n_col),
-        in_specs=[smem()] * 3,
-        out_specs=smem(),
-        out_shape=jax.ShapeDtypeStruct((size,), jnp.int32),
-        cost_estimate=pl.CostEstimate(flops=10**6, bytes_accessed=2**20, transcendentals=0),
-    )(leaf_first, leaf_owner, skeleton)
 
 
 def last_product(block, begun, places, last, n_col):
@@ -497,21 +501,18 @@
     n_col = lax.axis_size("col")
     n_row = lax.axis_size("row")
     own = sample_cols.T
-    group_rows = frontal.shape[0]
     depth = own.shape[1]
     cut = depth // 2 // LANES * LANES
     one = exchange(own, "row", 1)
     two = exchange(own, "row", 2)
-    *blocks, place_row, place_kind, edges = bring(
-        frontal, leaf_first, leaf_owner, depth, n_row, n_col
+    *blocks, place_row, place_kind, plan, edges = bring(
+        frontal, leaf_first, leaf_owner, skeleton.T, depth, n_row, n_col
     )
     one, two, edges = lax.optimization_barrier((one, two, edges))
     last = [exchange(two[:, :cut], "row", 1), exchange(one[:, cut:], "row", 2)]
     block_last, begun = near_product(frontal, own, edges, blocks, one, two)
     keep, swap = last_product(block_last, begun, (place_row, place_kind), last, n_col)
-    swap, leaf_first = lax.optimization_barrier((swap, leaf_first))
     swapped = exchange(swap, "col", 1)
-    plan = plan_of(leaf_first, leaf_owner, skeleton.T, group_rows, n_row, n_col)
     here, *away = squeeze(keep, swapped, n_col // 2)
     parts = [exchange(away[k - 1], "col", 2 * k) for k in range(n_col // 2 - 1, 0, -1)]
     mine, coeff, worst = leaf_work(here, parts, plan)

time: 43.3 us -> 42.8 us (0.988)
  waiting for transfers between devices: 2.59 us -> 5.23 us
  Pallas kernels: 17 us -> 14.8 us
  local copies, waits for them, and re-layouts: 0.68 us -> 0.03 us
    ppermute x8, waiting for transfers between devices: 2.59 us -> 5.23 us  [exchange(): return lax.ppermute(value, axis, pairs)]
    pallas_call x1 -> x0, Pallas kernels: 2.63 us -> none  [plan_of(): pl.pallas_call(functools.partial(plan_kernel, n_row, group_rows, 2 * grou...]
    unnamed x2 -> x0, local copies, waits for them, and re-layouts: 0.66 us -> none
  transfers between devices with their start and end apart: 8 -> 8, of which waited for: 2 -> 3; matrix products, arithmetic and copies ran while one was open for 0% -> 0% of each run, Pallas kernels for 31% -> 26%
where the time goes in v9:
time: 42.8 us; the launch traced here: 42.6 us
  Pallas kernels  14.8 us (35%)
  starting transfers between devices  11 us (26%)
  blocking collectives  10.3 us (24%)
  waiting for transfers between devices  5.23 us (12%)
  between operations  0.74 us (2%)
  other arithmetic  0.53 us (1%)
    ppermute x8, starting transfers between devices, exchange(): return lax.ppermute(value, axis, pairs)  11 us
    all_to_all x1, blocking collectives, largest(): return jnp.max(lax.all_to_all(every, axis, 0, 0), axis=0)  10.3 us
    pallas_call x1, Pallas kernels, near_product(): pl.pallas_call(near_kernel, in_specs=[smem(), hbm(), hbm()] + vmem(len(bl...  5.79 us
    ppermute x8, waiting for transfers between devices, exchange(): return lax.ppermute(value, axis, pairs)  5.23 us
    pallas_call x1, Pallas kernels, bring(): pl.pallas_call(functools.partial(bring_kernel, n_row, n_col), in_specs=[h...  5.17 us
    pallas_call x1, Pallas kernels, leaf_work(): pl.pallas_call(functools.partial(leaf_kernel, skel), in_specs=[smem()] +...  2.13 us
    pallas_call x1, Pallas kernels, last_product(): pl.pallas_call(last_kernel, in_specs=[smem()] * 2 + vmem(4), out_specs=vm...  1.52 us
  transfers between devices with their start and end apart: 8, of which 3 were waited for; matrix products, arithmetic and copies ran while one was open for 0% of the time, Pallas kernels for 26%

profile of v9, /device:TPU:0, one launch (start us, length us, event | category | flops | bytes accessed | tf_op | source)
XLA Modules:
  0.0 42.6 jit_solution(16891747633243282920)
XLA Ops:
  0.6 3.0 %collective-permute-start.1 = (bf16[64,1536]{1,0:T(8,128)(2,1)}, bf16[64,1536]{1,0:T(8,128)(2,1)S(1)}, u32[]{:S(2)}, u32[]{:S(2)}) collective-permute-start(bf16[64,1536]{1,0:T(8,128)(2,1)} %bitcast.8), channel_id=1, source_target_pairs={{0,16},{8,24},{16,0},{24,8},{1,17},{9,25},{17,1},{25,9},{2,18},{10... | collective-permute-start | bytes 589832 | tf_op jit(solution)/shard_map/ppermute | solution.py:491
  3.7 1.5 %collective-permute-start = (bf16[64,1536]{1,0:T(8,128)(2,1)}, bf16[64,1536]{1,0:T(8,128)(2,1)S(1)}, u32[]{:S(2)}, u32[]{:S(2)}) collective-permute-start(bf16[64,1536]{1,0:T(8,128)(2,1)} %bitcast.9), channel_id=1, source_target_pairs={{0,8},{8,0},{16,24},{24,16},{1,9},{9,1},{17,25},{25,17},{2,10},{10... | collective-permute-start | bytes 589832 | tf_op jit(solution)/shard_map/ppermute | solution.py:491
  5.2 5.2 %shard_map.76 = (bf16[1024,1536]{1,0:T(8,128)(2,1)S(1)}, bf16[1024,1536]{1,0:T(8,128)(2,1)S(1)}, bf16[1024,1536]{1,0:T(8,128)(2,1)S(1)}, s32[32]{0:T(128)S(1)}, ...) custom-call(s32[64]{0:T(128)} %leaf_first.1, s32[64]{0:T(128)} %leaf_owner.1, s32[16,64]{1,0:T(8,128)} %bitcast.12, ...), custom_call_target="tpu_custom_call" | custom-call | flops 3221225472 | bytes 50331648 | tf_op jit(solution)/shard_map/pallas_call | solution.py:247
  10.3 0.0 collective-permute-done.1.refs_4_
  10.3 0.0 collective-permute-done.refs_3_
  10.4 0.4 %collective-permute-start.3 = (bf16[64,768]{1,0:T(8,128)(2,1)S(1)}, bf16[64,768]{1,0:T(8,128)(2,1)S(1)}, u32[]{:S(2)}, u32[]{:S(2)}) collective-permute-start(bf16[64,768]{1,0:T(8,128)(2,1)S(1)} %slice.10), channel_id=1, source_target_pairs={{0,16},{8,24},{16,0},{24,8},{1,17},{9,25},{17,1},{25,9},{2,18},{10... | collective-permute-start | bytes 294920 | tf_op jit(solution)/shard_map/ppermute | solution.py:491
  10.8 1.5 %collective-permute-start.2 = (bf16[64,768]{1,0:T(8,128)(2,1)S(1)}, bf16[64,768]{1,0:T(8,128)(2,1)S(1)}, u32[]{:S(2)}, u32[]{:S(2)}) collective-permute-start(bf16[64,768]{1,0:T(8,128)(2,1)S(1)} %slice.9), channel_id=1, source_target_pairs={{0,8},{8,0},{16,24},{24,16},{1,9},{9,1},{17,25},{25,17},{2,10},{10... | collective-permute-start | bytes 294920 | tf_op jit(solution)/shard_map/ppermute | solution.py:491
  12.3 5.8 %shard_map.77 = (bf16[1024,1536]{1,0:T(8,128)(2,1)S(1)}, f32[1024,128]{1,0:T(8,128)S(1)}) custom-call(s32[16]{0:T(128)S(1)} %get-tuple-element.28.edges, bf16[1024,6144]{1,0:T(8,128)(2,1)} %frontal.3, bf16[64,1536]{1,0:T(8,128)(2,1)} %bitcast.10, bf16[1024,1536]{1,0:T(8,128)(2,1)S(1)} %get-tuple-element.29.refs_0_, ...), custom_call_target="tpu_custom_call" | custom-call | flops 3221225472 | bytes 50331648 | tf_op jit(solution)/shard_map/pallas_call | solution.py:274
  18.1 0.0 collective-permute-done.3.right
  18.1 0.0 collective-permute-done.2.left
  18.1 1.5 %shard_map.78 = (f32[512,128]{1,0:T(8,128)S(1)}, f32[512,128]{1,0:T(8,128)S(1)}) custom-call(s32[32]{0:T(128)S(1)} %get-tuple-element.25.place_row, s32[32]{0:T(128)S(1)} %get-tuple-element.26.place_kind, bf16[1024,1536]{1,0:T(8,128)(2,1)S(1)} %get-tuple-element.34.block, f32[1024,128]{1,0:T(8,128)S(1)} %get-tuple-element.35.begun, ...), custom_call_target="tpu_custom_call" | custom-call | flops 805306368 | bytes 12582912 | tf_op jit(solution)/shard_map/pallas_call | solution.py:295
  19.7 0.1 collective-permute-start.4
  19.8 1.5 %collective-permute-done.4.swapped = f32[512,128]{1,0:T(8,128)S(1)} collective-permute-done((f32[512,128]{1,0:T(8,128)S(1)}, f32[512,128]{1,0:T(8,128)S(1)}, u32[]{:S(2)}, u32[]{:S(2)}) %collective-permute-start.4) | collective-permute-done | bytes 262176 | tf_op jit(solution)/shard_map/ppermute | solution.py:491
  21.3 0.2 shard_map.79
  21.5 3.3 %collective-permute-start.5 = (s16[144,128]{1,0:T(8,128)(2,1)S(1)}, s16[144,128]{1,0:T(8,128)(2,1)S(1)}, u32[]{:S(2)}, u32[]{:S(2)}) collective-permute-start(s16[144,128]{1,0:T(8,128)(2,1)S(1)} %get-tuple-element.39), channel_id=1, source_target_pairs={{0,6},{1,7},{2,4},{3,5},{4,2},{5,3},{6,0},{7,1},{8,14},{9,15},{10,... | collective-permute-start | bytes 110600 | tf_op jit(solution)/shard_map/ppermute | solution.py:491
  24.8 0.0 collective-permute-start.6
  24.8 1.2 %collective-permute-start.7 = (s16[144,128]{1,0:T(8,128)(2,1)S(1)}, s16[144,128]{1,0:T(8,128)(2,1)S(1)}, u32[]{:S(2)}, u32[]{:S(2)}) collective-permute-start(s16[144,128]{1,0:T(8,128)(2,1)S(1)} %get-tuple-element.41), channel_id=1, source_target_pairs={{0,2},{1,3},{2,0},{3,1},{4,6},{5,7},{6,4},{7,5},{8,10},{9,11},{10,... | collective-permute-start | bytes 110600 | tf_op jit(solution)/shard_map/ppermute | solution.py:491
  25.9 1.6 %collective-permute-done.5.refs_1_ = s16[144,128]{1,0:T(8,128)(2,1)S(1)} collective-permute-done((s16[144,128]{1,0:T(8,128)(2,1)S(1)}, s16[144,128]{1,0:T(8,128)(2,1)S(1)}, u32[]{:S(2)}, u32[]{:S(2)}) %collective-permute-start.5) | collective-permute-done | bytes 36896 | tf_op jit(solution)/shard_map/ppermute | solution.py:491
  27.5 2.1 %collective-permute-done.6.refs_2_ = s16[144,128]{1,0:T(8,128)(2,1)S(1)} collective-permute-done((s16[144,128]{1,0:T(8,128)(2,1)S(1)}, s16[144,128]{1,0:T(8,128)(2,1)S(1)}, u32[]{:S(2)}, u32[]{:S(2)}) %collective-permute-start.6) | collective-permute-done | bytes 36896 | tf_op jit(solution)/shard_map/ppermute | solution.py:491
  29.6 0.0 collective-permute-done.7.refs_3_
  29.6 2.1 %shard_map.80 = (f32[64,256]{1,0:T(8,128)}, f32[16,256]{1,0:T(8,128)}, f32[1,128]{1,0:T(1,128)S(1)}) custom-call(s32[72]{0:T(128)S(1)} %get-tuple-element.24.plan, f32[128,128]{1,0:T(8,128)S(1)} %get-tuple-element.38.refs_0_, s16[144,128]{1,0:T(8,128)(2,1)S(1)} %collective-permute-done.5.refs_1_, s16[144,128]{1,0:T(8,128)(2,1)S(1)} %collective-permute-done.6.refs_2_, ...), custom_call_target="tpu_custom_call" | custom-call | tf_op jit(solution)/shard_map/pallas_call | solution.py:469
  31.8 10.3 %all_to_all.5 = f32[32,1,128]{2,1,0:T(1,128)S(1)} all-to-all(f32[32,1,128]{2,1,0:T(1,128)S(1)} %broadcast_in_dim.9), channel_id=1, replica_groups=mesh['row'=4,'col'=8] {'row','col'}, dimensions={0} | all-to-all | bytes 32768 | tf_op jit(solution)/shard_map/all_to_all | solution.py:497
  42.1 0.5 %reduce_max.11 = f32[128]{0:T(128)} reduce(f32[32,1,128]{2,0,1:T(8,128)S(1)} %bitcast.11, f32[]{:T(128)} %constant.0.clone.1), dimensions={0,1}, to_apply=%region_0.0 | reduce | flops 3968 | bytes 16900 | tf_op jit(solution)/shard_map/reduce_max | solution.py:497
  (3 shorter events, 0.0 us)
Async XLA Ops:
  0.6 9.7 %collective-permute-start.1 = (bf16[64,1536]{1,0:T(8,128)(2,1)}, bf16[64,1536]{1,0:T(8,128)(2,1)S(1)}, u32[]{:S(2)}, u32[]{:S(2)}) collective-permute-start(bf16[64,1536]{1,0:T(8,128)(2,1)} %bitcast.8), channel_id=1, source_target_pairs={{0,16},{8,24},{16,0},{24,8},{1,17},{9,25},{17,1},{25,9},{2,18},{10... | collective-permute-start | bytes 589832 | tf_op jit(solution)/shard_map/ppermute | solution.py:491
  3.7 6.7 %collective-permute-start = (bf16[64,1536]{1,0:T(8,128)(2,1)}, bf16[64,1536]{1,0:T(8,128)(2,1)S(1)}, u32[]{:S(2)}, u32[]{:S(2)}) collective-permute-start(bf16[64,1536]{1,0:T(8,128)(2,1)} %bitcast.9), channel_id=1, source_target_pairs={{0,8},{8,0},{16,24},{24,16},{1,9},{9,1},{17,25},{25,17},{2,10},{10... | collective-permute-start | bytes 589832 | tf_op jit(solution)/shard_map/ppermute | solution.py:491
  10.4 7.7 %collective-permute-start.3 = (bf16[64,768]{1,0:T(8,128)(2,1)S(1)}, bf16[64,768]{1,0:T(8,128)(2,1)S(1)}, u32[]{:S(2)}, u32[]{:S(2)}) collective-permute-start(bf16[64,768]{1,0:T(8,128)(2,1)S(1)} %slice.10), channel_id=1, source_target_pairs={{0,16},{8,24},{16,0},{24,8},{1,17},{9,25},{17,1},{25,9},{2,18},{10... | collective-permute-start | bytes 294920 | tf_op jit(solution)/shard_map/ppermute | solution.py:491
  10.8 7.3 %collective-permute-start.2 = (bf16[64,768]{1,0:T(8,128)(2,1)S(1)}, bf16[64,768]{1,0:T(8,128)(2,1)S(1)}, u32[]{:S(2)}, u32[]{:S(2)}) collective-permute-start(bf16[64,768]{1,0:T(8,128)(2,1)S(1)} %slice.9), channel_id=1, source_target_pairs={{0,8},{8,0},{16,24},{24,16},{1,9},{9,1},{17,25},{25,17},{2,10},{10... | collective-permute-start | bytes 294920 | tf_op jit(solution)/shard_map/ppermute | solution.py:491
  19.7 1.6 %collective-permute-start.4 = (f32[512,128]{1,0:T(8,128)S(1)}, f32[512,128]{1,0:T(8,128)S(1)}, u32[]{:S(2)}, u32[]{:S(2)}) collective-permute-start(f32[512,128]{1,0:T(8,128)S(1)} %get-tuple-element.37), channel_id=1, source_target_pairs={{0,1},{1,0},{2,3},{3,2},{4,5},{5,4},{6,7},{7,6},{8,9},{9,8},{10,11... | collective-permute-start | bytes 786440 | tf_op jit(solution)/shard_map/ppermute | solution.py:491
  21.5 6.0 %collective-permute-start.5 = (s16[144,128]{1,0:T(8,128)(2,1)S(1)}, s16[144,128]{1,0:T(8,128)(2,1)S(1)}, u32[]{:S(2)}, u32[]{:S(2)}) collective-permute-start(s16[144,128]{1,0:T(8,128)(2,1)S(1)} %get-tuple-element.39), channel_id=1, source_target_pairs={{0,6},{1,7},{2,4},{3,5},{4,2},{5,3},{6,0},{7,1},{8,14},{9,15},{10,... | collective-permute-start | bytes 110600 | tf_op jit(solution)/shard_map/ppermute | solution.py:491
  24.8 4.9 %collective-permute-start.6 = (s16[144,128]{1,0:T(8,128)(2,1)S(1)}, s16[144,128]{1,0:T(8,128)(2,1)S(1)}, u32[]{:S(2)}, u32[]{:S(2)}) collective-permute-start(s16[144,128]{1,0:T(8,128)(2,1)S(1)} %get-tuple-element.40), channel_id=1, source_target_pairs={{0,4},{1,5},{2,6},{3,7},{4,0},{5,1},{6,2},{7,3},{8,12},{9,13},{10,... | collective-permute-start | bytes 110600 | tf_op jit(solution)/shard_map/ppermute | solution.py:491
  24.8 4.9 %collective-permute-start.7 = (s16[144,128]{1,0:T(8,128)(2,1)S(1)}, s16[144,128]{1,0:T(8,128)(2,1)S(1)}, u32[]{:S(2)}, u32[]{:S(2)}) collective-permute-start(s16[144,128]{1,0:T(8,128)(2,1)S(1)} %get-tuple-element.41), channel_id=1, source_target_pairs={{0,2},{1,3},{2,0},{3,1},{4,6},{5,7},{6,4},{7,5},{8,10},{9,11},{10,... | collective-permute-start | bytes 110600 | tf_op jit(solution)/shard_map/ppermute | solution.py:491

commit v10 on v9

--- a/solution.py
+++ b/solution.py
@@ -11,7 +11,7 @@
 LANES = 128
 LEAF_MOST = 4
 PICKS = 8
-COPIES = 4
+COPIES = 1
 LEVELS = 32760.0
 EXTRA = 16
 PART = 1024
@@ -128,7 +128,7 @@
 
 
 def bring_kernel(n_row, n_col, leaf_first, leaf_owner, skeleton, frontal, *refs):
-    *blocks, place_row, place_kind, plan, edges, first, owners, skel, used, sems, block_sems = refs
+    *blocks, place_row, place_kind, plan, first, owners, skel, edges, used, sems, block_sems = refs
     group_rows, width = frontal.shape
     leaves = leaf_first.shape[0]
     per_group = leaves // n_row
@@ -181,22 +181,16 @@
     clear_runs(run_rows, width, edges, range(len(blocks)), blocks)
 
 
-def near_kernel(edges, frontal, own, *refs):
-    *blocks, one, two, block_last, total, near, sem, sems = refs
-    group_rows, width = frontal.shape
-    run_rows = group_rows // (edges.shape[0] // RUN_LEAVES)
+def near_kernel(own, *refs):
+    *blocks, one, two, total, near, sem = refs
     own_copy = pltpu.make_async_copy(own, near, sem)
-    copies = bring_block(frontal, len(blocks), block_last, sems)
-    for copy in [own_copy, *copies]:
-        copy.start()
-    for rows in parts_of(group_rows):
-        total[rows, :] = multiply([(blocks[1], 0, one), (blocks[2], 0, two)], None, rows)
+    own_copy.start()
+    items = [(blocks[1], 0, one), (blocks[2], 0, two)]
+    for rows in parts_of(total.shape[0]):
+        total[rows, :] = multiply(items, None, rows)
     own_copy.wait()
-    for rows in parts_of(group_rows):
+    for rows in parts_of(total.shape[0]):
         total[rows, :] = multiply([(blocks[0], 0, near)], total[rows, :], rows)
-    for copy in copies:
-        copy.wait()
-    clear_runs(run_rows, width, edges, [len(blocks)], [block_last])
 
 
 def last_kernel(place_row, place_kind, block, begun, left, right, keep, swap):
@@ -247,46 +241,39 @@
     return pl.pallas_call(
         functools.partial(bring_kernel, n_row, n_col),
         in_specs=[hbm()] * 4,
-        out_specs=vmem(n_row - 1) + [smem()] * 4,
-        out_shape=[block] * (n_row - 1)
+        out_specs=vmem(n_row) + [smem()] * 3,
+        out_shape=[block] * n_row
         + [
             units,
             units,
             jax.ShapeDtypeStruct((PICKS + LEAF_MOST * skeleton.shape[0],), jnp.int32),
-            jax.ShapeDtypeStruct((leaves // n_row,), jnp.int32),
         ],
         scratch_shapes=[
             pltpu.SMEM((leaves,), jnp.int32),
             pltpu.SMEM((leaves,), jnp.int32),
             pltpu.SMEM(skeleton.shape, jnp.int32),
+            pltpu.SMEM((leaves // n_row,), jnp.int32),
             pltpu.SMEM((n_col,), jnp.int32),
             pltpu.SemaphoreType.DMA((3,)),
-            pltpu.SemaphoreType.DMA((n_row - 1, COPIES)),
+            pltpu.SemaphoreType.DMA((n_row, COPIES)),
         ],
         cost_estimate=product_cost(frontal, 64, 4),
         compiler_params=pltpu.CompilerParams(vmem_limit_bytes=24 * 2**20),
     )(*(in_hbm(x) for x in (leaf_first, leaf_owner, skeleton, frontal)))
 
 
-def near_product(frontal, own, edges, blocks, one, two):
-    group_rows, width = frontal.shape
+def near_product(own, blocks, one, two):
+    group_rows = blocks[0].shape[0]
     samples = own.shape[0]
     return pl.pallas_call(
         near_kernel,
-        in_specs=[smem(), hbm(), hbm()] + vmem(len(blocks) + 2),
-        out_specs=vmem(2),
-        out_shape=[
-            jax.ShapeDtypeStruct(blocks[0].shape, frontal.dtype),
-            jax.ShapeDtypeStruct((group_rows, 2 * samples), jnp.float32),
-        ],
-        scratch_shapes=[
-            pltpu.VMEM(own.shape, own.dtype),
-            pltpu.SemaphoreType.DMA,
-            pltpu.SemaphoreType.DMA((COPIES,)),
-        ],
-        cost_estimate=product_cost(frontal, samples, 4),
+        in_specs=[hbm()] + vmem(len(blocks) + 2),
+        out_specs=vmem(),
+        out_shape=jax.ShapeDtypeStruct((group_rows, 2 * samples), jnp.float32),
+        scratch_shapes=[pltpu.VMEM(own.shape, own.dtype), pltpu.SemaphoreType.DMA],
+        cost_estimate=product_cost(blocks[0], samples, 12),
         compiler_params=pltpu.CompilerParams(vmem_limit_bytes=24 * 2**20),
-    )(edges, in_hbm(frontal), in_hbm(own), *blocks, one, two)
+    )(in_hbm(own), *blocks, one, two)
 
 
 def last_product(block, begun, places, last, n_col):
@@ -505,12 +492,12 @@
     cut = depth // 2 // LANES * LANES
     one = exchange(own, "row", 1)
     two = exchange(own, "row", 2)
-    *blocks, place_row, place_kind, plan, edges = bring(
+    *blocks, block_last, place_row, place_kind, plan = bring(
         frontal, leaf_first, leaf_owner, skeleton.T, depth, n_row, n_col
     )
-    one, two, edges = lax.optimization_barrier((one, two, edges))
+    one, two, plan = lax.optimization_barrier((one, two, plan))
     last = [exchange(two[:, :cut], "row", 1), exchange(one[:, cut:], "row", 2)]
-    block_last, begun = near_product(frontal, own, edges, blocks, one, two)
+    begun = near_product(own, blocks, one, two)
     keep, swap = last_product(block_last, begun, (place_row, place_kind), last, n_col)
     swapped = exchange(swap, "col", 1)
     here, *away = squeeze(keep, swapped, n_col // 2)

time: 42.8 us -> 42 us (0.981)
  starting transfers between devices: 11 us -> 10.2 us
  Pallas kernels: 14.8 us -> 14.3 us
    pallas_call x1, Pallas kernels: 5.79 us -> 4.35 us  [near_product(): pl.pallas_call(near_kernel, in_specs=[hbm()] + vmem(len(blocks) + 2), out...]
    pallas_call x1, Pallas kernels: 5.17 us -> 6.09 us  [bring(): pl.pallas_call(functools.partial(bring_kernel, n_row, n_col), in_specs=[h...]
    ppermute x8, starting transfers between devices: 11 us -> 10.2 us  [exchange(): return lax.ppermute(value, axis, pairs)]
  transfers between devices with their start and end apart: 8 -> 8, of which waited for: 3 -> 3; matrix products, arithmetic and copies ran while one was open for 0% -> 0% of each run, Pallas kernels for 26% -> 25%
where the time goes in v10:
time: 42 us; the launch traced here: 41.9 us
  Pallas kernels  14.3 us (34%)
  blocking collectives  10.5 us (25%)
  starting transfers between devices  10.2 us (24%)
  waiting for transfers between devices  5.61 us (13%)
  between operations  0.73 us (2%)
  other arithmetic  0.53 us (1%)
    all_to_all x1, blocking collectives, largest(): return jnp.max(lax.all_to_all(every, axis, 0, 0), axis=0)  10.5 us
    ppermute x8, starting transfers between devices, exchange(): return lax.ppermute(value, axis, pairs)  10.2 us
    pallas_call x1, Pallas kernels, bring(): pl.pallas_call(functools.partial(bring_kernel, n_row, n_col), in_specs=[h...  6.09 us
    ppermute x8, waiting for transfers between devices, exchange(): return lax.ppermute(value, axis, pairs)  5.61 us
    pallas_call x1, Pallas kernels, near_product(): pl.pallas_call(near_kernel, in_specs=[hbm()] + vmem(len(blocks) + 2), out...  4.35 us
    pallas_call x1, Pallas kernels, leaf_work(): pl.pallas_call(functools.partial(leaf_kernel, skel), in_specs=[smem()] +...  2.13 us
    pallas_call x1, Pallas kernels, last_product(): pl.pallas_call(last_kernel, in_specs=[smem()] * 2 + vmem(4), out_specs=vm...  1.52 us
  transfers between devices with their start and end apart: 8, of which 3 were waited for; matrix products, arithmetic and copies ran while one was open for 0% of the time, Pallas kernels for 25%

profile of v10, /device:TPU:0, one launch (start us, length us, event | category | flops | bytes accessed | tf_op | source)
XLA Modules:
  0.0 41.9 jit_solution(3423449023500602607)
XLA Ops:
  0.6 3.0 %collective-permute-start = (bf16[64,1536]{1,0:T(8,128)(2,1)}, bf16[64,1536]{1,0:T(8,128)(2,1)S(1)}, u32[]{:S(2)}, u32[]{:S(2)}) collective-permute-start(bf16[64,1536]{1,0:T(8,128)(2,1)} %bitcast.8), channel_id=1, source_target_pairs={{0,8},{8,0},{16,24},{24,16},{1,9},{9,1},{17,25},{25,17},{2,10},{10... | collective-permute-start | bytes 589832 | tf_op jit(solution)/shard_map/ppermute | solution.py:478
  3.6 1.5 %collective-permute-start.1 = (bf16[64,1536]{1,0:T(8,128)(2,1)}, bf16[64,1536]{1,0:T(8,128)(2,1)S(1)}, u32[]{:S(2)}, u32[]{:S(2)}) collective-permute-start(bf16[64,1536]{1,0:T(8,128)(2,1)} %bitcast.9), channel_id=1, source_target_pairs={{0,16},{8,24},{16,0},{24,8},{1,17},{9,25},{17,1},{25,9},{2,18},{10... | collective-permute-start | bytes 589832 | tf_op jit(solution)/shard_map/ppermute | solution.py:478
  5.2 6.1 %shard_map.76 = (bf16[1024,1536]{1,0:T(8,128)(2,1)S(1)}, bf16[1024,1536]{1,0:T(8,128)(2,1)S(1)}, bf16[1024,1536]{1,0:T(8,128)(2,1)S(1)}, bf16[1024,1536]{1,0:T(8...) custom-call(s32[64]{0:T(128)} %leaf_first.1, s32[64]{0:T(128)} %leaf_owner.1, s32[16,64]{1,0:T(8,128)} %bitcast.12, ...), custom_call_target="tpu_custom_call" | custom-call | flops 3221225472 | bytes 50331648 | tf_op jit(solution)/shard_map/pallas_call | solution.py:241
  11.3 0.0 collective-permute-done.refs_3_
  11.3 0.0 collective-permute-done.1.refs_4_
  11.3 0.6 %collective-permute-start.2 = (bf16[64,768]{1,0:T(8,128)(2,1)S(1)}, bf16[64,768]{1,0:T(8,128)(2,1)S(1)}, u32[]{:S(2)}, u32[]{:S(2)}) collective-permute-start(bf16[64,768]{1,0:T(8,128)(2,1)S(1)} %slice.9), channel_id=1, source_target_pairs={{0,8},{8,0},{16,24},{24,16},{1,9},{9,1},{17,25},{25,17},{2,10},{10... | collective-permute-start | bytes 294920 | tf_op jit(solution)/shard_map/ppermute | solution.py:478
  11.9 0.5 %collective-permute-start.3 = (bf16[64,768]{1,0:T(8,128)(2,1)S(1)}, bf16[64,768]{1,0:T(8,128)(2,1)S(1)}, u32[]{:S(2)}, u32[]{:S(2)}) collective-permute-start(bf16[64,768]{1,0:T(8,128)(2,1)S(1)} %slice.10), channel_id=1, source_target_pairs={{0,16},{8,24},{16,0},{24,8},{1,17},{9,25},{17,1},{25,9},{2,18},{10... | collective-permute-start | bytes 294920 | tf_op jit(solution)/shard_map/ppermute | solution.py:478
  12.4 4.4 %shard_map.77.begun = f32[1024,128]{1,0:T(8,128)S(1)} custom-call(bf16[64,1536]{1,0:T(8,128)(2,1)} %bitcast.10, bf16[1024,1536]{1,0:T(8,128)(2,1)S(1)} %get-tuple-element.27.refs_0_, bf16[1024,1536]{1,0:T(8,128)(2,1)S(1)} %get-tuple-element.28.refs_1_, bf16[1024,1536]{1,0:T(8,128)(2,1)S(1)} %get-tuple-element.29.refs_2_, ...), custom_call_target="tpu_custom_call" | custom-call | flops 2415919104 | bytes 37748736 | tf_op jit(solution)/shard_map/pallas_call | solution.py:268
  16.8 0.0 collective-permute-done.2.left
  16.8 0.0 collective-permute-done.3.right
  16.8 1.5 %shard_map.78 = (f32[512,128]{1,0:T(8,128)S(1)}, f32[512,128]{1,0:T(8,128)S(1)}) custom-call(s32[32]{0:T(128)S(1)} %get-tuple-element.24.place_row, s32[32]{0:T(128)S(1)} %get-tuple-element.25.place_kind, bf16[1024,1536]{1,0:T(8,128)(2,1)S(1)} %get-tuple-element.26.block, f32[1024,128]{1,0:T(8,128)S(1)} %shard_map.77.begun, ...), custom_call_target="tpu_custom_call" | custom-call | flops 805306368 | bytes 12582912 | tf_op jit(solution)/shard_map/pallas_call | solution.py:282
  18.3 0.1 collective-permute-start.4
  18.4 1.5 %collective-permute-done.4.swapped = f32[512,128]{1,0:T(8,128)S(1)} collective-permute-done((f32[512,128]{1,0:T(8,128)S(1)}, f32[512,128]{1,0:T(8,128)S(1)}, u32[]{:S(2)}, u32[]{:S(2)}) %collective-permute-start.4) | collective-permute-done | bytes 262176 | tf_op jit(solution)/shard_map/ppermute | solution.py:478
  19.9 0.2 shard_map.79
  20.1 3.7 %collective-permute-start.5 = (s16[144,128]{1,0:T(8,128)(2,1)S(1)}, s16[144,128]{1,0:T(8,128)(2,1)S(1)}, u32[]{:S(2)}, u32[]{:S(2)}) collective-permute-start(s16[144,128]{1,0:T(8,128)(2,1)S(1)} %get-tuple-element.35), channel_id=1, source_target_pairs={{0,6},{1,7},{2,4},{3,5},{4,2},{5,3},{6,0},{7,1},{8,14},{9,15},{10,... | collective-permute-start | bytes 110600 | tf_op jit(solution)/shard_map/ppermute | solution.py:478
  23.8 0.0 collective-permute-start.6
  23.8 0.8 %collective-permute-start.7 = (s16[144,128]{1,0:T(8,128)(2,1)S(1)}, s16[144,128]{1,0:T(8,128)(2,1)S(1)}, u32[]{:S(2)}, u32[]{:S(2)}) collective-permute-start(s16[144,128]{1,0:T(8,128)(2,1)S(1)} %get-tuple-element.37), channel_id=1, source_target_pairs={{0,2},{1,3},{2,0},{3,1},{4,6},{5,7},{6,4},{7,5},{8,10},{9,11},{10,... | collective-permute-start | bytes 110600 | tf_op jit(solution)/shard_map/ppermute | solution.py:478
  24.6 1.4 %collective-permute-done.5.refs_1_ = s16[144,128]{1,0:T(8,128)(2,1)S(1)} collective-permute-done((s16[144,128]{1,0:T(8,128)(2,1)S(1)}, s16[144,128]{1,0:T(8,128)(2,1)S(1)}, u32[]{:S(2)}, u32[]{:S(2)}) %collective-permute-start.5) | collective-permute-done | bytes 36896 | tf_op jit(solution)/shard_map/ppermute | solution.py:478
  25.9 2.7 %collective-permute-done.6.refs_2_ = s16[144,128]{1,0:T(8,128)(2,1)S(1)} collective-permute-done((s16[144,128]{1,0:T(8,128)(2,1)S(1)}, s16[144,128]{1,0:T(8,128)(2,1)S(1)}, u32[]{:S(2)}, u32[]{:S(2)}) %collective-permute-start.6) | collective-permute-done | bytes 36896 | tf_op jit(solution)/shard_map/ppermute | solution.py:478
  28.6 0.0 collective-permute-done.7.refs_3_
  28.6 2.1 %shard_map.80 = (f32[64,256]{1,0:T(8,128)}, f32[16,256]{1,0:T(8,128)}, f32[1,128]{1,0:T(1,128)S(1)}) custom-call(s32[72]{0:T(128)S(1)} %get-tuple-element.23.plan, f32[128,128]{1,0:T(8,128)S(1)} %get-tuple-element.34.refs_0_, s16[144,128]{1,0:T(8,128)(2,1)S(1)} %collective-permute-done.5.refs_1_, s16[144,128]{1,0:T(8,128)(2,1)S(1)} %collective-permute-done.6.refs_2_, ...), custom_call_target="tpu_custom_call" | custom-call | tf_op jit(solution)/shard_map/pallas_call | solution.py:456
  30.8 10.5 %all_to_all.5 = f32[32,1,128]{2,1,0:T(1,128)S(1)} all-to-all(f32[32,1,128]{2,1,0:T(1,128)S(1)} %broadcast_in_dim.9), channel_id=1, replica_groups=mesh['row'=4,'col'=8] {'row','col'}, dimensions={0} | all-to-all | bytes 32768 | tf_op jit(solution)/shard_map/all_to_all | solution.py:484
  41.3 0.5 %reduce_max.11 = f32[128]{0:T(128)} reduce(f32[32,1,128]{2,0,1:T(8,128)S(1)} %bitcast.11, f32[]{:T(128)} %constant.0.clone.1), dimensions={0,1}, to_apply=%region_0.0 | reduce | flops 3968 | bytes 16900 | tf_op jit(solution)/shard_map/reduce_max | solution.py:484
  (3 shorter events, 0.0 us)
Async XLA Ops:
  0.6 10.6 %collective-permute-start = (bf16[64,1536]{1,0:T(8,128)(2,1)}, bf16[64,1536]{1,0:T(8,128)(2,1)S(1)}, u32[]{:S(2)}, u32[]{:S(2)}) collective-permute-start(bf16[64,1536]{1,0:T(8,128)(2,1)} %bitcast.8), channel_id=1, source_target_pairs={{0,8},{8,0},{16,24},{24,16},{1,9},{9,1},{17,25},{25,17},{2,10},{10... | collective-permute-start | bytes 589832 | tf_op jit(solution)/shard_map/ppermute | solution.py:478
  3.6 7.6 %collective-permute-start.1 = (bf16[64,1536]{1,0:T(8,128)(2,1)}, bf16[64,1536]{1,0:T(8,128)(2,1)S(1)}, u32[]{:S(2)}, u32[]{:S(2)}) collective-permute-start(bf16[64,1536]{1,0:T(8,128)(2,1)} %bitcast.9), channel_id=1, source_target_pairs={{0,16},{8,24},{16,0},{24,8},{1,17},{9,25},{17,1},{25,9},{2,18},{10... | collective-permute-start | bytes 589832 | tf_op jit(solution)/shard_map/ppermute | solution.py:478
  11.3 5.5 %collective-permute-start.2 = (bf16[64,768]{1,0:T(8,128)(2,1)S(1)}, bf16[64,768]{1,0:T(8,128)(2,1)S(1)}, u32[]{:S(2)}, u32[]{:S(2)}) collective-permute-start(bf16[64,768]{1,0:T(8,128)(2,1)S(1)} %slice.9), channel_id=1, source_target_pairs={{0,8},{8,0},{16,24},{24,16},{1,9},{9,1},{17,25},{25,17},{2,10},{10... | collective-permute-start | bytes 294920 | tf_op jit(solution)/shard_map/ppermute | solution.py:478
  11.9 4.9 %collective-permute-start.3 = (bf16[64,768]{1,0:T(8,128)(2,1)S(1)}, bf16[64,768]{1,0:T(8,128)(2,1)S(1)}, u32[]{:S(2)}, u32[]{:S(2)}) collective-permute-start(bf16[64,768]{1,0:T(8,128)(2,1)S(1)} %slice.10), channel_id=1, source_target_pairs={{0,16},{8,24},{16,0},{24,8},{1,17},{9,25},{17,1},{25,9},{2,18},{10... | collective-permute-start | bytes 294920 | tf_op jit(solution)/shard_map/ppermute | solution.py:478
  18.3 1.6 %collective-permute-start.4 = (f32[512,128]{1,0:T(8,128)S(1)}, f32[512,128]{1,0:T(8,128)S(1)}, u32[]{:S(2)}, u32[]{:S(2)}) collective-permute-start(f32[512,128]{1,0:T(8,128)S(1)} %get-tuple-element.33), channel_id=1, source_target_pairs={{0,1},{1,0},{2,3},{3,2},{4,5},{5,4},{6,7},{7,6},{8,9},{9,8},{10,11... | collective-permute-start | bytes 786440 | tf_op jit(solution)/shard_map/ppermute | solution.py:478
  20.1 5.8 %collective-permute-start.5 = (s16[144,128]{1,0:T(8,128)(2,1)S(1)}, s16[144,128]{1,0:T(8,128)(2,1)S(1)}, u32[]{:S(2)}, u32[]{:S(2)}) collective-permute-start(s16[144,128]{1,0:T(8,128)(2,1)S(1)} %get-tuple-element.35), channel_id=1, source_target_pairs={{0,6},{1,7},{2,4},{3,5},{4,2},{5,3},{6,0},{7,1},{8,14},{9,15},{10,... | collective-permute-start | bytes 110600 | tf_op jit(solution)/shard_map/ppermute | solution.py:478
  23.8 4.9 %collective-permute-start.6 = (s16[144,128]{1,0:T(8,128)(2,1)S(1)}, s16[144,128]{1,0:T(8,128)(2,1)S(1)}, u32[]{:S(2)}, u32[]{:S(2)}) collective-permute-start(s16[144,128]{1,0:T(8,128)(2,1)S(1)} %get-tuple-element.36), channel_id=1, source_target_pairs={{0,4},{1,5},{2,6},{3,7},{4,0},{5,1},{6,2},{7,3},{8,12},{9,13},{10,... | collective-permute-start | bytes 110600 | tf_op jit(solution)/shard_map/ppermute | solution.py:478
  23.8 4.9 %collective-permute-start.7 = (s16[144,128]{1,0:T(8,128)(2,1)S(1)}, s16[144,128]{1,0:T(8,128)(2,1)S(1)}, u32[]{:S(2)}, u32[]{:S(2)}) collective-permute-start(s16[144,128]{1,0:T(8,128)(2,1)S(1)} %get-tuple-element.37), channel_id=1, source_target_pairs={{0,2},{1,3},{2,0},{3,1},{4,6},{5,7},{6,4},{7,5},{8,10},{9,11},{10,... | collective-permute-start | bytes 110600 | tf_op jit(solution)/shard_map/ppermute | solution.py:478

commit v11 on v10

--- a/solution.py
+++ b/solution.py
@@ -127,8 +127,9 @@
     plan[LEAF_MOST] = count
 
 
-def bring_kernel(n_row, n_col, leaf_first, leaf_owner, skeleton, frontal, *refs):
-    *blocks, place_row, place_kind, plan, first, owners, skel, edges, used, sems, block_sems = refs
+def bring_kernel(n_row, n_col, leaf_first, leaf_owner, skeleton, own, frontal, *refs):
+    *blocks, near, place_row, place_kind, plan = refs[: n_row + 4]
+    first, owners, skel, edges, used, sems, block_sems = refs[n_row + 4 :]
     group_rows, width = frontal.shape
     leaves = leaf_first.shape[0]
     per_group = leaves // n_row
@@ -141,6 +142,7 @@
         pltpu.make_async_copy(leaf_first, first, sems.at[0]),
         pltpu.make_async_copy(leaf_owner, owners, sems.at[1]),
         pltpu.make_async_copy(skeleton, skel, sems.at[2]),
+        pltpu.make_async_copy(own, near, sems.at[3]),
     ]
     for turn, block in enumerate(blocks):
         copies.extend(bring_block(frontal, turn, block, block_sems.at[turn]))
@@ -181,16 +183,11 @@
     clear_runs(run_rows, width, edges, range(len(blocks)), blocks)
 
 
-def near_kernel(own, *refs):
-    *blocks, one, two, total, near, sem = refs
-    own_copy = pltpu.make_async_copy(own, near, sem)
-    own_copy.start()
-    items = [(blocks[1], 0, one), (blocks[2], 0, two)]
+def near_kernel(*refs):
+    *blocks, own, one, two, total = refs
+    items = [(block, 0, slab) for block, slab in zip(blocks, (own, one, two))]
     for rows in parts_of(total.shape[0]):
         total[rows, :] = multiply(items, None, rows)
-    own_copy.wait()
-    for rows in parts_of(total.shape[0]):
-        total[rows, :] = multiply([(blocks[0], 0, near)], total[rows, :], rows)
 
 
 def last_kernel(place_row, place_kind, block, begun, left, right, keep, swap):
@@ -233,17 +230,19 @@
     return pl.CostEstimate(flops=flops, bytes_accessed=flops // samples, transcendentals=0)
 
 
-def bring(frontal, leaf_first, leaf_owner, skeleton, depth, n_row, n_col):
+def bring(frontal, own, leaf_first, leaf_owner, skeleton, n_row, n_col):
     group_rows, width = frontal.shape
+    depth = own.shape[1]
     leaves = leaf_first.shape[0]
     units = jax.ShapeDtypeStruct((group_rows // UNIT,), jnp.int32)
     block = jax.ShapeDtypeStruct((group_rows, depth), frontal.dtype)
     return pl.pallas_call(
         functools.partial(bring_kernel, n_row, n_col),
-        in_specs=[hbm()] * 4,
-        out_specs=vmem(n_row) + [smem()] * 3,
+        in_specs=[hbm()] * 5,
+        out_specs=vmem(n_row + 1) + [smem()] * 3,
         out_shape=[block] * n_row
         + [
+            jax.ShapeDtypeStruct(own.shape, own.dtype),
             units,
             units,
             jax.ShapeDtypeStruct((PICKS + LEAF_MOST * skeleton.shape[0],), jnp.int32),
@@ -254,26 +253,25 @@
             pltpu.SMEM(skeleton.shape, jnp.int32),
             pltpu.SMEM((leaves // n_row,), jnp.int32),
             pltpu.SMEM((n_col,), jnp.int32),
-            pltpu.SemaphoreType.DMA((3,)),
+            pltpu.SemaphoreType.DMA((4,)),
             pltpu.SemaphoreType.DMA((n_row, COPIES)),
         ],
         cost_estimate=product_cost(frontal, 64, 4),
         compiler_params=pltpu.CompilerParams(vmem_limit_bytes=24 * 2**20),
-    )(*(in_hbm(x) for x in (leaf_first, leaf_owner, skeleton, frontal)))
-
-
-def near_product(own, blocks, one, two):
+    )(*(in_hbm(x) for x in (leaf_first, leaf_owner, skeleton, own, frontal)))
+
+
+def near_product(blocks, slabs):
     group_rows = blocks[0].shape[0]
-    samples = own.shape[0]
+    samples = slabs[0].shape[0]
     return pl.pallas_call(
         near_kernel,
-        in_specs=[hbm()] + vmem(len(blocks) + 2),
+        in_specs=vmem(2 * len(blocks)),
         out_specs=vmem(),
         out_shape=jax.ShapeDtypeStruct((group_rows, 2 * samples), jnp.float32),
-        scratch_shapes=[pltpu.VMEM(own.shape, own.dtype), pltpu.SemaphoreType.DMA],
         cost_estimate=product_cost(blocks[0], samples, 12),
         compiler_params=pltpu.CompilerParams(vmem_limit_bytes=24 * 2**20),
-    )(in_hbm(own), *blocks, one, two)
+    )(*blocks, *slabs)
 
 
 def last_product(block, begun, places, last, n_col):
@@ -492,12 +490,12 @@
     cut = depth // 2 // LANES * LANES
     one = exchange(own, "row", 1)
     two = exchange(own, "row", 2)
-    *blocks, block_last, place_row, place_kind, plan = bring(
-        frontal, leaf_first, leaf_owner, skeleton.T, depth, n_row, n_col
+    *blocks, block_last, near, place_row, place_kind, plan = bring(
+        frontal, own, leaf_first, leaf_owner, skeleton.T, n_row, n_col
     )
     one, two, plan = lax.optimization_barrier((one, two, plan))
     last = [exchange(two[:, :cut], "row", 1), exchange(one[:, cut:], "row", 2)]
-    begun = near_product(own, blocks, one, two)
+    begun = near_product(blocks, (near, one, two))
     keep, swap = last_product(block_last, begun, (place_row, place_kind), last, n_col)
     swapped = exchange(swap, "col", 1)
     here, *away = squeeze(keep, swapped, n_col // 2)

time: 42 us -> 41.4 us (0.986)
  Pallas kernels: 14.3 us -> 12.6 us
  waiting for transfers between devices: 5.61 us -> 6.5 us
    pallas_call x1, Pallas kernels: 4.35 us -> 2.59 us  [near_product(): pl.pallas_call(near_kernel, in_specs=vmem(2 * len(blocks)), out_specs=vme...]
    ppermute x8, waiting for transfers between devices: 5.61 us -> 6.5 us  [exchange(): return lax.ppermute(value, axis, pairs)]
  transfers between devices with their start and end apart: 8 -> 8, of which waited for: 3 -> 5; matrix products, arithmetic and copies ran while one was open for 0% -> 0% of each run, Pallas kernels for 25% -> 21%
where the time goes in v11:
time: 41.4 us; the launch traced here: 41.2 us
  Pallas kernels  12.6 us (30%)
  blocking collectives  10.8 us (26%)
  starting transfers between devices  10.1 us (24%)
  waiting for transfers between devices  6.5 us (16%)
  between operations  0.72 us (2%)
  other arithmetic  0.53 us (1%)
    all_to_all x1, blocking collectives, largest(): return jnp.max(lax.all_to_all(every, axis, 0, 0), axis=0)  10.8 us
    ppermute x8, starting transfers between devices, exchange(): return lax.ppermute(value, axis, pairs)  10.1 us
    ppermute x8, waiting for transfers between devices, exchange(): return lax.ppermute(value, axis, pairs)  6.5 us
    pallas_call x1, Pallas kernels, bring(): pl.pallas_call(functools.partial(bring_kernel, n_row, n_col), in_specs=[h...  6.16 us
    pallas_call x1, Pallas kernels, near_product(): pl.pallas_call(near_kernel, in_specs=vmem(2 * len(blocks)), out_specs=vme...  2.59 us
    pallas_call x1, Pallas kernels, leaf_work(): pl.pallas_call(functools.partial(leaf_kernel, skel), in_specs=[smem()] +...  2.13 us
    pallas_call x1, Pallas kernels, last_product(): pl.pallas_call(last_kernel, in_specs=[smem()] * 2 + vmem(4), out_specs=vm...  1.51 us
  transfers between devices with their start and end apart: 8, of which 5 were waited for; matrix products, arithmetic and copies ran while one was open for 0% of the time, Pallas kernels for 21%

profile of v11, /device:TPU:0, one launch (start us, length us, event | category | flops | bytes accessed | tf_op | source)
XLA Modules:
  0.0 41.2 jit_solution(16690132738779750364)
XLA Ops:
  0.6 3.0 %collective-permute-start = (bf16[64,1536]{1,0:T(8,128)(2,1)}, bf16[64,1536]{1,0:T(8,128)(2,1)S(1)}, u32[]{:S(2)}, u32[]{:S(2)}) collective-permute-start(bf16[64,1536]{1,0:T(8,128)(2,1)} %bitcast.8), channel_id=1, source_target_pairs={{0,8},{8,0},{16,24},{24,16},{1,9},{9,1},{17,25},{25,17},{2,10},{10... | collective-permute-start | bytes 589832 | tf_op jit(solution)/shard_map/ppermute | solution.py:476
  3.6 1.5 %collective-permute-start.1 = (bf16[64,1536]{1,0:T(8,128)(2,1)}, bf16[64,1536]{1,0:T(8,128)(2,1)S(1)}, u32[]{:S(2)}, u32[]{:S(2)}) collective-permute-start(bf16[64,1536]{1,0:T(8,128)(2,1)} %bitcast.9), channel_id=1, source_target_pairs={{0,16},{8,24},{16,0},{24,8},{1,17},{9,25},{17,1},{25,9},{2,18},{10... | collective-permute-start | bytes 589832 | tf_op jit(solution)/shard_map/ppermute | solution.py:476
  5.2 6.2 %shard_map.76 = (bf16[1024,1536]{1,0:T(8,128)(2,1)S(1)}, bf16[1024,1536]{1,0:T(8,128)(2,1)S(1)}, bf16[1024,1536]{1,0:T(8,128)(2,1)S(1)}, bf16[1024,1536]{1,0:T(8...) custom-call(s32[64]{0:T(128)} %leaf_first.1, s32[64]{0:T(128)} %leaf_owner.1, ...), custom_call_target="tpu_custom_call" | custom-call | flops 3221225472 | bytes 50331648 | tf_op jit(solution)/shard_map/pallas_call | solution.py:239
  11.3 0.0 collective-permute-done.refs_4_
  11.3 0.0 collective-permute-done.1.refs_5_
  11.4 0.6 %collective-permute-start.2 = (bf16[64,768]{1,0:T(8,128)(2,1)S(1)}, bf16[64,768]{1,0:T(8,128)(2,1)S(1)}, u32[]{:S(2)}, u32[]{:S(2)}) collective-permute-start(bf16[64,768]{1,0:T(8,128)(2,1)S(1)} %slice.9), channel_id=1, source_target_pairs={{0,8},{8,0},{16,24},{24,16},{1,9},{9,1},{17,25},{25,17},{2,10},{10... | collective-permute-start | bytes 294920 | tf_op jit(solution)/shard_map/ppermute | solution.py:476
  12.0 0.4 %collective-permute-start.3 = (bf16[64,768]{1,0:T(8,128)(2,1)S(1)}, bf16[64,768]{1,0:T(8,128)(2,1)S(1)}, u32[]{:S(2)}, u32[]{:S(2)}) collective-permute-start(bf16[64,768]{1,0:T(8,128)(2,1)S(1)} %slice.10), channel_id=1, source_target_pairs={{0,16},{8,24},{16,0},{24,8},{1,17},{9,25},{17,1},{25,9},{2,18},{10... | collective-permute-start | bytes 294920 | tf_op jit(solution)/shard_map/ppermute | solution.py:476
  12.4 2.6 %shard_map.77.begun = f32[1024,128]{1,0:T(8,128)S(1)} custom-call(bf16[1024,1536]{1,0:T(8,128)(2,1)S(1)} %get-tuple-element.28.refs_0_, bf16[1024,1536]{1,0:T(8,128)(2,1)S(1)} %get-tuple-element.29.refs_1_, bf16[1024,1536]{1,0:T(8,128)(2,1)S(1)} %get-tuple-element.30.refs_2_, bf16[64,1536]{1,0:T(8,128)(2,1)S(1)} %get-tuple-element.31.refs_3_, ...), custom_call_target="tpu_custom_call" | custom-call | flops 2415919104 | bytes 37748736 | tf_op jit(solution)/shard_map/pallas_call | solution.py:267
  15.0 1.0 %collective-permute-done.2.left = bf16[64,768]{1,0:T(8,128)(2,1)S(1)} collective-permute-done((bf16[64,768]{1,0:T(8,128)(2,1)S(1)}, bf16[64,768]{1,0:T(8,128)(2,1)S(1)}, u32[]{:S(2)}, u32[]{:S(2)}) %collective-permute-start.2) | collective-permute-done | bytes 98336 | tf_op jit(solution)/shard_map/ppermute | solution.py:476
  16.0 0.6 %collective-permute-done.3.right = bf16[64,768]{1,0:T(8,128)(2,1)S(1)} collective-permute-done((bf16[64,768]{1,0:T(8,128)(2,1)S(1)}, bf16[64,768]{1,0:T(8,128)(2,1)S(1)}, u32[]{:S(2)}, u32[]{:S(2)}) %collective-permute-start.3) | collective-permute-done | bytes 98336 | tf_op jit(solution)/shard_map/ppermute | solution.py:476
  16.7 1.5 %shard_map.78 = (f32[512,128]{1,0:T(8,128)S(1)}, f32[512,128]{1,0:T(8,128)S(1)}) custom-call(s32[32]{0:T(128)S(1)} %get-tuple-element.25.place_row, s32[32]{0:T(128)S(1)} %get-tuple-element.26.place_kind, bf16[1024,1536]{1,0:T(8,128)(2,1)S(1)} %get-tuple-element.27.block, f32[1024,128]{1,0:T(8,128)S(1)} %shard_map.77.begun, ...), custom_call_target="tpu_custom_call" | custom-call | flops 805306368 | bytes 12582912 | tf_op jit(solution)/shard_map/pallas_call | solution.py:280
  18.2 0.1 collective-permute-start.4
  18.2 1.5 %collective-permute-done.4.swapped = f32[512,128]{1,0:T(8,128)S(1)} collective-permute-done((f32[512,128]{1,0:T(8,128)S(1)}, f32[512,128]{1,0:T(8,128)S(1)}, u32[]{:S(2)}, u32[]{:S(2)}) %collective-permute-start.4) | collective-permute-done | bytes 262176 | tf_op jit(solution)/shard_map/ppermute | solution.py:476
  19.8 0.2 shard_map.79
  20.0 2.9 %collective-permute-start.5 = (s16[144,128]{1,0:T(8,128)(2,1)S(1)}, s16[144,128]{1,0:T(8,128)(2,1)S(1)}, u32[]{:S(2)}, u32[]{:S(2)}) collective-permute-start(s16[144,128]{1,0:T(8,128)(2,1)S(1)} %get-tuple-element.37), channel_id=1, source_target_pairs={{0,6},{1,7},{2,4},{3,5},{4,2},{5,3},{6,0},{7,1},{8,14},{9,15},{10,... | collective-permute-start | bytes 110600 | tf_op jit(solution)/shard_map/ppermute | solution.py:476
  22.9 0.0 collective-permute-start.6
  22.9 1.5 %collective-permute-start.7 = (s16[144,128]{1,0:T(8,128)(2,1)S(1)}, s16[144,128]{1,0:T(8,128)(2,1)S(1)}, u32[]{:S(2)}, u32[]{:S(2)}) collective-permute-start(s16[144,128]{1,0:T(8,128)(2,1)S(1)} %get-tuple-element.39), channel_id=1, source_target_pairs={{0,2},{1,3},{2,0},{3,1},{4,6},{5,7},{6,4},{7,5},{8,10},{9,11},{10,... | collective-permute-start | bytes 110600 | tf_op jit(solution)/shard_map/ppermute | solution.py:476
  24.4 1.7 %collective-permute-done.5.refs_1_ = s16[144,128]{1,0:T(8,128)(2,1)S(1)} collective-permute-done((s16[144,128]{1,0:T(8,128)(2,1)S(1)}, s16[144,128]{1,0:T(8,128)(2,1)S(1)}, u32[]{:S(2)}, u32[]{:S(2)}) %collective-permute-start.5) | collective-permute-done | bytes 36896 | tf_op jit(solution)/shard_map/ppermute | solution.py:476
  26.1 1.6 %collective-permute-done.6.refs_2_ = s16[144,128]{1,0:T(8,128)(2,1)S(1)} collective-permute-done((s16[144,128]{1,0:T(8,128)(2,1)S(1)}, s16[144,128]{1,0:T(8,128)(2,1)S(1)}, u32[]{:S(2)}, u32[]{:S(2)}) %collective-permute-start.6) | collective-permute-done | bytes 36896 | tf_op jit(solution)/shard_map/ppermute | solution.py:476
  27.7 0.0 collective-permute-done.7.refs_3_
  27.7 2.1 %shard_map.80 = (f32[64,256]{1,0:T(8,128)}, f32[16,256]{1,0:T(8,128)}, f32[1,128]{1,0:T(1,128)S(1)}) custom-call(s32[72]{0:T(128)S(1)} %get-tuple-element.24.plan, f32[128,128]{1,0:T(8,128)S(1)} %get-tuple-element.36.refs_0_, s16[144,128]{1,0:T(8,128)(2,1)S(1)} %collective-permute-done.5.refs_1_, s16[144,128]{1,0:T(8,128)(2,1)S(1)} %collective-permute-done.6.refs_2_, ...), custom_call_target="tpu_custom_call" | custom-call | tf_op jit(solution)/shard_map/pallas_call | solution.py:454
  29.9 10.8 %all_to_all.5 = f32[32,1,128]{2,1,0:T(1,128)S(1)} all-to-all(f32[32,1,128]{2,1,0:T(1,128)S(1)} %broadcast_in_dim.9), channel_id=1, replica_groups=mesh['row'=4,'col'=8] {'row','col'}, dimensions={0} | all-to-all | bytes 32768 | tf_op jit(solution)/shard_map/all_to_all | solution.py:482
  40.7 0.5 %reduce_max.11 = f32[128]{0:T(128)} reduce(f32[32,1,128]{2,0,1:T(8,128)S(1)} %bitcast.11, f32[]{:T(128)} %constant.0.clone.1), dimensions={0,1}, to_apply=%region_0.0 | reduce | flops 3968 | bytes 16900 | tf_op jit(solution)/shard_map/reduce_max | solution.py:482
  (3 shorter events, 0.0 us)
Async XLA Ops:
  0.6 10.7 %collective-permute-start = (bf16[64,1536]{1,0:T(8,128)(2,1)}, bf16[64,1536]{1,0:T(8,128)(2,1)S(1)}, u32[]{:S(2)}, u32[]{:S(2)}) collective-permute-start(bf16[64,1536]{1,0:T(8,128)(2,1)} %bitcast.8), channel_id=1, source_target_pairs={{0,8},{8,0},{16,24},{24,16},{1,9},{9,1},{17,25},{25,17},{2,10},{10... | collective-permute-start | bytes 589832 | tf_op jit(solution)/shard_map/ppermute | solution.py:476
  3.6 7.7 %collective-permute-start.1 = (bf16[64,1536]{1,0:T(8,128)(2,1)}, bf16[64,1536]{1,0:T(8,128)(2,1)S(1)}, u32[]{:S(2)}, u32[]{:S(2)}) collective-permute-start(bf16[64,1536]{1,0:T(8,128)(2,1)} %bitcast.9), channel_id=1, source_target_pairs={{0,16},{8,24},{16,0},{24,8},{1,17},{9,25},{17,1},{25,9},{2,18},{10... | collective-permute-start | bytes 589832 | tf_op jit(solution)/shard_map/ppermute | solution.py:476
  11.4 4.7 %collective-permute-start.2 = (bf16[64,768]{1,0:T(8,128)(2,1)S(1)}, bf16[64,768]{1,0:T(8,128)(2,1)S(1)}, u32[]{:S(2)}, u32[]{:S(2)}) collective-permute-start(bf16[64,768]{1,0:T(8,128)(2,1)S(1)} %slice.9), channel_id=1, source_target_pairs={{0,8},{8,0},{16,24},{24,16},{1,9},{9,1},{17,25},{25,17},{2,10},{10... | collective-permute-start | bytes 294920 | tf_op jit(solution)/shard_map/ppermute | solution.py:476
  12.0 4.7 %collective-permute-start.3 = (bf16[64,768]{1,0:T(8,128)(2,1)S(1)}, bf16[64,768]{1,0:T(8,128)(2,1)S(1)}, u32[]{:S(2)}, u32[]{:S(2)}) collective-permute-start(bf16[64,768]{1,0:T(8,128)(2,1)S(1)} %slice.10), channel_id=1, source_target_pairs={{0,16},{8,24},{16,0},{24,8},{1,17},{9,25},{17,1},{25,9},{2,18},{10... | collective-permute-start | bytes 294920 | tf_op jit(solution)/shard_map/ppermute | solution.py:476
  18.2 1.6 %collective-permute-start.4 = (f32[512,128]{1,0:T(8,128)S(1)}, f32[512,128]{1,0:T(8,128)S(1)}, u32[]{:S(2)}, u32[]{:S(2)}) collective-permute-start(f32[512,128]{1,0:T(8,128)S(1)} %get-tuple-element.35), channel_id=1, source_target_pairs={{0,1},{1,0},{2,3},{3,2},{4,5},{5,4},{6,7},{7,6},{8,9},{9,8},{10,11... | collective-permute-start | bytes 786440 | tf_op jit(solution)/shard_map/ppermute | solution.py:476
  20.0 6.1 %collective-permute-start.5 = (s16[144,128]{1,0:T(8,128)(2,1)S(1)}, s16[144,128]{1,0:T(8,128)(2,1)S(1)}, u32[]{:S(2)}, u32[]{:S(2)}) collective-permute-start(s16[144,128]{1,0:T(8,128)(2,1)S(1)} %get-tuple-element.37), channel_id=1, source_target_pairs={{0,6},{1,7},{2,4},{3,5},{4,2},{5,3},{6,0},{7,1},{8,14},{9,15},{10,... | collective-permute-start | bytes 110600 | tf_op jit(solution)/shard_map/ppermute | solution.py:476
  22.9 4.9 %collective-permute-start.6 = (s16[144,128]{1,0:T(8,128)(2,1)S(1)}, s16[144,128]{1,0:T(8,128)(2,1)S(1)}, u32[]{:S(2)}, u32[]{:S(2)}) collective-permute-start(s16[144,128]{1,0:T(8,128)(2,1)S(1)} %get-tuple-element.38), channel_id=1, source_target_pairs={{0,4},{1,5},{2,6},{3,7},{4,0},{5,1},{6,2},{7,3},{8,12},{9,13},{10,... | collective-permute-start | bytes 110600 | tf_op jit(solution)/shard_map/ppermute | solution.py:476
  22.9 4.9 %collective-permute-start.7 = (s16[144,128]{1,0:T(8,128)(2,1)S(1)}, s16[144,128]{1,0:T(8,128)(2,1)S(1)}, u32[]{:S(2)}, u32[]{:S(2)}) collective-permute-start(s16[144,128]{1,0:T(8,128)(2,1)S(1)} %get-tuple-element.39), channel_id=1, source_target_pairs={{0,2},{1,3},{2,0},{3,1},{4,6},{5,7},{6,4},{7,5},{8,10},{9,11},{10,... | collective-permute-start | bytes 110600 | tf_op jit(solution)/shard_map/ppermute | solution.py:476

commit v12 on v11

--- a/solution.py
+++ b/solution.py
@@ -11,7 +11,7 @@
 LANES = 128
 LEAF_MOST = 4
 PICKS = 8
-COPIES = 1
+COPIES = 4
 LEVELS = 32760.0
 EXTRA = 16
 PART = 1024
@@ -27,7 +27,6 @@
     group_rows = edges.shape[0] // RUN_LEAVES * run_rows
     row_pos = lax.axis_index("row")
     first_col = lax.axis_index("col") * width
-    depth = width // lax.axis_size("row")
 
     def one(at, carry):
         run = at // (run_rows // LANES)
@@ -48,7 +47,7 @@
                 leaf_across += (across >= edge).astype(jnp.int32)
             column = jnp.clip(inside, 0, width - LANES)
             rows = pl.ds(pl.multiple_of(run * run_rows, run_rows), run_rows)
-            act((column // depth) ^ row_pos, rows, column, leaf_down == leaf_across)
+            act(rows, column, leaf_down == leaf_across)
 
         return carry
 
@@ -63,30 +62,18 @@
     return value
 
 
-def clear_runs(run_rows, width, edges, turns, blocks):
-    def act(here, rows, column, same):
-        for turn, block in zip(turns, blocks):
-
-            @pl.when(here == turn)
-            def _():
-                inside = lax.rem(column, block.shape[1])
-                lanes = pl.ds(pl.multiple_of(inside, LANES), LANES)
-                part = block[rows, lanes].astype(jnp.float32)
-                block[rows, lanes] = jnp.where(same, 0.0, part).astype(jnp.bfloat16)
-
-    leaf_blocks(run_rows, width, edges, act)
-
-
-def bring_block(frontal, turn, block, sems):
-    group_rows, depth = block.shape
-    begin = pl.multiple_of((lax.axis_index("row") ^ turn) * depth, LANES)
-    part = group_rows // COPIES
-    copies = []
-    for at in range(COPIES):
-        rows = pl.ds(at * part, part)
-        piece = frontal.at[rows, pl.ds(begin, depth)]
-        copies.append(pltpu.make_async_copy(piece, block.at[rows, :], sems.at[at]))
-    return copies
+def clear_runs(run_rows, edges, held):
+    def act(rows, column, same):
+        lanes = pl.ds(pl.multiple_of(column, LANES), LANES)
+        part = held[rows, lanes].astype(jnp.float32)
+        held[rows, lanes] = jnp.where(same, 0.0, part).astype(jnp.bfloat16)
+
+    leaf_blocks(run_rows, held.shape[1], edges, act)
+
+
+def columns_of(turn, width):
+    depth = width // lax.axis_size("row")
+    return pl.multiple_of((lax.axis_index("row") ^ turn) * depth, LANES)
 
 
 def parts_of(group_rows):
@@ -128,8 +115,7 @@
 
 
 def bring_kernel(n_row, n_col, leaf_first, leaf_owner, skeleton, own, frontal, *refs):
-    *blocks, near, place_row, place_kind, plan = refs[: n_row + 4]
-    first, owners, skel, edges, used, sems, block_sems = refs[n_row + 4 :]
+    held, near, place_row, place_kind, plan, first, owners, skel, edges, used, sems, row_sems = refs
     group_rows, width = frontal.shape
     leaves = leaf_first.shape[0]
     per_group = leaves // n_row
@@ -144,8 +130,10 @@
         pltpu.make_async_copy(skeleton, skel, sems.at[2]),
         pltpu.make_async_copy(own, near, sems.at[3]),
     ]
-    for turn, block in enumerate(blocks):
-        copies.extend(bring_block(frontal, turn, block, block_sems.at[turn]))
+    part = group_rows // COPIES
+    for at in range(COPIES):
+        rows = pl.ds(at * part, part)
+        copies.append(pltpu.make_async_copy(frontal.at[rows, :], held.at[rows, :], row_sems.at[at]))
     for copy in copies:
         copy.start()
 
@@ -180,23 +168,25 @@
     plan_leaves(n_row, group_rows, 2 * half, first, owners, skel, plan)
     for copy in copies[3:]:
         copy.wait()
-    clear_runs(run_rows, width, edges, range(len(blocks)), blocks)
-
-
-def near_kernel(*refs):
-    *blocks, own, one, two, total = refs
-    items = [(block, 0, slab) for block, slab in zip(blocks, (own, one, two))]
+    clear_runs(run_rows, edges, held)
+
+
+def near_kernel(held, own, one, two, total):
+    width = held.shape[1]
+    items = [(held, columns_of(turn, width), slab) for turn, slab in enumerate((own, one, two))]
     for rows in parts_of(total.shape[0]):
         total[rows, :] = multiply(items, None, rows)
 
 
-def last_kernel(place_row, place_kind, block, begun, left, right, keep, swap):
-    items = [(block, 0, left), (block, left.shape[1], right)]
+def last_kernel(place_row, place_kind, held, begun, left, right, keep, swap):
+    begin = columns_of(3, held.shape[1])
+    after = pl.multiple_of(begin + left.shape[1], LANES)
+    items = [(held, begin, left), (held, after, right)]
     wide = keep.shape[1]
     lane = lax.broadcasted_iota(jnp.int32, (UNIT, wide), 1) // (wide // 2)
     keep[...] = jnp.zeros(keep.shape, jnp.float32)
     swap[...] = jnp.zeros(swap.shape, jnp.float32)
-    for rows in parts_of(block.shape[0]):
+    for rows in parts_of(held.shape[0]):
         value = multiply(items, begun[rows, :], rows)
         for at in range(rows.size // UNIT):
             unit = rows.start // UNIT + at
@@ -232,16 +222,14 @@
 
 def bring(frontal, own, leaf_first, leaf_owner, skeleton, n_row, n_col):
     group_rows, width = frontal.shape
-    depth = own.shape[1]
     leaves = leaf_first.shape[0]
     units = jax.ShapeDtypeStruct((group_rows // UNIT,), jnp.int32)
-    block = jax.ShapeDtypeStruct((group_rows, depth), frontal.dtype)
     return pl.pallas_call(
         functools.partial(bring_kernel, n_row, n_col),
         in_specs=[hbm()] * 5,
-        out_specs=vmem(n_row + 1) + [smem()] * 3,
-        out_shape=[block] * n_row
-        + [
+        out_specs=vmem(2) + [smem()] * 3,
+        out_shape=[
+            jax.ShapeDtypeStruct(frontal.shape, frontal.dtype),
             jax.ShapeDtypeStruct(own.shape, own.dtype),
             units,
             units,
@@ -254,27 +242,26 @@
             pltpu.SMEM((leaves // n_row,), jnp.int32),
             pltpu.SMEM((n_col,), jnp.int32),
             pltpu.SemaphoreType.DMA((4,)),
-            pltpu.SemaphoreType.DMA((n_row, COPIES)),
+            pltpu.SemaphoreType.DMA((COPIES,)),
         ],
         cost_estimate=product_cost(frontal, 64, 4),
         compiler_params=pltpu.CompilerParams(vmem_limit_bytes=24 * 2**20),
     )(*(in_hbm(x) for x in (leaf_first, leaf_owner, skeleton, own, frontal)))
 
 
-def near_product(blocks, slabs):
-    group_rows = blocks[0].shape[0]
+def near_product(held, slabs):
     samples = slabs[0].shape[0]
     return pl.pallas_call(
         near_kernel,
-        in_specs=vmem(2 * len(blocks)),
+        in_specs=vmem(1 + len(slabs)),
         out_specs=vmem(),
-        out_shape=jax.ShapeDtypeStruct((group_rows, 2 * samples), jnp.float32),
-        cost_estimate=product_cost(blocks[0], samples, 12),
+        out_shape=jax.ShapeDtypeStruct((held.shape[0], 2 * samples), jnp.float32),
+        cost_estimate=product_cost(held, samples, 3),
         compiler_params=pltpu.CompilerParams(vmem_limit_bytes=24 * 2**20),
-    )(*blocks, *slabs)
-
-
-def last_product(block, begun, places, last, n_col):
+    )(held, *slabs)
+
+
+def last_product(held, begun, places, last, n_col):
     group_rows, wide = begun.shape
     laid = jax.ShapeDtypeStruct((group_rows // 2, wide), jnp.float32)
     return pl.pallas_call(
@@ -282,9 +269,9 @@
         in_specs=[smem()] * 2 + vmem(4),
         out_specs=vmem(2),
         out_shape=[laid, laid],
-        cost_estimate=product_cost(block, wide // 2, 4),
+        cost_estimate=product_cost(held, wide // 2, 1),
         compiler_params=pltpu.CompilerParams(vmem_limit_bytes=24 * 2**20),
-    )(*places, block, begun, *last)
+    )(*places, held, begun, *last)
 
 
 def squeeze_kernel(keep, swapped, here, *away):
@@ -477,9 +464,11 @@
 
 
 def largest(value, axis):
-    size = lax.axis_size(axis)
-    every = jnp.broadcast_to(value[None], (size, *value.shape))
-    return jnp.max(lax.all_to_all(every, axis, 0, 0), axis=0)
+    flip = 1
+    while flip < lax.axis_size(axis):
+        value = jnp.maximum(value, exchange(value, axis, flip))
+        flip *= 2
+    return value
 
 
 def local(frontal, sample_cols, leaf_first, leaf_owner, skeleton):
@@ -490,18 +479,18 @@
     cut = depth // 2 // LANES * LANES
     one = exchange(own, "row", 1)
     two = exchange(own, "row", 2)
-    *blocks, block_last, near, place_row, place_kind, plan = bring(
+    held, near, place_row, place_kind, plan = bring(
         frontal, own, leaf_first, leaf_owner, skeleton.T, n_row, n_col
     )
     one, two, plan = lax.optimization_barrier((one, two, plan))
     last = [exchange(two[:, :cut], "row", 1), exchange(one[:, cut:], "row", 2)]
-    begun = near_product(blocks, (near, one, two))
-    keep, swap = last_product(block_last, begun, (place_row, place_kind), last, n_col)
+    begun = near_product(held, (near, one, two))
+    keep, swap = last_product(held, begun, (place_row, place_kind), last, n_col)
     swapped = exchange(swap, "col", 1)
     here, *away = squeeze(keep, swapped, n_col // 2)
     parts = [exchange(away[k - 1], "col", 2 * k) for k in range(n_col // 2 - 1, 0, -1)]
     mine, coeff, worst = leaf_work(here, parts, plan)
-    worst = largest(worst, ("row", "col"))
+    worst = largest(largest(worst, "row"), "col")
     return (mine, coeff, worst[0, :1])
 
 

time: 41.4 us -> 46.8 us (1.13)
  waiting for transfers between devices: 6.5 us -> 17.5 us
  blocking collectives: 10.8 us -> 0 us
  starting transfers between devices: 10.1 us -> 15.5 us
    ppermute x8 -> x13, waiting for transfers between devices: 6.5 us -> 17.5 us  [exchange(): return lax.ppermute(value, axis, pairs)]
    all_to_all x1 -> x0, blocking collectives: 10.8 us -> none  [largest(): return jnp.max(lax.all_to_all(every, axis, 0, 0), axis=0)]
    ppermute x8 -> x13, starting transfers between devices: 10.1 us -> 15.5 us  [exchange(): return lax.ppermute(value, axis, pairs)]
    reduce_max x1 -> x0, other arithmetic: 0.53 us -> none  [largest(): return jnp.max(lax.all_to_all(every, axis, 0, 0), axis=0)]
    max x0 -> x5, other arithmetic: none -> 0.53 us  [largest(): value = jnp.maximum(value, exchange(value, axis, flip))]
  transfers between devices with their start and end apart: 8 -> 13, of which waited for: 5 -> 10; matrix products, arithmetic and copies ran while one was open for 0% -> 0% of each run, Pallas kernels for 21% -> 18%
where the time goes in v12:
time: 46.8 us; the launch traced here: 46.6 us
  waiting for transfers between devices  17.5 us (37%)
  starting transfers between devices  15.5 us (33%)
  Pallas kernels  12.4 us (26%)
  between operations  0.71 us (2%)
  other arithmetic  0.53 us (1%)
    ppermute x13, waiting for transfers between devices, exchange(): return lax.ppermute(value, axis, pairs)  17.5 us
    ppermute x13, starting transfers between devices, exchange(): return lax.ppermute(value, axis, pairs)  15.5 us
    pallas_call x1, Pallas kernels, bring(): pl.pallas_call(functools.partial(bring_kernel, n_row, n_col), in_specs=[h...  6.01 us
    pallas_call x1, Pallas kernels, near_product(): pl.pallas_call(near_kernel, in_specs=vmem(1 + len(slabs)), out_specs=vmem...  2.58 us
    pallas_call x1, Pallas kernels, leaf_work(): pl.pallas_call(functools.partial(leaf_kernel, skel), in_specs=[smem()] +...  2.12 us
    pallas_call x1, Pallas kernels, last_product(): pl.pallas_call(last_kernel, in_specs=[smem()] * 2 + vmem(4), out_specs=vm...  1.52 us
  transfers between devices with their start and end apart: 13, of which 10 were waited for; matrix products, arithmetic and copies ran while one was open for 0% of the time, Pallas kernels for 18%

profile of v12, /device:TPU:0, one launch (start us, length us, event | category | flops | bytes accessed | tf_op | source)
XLA Modules:
  0.0 46.6 jit_solution(17905136367309262309)
XLA Ops:
  0.6 3.0 %collective-permute-start = (bf16[64,1536]{1,0:T(8,128)(2,1)}, bf16[64,1536]{1,0:T(8,128)(2,1)S(1)}, u32[]{:S(2)}, u32[]{:S(2)}) collective-permute-start(bf16[64,1536]{1,0:T(8,128)(2,1)} %bitcast.4), channel_id=1, source_target_pairs={{0,8},{8,0},{16,24},{24,16},{1,9},{9,1},{17,25},{25,17},{2,10},{10... | collective-permute-start | bytes 589832 | tf_op jit(solution)/shard_map/ppermute | solution.py:463
  3.6 1.5 %collective-permute-start.1 = (bf16[64,1536]{1,0:T(8,128)(2,1)}, bf16[64,1536]{1,0:T(8,128)(2,1)S(1)}, u32[]{:S(2)}, u32[]{:S(2)}) collective-permute-start(bf16[64,1536]{1,0:T(8,128)(2,1)} %bitcast.5), channel_id=1, source_target_pairs={{0,16},{8,24},{16,0},{24,8},{1,17},{9,25},{17,1},{25,9},{2,18},{10... | collective-permute-start | bytes 589832 | tf_op jit(solution)/shard_map/ppermute | solution.py:463
  5.2 6.0 %shard_map.76 = (bf16[1024,6144]{1,0:T(8,128)(2,1)S(1)}, bf16[64,1536]{1,0:T(8,128)(2,1)S(1)}, s32[32]{0:T(128)S(1)}, s32[32]{0:T(128)S(1)}, s32[72]{0:T(128)S(1)}) custom-call(s32[64]{0:T(128)} %leaf_first.1, s32[64]{0:T(128)} %leaf_owner.1, s32[16,64]{1,0:T(8,128)} %bitcast.7, bf16[64,1536]{1,0:T(8,128)(2,1)} %bitcast.6, bf16[1024,6144]{1,0:T(8,128)(2,1)} %frontal.1), custom_call_target="tpu_custom_call" | custom-call | flops 3221225472 | bytes 50331648 | tf_op jit(solution)/shard_map/pallas_call | solution.py:227
  11.2 0.0 collective-permute-done.one
  11.2 0.0 collective-permute-done.1.two
  11.2 0.6 %collective-permute-start.2 = (bf16[64,768]{1,0:T(8,128)(2,1)S(1)}, bf16[64,768]{1,0:T(8,128)(2,1)S(1)}, u32[]{:S(2)}, u32[]{:S(2)}) collective-permute-start(bf16[64,768]{1,0:T(8,128)(2,1)S(1)} %slice.9), channel_id=1, source_target_pairs={{0,8},{8,0},{16,24},{24,16},{1,9},{9,1},{17,25},{25,17},{2,10},{10... | collective-permute-start | bytes 294920 | tf_op jit(solution)/shard_map/ppermute | solution.py:463
  11.8 0.6 %collective-permute-start.3 = (bf16[64,768]{1,0:T(8,128)(2,1)S(1)}, bf16[64,768]{1,0:T(8,128)(2,1)S(1)}, u32[]{:S(2)}, u32[]{:S(2)}) collective-permute-start(bf16[64,768]{1,0:T(8,128)(2,1)S(1)} %slice.10), channel_id=1, source_target_pairs={{0,16},{8,24},{16,0},{24,8},{1,17},{9,25},{17,1},{25,9},{2,18},{10... | collective-permute-start | bytes 294920 | tf_op jit(solution)/shard_map/ppermute | solution.py:463
  12.4 2.6 %shard_map.77.begun = f32[1024,128]{1,0:T(8,128)S(1)} custom-call(bf16[1024,6144]{1,0:T(8,128)(2,1)S(1)} %get-tuple-element.24.held, bf16[64,1536]{1,0:T(8,128)(2,1)S(1)} %get-tuple-element.25.own, bf16[64,1536]{1,0:T(8,128)(2,1)S(1)} %collective-permute-done.one, bf16[64,1536]{1,0:T(8,128)(2,1)S(1)} %collective-permute-done.1.two), custom_call_target="tpu_custom_call" | custom-call | flops 2415919104 | bytes 37748736 | tf_op jit(solution)/shard_map/pallas_call | solution.py:254
  15.0 0.9 %collective-permute-done.2.left = bf16[64,768]{1,0:T(8,128)(2,1)S(1)} collective-permute-done((bf16[64,768]{1,0:T(8,128)(2,1)S(1)}, bf16[64,768]{1,0:T(8,128)(2,1)S(1)}, u32[]{:S(2)}, u32[]{:S(2)}) %collective-permute-start.2) | collective-permute-done | bytes 98336 | tf_op jit(solution)/shard_map/ppermute | solution.py:463
  15.9 0.6 %collective-permute-done.3.right = bf16[64,768]{1,0:T(8,128)(2,1)S(1)} collective-permute-done((bf16[64,768]{1,0:T(8,128)(2,1)S(1)}, bf16[64,768]{1,0:T(8,128)(2,1)S(1)}, u32[]{:S(2)}, u32[]{:S(2)}) %collective-permute-start.3) | collective-permute-done | bytes 98336 | tf_op jit(solution)/shard_map/ppermute | solution.py:463
  16.5 1.5 %shard_map.78 = (f32[512,128]{1,0:T(8,128)S(1)}, f32[512,128]{1,0:T(8,128)S(1)}) custom-call(s32[32]{0:T(128)S(1)} %get-tuple-element.22.place_row, s32[32]{0:T(128)S(1)} %get-tuple-element.23.place_kind, bf16[1024,6144]{1,0:T(8,128)(2,1)S(1)} %get-tuple-element.24.held, f32[1024,128]{1,0:T(8,128)S(1)} %shard_map.77.begun, ...), custom_call_target="tpu_custom_call" | custom-call | flops 805306368 | bytes 12582912 | tf_op jit(solution)/shard_map/pallas_call | solution.py:267
  18.0 0.1 collective-permute-start.4
  18.1 1.5 %collective-permute-done.4.swapped = f32[512,128]{1,0:T(8,128)S(1)} collective-permute-done((f32[512,128]{1,0:T(8,128)S(1)}, f32[512,128]{1,0:T(8,128)S(1)}, u32[]{:S(2)}, u32[]{:S(2)}) %collective-permute-start.4) | collective-permute-done | bytes 262176 | tf_op jit(solution)/shard_map/ppermute | solution.py:463
  19.6 0.2 shard_map.79
  19.8 3.0 %collective-permute-start.5 = (s16[144,128]{1,0:T(8,128)(2,1)S(1)}, s16[144,128]{1,0:T(8,128)(2,1)S(1)}, u32[]{:S(2)}, u32[]{:S(2)}) collective-permute-start(s16[144,128]{1,0:T(8,128)(2,1)S(1)} %get-tuple-element.31), channel_id=1, source_target_pairs={{0,6},{1,7},{2,4},{3,5},{4,2},{5,3},{6,0},{7,1},{8,14},{9,15},{10,... | collective-permute-start | bytes 110600 | tf_op jit(solution)/shard_map/ppermute | solution.py:463
  22.9 0.0 collective-permute-start.6
  22.9 1.4 %collective-permute-start.7 = (s16[144,128]{1,0:T(8,128)(2,1)S(1)}, s16[144,128]{1,0:T(8,128)(2,1)S(1)}, u32[]{:S(2)}, u32[]{:S(2)}) collective-permute-start(s16[144,128]{1,0:T(8,128)(2,1)S(1)} %get-tuple-element.33), channel_id=1, source_target_pairs={{0,2},{1,3},{2,0},{3,1},{4,6},{5,7},{6,4},{7,5},{8,10},{9,11},{10,... | collective-permute-start | bytes 110600 | tf_op jit(solution)/shard_map/ppermute | solution.py:463
  24.3 1.8 %collective-permute-done.5.refs_1_ = s16[144,128]{1,0:T(8,128)(2,1)S(1)} collective-permute-done((s16[144,128]{1,0:T(8,128)(2,1)S(1)}, s16[144,128]{1,0:T(8,128)(2,1)S(1)}, u32[]{:S(2)}, u32[]{:S(2)}) %collective-permute-start.5) | collective-permute-done | bytes 36896 | tf_op jit(solution)/shard_map/ppermute | solution.py:463
  26.1 1.6 %collective-permute-done.6.refs_2_ = s16[144,128]{1,0:T(8,128)(2,1)S(1)} collective-permute-done((s16[144,128]{1,0:T(8,128)(2,1)S(1)}, s16[144,128]{1,0:T(8,128)(2,1)S(1)}, u32[]{:S(2)}, u32[]{:S(2)}) %collective-permute-start.6) | collective-permute-done | bytes 36896 | tf_op jit(solution)/shard_map/ppermute | solution.py:463
  27.7 0.0 collective-permute-done.7.refs_3_
  27.7 2.1 %shard_map.80 = (f32[64,256]{1,0:T(8,128)}, f32[16,256]{1,0:T(8,128)}, f32[1,128]{1,0:T(1,128)S(1)}) custom-call(s32[72]{0:T(128)S(1)} %get-tuple-element.21.plan, f32[128,128]{1,0:T(8,128)S(1)} %get-tuple-element.30.refs_0_, s16[144,128]{1,0:T(8,128)(2,1)S(1)} %collective-permute-done.5.refs_1_, s16[144,128]{1,0:T(8,128)(2,1)S(1)} %collective-permute-done.6.refs_2_, ...), custom_call_target="tpu_custom_call" | custom-call | tf_op jit(solution)/shard_map/pallas_call | solution.py:441
  29.9 1.6 %collective-permute-start.8 = (f32[1,128]{1,0:T(1,128)S(1)}, f32[1,128]{1,0:T(1,128)S(1)}, u32[]{:S(2)}, u32[]{:S(2)}) collective-permute-start(f32[1,128]{1,0:T(1,128)S(1)} %get-tuple-element.36), channel_id=1, source_target_pairs={{0,8},{8,0},{16,24},{24,16},{1,9},{9,1},{17,25},{25,17},{2,10},{10... | collective-permute-start | bytes 1544 | tf_op jit(solution)/shard_map/ppermute | solution.py:463
  31.4 2.1 %collective-permute-done.8 = f32[1,128]{1,0:T(1,128)S(1)} collective-permute-done((f32[1,128]{1,0:T(1,128)S(1)}, f32[1,128]{1,0:T(1,128)S(1)}, u32[]{:S(2)}, u32[]{:S(2)}) %collective-permute-start.8) | collective-permute-done | bytes 544 | tf_op jit(solution)/shard_map/ppermute | solution.py:463
  33.5 1.1 %collective-permute-start.9 = (f32[1,128]{1,0:T(1,128)S(1)}, f32[1,128]{1,0:T(1,128)S(1)}, u32[]{:S(2)}, u32[]{:S(2)}) collective-permute-start(f32[1,128]{1,0:T(1,128)S(1)} %max.15), channel_id=1, source_target_pairs={{0,16},{8,24},{16,0},{24,8},{1,17},{9,25},{17,1},{25,9},{2,18},{10... | collective-permute-start | bytes 1544 | tf_op jit(solution)/shard_map/ppermute | solution.py:463
  34.6 2.4 %collective-permute-done.9 = f32[1,128]{1,0:T(1,128)S(1)} collective-permute-done((f32[1,128]{1,0:T(1,128)S(1)}, f32[1,128]{1,0:T(1,128)S(1)}, u32[]{:S(2)}, u32[]{:S(2)}) %collective-permute-start.9) | collective-permute-done | bytes 544 | tf_op jit(solution)/shard_map/ppermute | solution.py:463
  37.0 0.0 collective-permute-start.10
  37.0 1.1 %collective-permute-done.10 = f32[1,128]{1,0:T(1,128)S(1)} collective-permute-done((f32[1,128]{1,0:T(1,128)S(1)}, f32[1,128]{1,0:T(1,128)S(1)}, u32[]{:S(2)}, u32[]{:S(2)}) %collective-permute-start.10) | collective-permute-done | bytes 544 | tf_op jit(solution)/shard_map/ppermute | solution.py:463
  38.1 0.5 %collective-permute-start.11 = (f32[1,128]{1,0:T(1,128)S(1)}, f32[1,128]{1,0:T(1,128)S(1)}, u32[]{:S(2)}, u32[]{:S(2)}) collective-permute-start(f32[1,128]{1,0:T(1,128)S(1)} %max.17), channel_id=1, source_target_pairs={{0,2},{1,3},{2,0},{3,1},{4,6},{5,7},{6,4},{7,5},{8,10},{9,11},{10,... | collective-permute-start | bytes 1544 | tf_op jit(solution)/shard_map/ppermute | solution.py:463
  38.6 3.0 %collective-permute-done.11 = f32[1,128]{1,0:T(1,128)S(1)} collective-permute-done((f32[1,128]{1,0:T(1,128)S(1)}, f32[1,128]{1,0:T(1,128)S(1)}, u32[]{:S(2)}, u32[]{:S(2)}) %collective-permute-start.11) | collective-permute-done | bytes 544 | tf_op jit(solution)/shard_map/ppermute | solution.py:463
  41.7 2.0 %collective-permute-start.12 = (f32[1,128]{1,0:T(1,128)S(1)}, f32[1,128]{1,0:T(1,128)S(1)}, u32[]{:S(2)}, u32[]{:S(2)}) collective-permute-start(f32[1,128]{1,0:T(1,128)S(1)} %max.18), channel_id=1, source_target_pairs={{0,4},{1,5},{2,6},{3,7},{4,0},{5,1},{6,2},{7,3},{8,12},{9,13},{10,... | collective-permute-start | bytes 1544 | tf_op jit(solution)/shard_map/ppermute | solution.py:463
  43.7 2.4 %collective-permute-done.12 = f32[1,128]{1,0:T(1,128)S(1)} collective-permute-done((f32[1,128]{1,0:T(1,128)S(1)}, f32[1,128]{1,0:T(1,128)S(1)}, u32[]{:S(2)}, u32[]{:S(2)}) %collective-permute-start.12) | collective-permute-done | bytes 544 | tf_op jit(solution)/shard_map/ppermute | solution.py:463
  46.1 0.5 %max.19 = f32[1,128]{1,0:T(1,128)} maximum(f32[1,128]{1,0:T(1,128)S(1)} %max.18, f32[1,128]{1,0:T(1,128)S(1)} %collective-permute-done.12) | non-fusion elementwise | flops 128 | bytes 1536 | tf_op jit(solution)/shard_map/max | solution.py:469
  (6 shorter events, 0.0 us)
Async XLA Ops:
  0.6 10.5 %collective-permute-start = (bf16[64,1536]{1,0:T(8,128)(2,1)}, bf16[64,1536]{1,0:T(8,128)(2,1)S(1)}, u32[]{:S(2)}, u32[]{:S(2)}) collective-permute-start(bf16[64,1536]{1,0:T(8,128)(2,1)} %bitcast.4), channel_id=1, source_target_pairs={{0,8},{8,0},{16,24},{24,16},{1,9},{9,1},{17,25},{25,17},{2,10},{10... | collective-permute-start | bytes 589832 | tf_op jit(solution)/shard_map/ppermute | solution.py:463
  3.6 7.5 %collective-permute-start.1 = (bf16[64,1536]{1,0:T(8,128)(2,1)}, bf16[64,1536]{1,0:T(8,128)(2,1)S(1)}, u32[]{:S(2)}, u32[]{:S(2)}) collective-permute-start(bf16[64,1536]{1,0:T(8,128)(2,1)} %bitcast.5), channel_id=1, source_target_pairs={{0,16},{8,24},{16,0},{24,8},{1,17},{9,25},{17,1},{25,9},{2,18},{10... | collective-permute-start | bytes 589832 | tf_op jit(solution)/shard_map/ppermute | solution.py:463
  11.2 4.7 %collective-permute-start.2 = (bf16[64,768]{1,0:T(8,128)(2,1)S(1)}, bf16[64,768]{1,0:T(8,128)(2,1)S(1)}, u32[]{:S(2)}, u32[]{:S(2)}) collective-permute-start(bf16[64,768]{1,0:T(8,128)(2,1)S(1)} %slice.9), channel_id=1, source_target_pairs={{0,8},{8,0},{16,24},{24,16},{1,9},{9,1},{17,25},{25,17},{2,10},{10... | collective-permute-start | bytes 294920 | tf_op jit(solution)/shard_map/ppermute | solution.py:463
  11.8 4.7 %collective-permute-start.3 = (bf16[64,768]{1,0:T(8,128)(2,1)S(1)}, bf16[64,768]{1,0:T(8,128)(2,1)S(1)}, u32[]{:S(2)}, u32[]{:S(2)}) collective-permute-start(bf16[64,768]{1,0:T(8,128)(2,1)S(1)} %slice.10), channel_id=1, source_target_pairs={{0,16},{8,24},{16,0},{24,8},{1,17},{9,25},{17,1},{25,9},{2,18},{10... | collective-permute-start | bytes 294920 | tf_op jit(solution)/shard_map/ppermute | solution.py:463
  18.0 1.6 %collective-permute-start.4 = (f32[512,128]{1,0:T(8,128)S(1)}, f32[512,128]{1,0:T(8,128)S(1)}, u32[]{:S(2)}, u32[]{:S(2)}) collective-permute-start(f32[512,128]{1,0:T(8,128)S(1)} %get-tuple-element.29), channel_id=1, source_target_pairs={{0,1},{1,0},{2,3},{3,2},{4,5},{5,4},{6,7},{7,6},{8,9},{9,8},{10,11... | collective-permute-start | bytes 786440 | tf_op jit(solution)/shard_map/ppermute | solution.py:463
  19.8 6.3 %collective-permute-start.5 = (s16[144,128]{1,0:T(8,128)(2,1)S(1)}, s16[144,128]{1,0:T(8,128)(2,1)S(1)}, u32[]{:S(2)}, u32[]{:S(2)}) collective-permute-start(s16[144,128]{1,0:T(8,128)(2,1)S(1)} %get-tuple-element.31), channel_id=1, source_target_pairs={{0,6},{1,7},{2,4},{3,5},{4,2},{5,3},{6,0},{7,1},{8,14},{9,15},{10,... | collective-permute-start | bytes 110600 | tf_op jit(solution)/shard_map/ppermute | solution.py:463
  22.9 4.9 %collective-permute-start.6 = (s16[144,128]{1,0:T(8,128)(2,1)S(1)}, s16[144,128]{1,0:T(8,128)(2,1)S(1)}, u32[]{:S(2)}, u32[]{:S(2)}) collective-permute-start(s16[144,128]{1,0:T(8,128)(2,1)S(1)} %get-tuple-element.32), channel_id=1, source_target_pairs={{0,4},{1,5},{2,6},{3,7},{4,0},{5,1},{6,2},{7,3},{8,12},{9,13},{10,... | collective-permute-start | bytes 110600 | tf_op jit(solution)/shard_map/ppermute | solution.py:463
  22.9 4.9 %collective-permute-start.7 = (s16[144,128]{1,0:T(8,128)(2,1)S(1)}, s16[144,128]{1,0:T(8,128)(2,1)S(1)}, u32[]{:S(2)}, u32[]{:S(2)}) collective-permute-start(s16[144,128]{1,0:T(8,128)(2,1)S(1)} %get-tuple-element.33), channel_id=1, source_target_pairs={{0,2},{1,3},{2,0},{3,1},{4,6},{5,7},{6,4},{7,5},{8,10},{9,11},{10,... | collective-permute-start | bytes 110600 | tf_op jit(solution)/shard_map/ppermute | solution.py:463
  29.9 3.6 %collective-permute-start.8 = (f32[1,128]{1,0:T(1,128)S(1)}, f32[1,128]{1,0:T(1,128)S(1)}, u32[]{:S(2)}, u32[]{:S(2)}) collective-permute-start(f32[1,128]{1,0:T(1,128)S(1)} %get-tuple-element.36), channel_id=1, source_target_pairs={{0,8},{8,0},{16,24},{24,16},{1,9},{9,1},{17,25},{25,17},{2,10},{10... | collective-permute-start | bytes 1544 | tf_op jit(solution)/shard_map/ppermute | solution.py:463
  33.5 3.5 %collective-permute-start.9 = (f32[1,128]{1,0:T(1,128)S(1)}, f32[1,128]{1,0:T(1,128)S(1)}, u32[]{:S(2)}, u32[]{:S(2)}) collective-permute-start(f32[1,128]{1,0:T(1,128)S(1)} %max.15), channel_id=1, source_target_pairs={{0,16},{8,24},{16,0},{24,8},{1,17},{9,25},{17,1},{25,9},{2,18},{10... | collective-permute-start | bytes 1544 | tf_op jit(solution)/shard_map/ppermute | solution.py:463
  37.0 1.1 %collective-permute-start.10 = (f32[1,128]{1,0:T(1,128)S(1)}, f32[1,128]{1,0:T(1,128)S(1)}, u32[]{:S(2)}, u32[]{:S(2)}) collective-permute-start(f32[1,128]{1,0:T(1,128)S(1)} %max.16), channel_id=1, source_target_pairs={{0,1},{1,0},{2,3},{3,2},{4,5},{5,4},{6,7},{7,6},{8,9},{9,8},{10,11... | collective-permute-start | bytes 1544 | tf_op jit(solution)/shard_map/ppermute | solution.py:463
  38.1 3.5 %collective-permute-start.11 = (f32[1,128]{1,0:T(1,128)S(1)}, f32[1,128]{1,0:T(1,128)S(1)}, u32[]{:S(2)}, u32[]{:S(2)}) collective-permute-start(f32[1,128]{1,0:T(1,128)S(1)} %max.17), channel_id=1, source_target_pairs={{0,2},{1,3},{2,0},{3,1},{4,6},{5,7},{6,4},{7,5},{8,10},{9,11},{10,... | collective-permute-start | bytes 1544 | tf_op jit(solution)/shard_map/ppermute | solution.py:463
  41.7 4.4 %collective-permute-start.12 = (f32[1,128]{1,0:T(1,128)S(1)}, f32[1,128]{1,0:T(1,128)S(1)}, u32[]{:S(2)}, u32[]{:S(2)}) collective-permute-start(f32[1,128]{1,0:T(1,128)S(1)} %max.18), channel_id=1, source_target_pairs={{0,4},{1,5},{2,6},{3,7},{4,0},{5,1},{6,2},{7,3},{8,12},{9,13},{10,... | collective-permute-start | bytes 1544 | tf_op jit(solution)/shard_map/ppermute | solution.py:463

commit v13 on v12

--- a/solution.py
+++ b/solution.py
@@ -178,10 +178,16 @@
         total[rows, :] = multiply(items, None, rows)
 
 
-def last_kernel(place_row, place_kind, held, begun, left, right, keep, swap):
-    begin = columns_of(3, held.shape[1])
-    after = pl.multiple_of(begin + left.shape[1], LANES)
-    items = [(held, begin, left), (held, after, right)]
+def left_kernel(held, begun, left, total):
+    items = [(held, columns_of(3, held.shape[1]), left)]
+    for rows in parts_of(total.shape[0]):
+        total[rows, :] = multiply(items, begun[rows, :], rows)
+
+
+def last_kernel(place_row, place_kind, held, begun, right, keep, swap):
+    width = held.shape[1]
+    cut = width // lax.axis_size("row") - right.shape[1]
+    items = [(held, pl.multiple_of(columns_of(3, width) + cut, LANES), right)]
     wide = keep.shape[1]
     lane = lax.broadcasted_iota(jnp.int32, (UNIT, wide), 1) // (wide // 2)
     keep[...] = jnp.zeros(keep.shape, jnp.float32)
@@ -261,17 +267,28 @@
     )(held, *slabs)
 
 
+def left_product(held, begun, left):
+    return pl.pallas_call(
+        left_kernel,
+        in_specs=vmem(3),
+        out_specs=vmem(),
+        out_shape=jax.ShapeDtypeStruct(begun.shape, jnp.float32),
+        cost_estimate=product_cost(held, left.shape[0], 1),
+        compiler_params=pltpu.CompilerParams(vmem_limit_bytes=24 * 2**20),
+    )(held, begun, left)
+
+
 def last_product(held, begun, places, last, n_col):
     group_rows, wide = begun.shape
     laid = jax.ShapeDtypeStruct((group_rows // 2, wide), jnp.float32)
     return pl.pallas_call(
         last_kernel,
-        in_specs=[smem()] * 2 + vmem(4),
+        in_specs=[smem()] * 2 + vmem(3),
         out_specs=vmem(2),
         out_shape=[laid, laid],
         cost_estimate=product_cost(held, wide // 2, 1),
         compiler_params=pltpu.CompilerParams(vmem_limit_bytes=24 * 2**20),
-    )(*places, held, begun, *last)
+    )(*places, held, begun, last)
 
 
 def squeeze_kernel(keep, swapped, here, *away):
@@ -464,11 +481,9 @@
 
 
 def largest(value, axis):
-    flip = 1
-    while flip < lax.axis_size(axis):
-        value = jnp.maximum(value, exchange(value, axis, flip))
-        flip *= 2
-    return value
+    size = lax.axis_size(axis)
+    every = jnp.broadcast_to(value[None], (size, *value.shape))
+    return jnp.max(lax.all_to_all(every, axis, 0, 0), axis=0)
 
 
 def local(frontal, sample_cols, leaf_first, leaf_owner, skeleton):
@@ -483,14 +498,16 @@
         frontal, own, leaf_first, leaf_owner, skeleton.T, n_row, n_col
     )
     one, two, plan = lax.optimization_barrier((one, two, plan))
-    last = [exchange(two[:, :cut], "row", 1), exchange(one[:, cut:], "row", 2)]
+    left = exchange(two[:, :cut], "row", 1)
+    right = exchange(one[:, cut:], "row", 2)
     begun = near_product(held, (near, one, two))
-    keep, swap = last_product(held, begun, (place_row, place_kind), last, n_col)
+    begun = left_product(held, begun, left)
+    keep, swap = last_product(held, begun, (place_row, place_kind), right, n_col)
     swapped = exchange(swap, "col", 1)
     here, *away = squeeze(keep, swapped, n_col // 2)
     parts = [exchange(away[k - 1], "col", 2 * k) for k in range(n_col // 2 - 1, 0, -1)]
     mine, coeff, worst = leaf_work(here, parts, plan)
-    worst = largest(largest(worst, "row"), "col")
+    worst = largest(worst, ("row", "col"))
     return (mine, coeff, worst[0, :1])
 
 

time: 46.8 us -> 40.4 us (0.86)
  waiting for transfers between devices: 17.5 us -> 6.54 us
  blocking collectives: 0 us -> 9.69 us
  starting transfers between devices: 15.5 us -> 10.1 us
    ppermute x13 -> x8, waiting for transfers between devices: 17.5 us -> 6.54 us  [exchange(): return lax.ppermute(value, axis, pairs)]
    all_to_all x0 -> x1, blocking collectives: none -> 9.69 us  [largest(): return jnp.max(lax.all_to_all(every, axis, 0, 0), axis=0)]
    ppermute x13 -> x8, starting transfers between devices: 15.5 us -> 10.1 us  [exchange(): return lax.ppermute(value, axis, pairs)]
    reduce_max x0 -> x1, other arithmetic: none -> 0.53 us  [largest(): return jnp.max(lax.all_to_all(every, axis, 0, 0), axis=0)]
    max x5 -> x0, other arithmetic: 0.53 us -> none  [largest(): value = jnp.maximum(value, exchange(value, axis, flip))]
    pallas_call x1 -> x2, Pallas kernels: 1.52 us -> 1.7 us  [the longest x1 1.13 us: last_product(): pl.pallas_call(last_kernel, in_specs=[smem()] * 2 + vmem(3), out_specs=vm...]
  transfers between devices with their start and end apart: 13 -> 8, of which waited for: 10 -> 4; matrix products, arithmetic and copies ran while one was open for 0% -> 0% of each run, Pallas kernels for 18% -> 23%
where the time goes in v13:
time: 40.4 us; the launch traced here: 40.3 us
  Pallas kernels  12.6 us (31%)
  starting transfers between devices  10.1 us (25%)
  blocking collectives  9.69 us (24%)
  waiting for transfers between devices  6.54 us (16%)
  between operations  0.73 us (2%)
  other arithmetic  0.53 us (1%)
    ppermute x8, starting transfers between devices, exchange(): return lax.ppermute(value, axis, pairs)  10.1 us
    all_to_all x1, blocking collectives, largest(): return jnp.max(lax.all_to_all(every, axis, 0, 0), axis=0)  9.69 us
    ppermute x8, waiting for transfers between devices, exchange(): return lax.ppermute(value, axis, pairs)  6.54 us
    pallas_call x1, Pallas kernels, bring(): pl.pallas_call(functools.partial(bring_kernel, n_row, n_col), in_specs=[h...  6.01 us
    pallas_call x1, Pallas kernels, near_product(): pl.pallas_call(near_kernel, in_specs=vmem(1 + len(slabs)), out_specs=vmem...  2.58 us
    pallas_call x1, Pallas kernels, leaf_work(): pl.pallas_call(functools.partial(leaf_kernel, skel), in_specs=[smem()] +...  2.13 us
    pallas_call x1, Pallas kernels, last_product(): pl.pallas_call(last_kernel, in_specs=[smem()] * 2 + vmem(3), out_specs=vm...  1.13 us
  transfers between devices with their start and end apart: 8, of which 4 were waited for; matrix products, arithmetic and copies ran while one was open for 0% of the time, Pallas kernels for 23%

profile of v13, /device:TPU:0, one launch (start us, length us, event | category | flops | bytes accessed | tf_op | source)
XLA Modules:
  0.0 40.3 jit_solution(16310263882985099813)
XLA Ops:
  0.6 3.0 %collective-permute-start.1 = (bf16[64,1536]{1,0:T(8,128)(2,1)}, bf16[64,1536]{1,0:T(8,128)(2,1)S(1)}, u32[]{:S(2)}, u32[]{:S(2)}) collective-permute-start(bf16[64,1536]{1,0:T(8,128)(2,1)} %bitcast.8), channel_id=1, source_target_pairs={{0,16},{8,24},{16,0},{24,8},{1,17},{9,25},{17,1},{25,9},{2,18},{10... | collective-permute-start | bytes 589832 | tf_op jit(solution)/shard_map/ppermute | solution.py:480
  3.7 1.5 %collective-permute-start = (bf16[64,1536]{1,0:T(8,128)(2,1)}, bf16[64,1536]{1,0:T(8,128)(2,1)S(1)}, u32[]{:S(2)}, u32[]{:S(2)}) collective-permute-start(bf16[64,1536]{1,0:T(8,128)(2,1)} %bitcast.9), channel_id=1, source_target_pairs={{0,8},{8,0},{16,24},{24,16},{1,9},{9,1},{17,25},{25,17},{2,10},{10... | collective-permute-start | bytes 589832 | tf_op jit(solution)/shard_map/ppermute | solution.py:480
  5.2 6.0 %shard_map.76 = (bf16[1024,6144]{1,0:T(8,128)(2,1)S(1)}, bf16[64,1536]{1,0:T(8,128)(2,1)S(1)}, s32[32]{0:T(128)S(1)}, s32[32]{0:T(128)S(1)}, s32[72]{0:T(128)S(1)}) custom-call(s32[64]{0:T(128)} %leaf_first.1, s32[64]{0:T(128)} %leaf_owner.1, s32[16,64]{1,0:T(8,128)} %bitcast.12, bf16[64,1536]{1,0:T(8,128)(2,1)} %bitcast.10, bf16[1024,6144]{1,0:T(8,128)(2,1)} %frontal.1), custom_call_target="tpu_custom_call" | custom-call | flops 3221225472 | bytes 50331648 | tf_op jit(solution)/shard_map/pallas_call | solution.py:233
  11.2 0.0 collective-permute-done.1.two
  11.2 0.0 collective-permute-done.one
  11.2 0.6 %collective-permute-start.2 = (bf16[64,768]{1,0:T(8,128)(2,1)S(1)}, bf16[64,768]{1,0:T(8,128)(2,1)S(1)}, u32[]{:S(2)}, u32[]{:S(2)}) collective-permute-start(bf16[64,768]{1,0:T(8,128)(2,1)S(1)} %slice.9), channel_id=1, source_target_pairs={{0,8},{8,0},{16,24},{24,16},{1,9},{9,1},{17,25},{25,17},{2,10},{10... | collective-permute-start | bytes 294920 | tf_op jit(solution)/shard_map/ppermute | solution.py:480
  11.8 0.5 %collective-permute-start.3 = (bf16[64,768]{1,0:T(8,128)(2,1)S(1)}, bf16[64,768]{1,0:T(8,128)(2,1)S(1)}, u32[]{:S(2)}, u32[]{:S(2)}) collective-permute-start(bf16[64,768]{1,0:T(8,128)(2,1)S(1)} %slice.10), channel_id=1, source_target_pairs={{0,16},{8,24},{16,0},{24,8},{1,17},{9,25},{17,1},{25,9},{2,18},{10... | collective-permute-start | bytes 294920 | tf_op jit(solution)/shard_map/ppermute | solution.py:480
  12.3 2.6 %shard_map.77.begun = f32[1024,128]{1,0:T(8,128)S(1)} custom-call(bf16[1024,6144]{1,0:T(8,128)(2,1)S(1)} %get-tuple-element.24.held, bf16[64,1536]{1,0:T(8,128)(2,1)S(1)} %get-tuple-element.25.own, bf16[64,1536]{1,0:T(8,128)(2,1)S(1)} %collective-permute-done.one, bf16[64,1536]{1,0:T(8,128)(2,1)S(1)} %collective-permute-done.1.two), custom_call_target="tpu_custom_call" | custom-call | flops 2415919104 | bytes 37748736 | tf_op jit(solution)/shard_map/pallas_call | solution.py:260
  14.9 1.0 %collective-permute-done.2.left = bf16[64,768]{1,0:T(8,128)(2,1)S(1)} collective-permute-done((bf16[64,768]{1,0:T(8,128)(2,1)S(1)}, bf16[64,768]{1,0:T(8,128)(2,1)S(1)}, u32[]{:S(2)}, u32[]{:S(2)}) %collective-permute-start.2) | collective-permute-done | bytes 98336 | tf_op jit(solution)/shard_map/ppermute | solution.py:480
  15.9 0.6 %shard_map.78.begun = f32[1024,128]{1,0:T(8,128)S(1)} custom-call(bf16[1024,6144]{1,0:T(8,128)(2,1)S(1)} %get-tuple-element.24.held, f32[1024,128]{1,0:T(8,128)S(1)} %shard_map.77.begun, bf16[64,768]{1,0:T(8,128)(2,1)S(1)} %collective-permute-done.2.left), custom_call_target="tpu_custom_call" | custom-call | flops 805306368 | bytes 12582912 | tf_op jit(solution)/shard_map/pallas_call | solution.py:271
  16.5 0.0 collective-permute-done.3.right
  16.5 1.1 %shard_map.79 = (f32[512,128]{1,0:T(8,128)S(1)}, f32[512,128]{1,0:T(8,128)S(1)}) custom-call(s32[32]{0:T(128)S(1)} %get-tuple-element.22.place_row, s32[32]{0:T(128)S(1)} %get-tuple-element.23.place_kind, bf16[1024,6144]{1,0:T(8,128)(2,1)S(1)} %get-tuple-element.24.held, f32[1024,128]{1,0:T(8,128)S(1)} %shard_map.78.begun, ...), custom_call_target="tpu_custom_call" | custom-call | flops 805306368 | bytes 12582912 | tf_op jit(solution)/shard_map/pallas_call | solution.py:284
  17.6 0.1 collective-permute-start.4
  17.7 1.5 %collective-permute-done.4.swapped = f32[512,128]{1,0:T(8,128)S(1)} collective-permute-done((f32[512,128]{1,0:T(8,128)S(1)}, f32[512,128]{1,0:T(8,128)S(1)}, u32[]{:S(2)}, u32[]{:S(2)}) %collective-permute-start.4) | collective-permute-done | bytes 262176 | tf_op jit(solution)/shard_map/ppermute | solution.py:480
  19.2 0.2 shard_map.80
  19.4 3.6 %collective-permute-start.5 = (s16[144,128]{1,0:T(8,128)(2,1)S(1)}, s16[144,128]{1,0:T(8,128)(2,1)S(1)}, u32[]{:S(2)}, u32[]{:S(2)}) collective-permute-start(s16[144,128]{1,0:T(8,128)(2,1)S(1)} %get-tuple-element.31), channel_id=1, source_target_pairs={{0,6},{1,7},{2,4},{3,5},{4,2},{5,3},{6,0},{7,1},{8,14},{9,15},{10,... | collective-permute-start | bytes 110600 | tf_op jit(solution)/shard_map/ppermute | solution.py:480
  23.0 0.0 collective-permute-start.6
  23.0 0.8 %collective-permute-start.7 = (s16[144,128]{1,0:T(8,128)(2,1)S(1)}, s16[144,128]{1,0:T(8,128)(2,1)S(1)}, u32[]{:S(2)}, u32[]{:S(2)}) collective-permute-start(s16[144,128]{1,0:T(8,128)(2,1)S(1)} %get-tuple-element.33), channel_id=1, source_target_pairs={{0,2},{1,3},{2,0},{3,1},{4,6},{5,7},{6,4},{7,5},{8,10},{9,11},{10,... | collective-permute-start | bytes 110600 | tf_op jit(solution)/shard_map/ppermute | solution.py:480
  23.9 1.4 %collective-permute-done.5.refs_1_ = s16[144,128]{1,0:T(8,128)(2,1)S(1)} collective-permute-done((s16[144,128]{1,0:T(8,128)(2,1)S(1)}, s16[144,128]{1,0:T(8,128)(2,1)S(1)}, u32[]{:S(2)}, u32[]{:S(2)}) %collective-permute-start.5) | collective-permute-done | bytes 36896 | tf_op jit(solution)/shard_map/ppermute | solution.py:480
  25.2 2.6 %collective-permute-done.6.refs_2_ = s16[144,128]{1,0:T(8,128)(2,1)S(1)} collective-permute-done((s16[144,128]{1,0:T(8,128)(2,1)S(1)}, s16[144,128]{1,0:T(8,128)(2,1)S(1)}, u32[]{:S(2)}, u32[]{:S(2)}) %collective-permute-start.6) | collective-permute-done | bytes 36896 | tf_op jit(solution)/shard_map/ppermute | solution.py:480
  27.9 0.0 collective-permute-done.7.refs_3_
  27.9 2.1 %shard_map.81 = (f32[64,256]{1,0:T(8,128)}, f32[16,256]{1,0:T(8,128)}, f32[1,128]{1,0:T(1,128)S(1)}) custom-call(s32[72]{0:T(128)S(1)} %get-tuple-element.21.plan, f32[128,128]{1,0:T(8,128)S(1)} %get-tuple-element.30.refs_0_, s16[144,128]{1,0:T(8,128)(2,1)S(1)} %collective-permute-done.5.refs_1_, s16[144,128]{1,0:T(8,128)(2,1)S(1)} %collective-permute-done.6.refs_2_, ...), custom_call_target="tpu_custom_call" | custom-call | tf_op jit(solution)/shard_map/pallas_call | solution.py:458
  30.0 9.7 %all_to_all.5 = f32[32,1,128]{2,1,0:T(1,128)S(1)} all-to-all(f32[32,1,128]{2,1,0:T(1,128)S(1)} %broadcast_in_dim.9), channel_id=1, replica_groups=mesh['row'=4,'col'=8] {'row','col'}, dimensions={0} | all-to-all | bytes 32768 | tf_op jit(solution)/shard_map/all_to_all | solution.py:486
  39.7 0.5 %reduce_max.11 = f32[128]{0:T(128)} reduce(f32[32,1,128]{2,0,1:T(8,128)S(1)} %bitcast.11, f32[]{:T(128)} %constant.0.clone.1), dimensions={0,1}, to_apply=%region_0.0 | reduce | flops 3968 | bytes 16900 | tf_op jit(solution)/shard_map/reduce_max | solution.py:486
  (3 shorter events, 0.0 us)
Async XLA Ops:
  0.6 10.5 %collective-permute-start.1 = (bf16[64,1536]{1,0:T(8,128)(2,1)}, bf16[64,1536]{1,0:T(8,128)(2,1)S(1)}, u32[]{:S(2)}, u32[]{:S(2)}) collective-permute-start(bf16[64,1536]{1,0:T(8,128)(2,1)} %bitcast.8), channel_id=1, source_target_pairs={{0,16},{8,24},{16,0},{24,8},{1,17},{9,25},{17,1},{25,9},{2,18},{10... | collective-permute-start | bytes 589832 | tf_op jit(solution)/shard_map/ppermute | solution.py:480
  3.7 7.5 %collective-permute-start = (bf16[64,1536]{1,0:T(8,128)(2,1)}, bf16[64,1536]{1,0:T(8,128)(2,1)S(1)}, u32[]{:S(2)}, u32[]{:S(2)}) collective-permute-start(bf16[64,1536]{1,0:T(8,128)(2,1)} %bitcast.9), channel_id=1, source_target_pairs={{0,8},{8,0},{16,24},{24,16},{1,9},{9,1},{17,25},{25,17},{2,10},{10... | collective-permute-start | bytes 589832 | tf_op jit(solution)/shard_map/ppermute | solution.py:480
  11.2 4.7 %collective-permute-start.2 = (bf16[64,768]{1,0:T(8,128)(2,1)S(1)}, bf16[64,768]{1,0:T(8,128)(2,1)S(1)}, u32[]{:S(2)}, u32[]{:S(2)}) collective-permute-start(bf16[64,768]{1,0:T(8,128)(2,1)S(1)} %slice.9), channel_id=1, source_target_pairs={{0,8},{8,0},{16,24},{24,16},{1,9},{9,1},{17,25},{25,17},{2,10},{10... | collective-permute-start | bytes 294920 | tf_op jit(solution)/shard_map/ppermute | solution.py:480
  11.8 4.7 %collective-permute-start.3 = (bf16[64,768]{1,0:T(8,128)(2,1)S(1)}, bf16[64,768]{1,0:T(8,128)(2,1)S(1)}, u32[]{:S(2)}, u32[]{:S(2)}) collective-permute-start(bf16[64,768]{1,0:T(8,128)(2,1)S(1)} %slice.10), channel_id=1, source_target_pairs={{0,16},{8,24},{16,0},{24,8},{1,17},{9,25},{17,1},{25,9},{2,18},{10... | collective-permute-start | bytes 294920 | tf_op jit(solution)/shard_map/ppermute | solution.py:480
  17.6 1.6 %collective-permute-start.4 = (f32[512,128]{1,0:T(8,128)S(1)}, f32[512,128]{1,0:T(8,128)S(1)}, u32[]{:S(2)}, u32[]{:S(2)}) collective-permute-start(f32[512,128]{1,0:T(8,128)S(1)} %get-tuple-element.29), channel_id=1, source_target_pairs={{0,1},{1,0},{2,3},{3,2},{4,5},{5,4},{6,7},{7,6},{8,9},{9,8},{10,11... | collective-permute-start | bytes 786440 | tf_op jit(solution)/shard_map/ppermute | solution.py:480
  19.4 5.8 %collective-permute-start.5 = (s16[144,128]{1,0:T(8,128)(2,1)S(1)}, s16[144,128]{1,0:T(8,128)(2,1)S(1)}, u32[]{:S(2)}, u32[]{:S(2)}) collective-permute-start(s16[144,128]{1,0:T(8,128)(2,1)S(1)} %get-tuple-element.31), channel_id=1, source_target_pairs={{0,6},{1,7},{2,4},{3,5},{4,2},{5,3},{6,0},{7,1},{8,14},{9,15},{10,... | collective-permute-start | bytes 110600 | tf_op jit(solution)/shard_map/ppermute | solution.py:480
  23.0 4.9 %collective-permute-start.6 = (s16[144,128]{1,0:T(8,128)(2,1)S(1)}, s16[144,128]{1,0:T(8,128)(2,1)S(1)}, u32[]{:S(2)}, u32[]{:S(2)}) collective-permute-start(s16[144,128]{1,0:T(8,128)(2,1)S(1)} %get-tuple-element.32), channel_id=1, source_target_pairs={{0,4},{1,5},{2,6},{3,7},{4,0},{5,1},{6,2},{7,3},{8,12},{9,13},{10,... | collective-permute-start | bytes 110600 | tf_op jit(solution)/shard_map/ppermute | solution.py:480
  23.0 4.9 %collective-permute-start.7 = (s16[144,128]{1,0:T(8,128)(2,1)S(1)}, s16[144,128]{1,0:T(8,128)(2,1)S(1)}, u32[]{:S(2)}, u32[]{:S(2)}) collective-permute-start(s16[144,128]{1,0:T(8,128)(2,1)S(1)} %get-tuple-element.33), channel_id=1, source_target_pairs={{0,2},{1,3},{2,0},{3,1},{4,6},{5,7},{6,4},{7,5},{8,10},{9,11},{10,... | collective-permute-start | bytes 110600 | tf_op jit(solution)/shard_map/ppermute | solution.py:480

commit v14 on v13

--- a/solution.py
+++ b/solution.py
@@ -491,7 +491,7 @@
     n_row = lax.axis_size("row")
     own = sample_cols.T
     depth = own.shape[1]
-    cut = depth // 2 // LANES * LANES
+    cut = depth * 3 // 5 // LANES * LANES
     one = exchange(own, "row", 1)
     two = exchange(own, "row", 2)
     held, near, place_row, place_kind, plan = bring(
@@ -505,7 +505,8 @@
     keep, swap = last_product(held, begun, (place_row, place_kind), right, n_col)
     swapped = exchange(swap, "col", 1)
     here, *away = squeeze(keep, swapped, n_col // 2)
-    parts = [exchange(away[k - 1], "col", 2 * k) for k in range(n_col // 2 - 1, 0, -1)]
+    flips = sorted(range(n_col // 2 - 1, 0, -1), key=lambda flip: flip != n_col // 4)
+    parts = [exchange(away[flip - 1], "col", 2 * flip) for flip in flips]
     mine, coeff, worst = leaf_work(here, parts, plan)
     worst = largest(worst, ("row", "col"))
     return (mine, coeff, worst[0, :1])

time: 40.4 us -> 41.7 us (1.032)
  blocking collectives: 9.69 us -> 10.9 us
  waiting for transfers between devices: 6.54 us -> 7.38 us
  starting transfers between devices: 10.1 us -> 9.37 us
    all_to_all x1, blocking collectives: 9.69 us -> 10.9 us  [largest(): return jnp.max(lax.all_to_all(every, axis, 0, 0), axis=0)]
    ppermute x8, waiting for transfers between devices: 6.54 us -> 7.38 us  [exchange(): return lax.ppermute(value, axis, pairs)]
    ppermute x8, starting transfers between devices: 10.1 us -> 9.37 us  [exchange(): return lax.ppermute(value, axis, pairs)]
  transfers between devices with their start and end apart: 8 -> 8, of which waited for: 4 -> 4; matrix products, arithmetic and copies ran while one was open for 0% -> 0% of each run, Pallas kernels for 23% -> 22%
where the time goes in v14:
time: 41.7 us; the launch traced here: 41.6 us
  Pallas kernels  12.6 us (30%)
  blocking collectives  10.9 us (26%)
  starting transfers between devices  9.37 us (22%)
  waiting for transfers between devices  7.38 us (18%)
  between operations  0.73 us (2%)
  other arithmetic  0.53 us (1%)
    all_to_all x1, blocking collectives, largest(): return jnp.max(lax.all_to_all(every, axis, 0, 0), axis=0)  10.9 us
    ppermute x8, starting transfers between devices, exchange(): return lax.ppermute(value, axis, pairs)  9.37 us
    ppermute x8, waiting for transfers between devices, exchange(): return lax.ppermute(value, axis, pairs)  7.38 us
    pallas_call x1, Pallas kernels, bring(): pl.pallas_call(functools.partial(bring_kernel, n_row, n_col), in_specs=[h...  6.01 us
    pallas_call x1, Pallas kernels, near_product(): pl.pallas_call(near_kernel, in_specs=vmem(1 + len(slabs)), out_specs=vmem...  2.58 us
    pallas_call x1, Pallas kernels, leaf_work(): pl.pallas_call(functools.partial(leaf_kernel, skel), in_specs=[smem()] +...  2.13 us
    pallas_call x1, Pallas kernels, last_product(): pl.pallas_call(last_kernel, in_specs=[smem()] * 2 + vmem(3), out_specs=vm...  1.1 us
  transfers between devices with their start and end apart: 8, of which 4 were waited for; matrix products, arithmetic and copies ran while one was open for 0% of the time, Pallas kernels for 22%

profile of v14, /device:TPU:0, one launch (start us, length us, event | category | flops | bytes accessed | tf_op | source)
XLA Modules:
  0.0 41.6 jit_solution(16590363217731606669)
XLA Ops:
  0.6 3.0 %collective-permute-start.1 = (bf16[64,1536]{1,0:T(8,128)(2,1)}, bf16[64,1536]{1,0:T(8,128)(2,1)S(1)}, u32[]{:S(2)}, u32[]{:S(2)}) collective-permute-start(bf16[64,1536]{1,0:T(8,128)(2,1)} %bitcast.8), channel_id=1, source_target_pairs={{0,16},{8,24},{16,0},{24,8},{1,17},{9,25},{17,1},{25,9},{2,18},{10... | collective-permute-start | bytes 589832 | tf_op jit(solution)/shard_map/ppermute | solution.py:480
  3.7 1.5 %collective-permute-start = (bf16[64,1536]{1,0:T(8,128)(2,1)}, bf16[64,1536]{1,0:T(8,128)(2,1)S(1)}, u32[]{:S(2)}, u32[]{:S(2)}) collective-permute-start(bf16[64,1536]{1,0:T(8,128)(2,1)} %bitcast.9), channel_id=1, source_target_pairs={{0,8},{8,0},{16,24},{24,16},{1,9},{9,1},{17,25},{25,17},{2,10},{10... | collective-permute-start | bytes 589832 | tf_op jit(solution)/shard_map/ppermute | solution.py:480
  5.2 6.0 %shard_map.76 = (bf16[1024,6144]{1,0:T(8,128)(2,1)S(1)}, bf16[64,1536]{1,0:T(8,128)(2,1)S(1)}, s32[32]{0:T(128)S(1)}, s32[32]{0:T(128)S(1)}, s32[72]{0:T(128)S(1)}) custom-call(s32[64]{0:T(128)} %leaf_first.1, s32[64]{0:T(128)} %leaf_owner.1, s32[16,64]{1,0:T(8,128)} %bitcast.12, bf16[64,1536]{1,0:T(8,128)(2,1)} %bitcast.10, bf16[1024,6144]{1,0:T(8,128)(2,1)} %frontal.1), custom_call_target="tpu_custom_call" | custom-call | flops 3221225472 | bytes 50331648 | tf_op jit(solution)/shard_map/pallas_call | solution.py:233
  11.2 0.0 collective-permute-done.1.two
  11.2 0.0 collective-permute-done.one
  11.2 0.6 %collective-permute-start.3 = (bf16[64,640]{1,0:T(8,128)(2,1)S(1)}, bf16[64,640]{1,0:T(8,128)(2,1)S(1)}, u32[]{:S(2)}, u32[]{:S(2)}) collective-permute-start(bf16[64,640]{1,0:T(8,128)(2,1)S(1)} %slice.10), channel_id=1, source_target_pairs={{0,16},{8,24},{16,0},{24,8},{1,17},{9,25},{17,1},{25,9},{2,18},{10... | collective-permute-start | bytes 245768 | tf_op jit(solution)/shard_map/ppermute | solution.py:480
  11.8 0.6 %collective-permute-start.2 = (bf16[64,896]{1,0:T(8,128)(2,1)S(1)}, bf16[64,896]{1,0:T(8,128)(2,1)S(1)}, u32[]{:S(2)}, u32[]{:S(2)}) collective-permute-start(bf16[64,896]{1,0:T(8,128)(2,1)S(1)} %slice.9), channel_id=1, source_target_pairs={{0,8},{8,0},{16,24},{24,16},{1,9},{9,1},{17,25},{25,17},{2,10},{10... | collective-permute-start | bytes 344072 | tf_op jit(solution)/shard_map/ppermute | solution.py:480
  12.4 2.6 %shard_map.77.begun = f32[1024,128]{1,0:T(8,128)S(1)} custom-call(bf16[1024,6144]{1,0:T(8,128)(2,1)S(1)} %get-tuple-element.24.held, bf16[64,1536]{1,0:T(8,128)(2,1)S(1)} %get-tuple-element.25.own, bf16[64,1536]{1,0:T(8,128)(2,1)S(1)} %collective-permute-done.one, bf16[64,1536]{1,0:T(8,128)(2,1)S(1)} %collective-permute-done.1.two), custom_call_target="tpu_custom_call" | custom-call | flops 2415919104 | bytes 37748736 | tf_op jit(solution)/shard_map/pallas_call | solution.py:260
  15.0 1.7 %collective-permute-done.2.left = bf16[64,896]{1,0:T(8,128)(2,1)S(1)} collective-permute-done((bf16[64,896]{1,0:T(8,128)(2,1)S(1)}, bf16[64,896]{1,0:T(8,128)(2,1)S(1)}, u32[]{:S(2)}, u32[]{:S(2)}) %collective-permute-start.2) | collective-permute-done | bytes 114720 | tf_op jit(solution)/shard_map/ppermute | solution.py:480
  16.7 0.6 %shard_map.78.begun = f32[1024,128]{1,0:T(8,128)S(1)} custom-call(bf16[1024,6144]{1,0:T(8,128)(2,1)S(1)} %get-tuple-element.24.held, f32[1024,128]{1,0:T(8,128)S(1)} %shard_map.77.begun, bf16[64,896]{1,0:T(8,128)(2,1)S(1)} %collective-permute-done.2.left), custom_call_target="tpu_custom_call" | custom-call | flops 805306368 | bytes 12582912 | tf_op jit(solution)/shard_map/pallas_call | solution.py:271
  17.3 0.0 collective-permute-done.3.right
  17.3 1.1 %shard_map.79 = (f32[512,128]{1,0:T(8,128)S(1)}, f32[512,128]{1,0:T(8,128)S(1)}) custom-call(s32[32]{0:T(128)S(1)} %get-tuple-element.22.place_row, s32[32]{0:T(128)S(1)} %get-tuple-element.23.place_kind, bf16[1024,6144]{1,0:T(8,128)(2,1)S(1)} %get-tuple-element.24.held, f32[1024,128]{1,0:T(8,128)S(1)} %shard_map.78.begun, ...), custom_call_target="tpu_custom_call" | custom-call | flops 805306368 | bytes 12582912 | tf_op jit(solution)/shard_map/pallas_call | solution.py:284
  18.4 0.1 collective-permute-start.4
  18.5 1.5 %collective-permute-done.4.swapped = f32[512,128]{1,0:T(8,128)S(1)} collective-permute-done((f32[512,128]{1,0:T(8,128)S(1)}, f32[512,128]{1,0:T(8,128)S(1)}, u32[]{:S(2)}, u32[]{:S(2)}) %collective-permute-start.4) | collective-permute-done | bytes 262176 | tf_op jit(solution)/shard_map/ppermute | solution.py:480
  20.0 0.2 shard_map.80
  20.2 2.0 %collective-permute-start.5 = (s16[144,128]{1,0:T(8,128)(2,1)S(1)}, s16[144,128]{1,0:T(8,128)(2,1)S(1)}, u32[]{:S(2)}, u32[]{:S(2)}) collective-permute-start(s16[144,128]{1,0:T(8,128)(2,1)S(1)} %get-tuple-element.31), channel_id=1, source_target_pairs={{0,4},{1,5},{2,6},{3,7},{4,0},{5,1},{6,2},{7,3},{8,12},{9,13},{10,... | collective-permute-start | bytes 110600 | tf_op jit(solution)/shard_map/ppermute | solution.py:480
  22.2 1.4 %collective-permute-start.6 = (s16[144,128]{1,0:T(8,128)(2,1)S(1)}, s16[144,128]{1,0:T(8,128)(2,1)S(1)}, u32[]{:S(2)}, u32[]{:S(2)}) collective-permute-start(s16[144,128]{1,0:T(8,128)(2,1)S(1)} %get-tuple-element.32), channel_id=1, source_target_pairs={{0,6},{1,7},{2,4},{3,5},{4,2},{5,3},{6,0},{7,1},{8,14},{9,15},{10,... | collective-permute-start | bytes 110600 | tf_op jit(solution)/shard_map/ppermute | solution.py:480
  23.6 0.2 collective-permute-start.7
  23.8 1.3 %collective-permute-done.5.refs_1_ = s16[144,128]{1,0:T(8,128)(2,1)S(1)} collective-permute-done((s16[144,128]{1,0:T(8,128)(2,1)S(1)}, s16[144,128]{1,0:T(8,128)(2,1)S(1)}, u32[]{:S(2)}, u32[]{:S(2)}) %collective-permute-start.5) | collective-permute-done | bytes 36896 | tf_op jit(solution)/shard_map/ppermute | solution.py:480
  25.1 2.9 %collective-permute-done.6.refs_2_ = s16[144,128]{1,0:T(8,128)(2,1)S(1)} collective-permute-done((s16[144,128]{1,0:T(8,128)(2,1)S(1)}, s16[144,128]{1,0:T(8,128)(2,1)S(1)}, u32[]{:S(2)}, u32[]{:S(2)}) %collective-permute-start.6) | collective-permute-done | bytes 36896 | tf_op jit(solution)/shard_map/ppermute | solution.py:480
  28.0 0.0 collective-permute-done.7.refs_3_
  28.0 2.1 %shard_map.81 = (f32[64,256]{1,0:T(8,128)}, f32[16,256]{1,0:T(8,128)}, f32[1,128]{1,0:T(1,128)S(1)}) custom-call(s32[72]{0:T(128)S(1)} %get-tuple-element.21.plan, f32[128,128]{1,0:T(8,128)S(1)} %get-tuple-element.30.refs_0_, s16[144,128]{1,0:T(8,128)(2,1)S(1)} %collective-permute-done.5.refs_1_, s16[144,128]{1,0:T(8,128)(2,1)S(1)} %collective-permute-done.6.refs_2_, ...), custom_call_target="tpu_custom_call" | custom-call | tf_op jit(solution)/shard_map/pallas_call | solution.py:458
  30.1 10.9 %all_to_all.5 = f32[32,1,128]{2,1,0:T(1,128)S(1)} all-to-all(f32[32,1,128]{2,1,0:T(1,128)S(1)} %broadcast_in_dim.9), channel_id=1, replica_groups=mesh['row'=4,'col'=8] {'row','col'}, dimensions={0} | all-to-all | bytes 32768 | tf_op jit(solution)/shard_map/all_to_all | solution.py:486
  41.0 0.5 %reduce_max.11 = f32[128]{0:T(128)} reduce(f32[32,1,128]{2,0,1:T(8,128)S(1)} %bitcast.11, f32[]{:T(128)} %constant.0.clone.1), dimensions={0,1}, to_apply=%region_0.0 | reduce | flops 3968 | bytes 16900 | tf_op jit(solution)/shard_map/reduce_max | solution.py:486
  (3 shorter events, 0.0 us)
Async XLA Ops:
  0.6 10.5 %collective-permute-start.1 = (bf16[64,1536]{1,0:T(8,128)(2,1)}, bf16[64,1536]{1,0:T(8,128)(2,1)S(1)}, u32[]{:S(2)}, u32[]{:S(2)}) collective-permute-start(bf16[64,1536]{1,0:T(8,128)(2,1)} %bitcast.8), channel_id=1, source_target_pairs={{0,16},{8,24},{16,0},{24,8},{1,17},{9,25},{17,1},{25,9},{2,18},{10... | collective-permute-start | bytes 589832 | tf_op jit(solution)/shard_map/ppermute | solution.py:480
  3.7 7.5 %collective-permute-start = (bf16[64,1536]{1,0:T(8,128)(2,1)}, bf16[64,1536]{1,0:T(8,128)(2,1)S(1)}, u32[]{:S(2)}, u32[]{:S(2)}) collective-permute-start(bf16[64,1536]{1,0:T(8,128)(2,1)} %bitcast.9), channel_id=1, source_target_pairs={{0,8},{8,0},{16,24},{24,16},{1,9},{9,1},{17,25},{25,17},{2,10},{10... | collective-permute-start | bytes 589832 | tf_op jit(solution)/shard_map/ppermute | solution.py:480
  11.2 6.1 %collective-permute-start.3 = (bf16[64,640]{1,0:T(8,128)(2,1)S(1)}, bf16[64,640]{1,0:T(8,128)(2,1)S(1)}, u32[]{:S(2)}, u32[]{:S(2)}) collective-permute-start(bf16[64,640]{1,0:T(8,128)(2,1)S(1)} %slice.10), channel_id=1, source_target_pairs={{0,16},{8,24},{16,0},{24,8},{1,17},{9,25},{17,1},{25,9},{2,18},{10... | collective-permute-start | bytes 245768 | tf_op jit(solution)/shard_map/ppermute | solution.py:480
  11.8 4.9 %collective-permute-start.2 = (bf16[64,896]{1,0:T(8,128)(2,1)S(1)}, bf16[64,896]{1,0:T(8,128)(2,1)S(1)}, u32[]{:S(2)}, u32[]{:S(2)}) collective-permute-start(bf16[64,896]{1,0:T(8,128)(2,1)S(1)} %slice.9), channel_id=1, source_target_pairs={{0,8},{8,0},{16,24},{24,16},{1,9},{9,1},{17,25},{25,17},{2,10},{10... | collective-permute-start | bytes 344072 | tf_op jit(solution)/shard_map/ppermute | solution.py:480
  18.4 1.6 %collective-permute-start.4 = (f32[512,128]{1,0:T(8,128)S(1)}, f32[512,128]{1,0:T(8,128)S(1)}, u32[]{:S(2)}, u32[]{:S(2)}) collective-permute-start(f32[512,128]{1,0:T(8,128)S(1)} %get-tuple-element.29), channel_id=1, source_target_pairs={{0,1},{1,0},{2,3},{3,2},{4,5},{5,4},{6,7},{7,6},{8,9},{9,8},{10,11... | collective-permute-start | bytes 786440 | tf_op jit(solution)/shard_map/ppermute | solution.py:480
  20.2 4.9 %collective-permute-start.5 = (s16[144,128]{1,0:T(8,128)(2,1)S(1)}, s16[144,128]{1,0:T(8,128)(2,1)S(1)}, u32[]{:S(2)}, u32[]{:S(2)}) collective-permute-start(s16[144,128]{1,0:T(8,128)(2,1)S(1)} %get-tuple-element.31), channel_id=1, source_target_pairs={{0,4},{1,5},{2,6},{3,7},{4,0},{5,1},{6,2},{7,3},{8,12},{9,13},{10,... | collective-permute-start | bytes 110600 | tf_op jit(solution)/shard_map/ppermute | solution.py:480
  22.2 5.8 %collective-permute-start.6 = (s16[144,128]{1,0:T(8,128)(2,1)S(1)}, s16[144,128]{1,0:T(8,128)(2,1)S(1)}, u32[]{:S(2)}, u32[]{:S(2)}) collective-permute-start(s16[144,128]{1,0:T(8,128)(2,1)S(1)} %get-tuple-element.32), channel_id=1, source_target_pairs={{0,6},{1,7},{2,4},{3,5},{4,2},{5,3},{6,0},{7,1},{8,14},{9,15},{10,... | collective-permute-start | bytes 110600 | tf_op jit(solution)/shard_map/ppermute | solution.py:480
  23.6 4.4 %collective-permute-start.7 = (s16[144,128]{1,0:T(8,128)(2,1)S(1)}, s16[144,128]{1,0:T(8,128)(2,1)S(1)}, u32[]{:S(2)}, u32[]{:S(2)}) collective-permute-start(s16[144,128]{1,0:T(8,128)(2,1)S(1)} %get-tuple-element.33), channel_id=1, source_target_pairs={{0,2},{1,3},{2,0},{3,1},{4,6},{5,7},{6,4},{7,5},{8,10},{9,11},{10,... | collective-permute-start | bytes 110600 | tf_op jit(solution)/shard_map/ppermute | solution.py:480
